TPU v7x, 128 devices: a whole 4x4x4 slice. The times are simulated.
128 devices in a mesh: rep: 8 (over x, z_hi), fsdp: 16 (over z_lo, y, core).
Axes of the slice: x: 4, y: 4, z: 4 (z_hi: 2, z_lo: 2; z = z_hi * 2 + z_lo), core: 2. Of those that a mesh axis runs over, the one named last changes fastest.
Arguments:
- deltas: bfloat16 [8, 8192, 1024], P('rep', 'fsdp'), may hold values from -3 to 3
- outer_weights: float32 [16, 8, 64, 1024], P('fsdp', 'rep'), may hold values from -6 to 6
- momentum: float32 [16, 8, 64, 1024], P('fsdp', 'rep'), may hold values from -3 to 3
- tokens: bfloat16 [65536, 8192], P(('rep', 'fsdp')), may hold values from -24 to 24
- key_cot: bfloat16 [65536, 1024], P(('rep', 'fsdp')), may hold values from -6 to 6
Outputs:
- new_outer: float32 [16, 8, 64, 1024], P('fsdp', 'rep')
- new_moment: float32 [16, 8, 64, 1024], P('fsdp', 'rep')
- new_weights: bfloat16 [8192, 1024], P('fsdp')
- keys: bfloat16 [65536, 1024], P(('rep', 'fsdp'))
- token_grad: bfloat16 [65536, 8192], P(('rep', 'fsdp'))
- weight_grad: float32 [8, 8192, 1024], P('rep', 'fsdp')
All inputs are finite; a program needn't handle non-finite values.
Results may differ from a plain program's by a relative error of at most 0.02.
Values may be sent and summed in bfloat16 or wider, within the bound.
No kernel may reach another device: no remote copies, remote signals or barrier semaphores. Data moves between devices by JAX's collectives and lax.ppermute only.
A program may use at most 192 MiB of HBM per device.

v0:
```python
import jax
import jax.numpy as jnp
from jax import lax
from jax.sharding import PartitionSpec as P

MOMENTUM_RATE = 0.9
OUTER_RATE = 0.7


def fold_maker(source, key_cot, weight_piece):
    key_sum = jnp.dot(source, weight_piece, preferred_element_type=jnp.float32)
    back_cols = lax.dot_general(
        key_cot, weight_piece, (((1,), (1,)), ((), ())), preferred_element_type=jnp.float32
    )
    return (key_sum, back_cols)


def per_device(deltas, outer_weights, momentum, tokens, key_cot):
    replicas = lax.axis_size("rep")
    summed = lax.psum_scatter(
        deltas[0].astype(jnp.float32).astype(jnp.bfloat16), "rep", scatter_dimension=0, tiled=True
    ).astype(jnp.float32)
    mean_delta = summed / replicas
    moment_next = MOMENTUM_RATE * momentum[0, 0] + mean_delta
    outer_next = outer_weights[0, 0] - OUTER_RATE * (mean_delta + MOMENTUM_RATE * moment_next)
    owned_rows = outer_next.astype(jnp.bfloat16)
    shard_weights = lax.all_gather(owned_rows, "rep", axis=0, tiled=True)
    unit_scale = tokens.shape[1] ** (-0.5)
    key_sum, back_sum = fold_maker(
        tokens, key_cot, lax.all_gather(shard_weights, "fsdp", axis=0, tiled=True)
    )
    keys_out = (key_sum * unit_scale).astype(jnp.bfloat16)
    grad_tokens = (back_sum * unit_scale).astype(jnp.bfloat16)
    grad_shard = lax.psum_scatter(
        (
            lax.dot_general(
                tokens, key_cot, (((0,), (0,)), ((), ())), preferred_element_type=jnp.float32
            )
            * unit_scale
        ).astype(jnp.bfloat16),
        "fsdp",
        scatter_dimension=0,
        tiled=True,
    ).astype(jnp.float32)
    return (
        outer_next[None, None],
        moment_next[None, None],
        shard_weights,
        keys_out,
        grad_tokens,
        grad_shard[None],
    )


def solution(mesh):
    return jax.shard_map(
        per_device,
        mesh=mesh,
        in_specs=(
            P("rep", "fsdp", None),
            P("fsdp", "rep", None, None),
            P("fsdp", "rep", None, None),
            P(("rep", "fsdp"), None),
            P(("rep", "fsdp"), None),
        ),
        out_specs=(
            P("fsdp", "rep", None, None),
            P("fsdp", "rep", None, None),
            P("fsdp", None),
            P(("rep", "fsdp"), None),
            P(("rep", "fsdp"), None),
            P("rep", "fsdp", None),
        ),
        check_vma=False,
    )
```

profile of v0, /device:TPU:1, one launch (start us, length us, event | category | flops | bytes accessed | tf_op | source)
XLA Modules:
  0.0 359.6 jit_solution(3357063640888648328)
XLA Ops:
  8.0 0.0 copy-start
  8.0 0.0 reduce-scatter.3.cloned.1.call-start
  8.1 0.7 reduce-scatter.3.cloned.1.call-update
  8.7 0.0 all-gather.3.cloned.1.call-start
  8.8 77.1 %reduce-scatter.3.cloned.1.call-done = bf16[64,1024]{1,0:T(8,128)(2,1)} async-done(((bf16[512,1024]{1,0:T(8,128)(2,1)}), bf16[64,1024]{1,0:T(8,128)(2,1)}) %reduce-scatter.3.cloned.1.call-update) | async-done | bytes 131088 | tf_op jit(solution)/shard_map/reduce_scatter | solution.py:20
  85.9 2.0 fusion.3
  87.9 0.0 all-gather.3.cloned.1.call-update
  87.9 0.0 reduce-scatter.5.cloned.1.call-start
  87.9 0.0 copy-done
  88.0 16.0 %multiply_convert_fusion = bf16[8192,1024]{1,0:T(8,128)(2,1)} fusion(bf16[512,8192]{1,0:T(8,128)(2,1)} %param.8, bf16[512,1024]{1,0:T(8,128)(2,1)S(1)} %copy-done), kind=kOutput, calls=%fused_computation | convolution fusion | flops 8606711808 | bytes 26214400 | tf_op jit(solution)/shard_map/dot_general | solution.py:36
  103.9 0.0 reduce-scatter.5.cloned.1.call-update
  103.9 0.2 all-gather.5.cloned.1.call-start
  104.2 111.9 %all-gather.3.cloned.1.call-done = bf16[512,1024]{1,0:T(8,128)(2,1)} async-done(((bf16[64,1024]{1,0:T(8,128)(2,1)}), bf16[512,1024]{1,0:T(8,128)(2,1)}) %all-gather.3.cloned.1.call-update) | async-done | bytes 1048592 | tf_op jit(solution)/shard_map/all_gather | solution.py:27
  216.1 0.0 all-gather.5.cloned.1.call-update
  216.1 0.0 reduce-scatter.5.cloned.1.call-done
  216.1 2.8 bitcast_convert_fusion
  218.9 87.0 %all-gather.5.cloned.1.call-done = bf16[8192,1024]{1,0:T(8,128)(2,1)} async-done(((bf16[512,1024]{1,0:T(8,128)(2,1)}), bf16[8192,1024]{1,0:T(8,128)(2,1)}) %all-gather.5.cloned.1.call-update) | async-done | bytes 16777232 | tf_op jit(solution)/shard_map/all_gather | solution.py:30
  306.0 16.9 %fusion = bf16[512,8192]{0,1:T(8,128)(2,1)} fusion(bf16[8192,1024]{1,0:T(8,128)(2,1)} %all-gather.5.cloned.1.call-done, bf16[512,1024]{1,0:T(8,128)(2,1)S(1)} %copy-done), kind=kOutput, calls=%fused_computation.2 | convolution fusion | flops 8598323200 | bytes 26214400 | tf_op jit(solution)/shard_map/dot_general | solution.py:12
  322.9 11.9 %copy.12 = bf16[512,8192]{1,0:T(8,128)(2,1)} copy(bf16[512,8192]{0,1:T(8,128)(2,1)} %fusion) | data formatting | bytes 16777216
  334.8 0.0 copy-start.2
  334.8 0.0 copy-start.1
  334.8 15.0 %fusion.1 = bf16[512,1024]{0,1:T(8,128)(2,1)S(1)} fusion(bf16[8192,1024]{1,0:T(8,128)(2,1)} %all-gather.5.cloned.1.call-done, bf16[512,8192]{1,0:T(8,128)(2,1)} %param.8), kind=kOutput, calls=%fused_computation.4 | convolution fusion | flops 8590983168 | bytes 26214400 | tf_op jit(solution)/shard_map/dot_general | solution.py:11
  349.9 1.3 copy.11
  351.2 0.0 copy-done.2
  351.2 1.0 copy.14
  352.2 0.0 copy-done.1
Async XLA Ops:
  8.0 79.9 %copy-start = (bf16[512,1024]{1,0:T(8,128)(2,1)S(1)}, bf16[512,1024]{1,0:T(8,128)(2,1)}, u32[]{:S(2)}) copy-start(bf16[512,1024]{1,0:T(8,128)(2,1)} %param.9) | copy-start | bytes 3145732
  8.0 77.8 %reduce-scatter.3.cloned.1.call-start = ((), (), s32[]{:S(2)}) async-start(), calls=%async_computation.2 | async-start | bytes 1179648 | tf_op jit(solution)/shard_map/reduce_scatter | solution.py:20
  8.7 207.3 %all-gather.3.cloned.1.call-start = ((), (), s32[]{:S(2)}) async-start(), calls=%async_computation.3 | async-start | bytes 1179648 | tf_op jit(solution)/shard_map/all_gather | solution.py:27
  87.9 128.2 %reduce-scatter.5.cloned.1.call-start = ((), (), s32[]{:S(2)}) async-start(), calls=%async_computation.5 | async-start | bytes 17825792 | tf_op jit(solution)/shard_map/reduce_scatter | solution.py:34
  103.9 202.0 %all-gather.5.cloned.1.call-start = ((), (), s32[]{:S(2)}) async-start(), calls=%async_computation.4 | async-start | bytes 17825792 | tf_op jit(solution)/shard_map/all_gather | solution.py:30
  334.8 16.4 %copy-start.2 = (bf16[512,1024]{1,0:T(8,128)(2,1)S(1)}, bf16[512,1024]{1,0:T(8,128)(2,1)}, u32[]{:S(2)}) copy-start(bf16[512,1024]{1,0:T(8,128)(2,1)} %all-gather.3.cloned.1.call-done) | copy-start | bytes 3145732
  334.8 17.3 %copy-start.1 = (bf16[512,1024]{1,0:T(8,128)(2,1)S(1)}, bf16[512,1024]{1,0:T(8,128)(2,1)}, u32[]{:S(2)}) copy-start(bf16[512,1024]{1,0:T(8,128)(2,1)} %param.9) | copy-start | bytes 3145732
Sparse Core Ops, SparseCore 0:
  12.5 73.3 reduce-scatter.2
  89.0 127.0 all-gather.2
Sparse Core Ops, SparseCore 1:
  104.0 97.6 reduce-scatter.4
  216.2 89.7 all-gather.4
where the time goes:
time: 360 us
  waiting for transfers between devices  277 us (77%)
  matrix products  47.9 us (13%)
  between operations  15.5 us (4%)
  local copies, waits for them, and re-layouts  14.2 us (4%)
  other arithmetic  4.8 us (1%)
    all_gather x1, waiting for transfers between devices, per_device(): shard_weights = lax.all_gather(owned_rows, 'rep', axis=0, tiled=True)  112 us
    all_gather x1, waiting for transfers between devices, per_device(): lax.all_gather(shard_weights, 'fsdp', axis=0, tiled=True)  87 us
    reduce_scatter x1, waiting for transfers between devices, per_device(): lax.psum_scatter(deltas[0].astype(jnp.float32).astype(jnp.bfloat16), 'rep...  77.1 us
    dot_general x1, matrix products, fold_maker(): lax.dot_general(key_cot, weight_piece, (((1,), (1,)), ((), ())), preferre...  16.9 us
    dot_general x1, matrix products, per_device(): lax.dot_general(tokens, key_cot, (((0,), (0,)), ((), ())), preferred_elem...  16 us
    dot_general x1, matrix products, fold_maker(): key_sum = jnp.dot(source, weight_piece, preferred_element_type=jnp.float32)  15 us
    unnamed x9, local copies, waits for them, and re-layouts  14.2 us
  transfers between devices with their start and end apart: 4, of which 3 were waited for; matrix products, arithmetic and copies ran while one was open for 5% of the time, Pallas kernels for 0%

commit v1 on v0

v1 whole, which is shorter than its diff:
```python
import itertools

import jax
import jax.numpy as jnp
import numpy as np
from jax import lax
from jax.experimental import pallas as pl
from jax.experimental.pallas import tpu as pltpu
from jax.sharding import Mesh, PartitionSpec as P

MOMENTUM_RATE = 0.9
OUTER_RATE = 0.7
AXES = ("x", "zh", "zl", "y", "c")
SIZES = (4, 2, 2, 4, 2)
TOK = 512
D = 8192
COLS = 1024
SCALE = D ** (-0.5)
VMEM = 48 * 1024 * 1024
ANY = pl.BlockSpec(memory_space=pl.ANY)
BF = jnp.bfloat16
F32 = jnp.float32


def permute(value, to):
    pairs = []
    for x, zh, zl, y, c in itertools.product(*[range(n) for n in SIZES]):
        tx, tz, ty, tc = to(x, zh * 2 + zl, y, c)
        tz = tz % 4
        target = (tx % 4, tz // 2, tz % 2, ty % 4, tc % 2)
        pairs.append(
            (
                int(np.ravel_multi_index((x, zh, zl, y, c), SIZES)),
                int(np.ravel_multi_index(target, SIZES)),
            )
        )
    return lax.ppermute(value, AXES, pairs)


def swap_core(value):
    return permute(value, lambda x, z, y, c: (x, z, y, 1 - c))


def ring_x(value):
    return permute(value, lambda x, z, y, c: (x + 1 - 2 * c, z, y, c))


def ring_z(value):
    return permute(value, lambda x, z, y, c: (x, z + 1 - 2 * c, y, c))


def ring_y(value):
    return permute(value, lambda x, z, y, c: (x, z, y + 1 - 2 * c, c))


def params(**more):
    return pltpu.CompilerParams(vmem_limit_bytes=VMEM, **more)


def half_kernel(at, tokens, out, held, in_sem, out_sem):
    c = at[4]
    loads = [
        pltpu.make_async_copy(
            tokens.at[:, pl.ds(pl.multiple_of((2 * g + 1 - c) * 512, 512), 512)],
            held.at[:, pl.ds(g * 512, 512)],
            in_sem.at[g],
        )
        for g in range(8)
    ]
    stores = [
        pltpu.make_async_copy(
            held.at[:, pl.ds(g * 512, 512)],
            out.at[:, pl.ds(g * 512, 512)],
            out_sem.at[g],
        )
        for g in range(8)
    ]
    for load in loads:
        load.start()
    for load, store in zip(loads, stores):
        load.wait()
        store.start()
    for store in stores:
        store.wait()


def other_half(at, tokens):
    return pl.pallas_call(
        half_kernel,
        out_shape=jax.ShapeDtypeStruct((TOK, D // 2), BF),
        in_specs=[pl.BlockSpec(memory_space=pltpu.SMEM), ANY],
        out_specs=ANY,
        scratch_shapes=[
            pltpu.VMEM((TOK, D // 2), BF),
            pltpu.SemaphoreType.DMA((8,)),
            pltpu.SemaphoreType.DMA((8,)),
        ],
        compiler_params=params(),
        cost_estimate=pl.CostEstimate(
            flops=0, bytes_accessed=2 * TOK * D, transcendentals=0
        ),
        name="half",
    )(at, tokens)


def grad_kernel(blocks, mine, theirs, cot, cot_theirs, out, *rest):
    dims = (((0,), (0,)), ((), ()))
    total = lax.dot_general(mine[...], cot[...], dims, preferred_element_type=F32)
    total += lax.dot_general(
        theirs[...], cot_theirs[...], dims, preferred_element_type=F32
    )
    total = (total * SCALE).astype(out.dtype)

    @pl.when(pl.program_id(0) == 0)
    def _():
        out[...] = total

    for more in rest:

        @pl.when(pl.program_id(0) > 0)
        def _(more=more):
            more[0] = total


def grad_blocks(blocks, core, tokens, tokens_theirs, cot, cot_theirs):
    count = len(blocks)
    table = jnp.stack([2 * g + core for g in blocks] + blocks).astype(jnp.int32)
    whole = pl.BlockSpec((TOK, COLS), lambda m, b: (0, 0))
    return pl.pallas_call(
        grad_kernel,
        out_shape=[
            jax.ShapeDtypeStruct((512, COLS), BF),
            jax.ShapeDtypeStruct((count - 1, 512, COLS), BF),
        ][: min(count, 2)],
        grid_spec=pltpu.PrefetchScalarGridSpec(
            num_scalar_prefetch=1,
            grid=(count,),
            in_specs=[
                pl.BlockSpec((TOK, 512), lambda m, b: (0, b[m])),
                pl.BlockSpec((TOK, 512), lambda m, b: (0, b[count + m])),
                whole,
                whole,
            ],
            out_specs=[
                whole,
                pl.BlockSpec((1, 512, COLS), lambda m, b: (jnp.maximum(m - 1, 0), 0, 0)),
            ][: min(count, 2)],
        ),
        compiler_params=params(),
        cost_estimate=pl.CostEstimate(
            flops=count * 4 * TOK * 512 * COLS,
            bytes_accessed=(count * 2 + 2) << 20,
            transcendentals=0,
        ),
        name="grad",
    )(table, tokens, tokens_theirs, cot, cot_theirs)


def w_pieces(kind, at, sources, mine, dy):
    z, y, c = at[1], at[2], at[4]
    core = c if mine else 1 - c
    if kind == "x":
        (chunk, xs) = sources
        pieces = [(chunk.at[pl.ds(zh * 4, 4)], zh) for zh in range(2)]
        columns = []
        for zl, d in itertools.product(range(2), range(2)):
            f = zl * 8 + ((y + d) & 3) * 2 + core
            columns.append((f * 512 + xs * 128, (zl * 2 + d) * 128, 128))
    else:
        (chunks, zs) = sources
        pieces = [
            (chunk.at[pl.ds(0, 4), dy], zc >> 1) for chunk, zc in zip(chunks, zs)
        ]
        f = (zs[0] & 1) * 8 + ((y + 2 + dy) & 3) * 2 + core
        columns = [(f * 512, 0, 512)]
    return pieces, columns


def fold_kernel(steps, pairs, first, last, *refs):
    refs = list(refs)
    at, tokens, cot = refs[:3]
    refs = refs[3:]
    x_mine = [refs.pop(0) for _ in steps]
    x_theirs = [refs.pop(0) for _ in steps]
    z_mine = [[refs.pop(0) for _ in pair] for pair in pairs]
    z_theirs = [[refs.pop(0) for _ in pair] for pair in pairs]
    if not first:
        acc_in, _, _ = refs.pop(0), refs.pop(0), refs.pop(0)
    grad_out, weights_out, key_out = refs.pop(0), refs.pop(0), refs.pop(0)
    w, tok, grad, cot_v, acc, w_sem, tok_sem, out_sem, own_sem, cot_sem, acc_sem = (
        refs[:11]
    )
    if last:
        key_v = refs[11]
    x, z, y, c = at[0], at[1], at[2], at[4]
    way = 1 - 2 * c

    groups = []
    for s, mine, theirs in zip(steps, x_mine, x_theirs):
        groups.append(("x", (mine, ((x - way * s + 8) & 3)), True, 0))
        groups.append(("x", (theirs, ((x + way * s + 8) & 3)), False, 0))
    for pair, mine, theirs in zip(pairs, z_mine, z_theirs):
        zs_mine = [((z - way * s + 8) & 3) for s in pair]
        zs_theirs = [((z + way * s + 8) & 3) for s in pair]
        for dy in range(2):
            groups.append(("z", (mine, zs_mine), True, dy))
            groups.append(("z", (theirs, zs_theirs), False, dy))
    count = len(groups)

    def loads(i):
        kind, sources, is_mine, dy = groups[i]
        slot = i % 3
        pieces, columns = w_pieces(kind, at, sources, is_mine, dy)
        for src, zh in pieces:
            pltpu.make_async_copy(src, w.at[slot, :, zh], w_sem.at[slot]).start()
        for a, b, n in columns:
            pltpu.make_async_copy(
                tokens.at[:, pl.ds(pl.multiple_of(a, 128), n)],
                tok.at[slot, :, pl.ds(b, n)],
                tok_sem.at[slot],
            ).start()

    def weights_store(i):
        kind, sources, is_mine, dy = groups[i]
        slot = i % 3
        return pltpu.make_async_copy(
            w.at[slot, (z & 1) * 2], weights_out.at[sources[1]], own_sem.at[slot]
        )

    def stores(i):
        kind, sources, is_mine, dy = groups[i]
        slot = i % 3
        _, columns = w_pieces(kind, at, sources, is_mine, dy)
        for a, b, n in columns:
            pltpu.make_async_copy(
                grad.at[slot, :, pl.ds(b, n)],
                grad_out.at[:, pl.ds(pl.multiple_of(a, 128), n)],
                out_sem.at[slot],
            ).start()

    def whole(buffer, sem, slot):
        return pltpu.make_async_copy(buffer.at[slot], buffer.at[slot], sem.at[slot])

    cot_copy = pltpu.make_async_copy(cot, cot_v, cot_sem)
    cot_copy.start()
    loads(0)
    loads(1)
    if first:
        acc[...] = jnp.zeros_like(acc)
    else:
        acc_copy = pltpu.make_async_copy(acc_in, acc, acc_sem)
        acc_copy.start()
    cot_copy.wait()

    @pl.loop(0, count)
    def _(i):
        slot = lax.rem(i, 3)
        for k in range(2, count):

            @pl.when(i + 2 == k)
            def _(k=k):
                loads(k)

        whole(w, w_sem, slot).wait()
        for k in range(count):
            if groups[k][0] == "x" and groups[k][2]:

                @pl.when(i == k)
                def _(k=k):
                    weights_store(k).start()

        @pl.when(i >= 3)
        def _():
            whole(grad, out_sem, slot).wait()

        rows = w[slot].reshape(512, COLS)
        out = lax.dot_general(
            cot_v[...], rows, (((1,), (1,)), ((), ())), preferred_element_type=F32
        )
        grad[slot] = (out * SCALE).astype(BF)
        for k in range(count):

            @pl.when(i == k)
            def _(k=k):
                stores(k)

        whole(tok, tok_sem, slot).wait()
        if not first:

            @pl.when(i == 0)
            def _():
                acc_copy.wait()

        acc[...] += jnp.dot(tok[slot], rows, preferred_element_type=F32)
        for k in range(count):
            if groups[k][0] == "x" and groups[k][2]:

                @pl.when(i == k)
                def _(k=k):
                    weights_store(k).wait()

    if last:
        key_v[...] = (acc[...] * SCALE).astype(BF)
        key_copy = pltpu.make_async_copy(key_v, key_out, acc_sem)
    else:
        key_copy = pltpu.make_async_copy(acc, key_out, acc_sem)
    key_copy.start()
    for i in range(max(count - 3, 0), count):
        whole(grad, out_sem, i % 3).wait()
    key_copy.wait()


def fold(at, tokens, cot, steps, x_mine, x_theirs, pairs, z_mine, z_theirs, carry, last):
    first = carry is None
    operands = [at, tokens, cot, *x_mine, *x_theirs]
    operands += list(itertools.chain(*z_mine)) + list(itertools.chain(*z_theirs))
    aliases = {}
    if not first:
        operands += [carry[2]]
        aliases = {len(operands): 0, len(operands) + 1: 1}
        operands += carry[:2]
    shapes = [
        jax.ShapeDtypeStruct((TOK, D), BF),
        jax.ShapeDtypeStruct((4, 2, 64, COLS), BF),
        jax.ShapeDtypeStruct((TOK, COLS), BF if last else F32),
    ]
    dma = pltpu.SemaphoreType.DMA
    scratch = [
        pltpu.VMEM((3, 4, 2, 64, COLS), BF),
        pltpu.VMEM((3, TOK, 512), BF),
        pltpu.VMEM((3, TOK, 512), BF),
        pltpu.VMEM((TOK, COLS), BF),
        pltpu.VMEM((TOK, COLS), F32),
        dma((3,)),
        dma((3,)),
        dma((3,)),
        dma((3,)),
        dma(()),
        dma(()),
    ]
    if last:
        scratch += [pltpu.VMEM((TOK, COLS), BF)]
    groups = 2 * len(steps) + 4 * len(pairs)

    def kernel(*refs):
        fold_kernel(steps, pairs, first, last, *refs)

    return pl.pallas_call(
        kernel,
        out_shape=shapes,
        in_specs=[pl.BlockSpec(memory_space=pltpu.SMEM)] + [ANY] * (len(operands) - 1),
        out_specs=[ANY] * len(shapes),
        scratch_shapes=scratch,
        input_output_aliases=aliases,
        compiler_params=params(),
        cost_estimate=pl.CostEstimate(
            flops=groups * 4 * TOK * 512 * COLS,
            bytes_accessed=groups * (2 << 20) + (4 << 20),
            transcendentals=0,
        ),
        name="fold",
    )(*operands)


def per_device(deltas, outer_weights, momentum, tokens, key_cot):
    x, zh, zl, y, c = [lax.axis_index(a) for a in AXES]
    z = zh * 2 + zl
    way = 1 - 2 * c
    at = jnp.stack([x, z, y, zl, c]).astype(jnp.int32)
    blocks = deltas[0]

    own_at = x * 2 + zh
    summed = lax.dynamic_slice_in_dim(blocks, own_at * 64, 64, 0).astype(F32)
    for dx, dh in ((2, 1), (1, 1), (3, 1), (2, 0), (0, 1), (1, 0), (3, 0)):
        there = ((x + dx) & 3) * 2 + ((zh + dh) & 1)
        piece = lax.dynamic_slice_in_dim(blocks, there * 64, 64, 0)
        got = permute(
            piece, lambda px, pz, py, pc: (px + dx, pz + 2 * dh, py, pc)
        )
        summed = summed + got.astype(F32)
    mean_delta = summed / 8
    moment_next = MOMENTUM_RATE * momentum[0, 0] + mean_delta
    outer_next = outer_weights[0, 0] - OUTER_RATE * (
        mean_delta + MOMENTUM_RATE * moment_next
    )
    owned = outer_next.astype(BF)

    tokens_theirs = swap_core(other_half(at, tokens))
    cot_theirs = swap_core(key_cot)

    def grads(half, steps, tokens_theirs):
        zl_to = 1 - zl if half == 0 else zl
        blocks = [zl_to * 4 + ((y - way * (s + 1) + 8) & 3) for s in steps]
        return grad_blocks(blocks, c, tokens, tokens_theirs, key_cot, cot_theirs)

    def add(*parts):
        total = parts[0].astype(F32)
        for part in parts[1:]:
            total = total + part.astype(F32)
        return total

    (first,) = grads(0, (0,), tokens_theirs)
    owned, first, late = lax.optimization_barrier((owned, first, tokens_theirs))
    second, rest = grads(0, (1, 2, 3), late)

    def rows_from(value, dx=0, dz=0, dy=0):
        return permute(
            value, lambda px, pz, py, pc: (px - dx, pz - dz, py - dy, pc)
        )

    def in_order(parts, here):
        whole = jnp.zeros((4, *parts[0].shape), BF)
        for d, part in enumerate(parts):
            whole = lax.dynamic_update_slice_in_dim(
                whole, part[None], (here + d) & 3, 0
            )
        return whole

    by_y = [owned] + [rows_from(owned, dy=d) for d in (1, 2, 3)]
    a0 = jnp.stack(by_y[:2])
    b0 = jnp.stack(by_y[2:])
    a0, b0, rest, late = lax.optimization_barrier((a0, b0, rest, late))
    first_b, rest_b = grads(1, (0, 1, 2, 3), late)
    a1 = in_order([a0] + [rows_from(a0, dz=d) for d in (1, 2, 3)], z)
    b1 = in_order([b0] + [rows_from(b0, dx=d) for d in (1, 2, 3)], x)
    a1, b1, rest_b = lax.optimization_barrier((a1, b1, rest_b))
    a_mine, b_mine = [a1], [b1]
    a_theirs, b_theirs = [swap_core(a1)], [swap_core(b1)]

    def fold_of(steps, pairs, carry, last):
        return fold(
            at, tokens, key_cot, steps,
            [a_mine[s].reshape(8, 64, COLS) for s in steps],
            [a_theirs[s].reshape(8, 64, COLS) for s in steps],
            pairs,
            [[b_mine[s] for s in pair] for pair in pairs],
            [[b_theirs[s] for s in pair] for pair in pairs],
            carry, last,
        )

    carry = None
    for s, pairs in ((1, ()), (2, ()), (3, ((0, 2),))):
        a_next, b_next = ring_x(a_mine[-1]), ring_z(b_mine[-1])
        carry = fold_of((s - 1,), pairs, carry, False)
        if s < 3:
            a_next, b_next, *carry = lax.optimization_barrier((a_next, b_next, *carry))
        a_mine.append(a_next)
        b_mine.append(b_next)
        a_theirs.append(swap_core(a_next))
        b_theirs.append(swap_core(b_next))
    grad_tokens, shard_weights, keys_out = fold_of((3,), ((1, 3),), carry, True)
    shard_weights = shard_weights.reshape(512, COLS)

    arrived = ring_y(first)
    arrived = ring_y(add(second, arrived).astype(BF))
    arrived = ring_y(add(rest[0], arrived).astype(BF))
    crossed = add(rest[1], arrived).astype(BF)
    crossed = permute(crossed, lambda px, pz, py, pc: (px, pz ^ 1, py, pc))
    arrived = ring_y(first_b)
    arrived = ring_y(add(rest_b[0], arrived).astype(BF))
    arrived = ring_y(add(rest_b[1], arrived).astype(BF))
    grad_shard = add(rest_b[2], arrived, crossed)

    return (
        outer_next[None, None],
        moment_next[None, None],
        shard_weights,
        keys_out,
        grad_tokens,
        grad_shard[None],
    )


def solution(mesh):
    fine = Mesh(mesh.devices.reshape(SIZES), AXES)
    rep, fsdp = ("x", "zh"), ("zl", "y", "c")
    return jax.shard_map(
        per_device,
        mesh=fine,
        in_specs=(
            P(rep, fsdp, None),
            P(fsdp, rep, None, None),
            P(fsdp, rep, None, None),
            P(AXES, None),
            P(AXES, None),
        ),
        out_specs=(
            P(fsdp, rep, None, None),
            P(fsdp, rep, None, None),
            P(fsdp, None),
            P(AXES, None),
            P(AXES, None),
            P(rep, fsdp, None),
        ),
        check_vma=False,
    )
```

time: 360 us -> 181 us (0.50)
  waiting for transfers between devices: 277 us -> 47.3 us
  Pallas kernels: 0 us -> 58.3 us
  starting transfers between devices: 0.34 us -> 57.8 us
  matrix products: 47.9 us -> 0 us
  between operations: 15.5 us -> 1.19 us
  local copies, waits for them, and re-layouts: 14.2 us -> 2.98 us
  other arithmetic: 4.8 us -> 13.3 us
    all_gather x2 -> x0, waiting for transfers between devices: 199 us -> none  [the longest x1 112 us: per_device(): shard_weights = lax.all_gather(owned_rows, 'rep', axis=0, tiled=True)]
    reduce_scatter x2 -> x0, waiting for transfers between devices: 77.1 us -> none  [the longest x1 77.1 us: per_device(): lax.psum_scatter(deltas[0].astype(jnp.float32).astype(jnp.bfloat16), 'rep...]
    pallas_call x0 -> x8, Pallas kernels: none -> 58.3 us  [the longest x4 35.9 us: fold(): pl.pallas_call(kernel, out_shape=shapes, in_specs=[pl.BlockSpec(memory_sp...]
    ppermute x0 -> x39, starting transfers between devices: none -> 57.8 us  [permute(): return lax.ppermute(value, AXES, pairs)]
    dot_general x3 -> x0, matrix products: 47.9 us -> none  [the longest x1 16.9 us: fold_maker(): lax.dot_general(key_cot, weight_piece, (((1,), (1,)), ((), ())), preferre...]
    ppermute x0 -> x39, waiting for transfers between devices: none -> 47.3 us  [permute(): return lax.ppermute(value, AXES, pairs)]
    unnamed x9 -> x20, local copies, waits for them, and re-layouts: 14.2 us -> 1.01 us
    convert_element_type x1 -> x6, other arithmetic: 2.01 us -> 10.4 us  [the longest x1 2.63 us: per_device(): crossed = add(rest[1], arrived).astype(BF)]
  transfers between devices with their start and end apart: 4 -> 39, of which waited for: 3 -> 12; matrix products, arithmetic and copies ran while one was open for 5% -> 8% of each run, Pallas kernels for 0% -> 21%
where the time goes in v1:
time: 181 us
  Pallas kernels  58.3 us (32%)
  starting transfers between devices  57.8 us (32%)
  waiting for transfers between devices  47.3 us (26%)
  other arithmetic  13.3 us (7%)
  local copies, waits for them, and re-layouts  2.98 us (2%)
    ppermute x39, starting transfers between devices, permute(): return lax.ppermute(value, AXES, pairs)  57.8 us
    ppermute x39, waiting for transfers between devices, permute(): return lax.ppermute(value, AXES, pairs)  47.3 us
    pallas_call x4, Pallas kernels, fold(): pl.pallas_call(kernel, out_shape=shapes, in_specs=[pl.BlockSpec(memory_sp...  35.9 us
    pallas_call x3, Pallas kernels, grad_blocks(): pl.pallas_call(grad_kernel, out_shape=[jax.ShapeDtypeStruct((512, COLS),...  18.1 us
    pallas_call x1, Pallas kernels, other_half(): pl.pallas_call(half_kernel, out_shape=jax.ShapeDtypeStruct((TOK, D // 2),...  4.25 us
  transfers between devices with their start and end apart: 39, of which 12 were waited for; matrix products, arithmetic and copies ran while one was open for 8% of the time, Pallas kernels for 21%

profile of v1, /device:TPU:1, one launch (start us, length us, event | category | flops | bytes accessed | tf_op | source)
XLA Modules:
  0.0 180.8 jit_solution(5608824528695265031)
XLA Ops:
  0.7 4.2 %half.1 = bf16[512,4096]{1,0:T(8,128)(2,1)} custom-call(s32[5]{0:T(128)S(1)} %stack.98.at.refs_0_, bf16[512,8192]{1,0:T(8,128)(2,1)} %refs_1_.7), custom_call_target="tpu_custom_call" | custom-call | bytes 8388608 | tf_op jit(solution)/shard_map/half/pallas_call | solution.py:88
  5.0 1.5 collective-permute-start.7
  6.6 1.3 dynamic-slice_bitcast_fusion.6
  7.9 6.2 %collective-permute-start = (bf16[64,1024]{1,0:T(8,128)(2,1)S(1)}, bf16[64,1024]{1,0:T(8,128)(2,1)S(1)}, u32[]{:S(2)}, u32[]{:S(2)}) collective-permute-start(bf16[64,1024]{1,0:T(8,128)(2,1)S(1)} %get-tuple-element.80), channel_id=1, source_target_pairs={{0,80},{1,81},{2,82},{3,83},{4,84},{5,85},{6,86},{7,87},{8,88},{9,... | collective-permute-start | bytes 393224 | tf_op jit(solution)/shard_map/ppermute | solution.py:37
  14.1 5.1 %collective-permute-start.2 = (bf16[64,1024]{1,0:T(8,128)(2,1)S(1)}, bf16[64,1024]{1,0:T(8,128)(2,1)}, u32[]{:S(2)}, u32[]{:S(2)}) collective-permute-start(bf16[64,1024]{1,0:T(8,128)(2,1)S(1)} %get-tuple-element.83), channel_id=1, source_target_pairs={{0,112},{1,113},{2,114},{3,115},{4,116},{5,117},{6,118},{7,119},{8... | collective-permute-start | bytes 393224 | tf_op jit(solution)/shard_map/ppermute | solution.py:37
  19.4 3.7 %collective-permute-done.1 = bf16[64,1024]{1,0:T(8,128)(2,1)S(1)} collective-permute-done((bf16[64,1024]{1,0:T(8,128)(2,1)S(1)}, bf16[64,1024]{1,0:T(8,128)(2,1)S(1)}, u32[]{:S(2)}, u32[]{:S(2)}) %collective-permute-start.1) | collective-permute-done | bytes 131104 | tf_op jit(solution)/shard_map/ppermute | solution.py:37
  23.1 1.2 collective-permute-start.4
  24.4 1.5 collective-permute-start.5
  25.9 1.2 collective-permute-start.6
  27.4 1.2 collective-permute-done.4
  28.6 1.0 collective-permute-done.5
  30.2 1.5 fusion.14
  31.6 3.1 %grad.3 = bf16[512,1024]{1,0:T(8,128)(2,1)S(1)} custom-call(s32[2]{0:T(128)S(1)} %pad_add_fusion.blocks, bf16[512,8192]{1,0:T(8,128)(2,1)} %refs_1_.7, bf16[512,4096]{1,0:T(8,128)(2,1)} %collective-permute-done.7.theirs, bf16[512,1024]{1,0:T(8,128)(2,1)S(1)} %copy-done, bf16[512,1024]{1,0:T(8,128)(2,1)S(1)} %collective-permute-done.8.cot_theirs), custom_call_target="tpu_custom_call" | custom-call | flops 1073741824 | bytes 4194304 | tf_op jit(solution)/shard_map/grad/pallas_call | solution.py:129
  34.7 3.0 %collective-permute-start.10 = (bf16[64,1024]{1,0:T(8,128)(2,1)S(1)}, bf16[64,1024]{1,0:T(8,128)(2,1)S(1)}, u32[]{:S(2)}, u32[]{:S(2)}) collective-permute-start(bf16[64,1024]{1,0:T(8,128)(2,1)S(1)} %get-tuple-element.42), channel_id=1, source_target_pairs={{0,4},{1,5},{2,6},{3,7},{4,0},{5,1},{6,2},{7,3},{8,12},{9,13},{10,... | collective-permute-start | bytes 393224 | tf_op jit(solution)/shard_map/ppermute | solution.py:37
  38.1 2.3 %collective-permute-start.9 = (bf16[64,1024]{1,0:T(8,128)(2,1)S(1)}, bf16[64,1024]{1,0:T(8,128)(2,1)S(1)}, u32[]{:S(2)}, u32[]{:S(2)}) collective-permute-start(bf16[64,1024]{1,0:T(8,128)(2,1)S(1)} %get-tuple-element.42), channel_id=1, source_target_pairs={{0,6},{1,7},{2,0},{3,1},{4,2},{5,3},{6,4},{7,5},{8,14},{9,15},{10,... | collective-permute-start | bytes 393224 | tf_op jit(solution)/shard_map/ppermute | solution.py:37
  40.4 6.3 %grad.4 = (bf16[512,1024]{1,0:T(8,128)(2,1)S(1)}, bf16[2,512,1024]{2,1,0:T(8,128)(2,1)S(1)}) custom-call(s32[6]{0:T(128)S(1)} %stack.114.blocks, bf16[512,8192]{1,0:T(8,128)(2,1)} %refs_1_.7, bf16[512,4096]{1,0:T(8,128)(2,1)} %collective-permute-done.7.theirs, bf16[512,1024]{1,0:T(8,128)(2,1)S(1)} %copy-done, ...), custom_call_target="tpu_custom_call" | custom-call | flops 3221225472 | bytes 8388608 | tf_op jit(solution)/shard_map/grad/pallas_call | solution.py:129
  46.8 2.2 %collective-permute-start.15 = (bf16[2,64,1024]{2,1,0:T(8,128)(2,1)S(1)}, bf16[2,64,1024]{2,1,0:T(8,128)(2,1)S(1)}, u32[]{:S(2)}, u32[]{:S(2)}) collective-permute-start(bf16[2,64,1024]{2,1,0:T(8,128)(2,1)S(1)} %pad_maximum_fusion.1), channel_id=1, source_target_pairs={{0,96},{1,97},{2,98},{3,99},{4,100},{5,101},{6,102},{7,103},{8,104... | collective-permute-start | bytes 786440 | tf_op jit(solution)/shard_map/ppermute | solution.py:37
  49.7 2.5 %collective-permute-start.12 = (bf16[2,64,1024]{2,1,0:T(8,128)(2,1)S(1)}, bf16[2,64,1024]{2,1,0:T(8,128)(2,1)S(1)}, u32[]{:S(2)}, u32[]{:S(2)}) collective-permute-start(bf16[2,64,1024]{2,1,0:T(8,128)(2,1)S(1)} %pad_maximum_fusion), channel_id=1, source_target_pairs={{0,24},{1,25},{2,26},{3,27},{4,28},{5,29},{6,30},{7,31},{8,0},{9,1... | collective-permute-start | bytes 786440 | tf_op jit(solution)/shard_map/ppermute | solution.py:37
  52.2 8.8 %grad.5 = (bf16[512,1024]{1,0:T(8,128)(2,1)S(1)}, bf16[3,512,1024]{2,1,0:T(8,128)(2,1)}) custom-call(s32[8]{0:T(128)S(1)} %stack.123.blocks, bf16[512,8192]{1,0:T(8,128)(2,1)} %refs_1_.7, bf16[512,4096]{1,0:T(8,128)(2,1)} %collective-permute-done.7.theirs, bf16[512,1024]{1,0:T(8,128)(2,1)S(1)} %copy-done, bf16[512,1024]{1,0:T(8,128)(2,1)S(1)} %collective-permute-done.8.cot_theirs), custom_call_target="tpu_custom_call" | custom-call | flops 4294967296 | bytes 10485760 | tf_op jit(solution)/shard_map/grad/pallas_call | solution.py:129
  62.2 6.0 %collective-permute-done.13 = bf16[2,64,1024]{2,1,0:T(8,128)(2,1)S(1)} collective-permute-done((bf16[2,64,1024]{2,1,0:T(8,128)(2,1)S(1)}, bf16[2,64,1024]{2,1,0:T(8,128)(2,1)S(1)}, u32[]{:S(2)}, u32[]{:S(2)}) %collective-permute-start.13) | collective-permute-done | bytes 262176 | tf_op jit(solution)/shard_map/ppermute | solution.py:37
  68.3 2.7 %collective-permute-done.14 = bf16[2,64,1024]{2,1,0:T(8,128)(2,1)S(1)} collective-permute-done((bf16[2,64,1024]{2,1,0:T(8,128)(2,1)S(1)}, bf16[2,64,1024]{2,1,0:T(8,128)(2,1)S(1)}, u32[]{:S(2)}, u32[]{:S(2)}) %collective-permute-start.14) | collective-permute-done | bytes 262176 | tf_op jit(solution)/shard_map/ppermute | solution.py:37
  71.0 7.2 %collective-permute-start.20 = (bf16[4,2,64,1024]{3,2,1,0:T(8,128)(2,1)S(1)}, bf16[4,2,64,1024]{3,2,1,0:T(8,128)(2,1)S(1)}, u32[]{:S(2)}, u32[]{:S(2)}) collective-permute-start(bf16[4,2,64,1024]{3,2,1,0:T(8,128)(2,1)S(1)} %bitcast_dynamic-update-slice_fusion.4), channel_id=1, source_target_pairs={{0,1},{1,0},{2,3},{3,2},{4,5},{5,4},{6,7},{7,6},{8,9},{9,8},{10,11... | collective-permute-start | bytes 3145736 | tf_op jit(solution)/shard_map/ppermute | solution.py:37
  78.2 1.6 collective-permute-start.18
  80.3 3.0 %collective-permute-start.32 = (bf16[512,1024]{1,0:T(8,128)(2,1)S(1)}, bf16[512,1024]{1,0:T(8,128)(2,1)}, u32[]{:S(2)}, u32[]{:S(2)}) collective-permute-start(bf16[512,1024]{1,0:T(8,128)(2,1)S(1)} %get-tuple-element.74), channel_id=1, source_target_pairs={{0,2},{1,7},{2,4},{3,1},{4,6},{5,3},{6,0},{7,5},{8,10},{9,15},{10,... | collective-permute-start | bytes 3145736 | tf_op jit(solution)/shard_map/ppermute | solution.py:37
  83.8 4.4 %fold.4 = (bf16[512,8192]{1,0:T(8,128)(2,1)}, bf16[4,2,64,1024]{3,2,1,0:T(8,128)(2,1)}, f32[512,1024]{1,0:T(8,128)S(1)}) custom-call(s32[5]{0:T(128)S(1)} %stack.98.at.refs_0_, bf16[512,8192]{1,0:T(8,128)(2,1)} %refs_1_.7, bf16[512,1024]{1,0:T(8,128)(2,1)S(1)} %copy-done, bf16[8,64,1024]{2,1,0:T(8,128)(2,1)S(1)} %bitcast.105, bf16[8,64,1024]{2,1,0:T(8,128)(2,1)S(1)} %bitcast.112), custom_call_target="tpu_custom_call" | custom-call | flops 2147483648 | bytes 8388608 | tf_op jit(solution)/shard_map/fold/pallas_call | solution.py:348
  88.2 4.2 %collective-permute-done.18 = bf16[4,2,64,1024]{3,2,1,0:T(8,128)(2,1)S(1)} collective-permute-done((bf16[4,2,64,1024]{3,2,1,0:T(8,128)(2,1)S(1)}, bf16[4,2,64,1024]{3,2,1,0:T(8,128)(2,1)S(1)}, u32[]{:S(2)}, u32[]{:S(2)}) %collective-permute-start.18) | collective-permute-done | bytes 1048608 | tf_op jit(solution)/shard_map/ppermute | solution.py:37
  92.4 1.5 collective-permute-done.19.refs_5_
  93.9 2.3 %collective-permute-start.23 = (bf16[4,2,64,1024]{3,2,1,0:T(8,128)(2,1)S(1)}, bf16[4,2,64,1024]{3,2,1,0:T(8,128)(2,1)S(1)}, u32[]{:S(2)}, u32[]{:S(2)}) collective-permute-start(bf16[4,2,64,1024]{3,2,1,0:T(8,128)(2,1)S(1)} %collective-permute-done.18), channel_id=1, source_target_pairs={{0,1},{1,0},{2,3},{3,2},{4,5},{5,4},{6,7},{7,6},{8,9},{9,8},{10,11... | collective-permute-start | bytes 3145736 | tf_op jit(solution)/shard_map/ppermute | solution.py:37
  96.2 1.9 %fusion.2 = bf16[512,1024]{1,0:T(8,128)(2,1)S(1)} fusion(bf16[512,1024]{1,0:T(8,128)(2,1)} %collective-permute-done.32, bf16[3,512,1024]{2,1,0:T(8,128)(2,1)} %get-tuple-element.73), kind=kLoop, calls=%fused_computation.5 | loop fusion | flops 2097152 | bytes 3145728 | tf_op jit(solution)/shard_map/convert_element_type | solution.py:460
  98.1 3.0 %collective-permute-start.33 = (bf16[512,1024]{1,0:T(8,128)(2,1)S(1)}, bf16[512,1024]{1,0:T(8,128)(2,1)}, u32[]{:S(2)}, u32[]{:S(2)}) collective-permute-start(bf16[512,1024]{1,0:T(8,128)(2,1)S(1)} %fusion.2), channel_id=1, source_target_pairs={{0,2},{1,7},{2,4},{3,1},{4,6},{5,3},{6,0},{7,5},{8,10},{9,15},{10,... | collective-permute-start | bytes 3145736 | tf_op jit(solution)/shard_map/ppermute | solution.py:37
  101.2 1.1 collective-permute-start.21
  102.2 4.0 %collective-permute-done.36 = bf16[512,1024]{1,0:T(8,128)(2,1)S(1)} collective-permute-done((bf16[512,1024]{1,0:T(8,128)(2,1)S(1)}, bf16[512,1024]{1,0:T(8,128)(2,1)S(1)}, u32[]{:S(2)}, u32[]{:S(2)}) %collective-permute-start.36) | collective-permute-done | bytes 1048608 | tf_op jit(solution)/shard_map/ppermute | solution.py:37
  106.3 1.4 fusion
  107.6 3.4 %collective-permute-start.37 = (bf16[512,1024]{1,0:T(8,128)(2,1)}, bf16[512,1024]{1,0:T(8,128)(2,1)}, u32[]{:S(2)}, u32[]{:S(2)}) collective-permute-start(bf16[512,1024]{1,0:T(8,128)(2,1)} %fusion), channel_id=1, source_target_pairs={{0,2},{1,7},{2,4},{3,1},{4,6},{5,3},{6,0},{7,5},{8,10},{9,15},{10,... | collective-permute-start | bytes 3145736 | tf_op jit(solution)/shard_map/ppermute | solution.py:37
  111.1 5.8 %fold.5 = (bf16[512,8192]{1,0:T(8,128)(2,1)}, bf16[4,2,64,1024]{3,2,1,0:T(8,128)(2,1)}, f32[512,1024]{1,0:T(8,128)S(1)}) custom-call(s32[5]{0:T(128)S(1)} %stack.98.at.refs_0_, bf16[512,8192]{1,0:T(8,128)(2,1)} %refs_1_.7, bf16[512,1024]{1,0:T(8,128)(2,1)S(1)} %copy-done, ...), custom_call_target="tpu_custom_call", output_to_operand_aliasing={{0}: (6, {}), {1}: (7, {})} | custom-call | flops 2147483648 | bytes 8388608 | tf_op jit(solution)/shard_map/fold/pallas_call | solution.py:348
  117.6 0.7 collective-permute-start.24
  118.3 10.6 %collective-permute-done.37 = bf16[512,1024]{1,0:T(8,128)(2,1)} collective-permute-done((bf16[512,1024]{1,0:T(8,128)(2,1)}, bf16[512,1024]{1,0:T(8,128)(2,1)}, u32[]{:S(2)}, u32[]{:S(2)}) %collective-permute-start.37) | collective-permute-done | bytes 1048608 | tf_op jit(solution)/shard_map/ppermute | solution.py:37
  128.8 2.6 %fusion.3 = bf16[512,1024]{1,0:T(8,128)(2,1)} fusion(bf16[512,1024]{1,0:T(8,128)(2,1)} %collective-permute-done.33, bf16[3,512,1024]{2,1,0:T(8,128)(2,1)S(1)} %copy-done.3), kind=kLoop, calls=%fused_computation.7 | loop fusion | flops 2097152 | bytes 3145728 | tf_op jit(solution)/shard_map/convert_element_type | solution.py:461
  131.5 2.6 %fusion.1 = bf16[512,1024]{1,0:T(8,128)(2,1)} fusion(bf16[512,1024]{1,0:T(8,128)(2,1)} %collective-permute-done.37, bf16[2,512,1024]{2,1,0:T(8,128)(2,1)S(1)} %get-tuple-element.75), kind=kLoop, calls=%fused_computation.3 | loop fusion | flops 2097152 | bytes 3145728 | tf_op jit(solution)/shard_map/convert_element_type | solution.py:457
  134.1 3.3 %collective-permute-start.34 = (bf16[512,1024]{1,0:T(8,128)(2,1)}, bf16[512,1024]{1,0:T(8,128)(2,1)S(1)}, u32[]{:S(2)}, u32[]{:S(2)}) collective-permute-start(bf16[512,1024]{1,0:T(8,128)(2,1)} %fusion.3), channel_id=1, source_target_pairs={{0,2},{1,7},{2,4},{3,1},{4,6},{5,3},{6,0},{7,5},{8,10},{9,15},{10,... | collective-permute-start | bytes 3145736 | tf_op jit(solution)/shard_map/ppermute | solution.py:37
  137.4 1.5 collective-permute-start.38
  139.4 6.9 %collective-permute-done.26.refs_6_ = bf16[4,2,64,1024]{3,2,1,0:T(8,128)(2,1)S(1)} collective-permute-done((bf16[4,2,64,1024]{3,2,1,0:T(8,128)(2,1)S(1)}, bf16[4,2,64,1024]{3,2,1,0:T(8,128)(2,1)S(1)}, u32[]{:S(2)}, u32[]{:S(2)}) %collective-permute-start.26) | collective-permute-done | bytes 1048608 | tf_op jit(solution)/shard_map/ppermute | solution.py:37
  146.3 0.9 fusion.13
  147.1 13.0 %fold.6 = (bf16[512,8192]{1,0:T(8,128)(2,1)}, bf16[4,2,64,1024]{3,2,1,0:T(8,128)(2,1)}, f32[512,1024]{1,0:T(8,128)}) custom-call(s32[5]{0:T(128)S(1)} %stack.98.at.refs_0_, bf16[512,8192]{1,0:T(8,128)(2,1)} %refs_1_.7, bf16[512,1024]{1,0:T(8,128)(2,1)S(1)} %copy-done, ...), custom_call_target="tpu_custom_call", output_to_operand_aliasing={{0}: (10, {}), {1}: (11, {})} | custom-call | flops 6442450944 | bytes 16777216 | tf_op jit(solution)/shard_map/fold/pallas_call | solution.py:348
  160.2 4.8 %collective-permute-done.38 = bf16[512,1024]{1,0:T(8,128)(2,1)S(1)} collective-permute-done((bf16[512,1024]{1,0:T(8,128)(2,1)}, bf16[512,1024]{1,0:T(8,128)(2,1)S(1)}, u32[]{:S(2)}, u32[]{:S(2)}) %collective-permute-start.38) | collective-permute-done | bytes 1048608 | tf_op jit(solution)/shard_map/ppermute | solution.py:37
  165.0 1.9 %fusion.5 = f32[1,512,1024]{2,1,0:T(8,128)} fusion(bf16[512,1024]{1,0:T(8,128)(2,1)S(1)} %collective-permute-done.38, bf16[512,1024]{1,0:T(8,128)(2,1)S(1)} %collective-permute-done.34, bf16[3,512,1024]{2,1,0:T(8,128)(2,1)S(1)} %copy-done.3), kind=kLoop, calls=%fused_computation.10 | loop fusion | flops 2621440 | bytes 5242880 | tf_op jit(solution)/shard_map/broadcast_in_dim | solution.py:470
  166.9 1.0 copy-done.5
  167.9 12.8 %fold.7 = (bf16[512,8192]{1,0:T(8,128)(2,1)}, bf16[4,2,64,1024]{3,2,1,0:T(8,128)(2,1)}, bf16[512,1024]{1,0:T(8,128)(2,1)}) custom-call(s32[5]{0:T(128)S(1)} %stack.98.at.refs_0_, bf16[512,8192]{1,0:T(8,128)(2,1)} %refs_1_.7, bf16[512,1024]{1,0:T(8,128)(2,1)S(1)} %copy-done, ...), custom_call_target="tpu_custom_call", output_to_operand_aliasing={{0}: (10, {}), {1}: (11, {})} | custom-call | flops 6442450944 | bytes 16777216 | tf_op jit(solution)/shard_map/fold/pallas_call | solution.py:348
  (83 shorter events, 5.8 us)
Async XLA Ops:
  0.7 5.8 %copy-start = (bf16[512,1024]{1,0:T(8,128)(2,1)S(1)}, bf16[512,1024]{1,0:T(8,128)(2,1)}, u32[]{:S(2)}) copy-start(bf16[512,1024]{1,0:T(8,128)(2,1)} %refs_2_.7) | copy-start | bytes 3145732
  5.0 25.2 %copy-start.6 = (f32[1,1,64,1024]{3,2,1,0:T(8,128)S(1)}, f32[1,1,64,1024]{3,2,1,0:T(8,128)}, u32[]{:S(2)}) copy-start(f32[1,1,64,1024]{3,2,1,0:T(8,128)} %param.7) | copy-start | bytes 786436
  5.0 25.2 %copy-start.7 = (f32[1,1,64,1024]{3,2,1,0:T(8,128)S(1)}, f32[1,1,64,1024]{3,2,1,0:T(8,128)}, u32[]{:S(2)}) copy-start(f32[1,1,64,1024]{3,2,1,0:T(8,128)} %param.6) | copy-start | bytes 786436
  5.0 26.6 %collective-permute-start.7 = (bf16[512,4096]{1,0:T(8,128)(2,1)}, bf16[512,4096]{1,0:T(8,128)(2,1)}, u32[]{:S(2)}, u32[]{:S(2)}) collective-permute-start(bf16[512,4096]{1,0:T(8,128)(2,1)} %half.1), channel_id=1, source_target_pairs={{0,1},{1,0},{2,3},{3,2},{4,5},{5,4},{6,7},{7,6},{8,9},{9,8},{10,11... | collective-permute-start | bytes 12582920 | tf_op jit(solution)/shard_map/ppermute | solution.py:37
  6.5 25.1 %collective-permute-start.8 = (bf16[512,1024]{1,0:T(8,128)(2,1)S(1)}, bf16[512,1024]{1,0:T(8,128)(2,1)S(1)}, u32[]{:S(2)}, u32[]{:S(2)}) collective-permute-start(bf16[512,1024]{1,0:T(8,128)(2,1)S(1)} %copy-done), channel_id=1, source_target_pairs={{0,1},{1,0},{2,3},{3,2},{4,5},{5,4},{6,7},{7,6},{8,9},{9,8},{10,11... | collective-permute-start | bytes 3145736 | tf_op jit(solution)/shard_map/ppermute | solution.py:37
  7.9 11.3 %collective-permute-start = (bf16[64,1024]{1,0:T(8,128)(2,1)S(1)}, bf16[64,1024]{1,0:T(8,128)(2,1)S(1)}, u32[]{:S(2)}, u32[]{:S(2)}) collective-permute-start(bf16[64,1024]{1,0:T(8,128)(2,1)S(1)} %get-tuple-element.80), channel_id=1, source_target_pairs={{0,80},{1,81},{2,82},{3,83},{4,84},{5,85},{6,86},{7,87},{8,88},{9,... | collective-permute-start | bytes 393224 | tf_op jit(solution)/shard_map/ppermute | solution.py:37
  14.1 9.0 %collective-permute-start.1 = (bf16[64,1024]{1,0:T(8,128)(2,1)S(1)}, bf16[64,1024]{1,0:T(8,128)(2,1)S(1)}, u32[]{:S(2)}, u32[]{:S(2)}) collective-permute-start(bf16[64,1024]{1,0:T(8,128)(2,1)S(1)} %get-tuple-element.84), channel_id=1, source_target_pairs={{0,48},{1,49},{2,50},{3,51},{4,52},{5,53},{6,54},{7,55},{8,56},{9,... | collective-permute-start | bytes 393224 | tf_op jit(solution)/shard_map/ppermute | solution.py:37
  14.1 10.2 %collective-permute-start.2 = (bf16[64,1024]{1,0:T(8,128)(2,1)S(1)}, bf16[64,1024]{1,0:T(8,128)(2,1)}, u32[]{:S(2)}, u32[]{:S(2)}) collective-permute-start(bf16[64,1024]{1,0:T(8,128)(2,1)S(1)} %get-tuple-element.83), channel_id=1, source_target_pairs={{0,112},{1,113},{2,114},{3,115},{4,116},{5,117},{6,118},{7,119},{8... | collective-permute-start | bytes 393224 | tf_op jit(solution)/shard_map/ppermute | solution.py:37
  19.2 6.7 %collective-permute-start.3 = (bf16[64,1024]{1,0:T(8,128)(2,1)S(1)}, bf16[64,1024]{1,0:T(8,128)(2,1)S(1)}, u32[]{:S(2)}, u32[]{:S(2)}) collective-permute-start(bf16[64,1024]{1,0:T(8,128)(2,1)S(1)} %get-tuple-element.82), channel_id=1, source_target_pairs={{0,64},{1,65},{2,66},{3,67},{4,68},{5,69},{6,70},{7,71},{8,72},{9,... | collective-permute-start | bytes 393224 | tf_op jit(solution)/shard_map/ppermute | solution.py:37
  23.1 6.4 %copy-start.8 = (bf16[64,1024]{1,0:T(8,128)(2,1)}, bf16[64,1024]{1,0:T(8,128)(2,1)S(1)}, u32[]{:S(2)}) copy-start(bf16[64,1024]{1,0:T(8,128)(2,1)S(1)} %collective-permute-done.1) | copy-start | bytes 393220
  23.1 5.4 %collective-permute-start.4 = (bf16[64,1024]{1,0:T(8,128)(2,1)S(1)}, bf16[64,1024]{1,0:T(8,128)(2,1)}, u32[]{:S(2)}, u32[]{:S(2)}) collective-permute-start(bf16[64,1024]{1,0:T(8,128)(2,1)S(1)} %get-tuple-element.81), channel_id=1, source_target_pairs={{0,16},{1,17},{2,18},{3,19},{4,20},{5,21},{6,22},{7,23},{8,24},{9,... | collective-permute-start | bytes 393224 | tf_op jit(solution)/shard_map/ppermute | solution.py:37
  24.4 5.1 %collective-permute-start.5 = (bf16[64,1024]{1,0:T(8,128)(2,1)S(1)}, bf16[64,1024]{1,0:T(8,128)(2,1)}, u32[]{:S(2)}, u32[]{:S(2)}) collective-permute-start(bf16[64,1024]{1,0:T(8,128)(2,1)S(1)} %get-tuple-element.86), channel_id=1, source_target_pairs={{0,32},{1,33},{2,34},{3,35},{4,36},{5,37},{6,38},{7,39},{8,40},{9,... | collective-permute-start | bytes 393224 | tf_op jit(solution)/shard_map/ppermute | solution.py:37
  25.9 3.6 %copy-start.9 = (bf16[64,1024]{1,0:T(8,128)(2,1)}, bf16[64,1024]{1,0:T(8,128)(2,1)S(1)}, u32[]{:S(2)}) copy-start(bf16[64,1024]{1,0:T(8,128)(2,1)S(1)} %collective-permute-done.3) | copy-start | bytes 393220
  25.9 4.2 %collective-permute-start.6 = (bf16[64,1024]{1,0:T(8,128)(2,1)S(1)}, bf16[64,1024]{1,0:T(8,128)(2,1)}, u32[]{:S(2)}, u32[]{:S(2)}) collective-permute-start(bf16[64,1024]{1,0:T(8,128)(2,1)S(1)} %get-tuple-element.85), channel_id=1, source_target_pairs={{0,96},{1,97},{2,98},{3,99},{4,100},{5,101},{6,102},{7,103},{8,104... | collective-permute-start | bytes 393224 | tf_op jit(solution)/shard_map/ppermute | solution.py:37
  34.7 12.0 %collective-permute-start.10 = (bf16[64,1024]{1,0:T(8,128)(2,1)S(1)}, bf16[64,1024]{1,0:T(8,128)(2,1)S(1)}, u32[]{:S(2)}, u32[]{:S(2)}) collective-permute-start(bf16[64,1024]{1,0:T(8,128)(2,1)S(1)} %get-tuple-element.42), channel_id=1, source_target_pairs={{0,4},{1,5},{2,6},{3,7},{4,0},{5,1},{6,2},{7,3},{8,12},{9,13},{10,... | collective-permute-start | bytes 393224 | tf_op jit(solution)/shard_map/ppermute | solution.py:37
  37.7 9.0 %collective-permute-start.11 = (bf16[64,1024]{1,0:T(8,128)(2,1)S(1)}, bf16[64,1024]{1,0:T(8,128)(2,1)S(1)}, u32[]{:S(2)}, u32[]{:S(2)}) collective-permute-start(bf16[64,1024]{1,0:T(8,128)(2,1)S(1)} %get-tuple-element.42), channel_id=1, source_target_pairs={{0,2},{1,3},{2,4},{3,5},{4,6},{5,7},{6,0},{7,1},{8,10},{9,11},{10,... | collective-permute-start | bytes 393224 | tf_op jit(solution)/shard_map/ppermute | solution.py:37
  38.1 8.7 %collective-permute-start.9 = (bf16[64,1024]{1,0:T(8,128)(2,1)S(1)}, bf16[64,1024]{1,0:T(8,128)(2,1)S(1)}, u32[]{:S(2)}, u32[]{:S(2)}) collective-permute-start(bf16[64,1024]{1,0:T(8,128)(2,1)S(1)} %get-tuple-element.42), channel_id=1, source_target_pairs={{0,6},{1,7},{2,0},{3,1},{4,2},{5,3},{6,4},{7,5},{8,14},{9,15},{10,... | collective-permute-start | bytes 393224 | tf_op jit(solution)/shard_map/ppermute | solution.py:37
  40.4 42.9 %collective-permute-start.35 = (bf16[512,1024]{1,0:T(8,128)(2,1)S(1)}, bf16[512,1024]{1,0:T(8,128)(2,1)S(1)}, u32[]{:S(2)}, u32[]{:S(2)}) collective-permute-start(bf16[512,1024]{1,0:T(8,128)(2,1)S(1)} %grad.3), channel_id=1, source_target_pairs={{0,2},{1,7},{2,4},{3,1},{4,6},{5,3},{6,0},{7,5},{8,10},{9,15},{10,... | collective-permute-start | bytes 3145736 | tf_op jit(solution)/shard_map/ppermute | solution.py:37
  46.8 14.5 %collective-permute-start.15 = (bf16[2,64,1024]{2,1,0:T(8,128)(2,1)S(1)}, bf16[2,64,1024]{2,1,0:T(8,128)(2,1)S(1)}, u32[]{:S(2)}, u32[]{:S(2)}) collective-permute-start(bf16[2,64,1024]{2,1,0:T(8,128)(2,1)S(1)} %pad_maximum_fusion.1), channel_id=1, source_target_pairs={{0,96},{1,97},{2,98},{3,99},{4,100},{5,101},{6,102},{7,103},{8,104... | collective-permute-start | bytes 786440 | tf_op jit(solution)/shard_map/ppermute | solution.py:37
  49.0 12.8 %collective-permute-start.16 = (bf16[2,64,1024]{2,1,0:T(8,128)(2,1)S(1)}, bf16[2,64,1024]{2,1,0:T(8,128)(2,1)S(1)}, u32[]{:S(2)}, u32[]{:S(2)}) collective-permute-start(bf16[2,64,1024]{2,1,0:T(8,128)(2,1)S(1)} %pad_maximum_fusion.1), channel_id=1, source_target_pairs={{0,64},{1,65},{2,66},{3,67},{4,68},{5,69},{6,70},{7,71},{8,72},{9,... | collective-permute-start | bytes 786440 | tf_op jit(solution)/shard_map/ppermute | solution.py:37
  49.0 13.1 %collective-permute-start.17 = (bf16[2,64,1024]{2,1,0:T(8,128)(2,1)S(1)}, bf16[2,64,1024]{2,1,0:T(8,128)(2,1)S(1)}, u32[]{:S(2)}, u32[]{:S(2)}) collective-permute-start(bf16[2,64,1024]{2,1,0:T(8,128)(2,1)S(1)} %pad_maximum_fusion.1), channel_id=1, source_target_pairs={{0,32},{1,33},{2,34},{3,35},{4,36},{5,37},{6,38},{7,39},{8,40},{9,... | collective-permute-start | bytes 786440 | tf_op jit(solution)/shard_map/ppermute | solution.py:37
  49.7 12.5 %collective-permute-start.12 = (bf16[2,64,1024]{2,1,0:T(8,128)(2,1)S(1)}, bf16[2,64,1024]{2,1,0:T(8,128)(2,1)S(1)}, u32[]{:S(2)}, u32[]{:S(2)}) collective-permute-start(bf16[2,64,1024]{2,1,0:T(8,128)(2,1)S(1)} %pad_maximum_fusion), channel_id=1, source_target_pairs={{0,24},{1,25},{2,26},{3,27},{4,28},{5,29},{6,30},{7,31},{8,0},{9,1... | collective-permute-start | bytes 786440 | tf_op jit(solution)/shard_map/ppermute | solution.py:37
  61.3 6.9 %collective-permute-start.13 = (bf16[2,64,1024]{2,1,0:T(8,128)(2,1)S(1)}, bf16[2,64,1024]{2,1,0:T(8,128)(2,1)S(1)}, u32[]{:S(2)}, u32[]{:S(2)}) collective-permute-start(bf16[2,64,1024]{2,1,0:T(8,128)(2,1)S(1)} %pad_maximum_fusion), channel_id=1, source_target_pairs={{0,16},{1,17},{2,18},{3,19},{4,20},{5,21},{6,22},{7,23},{8,24},{9,... | collective-permute-start | bytes 786440 | tf_op jit(solution)/shard_map/ppermute | solution.py:37
  61.8 9.2 %collective-permute-start.14 = (bf16[2,64,1024]{2,1,0:T(8,128)(2,1)S(1)}, bf16[2,64,1024]{2,1,0:T(8,128)(2,1)S(1)}, u32[]{:S(2)}, u32[]{:S(2)}) collective-permute-start(bf16[2,64,1024]{2,1,0:T(8,128)(2,1)S(1)} %pad_maximum_fusion), channel_id=1, source_target_pairs={{0,8},{1,9},{2,10},{3,11},{4,12},{5,13},{6,14},{7,15},{8,16},{9,17... | collective-permute-start | bytes 786440 | tf_op jit(solution)/shard_map/ppermute | solution.py:37
  71.0 12.8 %collective-permute-start.20 = (bf16[4,2,64,1024]{3,2,1,0:T(8,128)(2,1)S(1)}, bf16[4,2,64,1024]{3,2,1,0:T(8,128)(2,1)S(1)}, u32[]{:S(2)}, u32[]{:S(2)}) collective-permute-start(bf16[4,2,64,1024]{3,2,1,0:T(8,128)(2,1)S(1)} %bitcast_dynamic-update-slice_fusion.4), channel_id=1, source_target_pairs={{0,1},{1,0},{2,3},{3,2},{4,5},{5,4},{6,7},{7,6},{8,9},{9,8},{10,11... | collective-permute-start | bytes 3145736 | tf_op jit(solution)/shard_map/ppermute | solution.py:37
  78.2 14.2 %collective-permute-start.18 = (bf16[4,2,64,1024]{3,2,1,0:T(8,128)(2,1)S(1)}, bf16[4,2,64,1024]{3,2,1,0:T(8,128)(2,1)S(1)}, u32[]{:S(2)}, u32[]{:S(2)}) collective-permute-start(bf16[4,2,64,1024]{3,2,1,0:T(8,128)(2,1)S(1)} %bitcast_dynamic-update-slice_fusion.4), channel_id=1, source_target_pairs={{0,32},{1,97},{2,34},{3,99},{4,36},{5,101},{6,38},{7,103},{8,40},{... | collective-permute-start | bytes 3145736 | tf_op jit(solution)/shard_map/ppermute | solution.py:37
  79.8 14.0 %collective-permute-start.19 = (bf16[4,2,64,1024]{3,2,1,0:T(8,128)(2,1)S(1)}, bf16[4,2,64,1024]{3,2,1,0:T(8,128)(2,1)S(1)}, u32[]{:S(2)}, u32[]{:S(2)}) collective-permute-start(bf16[4,2,64,1024]{3,2,1,0:T(8,128)(2,1)S(1)} %bitcast_dynamic-update-slice_fusion.refs_5_), channel_id=1, source_target_pairs={{0,8},{1,25},{2,10},{3,27},{4,12},{5,29},{6,14},{7,31},{8,16},{9,1... | collective-permute-start | bytes 3145736 | tf_op jit(solution)/shard_map/ppermute | solution.py:37
  80.3 15.9 %collective-permute-start.32 = (bf16[512,1024]{1,0:T(8,128)(2,1)S(1)}, bf16[512,1024]{1,0:T(8,128)(2,1)}, u32[]{:S(2)}, u32[]{:S(2)}) collective-permute-start(bf16[512,1024]{1,0:T(8,128)(2,1)S(1)} %get-tuple-element.74), channel_id=1, source_target_pairs={{0,2},{1,7},{2,4},{3,1},{4,6},{5,3},{6,0},{7,5},{8,10},{9,15},{10,... | collective-permute-start | bytes 3145736 | tf_op jit(solution)/shard_map/ppermute | solution.py:37
  83.7 22.6 %collective-permute-start.36 = (bf16[512,1024]{1,0:T(8,128)(2,1)S(1)}, bf16[512,1024]{1,0:T(8,128)(2,1)S(1)}, u32[]{:S(2)}, u32[]{:S(2)}) collective-permute-start(bf16[512,1024]{1,0:T(8,128)(2,1)S(1)} %add_convert_fusion), channel_id=1, source_target_pairs={{0,2},{1,7},{2,4},{3,1},{4,6},{5,3},{6,0},{7,5},{8,10},{9,15},{10,... | collective-permute-start | bytes 3145736 | tf_op jit(solution)/shard_map/ppermute | solution.py:37
  88.2 19.5 %copy-start.2 = (f32[512,1024]{1,0:T(8,128)}, f32[512,1024]{1,0:T(8,128)S(1)}, u32[]{:S(2)}) copy-start(f32[512,1024]{1,0:T(8,128)S(1)} %get-tuple-element.56.refs_5_) | copy-start | bytes 6291460
  93.9 17.2 %collective-permute-start.23 = (bf16[4,2,64,1024]{3,2,1,0:T(8,128)(2,1)S(1)}, bf16[4,2,64,1024]{3,2,1,0:T(8,128)(2,1)S(1)}, u32[]{:S(2)}, u32[]{:S(2)}) collective-permute-start(bf16[4,2,64,1024]{3,2,1,0:T(8,128)(2,1)S(1)} %collective-permute-done.18), channel_id=1, source_target_pairs={{0,1},{1,0},{2,3},{3,2},{4,5},{5,4},{6,7},{7,6},{8,9},{9,8},{10,11... | collective-permute-start | bytes 3145736 | tf_op jit(solution)/shard_map/ppermute | solution.py:37
  98.1 19.4 %collective-permute-start.33 = (bf16[512,1024]{1,0:T(8,128)(2,1)S(1)}, bf16[512,1024]{1,0:T(8,128)(2,1)}, u32[]{:S(2)}, u32[]{:S(2)}) collective-permute-start(bf16[512,1024]{1,0:T(8,128)(2,1)S(1)} %fusion.2), channel_id=1, source_target_pairs={{0,2},{1,7},{2,4},{3,1},{4,6},{5,3},{6,0},{7,5},{8,10},{9,15},{10,... | collective-permute-start | bytes 3145736 | tf_op jit(solution)/shard_map/ppermute | solution.py:37
  101.2 15.7 %collective-permute-start.21 = (bf16[4,2,64,1024]{3,2,1,0:T(8,128)(2,1)S(1)}, bf16[4,2,64,1024]{3,2,1,0:T(8,128)(2,1)S(1)}, u32[]{:S(2)}, u32[]{:S(2)}) collective-permute-start(bf16[4,2,64,1024]{3,2,1,0:T(8,128)(2,1)S(1)} %collective-permute-done.18), channel_id=1, source_target_pairs={{0,32},{1,97},{2,34},{3,99},{4,36},{5,101},{6,38},{7,103},{8,40},{... | collective-permute-start | bytes 3145736 | tf_op jit(solution)/shard_map/ppermute | solution.py:37
  102.2 14.6 %collective-permute-start.22 = (bf16[4,2,64,1024]{3,2,1,0:T(8,128)(2,1)S(1)}, bf16[4,2,64,1024]{3,2,1,0:T(8,128)(2,1)S(1)}, u32[]{:S(2)}, u32[]{:S(2)}) collective-permute-start(bf16[4,2,64,1024]{3,2,1,0:T(8,128)(2,1)S(1)} %collective-permute-done.19.refs_5_), channel_id=1, source_target_pairs={{0,8},{1,25},{2,10},{3,27},{4,12},{5,29},{6,14},{7,31},{8,16},{9,1... | collective-permute-start | bytes 3145736 | tf_op jit(solution)/shard_map/ppermute | solution.py:37
  107.6 21.2 %collective-permute-start.37 = (bf16[512,1024]{1,0:T(8,128)(2,1)}, bf16[512,1024]{1,0:T(8,128)(2,1)}, u32[]{:S(2)}, u32[]{:S(2)}) collective-permute-start(bf16[512,1024]{1,0:T(8,128)(2,1)} %fusion), channel_id=1, source_target_pairs={{0,2},{1,7},{2,4},{3,1},{4,6},{5,3},{6,0},{7,5},{8,10},{9,15},{10,... | collective-permute-start | bytes 3145736 | tf_op jit(solution)/shard_map/ppermute | solution.py:37
  111.1 23.0 %collective-permute-start.30 = (bf16[4,2,64,1024]{3,2,1,0:T(8,128)(2,1)S(1)}, bf16[4,2,64,1024]{3,2,1,0:T(8,128)(2,1)}, u32[]{:S(2)}, u32[]{:S(2)}) collective-permute-start(bf16[4,2,64,1024]{3,2,1,0:T(8,128)(2,1)S(1)} %bitcast_dynamic-update-slice_fusion.refs_5_), channel_id=1, source_target_pairs={{0,1},{1,0},{2,3},{3,2},{4,5},{5,4},{6,7},{7,6},{8,9},{9,8},{10,11... | collective-permute-start | bytes 3145736 | tf_op jit(solution)/shard_map/ppermute | solution.py:37
  111.1 17.8 %copy-start.3 = (bf16[3,512,1024]{2,1,0:T(8,128)(2,1)S(1)}, bf16[3,512,1024]{2,1,0:T(8,128)(2,1)}, u32[]{:S(2)}) copy-start(bf16[3,512,1024]{2,1,0:T(8,128)(2,1)} %get-tuple-element.73) | copy-start | bytes 9437188
  116.8 17.2 %copy-start.1 = (f32[512,1024]{1,0:T(8,128)}, f32[512,1024]{1,0:T(8,128)S(1)}, u32[]{:S(2)}) copy-start(f32[512,1024]{1,0:T(8,128)S(1)} %get-tuple-element.64.refs_9_) | copy-start | bytes 6291460
  116.9 20.5 %collective-permute-start.29 = (bf16[4,2,64,1024]{3,2,1,0:T(8,128)(2,1)S(1)}, bf16[4,2,64,1024]{3,2,1,0:T(8,128)(2,1)S(1)}, u32[]{:S(2)}, u32[]{:S(2)}) collective-permute-start(bf16[4,2,64,1024]{3,2,1,0:T(8,128)(2,1)S(1)} %collective-permute-done.21), channel_id=1, source_target_pairs={{0,1},{1,0},{2,3},{3,2},{4,5},{5,4},{6,7},{7,6},{8,9},{9,8},{10,11... | collective-permute-start | bytes 3145736 | tf_op jit(solution)/shard_map/ppermute | solution.py:37
  117.5 21.4 %collective-permute-start.31 = (bf16[4,2,64,1024]{3,2,1,0:T(8,128)(2,1)S(1)}, bf16[4,2,64,1024]{3,2,1,0:T(8,128)(2,1)S(1)}, u32[]{:S(2)}, u32[]{:S(2)}) collective-permute-start(bf16[4,2,64,1024]{3,2,1,0:T(8,128)(2,1)S(1)} %collective-permute-done.22.refs_6_), channel_id=1, source_target_pairs={{0,1},{1,0},{2,3},{3,2},{4,5},{5,4},{6,7},{7,6},{8,9},{9,8},{10,11... | collective-permute-start | bytes 3145736 | tf_op jit(solution)/shard_map/ppermute | solution.py:37
  117.6 21.3 %collective-permute-start.24 = (bf16[4,2,64,1024]{3,2,1,0:T(8,128)(2,1)S(1)}, bf16[4,2,64,1024]{3,2,1,0:T(8,128)(2,1)S(1)}, u32[]{:S(2)}, u32[]{:S(2)}) collective-permute-start(bf16[4,2,64,1024]{3,2,1,0:T(8,128)(2,1)S(1)} %collective-permute-done.21), channel_id=1, source_target_pairs={{0,32},{1,97},{2,34},{3,99},{4,36},{5,101},{6,38},{7,103},{8,40},{... | collective-permute-start | bytes 3145736 | tf_op jit(solution)/shard_map/ppermute | solution.py:37
  128.8 17.4 %collective-permute-start.26 = (bf16[4,2,64,1024]{3,2,1,0:T(8,128)(2,1)S(1)}, bf16[4,2,64,1024]{3,2,1,0:T(8,128)(2,1)S(1)}, u32[]{:S(2)}, u32[]{:S(2)}) collective-permute-start(bf16[4,2,64,1024]{3,2,1,0:T(8,128)(2,1)S(1)} %collective-permute-done.22.refs_6_), channel_id=1, source_target_pairs={{0,8},{1,25},{2,10},{3,27},{4,12},{5,29},{6,14},{7,31},{8,16},{9,1... | collective-permute-start | bytes 3145736 | tf_op jit(solution)/shard_map/ppermute | solution.py:37
  134.1 26.1 %collective-permute-start.34 = (bf16[512,1024]{1,0:T(8,128)(2,1)}, bf16[512,1024]{1,0:T(8,128)(2,1)S(1)}, u32[]{:S(2)}, u32[]{:S(2)}) collective-permute-start(bf16[512,1024]{1,0:T(8,128)(2,1)} %fusion.3), channel_id=1, source_target_pairs={{0,2},{1,7},{2,4},{3,1},{4,6},{5,3},{6,0},{7,5},{8,10},{9,15},{10,... | collective-permute-start | bytes 3145736 | tf_op jit(solution)/shard_map/ppermute | solution.py:37
  137.4 27.6 %collective-permute-start.38 = (bf16[512,1024]{1,0:T(8,128)(2,1)}, bf16[512,1024]{1,0:T(8,128)(2,1)S(1)}, u32[]{:S(2)}, u32[]{:S(2)}) collective-permute-start(bf16[512,1024]{1,0:T(8,128)(2,1)} %fusion.1), channel_id=1, source_target_pairs={{0,8},{1,9},{2,10},{3,11},{4,12},{5,13},{6,14},{7,15},{8,0},{9,1},... | collective-permute-start | bytes 3145736 | tf_op jit(solution)/shard_map/ppermute | solution.py:37
  138.9 7.4 %copy-start.4 = (bf16[4,2,64,1024]{3,2,1,0:T(8,128)(2,1)}, bf16[4,2,64,1024]{3,2,1,0:T(8,128)(2,1)S(1)}, u32[]{:S(2)}) copy-start(bf16[4,2,64,1024]{3,2,1,0:T(8,128)(2,1)S(1)} %collective-permute-done.31.refs_8_) | copy-start | bytes 3145732
  138.9 28.0 %collective-permute-start.27 = (bf16[4,2,64,1024]{3,2,1,0:T(8,128)(2,1)S(1)}, bf16[4,2,64,1024]{3,2,1,0:T(8,128)(2,1)S(1)}, u32[]{:S(2)}, u32[]{:S(2)}) collective-permute-start(bf16[4,2,64,1024]{3,2,1,0:T(8,128)(2,1)S(1)} %collective-permute-done.19.refs_5_), channel_id=1, source_target_pairs={{0,1},{1,0},{2,3},{3,2},{4,5},{5,4},{6,7},{7,6},{8,9},{9,8},{10,11... | collective-permute-start | bytes 3145736 | tf_op jit(solution)/shard_map/ppermute | solution.py:37
  138.9 28.0 %collective-permute-start.25 = (bf16[4,2,64,1024]{3,2,1,0:T(8,128)(2,1)S(1)}, bf16[4,2,64,1024]{3,2,1,0:T(8,128)(2,1)S(1)}, u32[]{:S(2)}, u32[]{:S(2)}) collective-permute-start(bf16[4,2,64,1024]{3,2,1,0:T(8,128)(2,1)S(1)} %collective-permute-done.24), channel_id=1, source_target_pairs={{0,1},{1,0},{2,3},{3,2},{4,5},{5,4},{6,7},{7,6},{8,9},{9,8},{10,11... | collective-permute-start | bytes 3145736 | tf_op jit(solution)/shard_map/ppermute | solution.py:37
  146.3 20.6 %collective-permute-start.28 = (bf16[4,2,64,1024]{3,2,1,0:T(8,128)(2,1)S(1)}, bf16[4,2,64,1024]{3,2,1,0:T(8,128)(2,1)}, u32[]{:S(2)}, u32[]{:S(2)}) collective-permute-start(bf16[4,2,64,1024]{3,2,1,0:T(8,128)(2,1)S(1)} %collective-permute-done.26.refs_6_), channel_id=1, source_target_pairs={{0,1},{1,0},{2,3},{3,2},{4,5},{5,4},{6,7},{7,6},{8,9},{9,8},{10,11... | collective-permute-start | bytes 3145736 | tf_op jit(solution)/shard_map/ppermute | solution.py:37
  (1 other events, 1.0 us)

commit v2 on v1

--- a/solution.py
+++ b/solution.py
@@ -39,14 +39,6 @@
 
 def swap_core(value):
     return permute(value, lambda x, z, y, c: (x, z, y, 1 - c))
-
-
-def ring_x(value):
-    return permute(value, lambda x, z, y, c: (x + 1 - 2 * c, z, y, c))
-
-
-def ring_z(value):
-    return permute(value, lambda x, z, y, c: (x, z + 1 - 2 * c, y, c))
 
 
 def ring_y(value):
@@ -148,42 +140,23 @@
         ),
         compiler_params=params(),
         cost_estimate=pl.CostEstimate(
-            flops=count * 4 * TOK * 512 * COLS,
-            bytes_accessed=(count * 2 + 2) << 20,
+            flops=0,
+            bytes_accessed=1 << 20,
             transcendentals=0,
         ),
         name="grad",
     )(table, tokens, tokens_theirs, cot, cot_theirs)
 
 
-def w_pieces(kind, at, sources, mine, dy):
-    z, y, c = at[1], at[2], at[4]
-    core = c if mine else 1 - c
-    if kind == "x":
-        (chunk, xs) = sources
-        pieces = [(chunk.at[pl.ds(zh * 4, 4)], zh) for zh in range(2)]
-        columns = []
-        for zl, d in itertools.product(range(2), range(2)):
-            f = zl * 8 + ((y + d) & 3) * 2 + core
-            columns.append((f * 512 + xs * 128, (zl * 2 + d) * 128, 128))
-    else:
-        (chunks, zs) = sources
-        pieces = [
-            (chunk.at[pl.ds(0, 4), dy], zc >> 1) for chunk, zc in zip(chunks, zs)
-        ]
-        f = (zs[0] & 1) * 8 + ((y + 2 + dy) & 3) * 2 + core
-        columns = [(f * 512, 0, 512)]
-    return pieces, columns
-
-
-def fold_kernel(steps, pairs, first, last, *refs):
+OFFSETS = (0, -1, 2, 1)
+
+
+def fold_kernel(groups, chunks, first, last, *refs):
     refs = list(refs)
     at, tokens, cot = refs[:3]
     refs = refs[3:]
-    x_mine = [refs.pop(0) for _ in steps]
-    x_theirs = [refs.pop(0) for _ in steps]
-    z_mine = [[refs.pop(0) for _ in pair] for pair in pairs]
-    z_theirs = [[refs.pop(0) for _ in pair] for pair in pairs]
+    mine = {key: refs.pop(0) for key in chunks}
+    theirs = {key: refs.pop(0) for key in chunks}
     if not first:
         acc_in, _, _ = refs.pop(0), refs.pop(0), refs.pop(0)
     grad_out, weights_out, key_out = refs.pop(0), refs.pop(0), refs.pop(0)
@@ -193,45 +166,86 @@
     if last:
         key_v = refs[11]
     x, z, y, c = at[0], at[1], at[2], at[4]
-    way = 1 - 2 * c
-
-    groups = []
-    for s, mine, theirs in zip(steps, x_mine, x_theirs):
-        groups.append(("x", (mine, ((x - way * s + 8) & 3)), True, 0))
-        groups.append(("x", (theirs, ((x + way * s + 8) & 3)), False, 0))
-    for pair, mine, theirs in zip(pairs, z_mine, z_theirs):
-        zs_mine = [((z - way * s + 8) & 3) for s in pair]
-        zs_theirs = [((z + way * s + 8) & 3) for s in pair]
-        for dy in range(2):
-            groups.append(("z", (mine, zs_mine), True, dy))
-            groups.append(("z", (theirs, zs_theirs), False, dy))
+
+    def part(held, s, dy):
+        return held[s, dy] if (s, dy) in held else held[s].at[dy]
+
+    def x_of(s):
+        return (x + OFFSETS[s] + 4) & 3
+
+    def z_of(s):
+        return (z + OFFSETS[s] + 4) & 3
+
+    def columns_of(group):
+        if group[0] == "x":
+            _, s, dy = group
+            return [
+                (
+                    (zl * 8 + ((y + dy) & 3) * 2 + p) * 512 + x_of(s) * 128,
+                    (zl * 2 + p) * 128,
+                    128,
+                )
+                for zl in range(2)
+                for p in range(2)
+            ]
+        _, (s, t), dy, p = group
+        return [(((z_of(s) & 1) * 8 + ((y + 2 + dy) & 3) * 2 + p) * 512, 0, 512)]
+
+    def load_weights(group, slot):
+        def start(held):
+            if group[0] == "x":
+                _, s, dy = group
+                for zl, zh in itertools.product(range(2), range(2)):
+                    pltpu.make_async_copy(
+                        part(held, s, dy).at[zh * 2 + zl],
+                        w.at[slot, pl.ds(zl * 2, 2), zh],
+                        w_sem.at[slot],
+                    ).start()
+            else:
+                _, pair, dy, p = group
+                for s in pair:
+                    pltpu.make_async_copy(
+                        part(held, s, dy).at[:, p],
+                        w.at[slot, :, z_of(s) >> 1],
+                        w_sem.at[slot],
+                    ).start()
+
+        here = 0 if group[0] == "x" else 1
+
+        @pl.when(c == here)
+        def _():
+            start(mine)
+
+        @pl.when(c != here)
+        def _():
+            start(theirs)
+
     count = len(groups)
 
     def loads(i):
-        kind, sources, is_mine, dy = groups[i]
         slot = i % 3
-        pieces, columns = w_pieces(kind, at, sources, is_mine, dy)
-        for src, zh in pieces:
-            pltpu.make_async_copy(src, w.at[slot, :, zh], w_sem.at[slot]).start()
-        for a, b, n in columns:
+        load_weights(groups[i], slot)
+        for a, b, n in columns_of(groups[i]):
             pltpu.make_async_copy(
                 tokens.at[:, pl.ds(pl.multiple_of(a, 128), n)],
                 tok.at[slot, :, pl.ds(b, n)],
                 tok_sem.at[slot],
             ).start()
 
+    def holds_own(group):
+        return group[0] == "x" and group[2] == 0
+
     def weights_store(i):
-        kind, sources, is_mine, dy = groups[i]
         slot = i % 3
         return pltpu.make_async_copy(
-            w.at[slot, (z & 1) * 2], weights_out.at[sources[1]], own_sem.at[slot]
+            w.at[slot, (z & 1) * 2 + c],
+            weights_out.at[x_of(groups[i][1])],
+            own_sem.at[slot],
         )
 
     def stores(i):
-        kind, sources, is_mine, dy = groups[i]
         slot = i % 3
-        _, columns = w_pieces(kind, at, sources, is_mine, dy)
-        for a, b, n in columns:
+        for a, b, n in columns_of(groups[i]):
             pltpu.make_async_copy(
                 grad.at[slot, :, pl.ds(b, n)],
                 grad_out.at[:, pl.ds(pl.multiple_of(a, 128), n)],
@@ -263,7 +277,7 @@
 
         whole(w, w_sem, slot).wait()
         for k in range(count):
-            if groups[k][0] == "x" and groups[k][2]:
+            if holds_own(groups[k]):
 
                 @pl.when(i == k)
                 def _(k=k):
@@ -293,7 +307,7 @@
 
         acc[...] += jnp.dot(tok[slot], rows, preferred_element_type=F32)
         for k in range(count):
-            if groups[k][0] == "x" and groups[k][2]:
+            if holds_own(groups[k]):
 
                 @pl.when(i == k)
                 def _(k=k):
@@ -310,10 +324,9 @@
     key_copy.wait()
 
 
-def fold(at, tokens, cot, steps, x_mine, x_theirs, pairs, z_mine, z_theirs, carry, last):
+def fold(at, tokens, cot, groups, mine, theirs, carry, last):
     first = carry is None
-    operands = [at, tokens, cot, *x_mine, *x_theirs]
-    operands += list(itertools.chain(*z_mine)) + list(itertools.chain(*z_theirs))
+    operands = [at, tokens, cot, *mine.values(), *theirs.values()]
     aliases = {}
     if not first:
         operands += [carry[2]]
@@ -340,10 +353,8 @@
     ]
     if last:
         scratch += [pltpu.VMEM((TOK, COLS), BF)]
-    groups = 2 * len(steps) + 4 * len(pairs)
-
     def kernel(*refs):
-        fold_kernel(steps, pairs, first, last, *refs)
+        fold_kernel(groups, list(mine), first, last, *refs)
 
     return pl.pallas_call(
         kernel,
@@ -354,8 +365,7 @@
         input_output_aliases=aliases,
         compiler_params=params(),
         cost_estimate=pl.CostEstimate(
-            flops=groups * 4 * TOK * 512 * COLS,
-            bytes_accessed=groups * (2 << 20) + (4 << 20),
+            flops=0, bytes_accessed=1 << 20,
             transcendentals=0,
         ),
         name="fold",
@@ -369,28 +379,14 @@
     at = jnp.stack([x, z, y, zl, c]).astype(jnp.int32)
     blocks = deltas[0]
 
-    own_at = x * 2 + zh
-    summed = lax.dynamic_slice_in_dim(blocks, own_at * 64, 64, 0).astype(F32)
-    for dx, dh in ((2, 1), (1, 1), (3, 1), (2, 0), (0, 1), (1, 0), (3, 0)):
-        there = ((x + dx) & 3) * 2 + ((zh + dh) & 1)
-        piece = lax.dynamic_slice_in_dim(blocks, there * 64, 64, 0)
-        got = permute(
-            piece, lambda px, pz, py, pc: (px + dx, pz + 2 * dh, py, pc)
-        )
-        summed = summed + got.astype(F32)
-    mean_delta = summed / 8
-    moment_next = MOMENTUM_RATE * momentum[0, 0] + mean_delta
-    outer_next = outer_weights[0, 0] - OUTER_RATE * (
-        mean_delta + MOMENTUM_RATE * moment_next
-    )
-    owned = outer_next.astype(BF)
-
     tokens_theirs = swap_core(other_half(at, tokens))
     cot_theirs = swap_core(key_cot)
 
-    def grads(half, steps, tokens_theirs):
-        zl_to = 1 - zl if half == 0 else zl
-        blocks = [zl_to * 4 + ((y - way * (s + 1) + 8) & 3) for s in steps]
+    def grads(which, tokens_theirs):
+        blocks = [
+            (zl if half else 1 - zl) * 4 + ((y - way * (s + 1) + 8) & 3)
+            for half, s in which
+        ]
         return grad_blocks(blocks, c, tokens, tokens_theirs, key_cot, cot_theirs)
 
     def add(*parts):
@@ -399,67 +395,105 @@
             total = total + part.astype(F32)
         return total
 
-    (first,) = grads(0, (0,), tokens_theirs)
-    owned, first, late = lax.optimization_barrier((owned, first, tokens_theirs))
-    second, rest = grads(0, (1, 2, 3), late)
-
-    def rows_from(value, dx=0, dz=0, dy=0):
+    by_x = blocks.reshape(4, 2, 64, COLS)
+    got = []
+    for d in (2, 1, 3):
+        piece = lax.dynamic_index_in_dim(by_x, (x + d) & 3, 0, False)
+        got.append(permute(piece, lambda px, pz, py, pc: (px + d, pz, py, pc)))
+    first, first_b = grads([(0, 0), (1, 0)], tokens_theirs)
+    *got, first, first_b = lax.optimization_barrier((*got, first, first_b[0]))
+    arrived, arrived_b = ring_y(first), ring_y(first_b)
+    part = add(lax.dynamic_index_in_dim(by_x, x, 0, False), *got)
+    crossing = lax.dynamic_index_in_dim(part, 1 - zh, 0, False).astype(BF)
+    crossing = permute(crossing, lambda px, pz, py, pc: (px, pz + 2, py, pc))
+    summed = add(lax.dynamic_index_in_dim(part, zh, 0, False), crossing)
+    mean_delta = summed / 8
+    moment_next = MOMENTUM_RATE * momentum[0, 0] + mean_delta
+    outer_next = outer_weights[0, 0] - OUTER_RATE * (
+        mean_delta + MOMENTUM_RATE * moment_next
+    )
+    owned = outer_next.astype(BF)
+
+    def short_way(value, d):
         return permute(
-            value, lambda px, pz, py, pc: (px - dx, pz - dz, py - dy, pc)
+            value,
+            lambda px, pz, py, pc: (px - d * pc, pz - d * (1 - pc), py, pc),
+        )
+
+    def long_way(value, d):
+        return permute(
+            value,
+            lambda px, pz, py, pc: (px + d * (1 - pc), pz + d * pc, py, pc),
         )
 
     def in_order(parts, here):
-        whole = jnp.zeros((4, *parts[0].shape), BF)
+        whole = jnp.zeros((2, 4, 2, 64, COLS), BF)
         for d, part in enumerate(parts):
             whole = lax.dynamic_update_slice_in_dim(
-                whole, part[None], (here + d) & 3, 0
+                whole, part[:, None], (here + d) & 3, 1
             )
         return whole
 
-    by_y = [owned] + [rows_from(owned, dy=d) for d in (1, 2, 3)]
-    a0 = jnp.stack(by_y[:2])
-    b0 = jnp.stack(by_y[2:])
-    a0, b0, rest, late = lax.optimization_barrier((a0, b0, rest, late))
-    first_b, rest_b = grads(1, (0, 1, 2, 3), late)
-    a1 = in_order([a0] + [rows_from(a0, dz=d) for d in (1, 2, 3)], z)
-    b1 = in_order([b0] + [rows_from(b0, dx=d) for d in (1, 2, 3)], x)
-    a1, b1, rest_b = lax.optimization_barrier((a1, b1, rest_b))
-    a_mine, b_mine = [a1], [b1]
-    a_theirs, b_theirs = [swap_core(a1)], [swap_core(b1)]
-
-    def fold_of(steps, pairs, carry, last):
+    owned, late = lax.optimization_barrier((owned, tokens_theirs))
+    second, second_b = grads([(0, 1), (1, 1)], late)
+    other, arrived = lax.optimization_barrier((swap_core(owned), arrived))
+    both = jnp.where(c == 0, jnp.stack([owned, other]), jnp.stack([other, owned]))
+    near = permute(both, lambda px, pz, py, pc: (px, pz, py - 1 + 2 * pc, pc))
+    far = permute(both, lambda px, pz, py, pc: (px, pz, py + 2 * pc, pc))
+    c0 = jnp.stack([far, near])
+    c0, second, second_b, late = lax.optimization_barrier(
+        (c0, second, second_b[0], late)
+    )
+    third, rest = grads([(0, 2), (0, 3), (1, 2), (1, 3)], late)
+    parts = [short_way(c0, d) for d in (1, 2, 3)]
+    arrived = ring_y(add(second, arrived).astype(BF))
+    parts[0], arrived_b = lax.optimization_barrier((parts[0], arrived_b))
+    c1 = in_order([c0] + parts, jnp.where(c == 0, z, x))
+    c1, third, rest, arrived = lax.optimization_barrier((c1, third, rest, arrived))
+
+    mine, theirs = {0: c1}, {0: swap_core(c1)}
+    mine[1], mine[3] = long_way(c1, 1), long_way(c1, -1)
+
+    def fold_of(groups, keys, carry, last):
         return fold(
-            at, tokens, key_cot, steps,
-            [a_mine[s].reshape(8, 64, COLS) for s in steps],
-            [a_theirs[s].reshape(8, 64, COLS) for s in steps],
-            pairs,
-            [[b_mine[s] for s in pair] for pair in pairs],
-            [[b_theirs[s] for s in pair] for pair in pairs],
-            carry, last,
-        )
-
-    carry = None
-    for s, pairs in ((1, ()), (2, ()), (3, ((0, 2),))):
-        a_next, b_next = ring_x(a_mine[-1]), ring_z(b_mine[-1])
-        carry = fold_of((s - 1,), pairs, carry, False)
-        if s < 3:
-            a_next, b_next, *carry = lax.optimization_barrier((a_next, b_next, *carry))
-        a_mine.append(a_next)
-        b_mine.append(b_next)
-        a_theirs.append(swap_core(a_next))
-        b_theirs.append(swap_core(b_next))
-    grad_tokens, shard_weights, keys_out = fold_of((3,), ((1, 3),), carry, True)
+            at, tokens, key_cot, groups,
+            {k: mine[k] for k in keys}, {k: theirs[k] for k in keys}, carry, last,
+        )
+
+    carry = fold_of([("x", 0, 0), ("x", 0, 1)], [0], None, False)
+    arrived = ring_y(add(third, arrived).astype(BF))
+    mine[1], mine[3], arrived, arrived_b, *carry = lax.optimization_barrier(
+        (mine[1], mine[3], arrived, arrived_b, *carry)
+    )
+    mine[2, 0] = long_way(mine[1][0], 1)
+    mine[2, 1] = long_way(mine[3][1], -1)
+    theirs[1], theirs[3] = swap_core(mine[1]), swap_core(mine[3])
+    crossed = add(rest[0], arrived).astype(BF)
+    crossed = [
+        permute(half, lambda px, pz, py, pc: (px, pz ^ 1, py, pc))
+        for half in (crossed[:256], crossed[256:])
+    ]
+    arrived_b = ring_y(add(second_b, arrived_b).astype(BF))
+    carry = fold_of(
+        [("x", s, dy) for s in (1, 3) for dy in range(2)]
+        + [("z", (1, 3), dy, p) for dy in range(2) for p in range(2)],
+        [1, 3], carry, False,
+    )
+    mine[2, 0], mine[2, 1], arrived_b, crossed[0], *carry = lax.optimization_barrier(
+        (mine[2, 0], mine[2, 1], arrived_b, crossed[0], *carry)
+    )
+    theirs[2, 0], theirs[2, 1] = swap_core(mine[2, 0]), swap_core(mine[2, 1])
+    arrived_b = ring_y(add(rest[1], arrived_b).astype(BF))
+    grad_tokens, shard_weights, keys_out = fold_of(
+        [("x", 2, dy) for dy in range(2)]
+        + [("z", (0, 2), dy, p) for dy in range(2) for p in range(2)],
+        [0, (2, 0), (2, 1)], carry, True,
+    )
+    arrived_b, *crossed, keys_out = lax.optimization_barrier(
+        (arrived_b, *crossed, keys_out)
+    )
+    grad_shard = add(rest[2], arrived_b, jnp.concatenate(crossed))
     shard_weights = shard_weights.reshape(512, COLS)
-
-    arrived = ring_y(first)
-    arrived = ring_y(add(second, arrived).astype(BF))
-    arrived = ring_y(add(rest[0], arrived).astype(BF))
-    crossed = add(rest[1], arrived).astype(BF)
-    crossed = permute(crossed, lambda px, pz, py, pc: (px, pz ^ 1, py, pc))
-    arrived = ring_y(first_b)
-    arrived = ring_y(add(rest_b[0], arrived).astype(BF))
-    arrived = ring_y(add(rest_b[1], arrived).astype(BF))
-    grad_shard = add(rest_b[2], arrived, crossed)
 
     return (
         outer_next[None, None],

time: 181 us -> 156 us (0.86)
  starting transfers between devices: 57.8 us -> 38.4 us
  waiting for transfers between devices: 47.3 us -> 39.1 us
  local copies, waits for them, and re-layouts: 2.98 us -> 6.38 us
    ppermute x39 -> x29, starting transfers between devices: 57.8 us -> 38.4 us  [permute(): return lax.ppermute(value, AXES, pairs)]
    ppermute x39 -> x29, waiting for transfers between devices: 47.3 us -> 39.1 us  [permute(): return lax.ppermute(value, AXES, pairs)]
    convert_element_type x4, other arithmetic: 8.55 us -> 4.29 us  [the longest x1 1.84 us: per_device(): arrived_b = ring_y(add(second_b, arrived_b).astype(BF))]
    dynamic_update_slice x8 -> x4, local copies, waits for them, and re-layouts: 0.18 us -> 3.29 us  [in_order(): lax.dynamic_update_slice_in_dim(whole, part[:, None], here + d & 3, 1)]
    pallas_call x4 -> x3, Pallas kernels: 35.9 us -> 33.7 us  [fold(): pl.pallas_call(kernel, out_shape=shapes, in_specs=[pl.BlockSpec(memory_sp...]
    convert_element_type x1, other arithmetic: 0.41 us -> 2.6 us  [per_device(): arrived = ring_y(add(second, arrived).astype(BF))]
    another operation x2 -> x1, other arithmetic: 0.06 us -> 1.87 us  [per_device(): c0 = jnp.stack([far, near])]
  transfers between devices with their start and end apart: 39 -> 29, of which waited for: 12 -> 13; matrix products, arithmetic and copies ran while one was open for 8% -> 10% of each run, Pallas kernels for 21% -> 34%
where the time goes in v2:
time: 156 us
  Pallas kernels  57.7 us (37%)
  waiting for transfers between devices  39.1 us (25%)
  starting transfers between devices  38.4 us (25%)
  other arithmetic  13.1 us (8%)
  local copies, waits for them, and re-layouts  6.38 us (4%)
    ppermute x29, waiting for transfers between devices, permute(): return lax.ppermute(value, AXES, pairs)  39.1 us
    ppermute x29, starting transfers between devices, permute(): return lax.ppermute(value, AXES, pairs)  38.4 us
    pallas_call x3, Pallas kernels, fold(): pl.pallas_call(kernel, out_shape=shapes, in_specs=[pl.BlockSpec(memory_sp...  33.7 us
    pallas_call x3, Pallas kernels, grad_blocks(): pl.pallas_call(grad_kernel, out_shape=[jax.ShapeDtypeStruct((512, COLS),...  19.7 us
    pallas_call x1, Pallas kernels, other_half(): pl.pallas_call(half_kernel, out_shape=jax.ShapeDtypeStruct((TOK, D // 2),...  4.33 us
    dynamic_update_slice x4, local copies, waits for them, and re-layouts, in_order(): lax.dynamic_update_slice_in_dim(whole, part[:, None], here + d & 3, 1)  3.29 us
  transfers between devices with their start and end apart: 29, of which 13 were waited for; matrix products, arithmetic and copies ran while one was open for 10% of the time, Pallas kernels for 34%

profile of v2, /device:TPU:1, one launch (start us, length us, event | category | flops | bytes accessed | tf_op | source)
XLA Modules:
  0.0 155.6 jit_solution(15531603505267983869)
XLA Ops:
  0.7 4.3 %half.1 = bf16[512,4096]{1,0:T(8,128)(2,1)} custom-call(s32[5]{0:T(128)S(1)} %stack.108.at.refs_0_, bf16[512,8192]{1,0:T(8,128)(2,1)} %refs_1_.5), custom_call_target="tpu_custom_call" | custom-call | bytes 8388608 | tf_op jit(solution)/shard_map/half/pallas_call | solution.py:80
  5.1 1.5 collective-permute-start.3
  6.7 0.9 dynamic-slice_bitcast_fusion
  7.5 2.8 %collective-permute-start = (bf16[2,64,1024]{2,1,0:T(8,128)(2,1)}, bf16[2,64,1024]{2,1,0:T(8,128)(2,1)S(1)}, u32[]{:S(2)}, u32[]{:S(2)}) collective-permute-start(bf16[2,64,1024]{2,1,0:T(8,128)(2,1)} %get-tuple-element.116), channel_id=1, source_target_pairs={{0,64},{1,65},{2,66},{3,67},{4,68},{5,69},{6,70},{7,71},{8,72},{9,... | collective-permute-start | bytes 786440 | tf_op jit(solution)/shard_map/ppermute | solution.py:37
  10.7 2.4 %collective-permute-start.2 = (bf16[2,64,1024]{2,1,0:T(8,128)(2,1)S(1)}, bf16[2,64,1024]{2,1,0:T(8,128)(2,1)}, u32[]{:S(2)}, u32[]{:S(2)}) collective-permute-start(bf16[2,64,1024]{2,1,0:T(8,128)(2,1)S(1)} %get-tuple-element.114), channel_id=1, source_target_pairs={{0,96},{1,97},{2,98},{3,99},{4,100},{5,101},{6,102},{7,103},{8,104... | collective-permute-start | bytes 786440 | tf_op jit(solution)/shard_map/ppermute | solution.py:37
  13.1 1.6 %collective-permute-done.4.cot_theirs = bf16[512,1024]{1,0:T(8,128)(2,1)S(1)} collective-permute-done((bf16[512,1024]{1,0:T(8,128)(2,1)S(1)}, bf16[512,1024]{1,0:T(8,128)(2,1)S(1)}, u32[]{:S(2)}, u32[]{:S(2)}) %collective-permute-start.4) | collective-permute-done | bytes 1048608 | tf_op jit(solution)/shard_map/ppermute | solution.py:37
  15.2 6.1 %grad.3 = (bf16[512,1024]{1,0:T(8,128)(2,1)}, bf16[1,512,1024]{2,1,0:T(8,128)(2,1)}) custom-call(s32[4]{0:T(128)S(1)} %pad_add_fusion.blocks, bf16[512,8192]{1,0:T(8,128)(2,1)} %refs_1_.5, bf16[512,4096]{1,0:T(8,128)(2,1)} %collective-permute-done.3.theirs, bf16[512,1024]{1,0:T(8,128)(2,1)S(1)} %copy-done, ...), custom_call_target="tpu_custom_call" | custom-call | bytes 1048576 | tf_op jit(solution)/shard_map/grad/pallas_call | solution.py:121
  21.3 1.8 %collective-permute-done.1 = bf16[2,64,1024]{2,1,0:T(8,128)(2,1)S(1)} collective-permute-done((bf16[2,64,1024]{2,1,0:T(8,128)(2,1)}, bf16[2,64,1024]{2,1,0:T(8,128)(2,1)S(1)}, u32[]{:S(2)}, u32[]{:S(2)}) %collective-permute-start.1) | collective-permute-done | bytes 262176 | tf_op jit(solution)/shard_map/ppermute | solution.py:37
  23.1 2.8 %collective-permute-start.7 = (bf16[512,1024]{1,0:T(8,128)(2,1)}, bf16[512,1024]{1,0:T(8,128)(2,1)}, u32[]{:S(2)}, u32[]{:S(2)}) collective-permute-start(bf16[512,1024]{1,0:T(8,128)(2,1)} %get-tuple-element.64), channel_id=1, source_target_pairs={{0,2},{1,7},{2,4},{3,1},{4,6},{5,3},{6,0},{7,5},{8,10},{9,15},{10,... | collective-permute-start | bytes 3145736 | tf_op jit(solution)/shard_map/ppermute | solution.py:37
  25.9 1.3 fusion.5
  27.3 3.7 %collective-permute-start.5 = (bf16[64,1024]{1,0:T(8,128)(2,1)S(1)}, bf16[64,1024]{1,0:T(8,128)(2,1)S(1)}, u32[]{:S(2)}, u32[]{:S(2)}) collective-permute-start(bf16[64,1024]{1,0:T(8,128)(2,1)S(1)} %fusion.8), channel_id=1, source_target_pairs={{0,16},{1,17},{2,18},{3,19},{4,20},{5,21},{6,22},{7,23},{8,24},{9,... | collective-permute-start | bytes 393224 | tf_op jit(solution)/shard_map/ppermute | solution.py:37
  31.0 3.5 %collective-permute-done.5 = bf16[64,1024]{1,0:T(8,128)(2,1)S(1)} collective-permute-done((bf16[64,1024]{1,0:T(8,128)(2,1)S(1)}, bf16[64,1024]{1,0:T(8,128)(2,1)S(1)}, u32[]{:S(2)}, u32[]{:S(2)}) %collective-permute-start.5) | collective-permute-done | bytes 131104 | tf_op jit(solution)/shard_map/ppermute | solution.py:37
  34.5 0.9 fusion.9
  35.8 1.2 collective-permute-start.11
  37.0 1.0 collective-permute-done.7
  38.0 4.3 %collective-permute-start.8 = (bf16[2,64,1024]{2,1,0:T(8,128)(2,1)S(1)}, bf16[2,64,1024]{2,1,0:T(8,128)(2,1)}, u32[]{:S(2)}, u32[]{:S(2)}) collective-permute-start(bf16[2,64,1024]{2,1,0:T(8,128)(2,1)S(1)} %maximum_select_fusion), channel_id=1, source_target_pairs={{0,0},{1,5},{2,2},{3,7},{4,4},{5,1},{6,6},{7,3},{8,8},{9,13},{10,1... | collective-permute-start | bytes 786440 | tf_op jit(solution)/shard_map/ppermute | solution.py:37
  42.3 1.4 collective-permute-start.9
  43.8 4.8 %grad.4 = (bf16[512,1024]{1,0:T(8,128)(2,1)S(1)}, bf16[1,512,1024]{2,1,0:T(8,128)(2,1)S(1)}) custom-call(s32[4]{0:T(128)S(1)} %pad_add_fusion.1.blocks, bf16[512,8192]{1,0:T(8,128)(2,1)} %refs_1_.5, bf16[512,4096]{1,0:T(8,128)(2,1)} %collective-permute-done.3.theirs, bf16[512,1024]{1,0:T(8,128)(2,1)S(1)} %copy-done, ...), custom_call_target="tpu_custom_call" | custom-call | bytes 1048576 | tf_op jit(solution)/shard_map/grad/pallas_call | solution.py:121
  48.5 1.1 collective-permute-done.8
  49.6 4.5 %collective-permute-done.9 = bf16[2,64,1024]{2,1,0:T(8,128)(2,1)} collective-permute-done((bf16[2,64,1024]{2,1,0:T(8,128)(2,1)S(1)}, bf16[2,64,1024]{2,1,0:T(8,128)(2,1)}, u32[]{:S(2)}, u32[]{:S(2)}) %collective-permute-start.9) | collective-permute-done | bytes 262176 | tf_op jit(solution)/shard_map/ppermute | solution.py:37
  54.1 1.9 %pad_maximum_fusion = bf16[2,2,64,1024]{3,2,1,0:T(8,128)(2,1)} fusion(bf16[1,2,64,1024]{3,2,1,0:T(8,128)(2,1)} %bitcast.24, bf16[1,2,64,1024]{3,2,1,0:T(8,128)(2,1)} %bitcast.23), kind=kLoop, calls=%fused_computation.12 | loop fusion | flops 262144 | bytes 1048576 | tf_op jit(solution)/shard_map/stack | solution.py:443
  56.0 2.6 %collective-permute-start.10 = (bf16[2,2,64,1024]{3,2,1,0:T(8,128)(2,1)}, bf16[2,2,64,1024]{3,2,1,0:T(8,128)(2,1)}, u32[]{:S(2)}, u32[]{:S(2)}) collective-permute-start(bf16[2,2,64,1024]{3,2,1,0:T(8,128)(2,1)} %pad_maximum_fusion), channel_id=1, source_target_pairs={{0,24},{1,97},{2,26},{3,99},{4,28},{5,101},{6,30},{7,103},{8,0},{9... | collective-permute-start | bytes 1572872 | tf_op jit(solution)/shard_map/ppermute | solution.py:37
  58.5 2.6 %add_convert_fusion.2 = bf16[512,1024]{1,0:T(8,128)(2,1)} fusion(bf16[512,1024]{1,0:T(8,128)(2,1)} %collective-permute-done.7, bf16[512,1024]{1,0:T(8,128)(2,1)S(1)} %get-tuple-element.75), kind=kLoop, calls=%fused_computation.9 | loop fusion | flops 2097152 | bytes 3145728 | tf_op jit(solution)/shard_map/convert_element_type | solution.py:449
  61.1 3.4 %collective-permute-start.14 = (bf16[512,1024]{1,0:T(8,128)(2,1)}, bf16[512,1024]{1,0:T(8,128)(2,1)}, u32[]{:S(2)}, u32[]{:S(2)}) collective-permute-start(bf16[512,1024]{1,0:T(8,128)(2,1)} %add_convert_fusion.2), channel_id=1, source_target_pairs={{0,2},{1,7},{2,4},{3,1},{4,6},{5,3},{6,0},{7,5},{8,10},{9,15},{10,... | collective-permute-start | bytes 3145736 | tf_op jit(solution)/shard_map/ppermute | solution.py:37
  64.6 0.5 collective-permute-start.12
  65.5 1.1 bitcast_dynamic-update-slice_fusion.2
  66.6 8.8 %grad.5 = (bf16[512,1024]{1,0:T(8,128)(2,1)S(1)}, bf16[3,512,1024]{2,1,0:T(8,128)(2,1)}) custom-call(s32[8]{0:T(128)S(1)} %stack.129.blocks, bf16[512,8192]{1,0:T(8,128)(2,1)} %refs_1_.5, bf16[512,4096]{1,0:T(8,128)(2,1)} %collective-permute-done.3.theirs, bf16[512,1024]{1,0:T(8,128)(2,1)S(1)} %copy-done, bf16[512,1024]{1,0:T(8,128)(2,1)S(1)} %collective-permute-done.4.cot_theirs), custom_call_target="tpu_custom_call" | custom-call | bytes 1048576 | tf_op jit(solution)/shard_map/grad/pallas_call | solution.py:121
  75.4 1.1 bitcast_dynamic-update-slice_fusion.1
  76.5 1.1 bitcast_dynamic-update-slice_fusion
  77.6 2.3 %collective-permute-done.13 = bf16[2,2,64,1024]{3,2,1,0:T(8,128)(2,1)S(1)} collective-permute-done((bf16[2,2,64,1024]{3,2,1,0:T(8,128)(2,1)}, bf16[2,2,64,1024]{3,2,1,0:T(8,128)(2,1)S(1)}, u32[]{:S(2)}, u32[]{:S(2)}) %collective-permute-start.13) | collective-permute-done | bytes 524320 | tf_op jit(solution)/shard_map/ppermute | solution.py:37
  80.1 1.6 %collective-permute-start.15 = (bf16[2,4,2,64,1024]{4,3,2,1,0:T(8,128)(2,1)S(1)}, bf16[2,4,2,64,1024]{4,3,2,1,0:T(8,128)(2,1)S(1)}, u32[]{:S(2)}, u32[]{:S(2)}) collective-permute-start(bf16[2,4,2,64,1024]{4,3,2,1,0:T(8,128)(2,1)S(1)} %bitcast_dynamic-update-slice_fusion.3.refs_3_), channel_id=1, source_target_pairs={{0,32},{1,9},{2,34},{3,11},{4,36},{5,13},{6,38},{7,15},{8,40},{9,1... | collective-permute-start | bytes 6291464 | tf_op jit(solution)/shard_map/ppermute | solution.py:37
  81.7 2.2 %collective-permute-start.16 = (bf16[2,4,2,64,1024]{4,3,2,1,0:T(8,128)(2,1)S(1)}, bf16[2,4,2,64,1024]{4,3,2,1,0:T(8,128)(2,1)S(1)}, u32[]{:S(2)}, u32[]{:S(2)}) collective-permute-start(bf16[2,4,2,64,1024]{4,3,2,1,0:T(8,128)(2,1)S(1)} %bitcast_dynamic-update-slice_fusion.3.refs_3_), channel_id=1, source_target_pairs={{0,96},{1,25},{2,98},{3,27},{4,100},{5,29},{6,102},{7,31},{8,104},... | collective-permute-start | bytes 6291464 | tf_op jit(solution)/shard_map/ppermute | solution.py:37
  83.9 1.6 %add_convert_fusion.1 = bf16[512,1024]{1,0:T(8,128)(2,1)S(1)} fusion(bf16[512,1024]{1,0:T(8,128)(2,1)} %collective-permute-done.14, bf16[512,1024]{1,0:T(8,128)(2,1)S(1)} %get-tuple-element.78), kind=kLoop, calls=%fused_computation.8 | loop fusion | flops 2097152 | bytes 3145728 | tf_op jit(solution)/shard_map/convert_element_type | solution.py:464
  85.6 1.3 copy-done.4
  86.9 5.2 %fold.3 = (bf16[512,8192]{1,0:T(8,128)(2,1)}, bf16[4,2,64,1024]{3,2,1,0:T(8,128)(2,1)}, f32[512,1024]{1,0:T(8,128)S(1)}) custom-call(s32[5]{0:T(128)S(1)} %stack.108.at.refs_0_, bf16[512,8192]{1,0:T(8,128)(2,1)} %refs_1_.5, bf16[512,1024]{1,0:T(8,128)(2,1)S(1)} %copy-done, bf16[2,4,2,64,1024]{4,3,2,1,0:T(8,128)(2,1)S(1)} %bitcast_dynamic-update-slice_fusion.3.refs_3_, ...), custom_call_target="tpu_custom_call" | custom-call | bytes 1048576 | tf_op jit(solution)/shard_map/fold/pallas_call | solution.py:359
  92.2 7.3 %collective-permute-done.17 = bf16[512,1024]{1,0:T(8,128)(2,1)S(1)} collective-permute-done((bf16[512,1024]{1,0:T(8,128)(2,1)S(1)}, bf16[512,1024]{1,0:T(8,128)(2,1)S(1)}, u32[]{:S(2)}, u32[]{:S(2)}) %collective-permute-start.17) | collective-permute-done | bytes 1048608 | tf_op jit(solution)/shard_map/ppermute | solution.py:37
  99.5 7.9 %collective-permute-done.15.refs_3_ = bf16[2,4,2,64,1024]{4,3,2,1,0:T(8,128)(2,1)S(1)} collective-permute-done((bf16[2,4,2,64,1024]{4,3,2,1,0:T(8,128)(2,1)S(1)}, bf16[2,4,2,64,1024]{4,3,2,1,0:T(8,128)(2,1)S(1)}, u32[]{:S(2)}, u32[]{:S(2)}) %collective-permute-start.15) | collective-permute-done | bytes 2097184 | tf_op jit(solution)/shard_map/ppermute | solution.py:37
  108.0 1.8 %add_convert_fusion = bf16[512,1024]{1,0:T(8,128)(2,1)S(1)} fusion(bf16[512,1024]{1,0:T(8,128)(2,1)} %collective-permute-done.11, bf16[512,1024]{1,0:T(8,128)(2,1)S(1)} %bitcast.91), kind=kLoop, calls=%fused_computation.7 | loop fusion | flops 2097152 | bytes 3145728 | tf_op jit(solution)/shard_map/convert_element_type | solution.py:476
  110.0 1.3 collective-permute-start.19
  111.4 2.2 %collective-permute-start.20 = (bf16[4,2,64,1024]{3,2,1,0:T(8,128)(2,1)S(1)}, bf16[4,2,64,1024]{3,2,1,0:T(8,128)(2,1)S(1)}, u32[]{:S(2)}, u32[]{:S(2)}) collective-permute-start(bf16[4,2,64,1024]{3,2,1,0:T(8,128)(2,1)S(1)} %slice_bitcast_fusion), channel_id=1, source_target_pairs={{0,96},{1,25},{2,98},{3,27},{4,100},{5,29},{6,102},{7,31},{8,104},... | collective-permute-start | bytes 3145736 | tf_op jit(solution)/shard_map/ppermute | solution.py:37
  114.1 1.2 collective-permute-start.22
  115.5 15.6 %fold.4 = (bf16[512,8192]{1,0:T(8,128)(2,1)}, bf16[4,2,64,1024]{3,2,1,0:T(8,128)(2,1)}, f32[512,1024]{1,0:T(8,128)S(1)}) custom-call(s32[5]{0:T(128)S(1)} %stack.108.at.refs_0_, bf16[512,8192]{1,0:T(8,128)(2,1)} %refs_1_.5, bf16[512,1024]{1,0:T(8,128)(2,1)S(1)} %copy-done, ...), custom_call_target="tpu_custom_call", output_to_operand_aliasing={{0}: (8, {}), {1}: (9, {})} | custom-call | bytes 1048576 | tf_op jit(solution)/shard_map/fold/pallas_call | solution.py:359
  131.1 5.4 %collective-permute-done.22 = bf16[256,1024]{1,0:T(8,128)(2,1)S(1)} collective-permute-done((bf16[256,1024]{1,0:T(8,128)(2,1)S(1)}, bf16[256,1024]{1,0:T(8,128)(2,1)S(1)}, u32[]{:S(2)}, u32[]{:S(2)}) %collective-permute-start.22) | collective-permute-done | bytes 524320 | tf_op jit(solution)/shard_map/ppermute | solution.py:37
  137.6 1.1 collective-permute-start.27
  138.7 0.6 collective-permute-done.25.refs_7_
  139.3 1.5 collective-permute-done.26.refs_8_
  140.8 12.8 %fold.5 = (bf16[512,8192]{1,0:T(8,128)(2,1)}, bf16[4,2,64,1024]{3,2,1,0:T(8,128)(2,1)}, bf16[512,1024]{1,0:T(8,128)(2,1)}) custom-call(s32[5]{0:T(128)S(1)} %stack.108.at.refs_0_, bf16[512,8192]{1,0:T(8,128)(2,1)} %refs_1_.5, bf16[512,1024]{1,0:T(8,128)(2,1)S(1)} %copy-done, ...), custom_call_target="tpu_custom_call", output_to_operand_aliasing={{0}: (10, {}), {1}: (11, {})} | custom-call | bytes 1048576 | tf_op jit(solution)/shard_map/fold/pallas_call | solution.py:359
  153.6 1.9 %fusion.1 = f32[1,512,1024]{2,1,0:T(8,128)} fusion(bf16[512,1024]{1,0:T(8,128)(2,1)S(1)} %collective-permute-done.27, bf16[256,1024]{1,0:T(8,128)(2,1)S(1)} %collective-permute-done.28, bf16[256,1024]{1,0:T(8,128)(2,1)S(1)} %collective-permute-done.22, bf16[3,512,1024]{2,1,0:T(8,128)(2,1)S(1)} %copy-done.6), kind=kLoop, calls=%fused_computation.2 | loop fusion | flops 4194304 | bytes 5242880 | tf_op jit(solution)/shard_map/broadcast_in_dim | solution.py:504
  (71 shorter events, 4.7 us)
Async XLA Ops:
  0.7 5.8 %copy-start = (bf16[512,1024]{1,0:T(8,128)(2,1)S(1)}, bf16[512,1024]{1,0:T(8,128)(2,1)}, u32[]{:S(2)}) copy-start(bf16[512,1024]{1,0:T(8,128)(2,1)} %refs_2_.5) | copy-start | bytes 3145732
  0.7 5.9 %copy-start.10 = (bf16[1,512,1024]{2,1,0:T(8,128)(2,1)S(1)}, bf16[1,512,1024]{2,1,0:T(8,128)(2,1)}, u32[]{:S(2)}) copy-start(bf16[1,512,1024]{2,1,0:T(8,128)(2,1)} %param.5) | copy-start | bytes 3145732
  5.1 10.1 %collective-permute-start.3 = (bf16[512,4096]{1,0:T(8,128)(2,1)}, bf16[512,4096]{1,0:T(8,128)(2,1)}, u32[]{:S(2)}, u32[]{:S(2)}) collective-permute-start(bf16[512,4096]{1,0:T(8,128)(2,1)} %half.1), channel_id=1, source_target_pairs={{0,1},{1,0},{2,3},{3,2},{4,5},{5,4},{6,7},{7,6},{8,9},{9,8},{10,11... | collective-permute-start | bytes 12582920 | tf_op jit(solution)/shard_map/ppermute | solution.py:37
  6.6 8.2 %collective-permute-start.4 = (bf16[512,1024]{1,0:T(8,128)(2,1)S(1)}, bf16[512,1024]{1,0:T(8,128)(2,1)S(1)}, u32[]{:S(2)}, u32[]{:S(2)}) collective-permute-start(bf16[512,1024]{1,0:T(8,128)(2,1)S(1)} %copy-done), channel_id=1, source_target_pairs={{0,1},{1,0},{2,3},{3,2},{4,5},{5,4},{6,7},{7,6},{8,9},{9,8},{10,11... | collective-permute-start | bytes 3145736 | tf_op jit(solution)/shard_map/ppermute | solution.py:37
  7.5 13.7 %collective-permute-start = (bf16[2,64,1024]{2,1,0:T(8,128)(2,1)}, bf16[2,64,1024]{2,1,0:T(8,128)(2,1)S(1)}, u32[]{:S(2)}, u32[]{:S(2)}) collective-permute-start(bf16[2,64,1024]{2,1,0:T(8,128)(2,1)} %get-tuple-element.116), channel_id=1, source_target_pairs={{0,64},{1,65},{2,66},{3,67},{4,68},{5,69},{6,70},{7,71},{8,72},{9,... | collective-permute-start | bytes 786440 | tf_op jit(solution)/shard_map/ppermute | solution.py:37
  10.4 12.7 %collective-permute-start.1 = (bf16[2,64,1024]{2,1,0:T(8,128)(2,1)}, bf16[2,64,1024]{2,1,0:T(8,128)(2,1)S(1)}, u32[]{:S(2)}, u32[]{:S(2)}) collective-permute-start(bf16[2,64,1024]{2,1,0:T(8,128)(2,1)} %get-tuple-element.115), channel_id=1, source_target_pairs={{0,32},{1,33},{2,34},{3,35},{4,36},{5,37},{6,38},{7,39},{8,40},{9,... | collective-permute-start | bytes 786440 | tf_op jit(solution)/shard_map/ppermute | solution.py:37
  10.7 12.4 %collective-permute-start.2 = (bf16[2,64,1024]{2,1,0:T(8,128)(2,1)S(1)}, bf16[2,64,1024]{2,1,0:T(8,128)(2,1)}, u32[]{:S(2)}, u32[]{:S(2)}) collective-permute-start(bf16[2,64,1024]{2,1,0:T(8,128)(2,1)S(1)} %get-tuple-element.114), channel_id=1, source_target_pairs={{0,96},{1,97},{2,98},{3,99},{4,100},{5,101},{6,102},{7,103},{8,104... | collective-permute-start | bytes 786440 | tf_op jit(solution)/shard_map/ppermute | solution.py:37
  13.1 21.4 %copy-start.11 = (f32[1,1,64,1024]{3,2,1,0:T(8,128)S(1)}, f32[1,1,64,1024]{3,2,1,0:T(8,128)}, u32[]{:S(2)}) copy-start(f32[1,1,64,1024]{3,2,1,0:T(8,128)} %param.7) | copy-start | bytes 786436
  13.1 21.4 %copy-start.12 = (f32[1,1,64,1024]{3,2,1,0:T(8,128)S(1)}, f32[1,1,64,1024]{3,2,1,0:T(8,128)}, u32[]{:S(2)}) copy-start(f32[1,1,64,1024]{3,2,1,0:T(8,128)} %param.6) | copy-start | bytes 786436
  21.3 4.6 %copy-start.13 = (bf16[2,64,1024]{2,1,0:T(8,128)(2,1)}, bf16[2,64,1024]{2,1,0:T(8,128)(2,1)S(1)}, u32[]{:S(2)}) copy-start(bf16[2,64,1024]{2,1,0:T(8,128)(2,1)S(1)} %collective-permute-done) | copy-start | bytes 786436
  23.1 2.8 %copy-start.14 = (bf16[2,64,1024]{2,1,0:T(8,128)(2,1)}, bf16[2,64,1024]{2,1,0:T(8,128)(2,1)S(1)}, u32[]{:S(2)}) copy-start(bf16[2,64,1024]{2,1,0:T(8,128)(2,1)S(1)} %collective-permute-done.1) | copy-start | bytes 786436
  23.1 14.9 %collective-permute-start.7 = (bf16[512,1024]{1,0:T(8,128)(2,1)}, bf16[512,1024]{1,0:T(8,128)(2,1)}, u32[]{:S(2)}, u32[]{:S(2)}) collective-permute-start(bf16[512,1024]{1,0:T(8,128)(2,1)} %get-tuple-element.64), channel_id=1, source_target_pairs={{0,2},{1,7},{2,4},{3,1},{4,6},{5,3},{6,0},{7,5},{8,10},{9,15},{10,... | collective-permute-start | bytes 3145736 | tf_op jit(solution)/shard_map/ppermute | solution.py:37
  27.3 7.2 %collective-permute-start.5 = (bf16[64,1024]{1,0:T(8,128)(2,1)S(1)}, bf16[64,1024]{1,0:T(8,128)(2,1)S(1)}, u32[]{:S(2)}, u32[]{:S(2)}) collective-permute-start(bf16[64,1024]{1,0:T(8,128)(2,1)S(1)} %fusion.8), channel_id=1, source_target_pairs={{0,16},{1,17},{2,18},{3,19},{4,20},{5,21},{6,22},{7,23},{8,24},{9,... | collective-permute-start | bytes 393224 | tf_op jit(solution)/shard_map/ppermute | solution.py:37
  35.4 1.6 %collective-permute-start.6 = (bf16[64,1024]{1,0:T(8,128)(2,1)S(1)}, bf16[64,1024]{1,0:T(8,128)(2,1)S(1)}, u32[]{:S(2)}, u32[]{:S(2)}) collective-permute-start(bf16[64,1024]{1,0:T(8,128)(2,1)S(1)} %get-tuple-element.63), channel_id=1, source_target_pairs={{0,1},{1,0},{2,3},{3,2},{4,5},{5,4},{6,7},{7,6},{8,9},{9,8},{10,11... | collective-permute-start | bytes 393224 | tf_op jit(solution)/shard_map/ppermute | solution.py:37
  35.8 39.6 %collective-permute-start.11 = (bf16[512,1024]{1,0:T(8,128)(2,1)}, bf16[512,1024]{1,0:T(8,128)(2,1)}, u32[]{:S(2)}, u32[]{:S(2)}) collective-permute-start(bf16[512,1024]{1,0:T(8,128)(2,1)} %bitcast.15), channel_id=1, source_target_pairs={{0,2},{1,7},{2,4},{3,1},{4,6},{5,3},{6,0},{7,5},{8,10},{9,15},{10,... | collective-permute-start | bytes 3145736 | tf_op jit(solution)/shard_map/ppermute | solution.py:37
  38.0 11.6 %collective-permute-start.8 = (bf16[2,64,1024]{2,1,0:T(8,128)(2,1)S(1)}, bf16[2,64,1024]{2,1,0:T(8,128)(2,1)}, u32[]{:S(2)}, u32[]{:S(2)}) collective-permute-start(bf16[2,64,1024]{2,1,0:T(8,128)(2,1)S(1)} %maximum_select_fusion), channel_id=1, source_target_pairs={{0,0},{1,5},{2,2},{3,7},{4,4},{5,1},{6,6},{7,3},{8,8},{9,13},{10,1... | collective-permute-start | bytes 786440 | tf_op jit(solution)/shard_map/ppermute | solution.py:37
  42.3 11.8 %collective-permute-start.9 = (bf16[2,64,1024]{2,1,0:T(8,128)(2,1)S(1)}, bf16[2,64,1024]{2,1,0:T(8,128)(2,1)}, u32[]{:S(2)}, u32[]{:S(2)}) collective-permute-start(bf16[2,64,1024]{2,1,0:T(8,128)(2,1)S(1)} %maximum_select_fusion), channel_id=1, source_target_pairs={{0,6},{1,3},{2,0},{3,5},{4,2},{5,7},{6,4},{7,1},{8,14},{9,11},{10,... | collective-permute-start | bytes 786440 | tf_op jit(solution)/shard_map/ppermute | solution.py:37
  56.0 19.4 %collective-permute-start.10 = (bf16[2,2,64,1024]{3,2,1,0:T(8,128)(2,1)}, bf16[2,2,64,1024]{3,2,1,0:T(8,128)(2,1)}, u32[]{:S(2)}, u32[]{:S(2)}) collective-permute-start(bf16[2,2,64,1024]{3,2,1,0:T(8,128)(2,1)} %pad_maximum_fusion), channel_id=1, source_target_pairs={{0,24},{1,97},{2,26},{3,99},{4,28},{5,101},{6,30},{7,103},{8,0},{9... | collective-permute-start | bytes 1572872 | tf_op jit(solution)/shard_map/ppermute | solution.py:37
  61.1 18.9 %collective-permute-start.14 = (bf16[512,1024]{1,0:T(8,128)(2,1)}, bf16[512,1024]{1,0:T(8,128)(2,1)}, u32[]{:S(2)}, u32[]{:S(2)}) collective-permute-start(bf16[512,1024]{1,0:T(8,128)(2,1)} %add_convert_fusion.2), channel_id=1, source_target_pairs={{0,2},{1,7},{2,4},{3,1},{4,6},{5,3},{6,0},{7,5},{8,10},{9,15},{10,... | collective-permute-start | bytes 3145736 | tf_op jit(solution)/shard_map/ppermute | solution.py:37
  64.6 11.9 %collective-permute-start.12 = (bf16[2,2,64,1024]{3,2,1,0:T(8,128)(2,1)}, bf16[2,2,64,1024]{3,2,1,0:T(8,128)(2,1)}, u32[]{:S(2)}, u32[]{:S(2)}) collective-permute-start(bf16[2,2,64,1024]{3,2,1,0:T(8,128)(2,1)} %pad_maximum_fusion), channel_id=1, source_target_pairs={{0,16},{1,65},{2,18},{3,67},{4,20},{5,69},{6,22},{7,71},{8,24},{9,... | collective-permute-start | bytes 1572872 | tf_op jit(solution)/shard_map/ppermute | solution.py:37
  65.2 14.8 %collective-permute-start.13 = (bf16[2,2,64,1024]{3,2,1,0:T(8,128)(2,1)}, bf16[2,2,64,1024]{3,2,1,0:T(8,128)(2,1)S(1)}, u32[]{:S(2)}, u32[]{:S(2)}) collective-permute-start(bf16[2,2,64,1024]{3,2,1,0:T(8,128)(2,1)} %pad_maximum_fusion), channel_id=1, source_target_pairs={{0,8},{1,33},{2,10},{3,35},{4,12},{5,37},{6,14},{7,39},{8,16},{9,4... | collective-permute-start | bytes 1572872 | tf_op jit(solution)/shard_map/ppermute | solution.py:37
  80.0 12.2 %copy-start.1 = (bf16[2,4,2,64,1024]{4,3,2,1,0:T(8,128)(2,1)}, bf16[2,4,2,64,1024]{4,3,2,1,0:T(8,128)(2,1)S(1)}, u32[]{:S(2)}) copy-start(bf16[2,4,2,64,1024]{4,3,2,1,0:T(8,128)(2,1)S(1)} %bitcast_dynamic-update-slice_fusion.3.refs_3_) | copy-start | bytes 6291460
  80.0 5.6 %collective-permute-start.18 = (bf16[2,4,2,64,1024]{4,3,2,1,0:T(8,128)(2,1)S(1)}, bf16[2,4,2,64,1024]{4,3,2,1,0:T(8,128)(2,1)S(1)}, u32[]{:S(2)}, u32[]{:S(2)}) collective-permute-start(bf16[2,4,2,64,1024]{4,3,2,1,0:T(8,128)(2,1)S(1)} %bitcast_dynamic-update-slice_fusion.3.refs_3_), channel_id=1, source_target_pairs={{0,1},{1,0},{2,3},{3,2},{4,5},{5,4},{6,7},{7,6},{8,9},{9,8},{10,11... | collective-permute-start | bytes 6291464 | tf_op jit(solution)/shard_map/ppermute | solution.py:37
  80.1 27.3 %collective-permute-start.15 = (bf16[2,4,2,64,1024]{4,3,2,1,0:T(8,128)(2,1)S(1)}, bf16[2,4,2,64,1024]{4,3,2,1,0:T(8,128)(2,1)S(1)}, u32[]{:S(2)}, u32[]{:S(2)}) collective-permute-start(bf16[2,4,2,64,1024]{4,3,2,1,0:T(8,128)(2,1)S(1)} %bitcast_dynamic-update-slice_fusion.3.refs_3_), channel_id=1, source_target_pairs={{0,32},{1,9},{2,34},{3,11},{4,36},{5,13},{6,38},{7,15},{8,40},{9,1... | collective-permute-start | bytes 6291464 | tf_op jit(solution)/shard_map/ppermute | solution.py:37
  81.7 25.8 %collective-permute-start.16 = (bf16[2,4,2,64,1024]{4,3,2,1,0:T(8,128)(2,1)S(1)}, bf16[2,4,2,64,1024]{4,3,2,1,0:T(8,128)(2,1)S(1)}, u32[]{:S(2)}, u32[]{:S(2)}) collective-permute-start(bf16[2,4,2,64,1024]{4,3,2,1,0:T(8,128)(2,1)S(1)} %bitcast_dynamic-update-slice_fusion.3.refs_3_), channel_id=1, source_target_pairs={{0,96},{1,25},{2,98},{3,27},{4,100},{5,29},{6,102},{7,31},{8,104},... | collective-permute-start | bytes 6291464 | tf_op jit(solution)/shard_map/ppermute | solution.py:37
  85.5 14.0 %collective-permute-start.17 = (bf16[512,1024]{1,0:T(8,128)(2,1)S(1)}, bf16[512,1024]{1,0:T(8,128)(2,1)S(1)}, u32[]{:S(2)}, u32[]{:S(2)}) collective-permute-start(bf16[512,1024]{1,0:T(8,128)(2,1)S(1)} %add_convert_fusion.1), channel_id=1, source_target_pairs={{0,2},{1,7},{2,4},{3,1},{4,6},{5,3},{6,0},{7,5},{8,10},{9,15},{10,... | collective-permute-start | bytes 3145736 | tf_op jit(solution)/shard_map/ppermute | solution.py:37
  85.6 1.3 copy-start.4
  92.2 17.8 %copy-start.2 = (f32[512,1024]{1,0:T(8,128)}, f32[512,1024]{1,0:T(8,128)S(1)}, u32[]{:S(2)}) copy-start(f32[512,1024]{1,0:T(8,128)S(1)} %get-tuple-element.90.refs_7_) | copy-start | bytes 6291460
  99.5 10.4 %copy-start.8 = (bf16[512,1024]{1,0:T(8,128)(2,1)}, bf16[512,1024]{1,0:T(8,128)(2,1)S(1)}, u32[]{:S(2)}) copy-start(bf16[512,1024]{1,0:T(8,128)(2,1)S(1)} %collective-permute-done.17) | copy-start | bytes 3145732
  107.4 3.9 %copy-start.5 = (bf16[2,4,2,64,1024]{4,3,2,1,0:T(8,128)(2,1)}, bf16[2,4,2,64,1024]{4,3,2,1,0:T(8,128)(2,1)S(1)}, u32[]{:S(2)}) copy-start(bf16[2,4,2,64,1024]{4,3,2,1,0:T(8,128)(2,1)S(1)} %collective-permute-done.16.refs_4_) | copy-start | bytes 6291460
  107.4 6.7 %collective-permute-start.23 = (bf16[2,4,2,64,1024]{4,3,2,1,0:T(8,128)(2,1)S(1)}, bf16[2,4,2,64,1024]{4,3,2,1,0:T(8,128)(2,1)S(1)}, u32[]{:S(2)}, u32[]{:S(2)}) collective-permute-start(bf16[2,4,2,64,1024]{4,3,2,1,0:T(8,128)(2,1)S(1)} %collective-permute-done.15.refs_3_), channel_id=1, source_target_pairs={{0,1},{1,0},{2,3},{3,2},{4,5},{5,4},{6,7},{7,6},{8,9},{9,8},{10,11... | collective-permute-start | bytes 6291464 | tf_op jit(solution)/shard_map/ppermute | solution.py:37
  107.8 7.6 %collective-permute-start.24 = (bf16[2,4,2,64,1024]{4,3,2,1,0:T(8,128)(2,1)S(1)}, bf16[2,4,2,64,1024]{4,3,2,1,0:T(8,128)(2,1)}, u32[]{:S(2)}, u32[]{:S(2)}) collective-permute-start(bf16[2,4,2,64,1024]{4,3,2,1,0:T(8,128)(2,1)S(1)} %collective-permute-done.16.refs_4_), channel_id=1, source_target_pairs={{0,1},{1,0},{2,3},{3,2},{4,5},{5,4},{6,7},{7,6},{8,9},{9,8},{10,11... | collective-permute-start | bytes 6291464 | tf_op jit(solution)/shard_map/ppermute | solution.py:37
  109.8 3.8 %copy-start.6 = (bf16[3,512,1024]{2,1,0:T(8,128)(2,1)S(1)}, bf16[3,512,1024]{2,1,0:T(8,128)(2,1)}, u32[]{:S(2)}) copy-start(bf16[3,512,1024]{2,1,0:T(8,128)(2,1)} %get-tuple-element.88) | copy-start | bytes 9437188
  109.8 26.7 %collective-permute-start.21 = (bf16[512,1024]{1,0:T(8,128)(2,1)S(1)}, bf16[512,1024]{1,0:T(8,128)(2,1)S(1)}, u32[]{:S(2)}, u32[]{:S(2)}) collective-permute-start(bf16[512,1024]{1,0:T(8,128)(2,1)S(1)} %add_convert_fusion), channel_id=1, source_target_pairs={{0,2},{1,7},{2,4},{3,1},{4,6},{5,3},{6,0},{7,5},{8,10},{9,15},{10,... | collective-permute-start | bytes 3145736 | tf_op jit(solution)/shard_map/ppermute | solution.py:37
  110.0 3.6 %copy-start.9 = (bf16[512,1024]{1,0:T(8,128)(2,1)S(1)}, bf16[512,1024]{1,0:T(8,128)(2,1)}, u32[]{:S(2)}) copy-start(bf16[512,1024]{1,0:T(8,128)(2,1)} %copy-done.8) | copy-start | bytes 3145732
  110.0 26.5 %collective-permute-start.19 = (bf16[4,2,64,1024]{3,2,1,0:T(8,128)(2,1)S(1)}, bf16[4,2,64,1024]{3,2,1,0:T(8,128)(2,1)S(1)}, u32[]{:S(2)}, u32[]{:S(2)}) collective-permute-start(bf16[4,2,64,1024]{3,2,1,0:T(8,128)(2,1)S(1)} %slice_bitcast_fusion.1), channel_id=1, source_target_pairs={{0,32},{1,9},{2,34},{3,11},{4,36},{5,13},{6,38},{7,15},{8,40},{9,1... | collective-permute-start | bytes 3145736 | tf_op jit(solution)/shard_map/ppermute | solution.py:37
  111.4 25.1 %collective-permute-start.20 = (bf16[4,2,64,1024]{3,2,1,0:T(8,128)(2,1)S(1)}, bf16[4,2,64,1024]{3,2,1,0:T(8,128)(2,1)S(1)}, u32[]{:S(2)}, u32[]{:S(2)}) collective-permute-start(bf16[4,2,64,1024]{3,2,1,0:T(8,128)(2,1)S(1)} %slice_bitcast_fusion), channel_id=1, source_target_pairs={{0,96},{1,25},{2,98},{3,27},{4,100},{5,29},{6,102},{7,31},{8,104},... | collective-permute-start | bytes 3145736 | tf_op jit(solution)/shard_map/ppermute | solution.py:37
  114.1 1.4 copy-start.7
  114.1 22.4 %collective-permute-start.22 = (bf16[256,1024]{1,0:T(8,128)(2,1)S(1)}, bf16[256,1024]{1,0:T(8,128)(2,1)S(1)}, u32[]{:S(2)}, u32[]{:S(2)}) collective-permute-start(bf16[256,1024]{1,0:T(8,128)(2,1)S(1)} %get-tuple-element.113), channel_id=1, source_target_pairs={{0,8},{1,9},{2,10},{3,11},{4,12},{5,13},{6,14},{7,15},{8,0},{9,1},... | collective-permute-start | bytes 1572872 | tf_op jit(solution)/shard_map/ppermute | solution.py:37
  131.1 9.7 %copy-start.3 = (f32[512,1024]{1,0:T(8,128)}, f32[512,1024]{1,0:T(8,128)S(1)}, u32[]{:S(2)}) copy-start(f32[512,1024]{1,0:T(8,128)S(1)} %get-tuple-element.98.refs_9_) | copy-start | bytes 6291460
  136.5 2.7 %collective-permute-start.25 = (bf16[4,2,64,1024]{3,2,1,0:T(8,128)(2,1)S(1)}, bf16[4,2,64,1024]{3,2,1,0:T(8,128)(2,1)S(1)}, u32[]{:S(2)}, u32[]{:S(2)}) collective-permute-start(bf16[4,2,64,1024]{3,2,1,0:T(8,128)(2,1)S(1)} %collective-permute-done.19.refs_4_), channel_id=1, source_target_pairs={{0,1},{1,0},{2,3},{3,2},{4,5},{5,4},{6,7},{7,6},{8,9},{9,8},{10,11... | collective-permute-start | bytes 3145736 | tf_op jit(solution)/shard_map/ppermute | solution.py:37
  136.6 4.1 %collective-permute-start.26 = (bf16[4,2,64,1024]{3,2,1,0:T(8,128)(2,1)S(1)}, bf16[4,2,64,1024]{3,2,1,0:T(8,128)(2,1)S(1)}, u32[]{:S(2)}, u32[]{:S(2)}) collective-permute-start(bf16[4,2,64,1024]{3,2,1,0:T(8,128)(2,1)S(1)} %collective-permute-done.20.refs_5_), channel_id=1, source_target_pairs={{0,1},{1,0},{2,3},{3,2},{4,5},{5,4},{6,7},{7,6},{8,9},{9,8},{10,11... | collective-permute-start | bytes 3145736 | tf_op jit(solution)/shard_map/ppermute | solution.py:37
  137.6 16.1 %collective-permute-start.27 = (bf16[512,1024]{1,0:T(8,128)(2,1)S(1)}, bf16[512,1024]{1,0:T(8,128)(2,1)S(1)}, u32[]{:S(2)}, u32[]{:S(2)}) collective-permute-start(bf16[512,1024]{1,0:T(8,128)(2,1)S(1)} %fusion.2), channel_id=1, source_target_pairs={{0,2},{1,7},{2,4},{3,1},{4,6},{5,3},{6,0},{7,5},{8,10},{9,15},{10,... | collective-permute-start | bytes 3145736 | tf_op jit(solution)/shard_map/ppermute | solution.py:37
  138.7 14.9 %collective-permute-start.28 = (bf16[256,1024]{1,0:T(8,128)(2,1)S(1)}, bf16[256,1024]{1,0:T(8,128)(2,1)S(1)}, u32[]{:S(2)}, u32[]{:S(2)}) collective-permute-start(bf16[256,1024]{1,0:T(8,128)(2,1)S(1)} %get-tuple-element.112), channel_id=1, source_target_pairs={{0,8},{1,9},{2,10},{3,11},{4,12},{5,13},{6,14},{7,15},{8,0},{9,1},... | collective-permute-start | bytes 1572872 | tf_op jit(solution)/shard_map/ppermute | solution.py:37

commit v3 on v2

--- a/solution.py
+++ b/solution.py
@@ -1,3 +1,4 @@
+import functools
 import itertools
 
 import jax
@@ -95,31 +96,35 @@
     )(at, tokens)
 
 
-def grad_kernel(blocks, mine, theirs, cot, cot_theirs, out, *rest):
+def grad_kernel(adds, blocks, mine, theirs, cot, cot_theirs, *refs):
+    arrived, (out, *rest) = refs[:adds], refs[adds:]
     dims = (((0,), (0,)), ((), ()))
     total = lax.dot_general(mine[...], cot[...], dims, preferred_element_type=F32)
     total += lax.dot_general(
         theirs[...], cot_theirs[...], dims, preferred_element_type=F32
     )
-    total = (total * SCALE).astype(out.dtype)
+    total = total * SCALE
 
     @pl.when(pl.program_id(0) == 0)
     def _():
-        out[...] = total
+        first = total
+        for part in arrived:
+            first = first + part[...].astype(F32)
+        out[...] = first.astype(BF)
 
     for more in rest:
 
         @pl.when(pl.program_id(0) > 0)
         def _(more=more):
-            more[0] = total
-
-
-def grad_blocks(blocks, core, tokens, tokens_theirs, cot, cot_theirs):
+            more[0] = total.astype(BF)
+
+
+def grad_blocks(blocks, core, tokens, tokens_theirs, cot, cot_theirs, arrived):
     count = len(blocks)
     table = jnp.stack([2 * g + core for g in blocks] + blocks).astype(jnp.int32)
     whole = pl.BlockSpec((TOK, COLS), lambda m, b: (0, 0))
     return pl.pallas_call(
-        grad_kernel,
+        functools.partial(grad_kernel, len(arrived)),
         out_shape=[
             jax.ShapeDtypeStruct((512, COLS), BF),
             jax.ShapeDtypeStruct((count - 1, 512, COLS), BF),
@@ -132,7 +137,8 @@
                 pl.BlockSpec((TOK, 512), lambda m, b: (0, b[count + m])),
                 whole,
                 whole,
-            ],
+            ]
+            + [whole] * len(arrived),
             out_specs=[
                 whole,
                 pl.BlockSpec((1, 512, COLS), lambda m, b: (jnp.maximum(m - 1, 0), 0, 0)),
@@ -140,23 +146,23 @@
         ),
         compiler_params=params(),
         cost_estimate=pl.CostEstimate(
-            flops=0,
-            bytes_accessed=1 << 20,
+            flops=count * 4 * TOK * 512 * COLS,
+            bytes_accessed=(count * 2 + 2) << 20,
             transcendentals=0,
         ),
         name="grad",
-    )(table, tokens, tokens_theirs, cot, cot_theirs)
+    )(table, tokens, tokens_theirs, cot, cot_theirs, *arrived)
 
 
 OFFSETS = (0, -1, 2, 1)
 
 
-def fold_kernel(groups, chunks, first, last, *refs):
+def fold_kernel(groups, mine, theirs, first, last, *refs):
     refs = list(refs)
     at, tokens, cot = refs[:3]
     refs = refs[3:]
-    mine = {key: refs.pop(0) for key in chunks}
-    theirs = {key: refs.pop(0) for key in chunks}
+    mine = {key: refs.pop(0) for key in mine}
+    theirs = {key: refs.pop(0) for key in theirs}
     if not first:
         acc_in, _, _ = refs.pop(0), refs.pop(0), refs.pop(0)
     grad_out, weights_out, key_out = refs.pop(0), refs.pop(0), refs.pop(0)
@@ -191,7 +197,17 @@
         _, (s, t), dy, p = group
         return [(((z_of(s) & 1) * 8 + ((y + 2 + dy) & 3) * 2 + p) * 512, 0, 512)]
 
-    def load_weights(group, slot):
+    def each(i, do):
+        if groups[i][0] == groups[i][1]:
+            do(groups[i][0], None)
+            return
+        for core, group in enumerate(groups[i]):
+
+            @pl.when(c == core)
+            def _(group=group, core=core):
+                do(group, core)
+
+    def load_weights(group, slot, core):
         def start(held):
             if group[0] == "x":
                 _, s, dy = group
@@ -211,6 +227,9 @@
                     ).start()
 
         here = 0 if group[0] == "x" else 1
+        if core is not None:
+            start(mine if core == here else theirs)
+            return
 
         @pl.when(c == here)
         def _():
@@ -224,33 +243,48 @@
 
     def loads(i):
         slot = i % 3
-        load_weights(groups[i], slot)
-        for a, b, n in columns_of(groups[i]):
-            pltpu.make_async_copy(
-                tokens.at[:, pl.ds(pl.multiple_of(a, 128), n)],
-                tok.at[slot, :, pl.ds(b, n)],
-                tok_sem.at[slot],
-            ).start()
+
+        def start(group, core):
+            load_weights(group, slot, core)
+            for a, b, n in columns_of(group):
+                pltpu.make_async_copy(
+                    tokens.at[:, pl.ds(pl.multiple_of(a, 128), n)],
+                    tok.at[slot, :, pl.ds(b, n)],
+                    tok_sem.at[slot],
+                ).start()
+
+        each(i, start)
 
     def holds_own(group):
         return group[0] == "x" and group[2] == 0
 
-    def weights_store(i):
+    def weights_store(i, do):
         slot = i % 3
-        return pltpu.make_async_copy(
-            w.at[slot, (z & 1) * 2 + c],
-            weights_out.at[x_of(groups[i][1])],
-            own_sem.at[slot],
-        )
+
+        def copy(group, core):
+            if holds_own(group):
+                do(
+                    pltpu.make_async_copy(
+                        w.at[slot, (z & 1) * 2 + c],
+                        weights_out.at[x_of(group[1])],
+                        own_sem.at[slot],
+                    )
+                )
+
+        each(i, copy)
 
     def stores(i):
         slot = i % 3
-        for a, b, n in columns_of(groups[i]):
-            pltpu.make_async_copy(
-                grad.at[slot, :, pl.ds(b, n)],
-                grad_out.at[:, pl.ds(pl.multiple_of(a, 128), n)],
-                out_sem.at[slot],
-            ).start()
+
+        def start(group, core):
+            for a, b, n in columns_of(group):
+                pltpu.make_async_copy(
+                    grad.at[slot, :, pl.ds(b, n)],
+                    grad_out.at[:, pl.ds(pl.multiple_of(a, 128), n)],
+                    out_sem.at[slot],
+                ).start()
+
+        each(i, start)
 
     def whole(buffer, sem, slot):
         return pltpu.make_async_copy(buffer.at[slot], buffer.at[slot], sem.at[slot])
@@ -277,11 +311,11 @@
 
         whole(w, w_sem, slot).wait()
         for k in range(count):
-            if holds_own(groups[k]):
+            if any(map(holds_own, groups[k])):
 
                 @pl.when(i == k)
                 def _(k=k):
-                    weights_store(k).start()
+                    weights_store(k, lambda copy: copy.start())
 
         @pl.when(i >= 3)
         def _():
@@ -307,11 +341,11 @@
 
         acc[...] += jnp.dot(tok[slot], rows, preferred_element_type=F32)
         for k in range(count):
-            if holds_own(groups[k]):
+            if any(map(holds_own, groups[k])):
 
                 @pl.when(i == k)
                 def _(k=k):
-                    weights_store(k).wait()
+                    weights_store(k, lambda copy: copy.wait())
 
     if last:
         key_v[...] = (acc[...] * SCALE).astype(BF)
@@ -354,7 +388,7 @@
     if last:
         scratch += [pltpu.VMEM((TOK, COLS), BF)]
     def kernel(*refs):
-        fold_kernel(groups, list(mine), first, last, *refs)
+        fold_kernel(groups, list(mine), list(theirs), first, last, *refs)
 
     return pl.pallas_call(
         kernel,
@@ -382,12 +416,14 @@
     tokens_theirs = swap_core(other_half(at, tokens))
     cot_theirs = swap_core(key_cot)
 
-    def grads(which, tokens_theirs):
+    def grads(which, tokens_theirs, *arrived):
         blocks = [
             (zl if half else 1 - zl) * 4 + ((y - way * (s + 1) + 8) & 3)
             for half, s in which
         ]
-        return grad_blocks(blocks, c, tokens, tokens_theirs, key_cot, cot_theirs)
+        return grad_blocks(
+            blocks, c, tokens, tokens_theirs, key_cot, cot_theirs, arrived
+        )
 
     def add(*parts):
         total = parts[0].astype(F32)
@@ -434,34 +470,33 @@
             )
         return whole
 
-    owned, late = lax.optimization_barrier((owned, tokens_theirs))
-    second, second_b = grads([(0, 1), (1, 1)], late)
-    other, arrived = lax.optimization_barrier((swap_core(owned), arrived))
+    other = swap_core(owned)
     both = jnp.where(c == 0, jnp.stack([owned, other]), jnp.stack([other, owned]))
     near = permute(both, lambda px, pz, py, pc: (px, pz, py - 1 + 2 * pc, pc))
     far = permute(both, lambda px, pz, py, pc: (px, pz, py + 2 * pc, pc))
     c0 = jnp.stack([far, near])
-    c0, second, second_b, late = lax.optimization_barrier(
-        (c0, second, second_b[0], late)
-    )
-    third, rest = grads([(0, 2), (0, 3), (1, 2), (1, 3)], late)
+    c0, late = lax.optimization_barrier((c0, tokens_theirs))
+    second, second_b = grads([(0, 1), (1, 1)], late, arrived)
     parts = [short_way(c0, d) for d in (1, 2, 3)]
-    arrived = ring_y(add(second, arrived).astype(BF))
+    arrived = ring_y(second)
     parts[0], arrived_b = lax.optimization_barrier((parts[0], arrived_b))
+    second_b = second_b[0]
     c1 = in_order([c0] + parts, jnp.where(c == 0, z, x))
-    c1, third, rest, arrived = lax.optimization_barrier((c1, third, rest, arrived))
+    c1, late = lax.optimization_barrier((c1, late))
+    third, rest = grads([(0, 2), (0, 3), (1, 2), (1, 3)], late, arrived)
 
     mine, theirs = {0: c1}, {0: swap_core(c1)}
     mine[1], mine[3] = long_way(c1, 1), long_way(c1, -1)
 
-    def fold_of(groups, keys, carry, last):
+    def fold_of(groups, keys, keys_theirs, carry, last):
         return fold(
             at, tokens, key_cot, groups,
-            {k: mine[k] for k in keys}, {k: theirs[k] for k in keys}, carry, last,
-        )
-
-    carry = fold_of([("x", 0, 0), ("x", 0, 1)], [0], None, False)
-    arrived = ring_y(add(third, arrived).astype(BF))
+            {k: mine[k] for k in keys}, {k: theirs[k] for k in keys_theirs}, carry, last,
+        )
+
+    own = [("x", 0, 0), ("x", 0, 1)]
+    carry = fold_of(list(zip(own, own)), [0], [0], None, False)
+    arrived = ring_y(third)
     mine[1], mine[3], arrived, arrived_b, *carry = lax.optimization_barrier(
         (mine[1], mine[3], arrived, arrived_b, *carry)
     )
@@ -471,23 +506,24 @@
     crossed = add(rest[0], arrived).astype(BF)
     crossed = [
         permute(half, lambda px, pz, py, pc: (px, pz ^ 1, py, pc))
-        for half in (crossed[:256], crossed[256:])
+        for half in (crossed[:192], crossed[192:])
     ]
     arrived_b = ring_y(add(second_b, arrived_b).astype(BF))
-    carry = fold_of(
-        [("x", s, dy) for s in (1, 3) for dy in range(2)]
-        + [("z", (1, 3), dy, p) for dy in range(2) for p in range(2)],
-        [1, 3], carry, False,
-    )
+    near_a = [("x", s, dy) for s in (1, 3) for dy in range(2)]
+    near_b = [("z", (1, 3), dy, p) for dy in range(2) for p in range(2)]
+    carry = fold_of(list(zip(near_a, near_b)), [1, 3], [], carry, False)
+    carry = fold_of(list(zip(near_b, near_a)), [], [1, 3], carry, False)
     mine[2, 0], mine[2, 1], arrived_b, crossed[0], *carry = lax.optimization_barrier(
         (mine[2, 0], mine[2, 1], arrived_b, crossed[0], *carry)
     )
     theirs[2, 0], theirs[2, 1] = swap_core(mine[2, 0]), swap_core(mine[2, 1])
     arrived_b = ring_y(add(rest[1], arrived_b).astype(BF))
+    far_a = [("x", 2, dy) for dy in range(2)]
+    far_b = [("z", (0, 2), dy, p) for dy in range(2) for p in range(2)]
+    keys = [0, (2, 0), (2, 1)]
+    carry = fold_of(list(zip(far_a, far_b[:2])), keys, [], carry, False)
     grad_tokens, shard_weights, keys_out = fold_of(
-        [("x", 2, dy) for dy in range(2)]
-        + [("z", (0, 2), dy, p) for dy in range(2) for p in range(2)],
-        [0, (2, 0), (2, 1)], carry, True,
+        list(zip(far_b, far_b[2:] + far_a)), keys, keys, carry, True
     )
     arrived_b, *crossed, keys_out = lax.optimization_barrier(
         (arrived_b, *crossed, keys_out)

time: 156 us -> 168 us (1.077)
  starting transfers between devices: 38.4 us -> 48.7 us
  other arithmetic: 13.1 us -> 6.9 us
  Pallas kernels: 57.7 us -> 62.5 us
  local copies, waits for them, and re-layouts: 6.38 us -> 11 us
  waiting for transfers between devices: 39.1 us -> 37.2 us
    ppermute x29, starting transfers between devices: 38.4 us -> 48.7 us  [permute(): return lax.ppermute(value, AXES, pairs)]
    convert_element_type x2 -> x0, other arithmetic: 4.24 us -> none  [the longest x1 2.6 us: per_device(): arrived = ring_y(add(second, arrived).astype(BF))]
    pallas_call x3 -> x5, Pallas kernels: 33.7 us -> 37.3 us  [fold(): pl.pallas_call(kernel, out_shape=shapes, in_specs=[pl.BlockSpec(memory_sp...]
    unnamed x30 -> x32, local copies, waits for them, and re-layouts: 1.58 us -> 4.93 us
    dynamic_update_slice x4, local copies, waits for them, and re-layouts: 3.29 us -> 0.18 us  [in_order(): lax.dynamic_update_slice_in_dim(whole, part[:, None], here + d & 3, 1)]
    squeeze x1, local copies, waits for them, and re-layouts: 0.07 us -> 2.28 us  [per_device(): mine[2, 1] = long_way(mine[3][1], -1)]
    squeeze x1, local copies, waits for them, and re-layouts: 0.07 us -> 2.26 us  [per_device(): mine[2, 0] = long_way(mine[1][0], 1)]
    ppermute x29, waiting for transfers between devices: 39.1 us -> 37.2 us  [permute(): return lax.ppermute(value, AXES, pairs)]
  transfers between devices with their start and end apart: 29 -> 29, of which waited for: 13 -> 10; matrix products, arithmetic and copies ran while one was open for 10% -> 6% of each run, Pallas kernels for 34% -> 35%
where the time goes in v3:
time: 168 us; the launch traced here: 167 us
  Pallas kernels  62.5 us (37%)
  starting transfers between devices  48.7 us (29%)
  waiting for transfers between devices  37.2 us (22%)
  local copies, waits for them, and re-layouts  11 us (7%)
  other arithmetic  6.9 us (4%)
    ppermute x29, starting transfers between devices, permute(): return lax.ppermute(value, AXES, pairs)  48.7 us
    pallas_call x5, Pallas kernels, fold(): pl.pallas_call(kernel, out_shape=shapes, in_specs=[pl.BlockSpec(memory_sp...  37.3 us
    ppermute x29, waiting for transfers between devices, permute(): return lax.ppermute(value, AXES, pairs)  37.2 us
    pallas_call x3, Pallas kernels, grad_blocks(): pl.pallas_call(functools.partial(grad_kernel, len(arrived)), out_shape=[j...  20.9 us
    unnamed x32, local copies, waits for them, and re-layouts  4.93 us
    pallas_call x1, Pallas kernels, other_half(): pl.pallas_call(half_kernel, out_shape=jax.ShapeDtypeStruct((TOK, D // 2),...  4.33 us
  transfers between devices with their start and end apart: 29, of which 10 were waited for; matrix products, arithmetic and copies ran while one was open for 6% of the time, Pallas kernels for 35%

profile of v3, /device:TPU:1, one launch (start us, length us, event | category | flops | bytes accessed | tf_op | source)
XLA Modules:
  0.0 167.4 jit_solution(12952102514676291513)
XLA Ops:
  0.7 4.3 %half.1 = bf16[512,4096]{1,0:T(8,128)(2,1)} custom-call(s32[5]{0:T(128)S(1)} %stack.108.at.refs_0_, bf16[512,8192]{1,0:T(8,128)(2,1)} %refs_1_.9), custom_call_target="tpu_custom_call" | custom-call | bytes 8388608 | tf_op jit(solution)/shard_map/half/pallas_call | solution.py:81
  5.1 1.5 collective-permute-start.3
  6.7 0.9 dynamic-slice_bitcast_fusion
  7.5 2.8 %collective-permute-start = (bf16[2,64,1024]{2,1,0:T(8,128)(2,1)}, bf16[2,64,1024]{2,1,0:T(8,128)(2,1)S(1)}, u32[]{:S(2)}, u32[]{:S(2)}) collective-permute-start(bf16[2,64,1024]{2,1,0:T(8,128)(2,1)} %get-tuple-element.110), channel_id=1, source_target_pairs={{0,64},{1,65},{2,66},{3,67},{4,68},{5,69},{6,70},{7,71},{8,72},{9,... | collective-permute-start | bytes 786440 | tf_op jit(solution)/shard_map/ppermute | solution.py:38
  10.7 2.4 %collective-permute-start.2 = (bf16[2,64,1024]{2,1,0:T(8,128)(2,1)S(1)}, bf16[2,64,1024]{2,1,0:T(8,128)(2,1)}, u32[]{:S(2)}, u32[]{:S(2)}) collective-permute-start(bf16[2,64,1024]{2,1,0:T(8,128)(2,1)S(1)} %get-tuple-element.108), channel_id=1, source_target_pairs={{0,96},{1,97},{2,98},{3,99},{4,100},{5,101},{6,102},{7,103},{8,104... | collective-permute-start | bytes 786440 | tf_op jit(solution)/shard_map/ppermute | solution.py:38
  13.1 1.6 collective-permute-done.4.cot_theirs
  15.2 5.7 %grad.3 = (bf16[512,1024]{1,0:T(8,128)(2,1)S(1)}, bf16[1,512,1024]{2,1,0:T(8,128)(2,1)}) custom-call(s32[4]{0:T(128)S(1)} %pad_add_fusion.blocks, bf16[512,8192]{1,0:T(8,128)(2,1)} %refs_1_.9, bf16[512,4096]{1,0:T(8,128)(2,1)} %collective-permute-done.3.theirs, bf16[512,1024]{1,0:T(8,128)(2,1)S(1)} %copy-done, ...), custom_call_target="tpu_custom_call" | custom-call | flops 2147483648 | bytes 6291456 | tf_op jit(solution)/shard_map/grad/pallas_call | solution.py:126
  20.9 1.0 copy-done.11
  21.8 1.4 collective-permute-done.1
  23.2 1.3 fusion.6
  24.5 3.8 %collective-permute-start.5 = (bf16[64,1024]{1,0:T(8,128)(2,1)S(1)}, bf16[64,1024]{1,0:T(8,128)(2,1)S(1)}, u32[]{:S(2)}, u32[]{:S(2)}) collective-permute-start(bf16[64,1024]{1,0:T(8,128)(2,1)S(1)} %fusion.9), channel_id=1, source_target_pairs={{0,16},{1,17},{2,18},{3,19},{4,20},{5,21},{6,22},{7,23},{8,24},{9,... | collective-permute-start | bytes 393224 | tf_op jit(solution)/shard_map/ppermute | solution.py:38
  28.3 2.7 %collective-permute-start.15 = (bf16[512,1024]{1,0:T(8,128)(2,1)}, bf16[512,1024]{1,0:T(8,128)(2,1)}, u32[]{:S(2)}, u32[]{:S(2)}) collective-permute-start(bf16[512,1024]{1,0:T(8,128)(2,1)} %copy-done.11), channel_id=1, source_target_pairs={{0,2},{1,7},{2,4},{3,1},{4,6},{5,3},{6,0},{7,5},{8,10},{9,15},{10,... | collective-permute-start | bytes 3145736 | tf_op jit(solution)/shard_map/ppermute | solution.py:38
  31.0 0.6 collective-permute-done.5
  31.6 0.9 fusion.10
  32.5 1.2 collective-permute-start.6
  33.6 2.7 %collective-permute-start.10 = (bf16[512,1024]{1,0:T(8,128)(2,1)}, bf16[512,1024]{1,0:T(8,128)(2,1)}, u32[]{:S(2)}, u32[]{:S(2)}) collective-permute-start(bf16[512,1024]{1,0:T(8,128)(2,1)} %bitcast.15), channel_id=1, source_target_pairs={{0,2},{1,7},{2,4},{3,1},{4,6},{5,3},{6,0},{7,5},{8,10},{9,15},{10,... | collective-permute-start | bytes 3145736 | tf_op jit(solution)/shard_map/ppermute | solution.py:38
  36.4 3.1 %collective-permute-start.7 = (bf16[2,64,1024]{2,1,0:T(8,128)(2,1)S(1)}, bf16[2,64,1024]{2,1,0:T(8,128)(2,1)S(1)}, u32[]{:S(2)}, u32[]{:S(2)}) collective-permute-start(bf16[2,64,1024]{2,1,0:T(8,128)(2,1)S(1)} %maximum_select_fusion), channel_id=1, source_target_pairs={{0,0},{1,5},{2,2},{3,7},{4,4},{5,1},{6,6},{7,3},{8,8},{9,13},{10,1... | collective-permute-start | bytes 786440 | tf_op jit(solution)/shard_map/ppermute | solution.py:38
  39.9 8.0 %collective-permute-done.7 = bf16[2,64,1024]{2,1,0:T(8,128)(2,1)S(1)} collective-permute-done((bf16[2,64,1024]{2,1,0:T(8,128)(2,1)S(1)}, bf16[2,64,1024]{2,1,0:T(8,128)(2,1)S(1)}, u32[]{:S(2)}, u32[]{:S(2)}) %collective-permute-start.7) | collective-permute-done | bytes 262176 | tf_op jit(solution)/shard_map/ppermute | solution.py:38
  47.9 3.7 %collective-permute-done.8 = bf16[2,64,1024]{2,1,0:T(8,128)(2,1)S(1)} collective-permute-done((bf16[2,64,1024]{2,1,0:T(8,128)(2,1)S(1)}, bf16[2,64,1024]{2,1,0:T(8,128)(2,1)S(1)}, u32[]{:S(2)}, u32[]{:S(2)}) %collective-permute-start.8) | collective-permute-done | bytes 262176 | tf_op jit(solution)/shard_map/ppermute | solution.py:38
  51.7 2.5 %collective-permute-start.9 = (bf16[2,2,64,1024]{3,2,1,0:T(8,128)(2,1)S(1)}, bf16[2,2,64,1024]{3,2,1,0:T(8,128)(2,1)S(1)}, u32[]{:S(2)}, u32[]{:S(2)}) collective-permute-start(bf16[2,2,64,1024]{3,2,1,0:T(8,128)(2,1)S(1)} %pad_maximum_fusion), channel_id=1, source_target_pairs={{0,24},{1,97},{2,26},{3,99},{4,28},{5,101},{6,30},{7,103},{8,0},{9... | collective-permute-start | bytes 1572872 | tf_op jit(solution)/shard_map/ppermute | solution.py:38
  54.3 0.5 collective-permute-start.11
  55.2 6.1 %grad.4 = (bf16[512,1024]{1,0:T(8,128)(2,1)}, bf16[1,512,1024]{2,1,0:T(8,128)(2,1)S(1)}) custom-call(s32[4]{0:T(128)S(1)} %pad_add_fusion.1.blocks, bf16[512,8192]{1,0:T(8,128)(2,1)} %refs_1_.9, bf16[512,4096]{1,0:T(8,128)(2,1)} %collective-permute-done.3.theirs, bf16[512,1024]{1,0:T(8,128)(2,1)S(1)} %copy-done, bf16[512,1024]{1,0:T(8,128)(2,1)S(1)} %copy-done.3, ...), custom_call_target="tpu_custom_call" | custom-call | flops 2147483648 | bytes 6291456 | tf_op jit(solution)/shard_map/grad/pallas_call | solution.py:126
  61.3 4.6 %collective-permute-done.9 = bf16[2,2,64,1024]{3,2,1,0:T(8,128)(2,1)S(1)} collective-permute-done((bf16[2,2,64,1024]{3,2,1,0:T(8,128)(2,1)S(1)}, bf16[2,2,64,1024]{3,2,1,0:T(8,128)(2,1)S(1)}, u32[]{:S(2)}, u32[]{:S(2)}) %collective-permute-start.9) | collective-permute-done | bytes 524320 | tf_op jit(solution)/shard_map/ppermute | solution.py:38
  65.9 10.1 %collective-permute-start.16 = (bf16[512,1024]{1,0:T(8,128)(2,1)}, bf16[512,1024]{1,0:T(8,128)(2,1)}, u32[]{:S(2)}, u32[]{:S(2)}) collective-permute-start(bf16[512,1024]{1,0:T(8,128)(2,1)} %get-tuple-element.68), channel_id=1, source_target_pairs={{0,2},{1,7},{2,4},{3,1},{4,6},{5,3},{6,0},{7,5},{8,10},{9,15},{10,... | collective-permute-start | bytes 3145736 | tf_op jit(solution)/shard_map/ppermute | solution.py:38
  76.4 0.6 collective-permute-start.13
  76.9 2.2 %collective-permute-start.14 = (bf16[2,4,2,64,1024]{4,3,2,1,0:T(8,128)(2,1)S(1)}, bf16[2,4,2,64,1024]{4,3,2,1,0:T(8,128)(2,1)}, u32[]{:S(2)}, u32[]{:S(2)}) collective-permute-start(bf16[2,4,2,64,1024]{4,3,2,1,0:T(8,128)(2,1)S(1)} %bitcast_dynamic-update-slice_fusion.3.refs_3_), channel_id=1, source_target_pairs={{0,96},{1,25},{2,98},{3,27},{4,100},{5,29},{6,102},{7,31},{8,104},... | collective-permute-start | bytes 6291464 | tf_op jit(solution)/shard_map/ppermute | solution.py:38
  79.2 9.5 %collective-permute-done.16.refs_0_ = bf16[512,1024]{1,0:T(8,128)(2,1)} collective-permute-done((bf16[512,1024]{1,0:T(8,128)(2,1)}, bf16[512,1024]{1,0:T(8,128)(2,1)}, u32[]{:S(2)}, u32[]{:S(2)}) %collective-permute-start.16) | collective-permute-done | bytes 1048608 | tf_op jit(solution)/shard_map/ppermute | solution.py:38
  88.7 1.2 copy-done.4
  90.0 9.1 %grad.5 = (bf16[512,1024]{1,0:T(8,128)(2,1)S(1)}, bf16[3,512,1024]{2,1,0:T(8,128)(2,1)}) custom-call(s32[8]{0:T(128)S(1)} %stack.124.blocks, bf16[512,8192]{1,0:T(8,128)(2,1)} %refs_1_.9, bf16[512,4096]{1,0:T(8,128)(2,1)} %collective-permute-done.3.theirs, bf16[512,1024]{1,0:T(8,128)(2,1)S(1)} %copy-done, bf16[512,1024]{1,0:T(8,128)(2,1)S(1)} %copy-done.4, ...), custom_call_target="tpu_custom_call" | custom-call | flops 4294967296 | bytes 10485760 | tf_op jit(solution)/shard_map/grad/pallas_call | solution.py:126
  99.1 2.8 %collective-permute-start.17 = (bf16[512,1024]{1,0:T(8,128)(2,1)S(1)}, bf16[512,1024]{1,0:T(8,128)(2,1)S(1)}, u32[]{:S(2)}, u32[]{:S(2)}) collective-permute-start(bf16[512,1024]{1,0:T(8,128)(2,1)S(1)} %get-tuple-element.69), channel_id=1, source_target_pairs={{0,2},{1,7},{2,4},{3,1},{4,6},{5,3},{6,0},{7,5},{8,10},{9,15},{10,... | collective-permute-start | bytes 3145736 | tf_op jit(solution)/shard_map/ppermute | solution.py:38
  101.9 5.2 %fold.5 = (bf16[512,8192]{1,0:T(8,128)(2,1)}, bf16[4,2,64,1024]{3,2,1,0:T(8,128)(2,1)}, f32[512,1024]{1,0:T(8,128)S(1)}) custom-call(s32[5]{0:T(128)S(1)} %stack.108.at.refs_0_, bf16[512,8192]{1,0:T(8,128)(2,1)} %refs_1_.9, bf16[512,1024]{1,0:T(8,128)(2,1)S(1)} %copy-done, bf16[2,4,2,64,1024]{4,3,2,1,0:T(8,128)(2,1)S(1)} %bitcast_dynamic-update-slice_fusion.3.refs_3_, ...), custom_call_target="tpu_custom_call" | custom-call | bytes 1048576 | tf_op jit(solution)/shard_map/fold/pallas_call | solution.py:393
  107.1 6.6 %collective-permute-done.17 = bf16[512,1024]{1,0:T(8,128)(2,1)S(1)} collective-permute-done((bf16[512,1024]{1,0:T(8,128)(2,1)S(1)}, bf16[512,1024]{1,0:T(8,128)(2,1)S(1)}, u32[]{:S(2)}, u32[]{:S(2)}) %collective-permute-start.17) | collective-permute-done | bytes 1048608 | tf_op jit(solution)/shard_map/ppermute | solution.py:38
  114.2 2.3 %slice_bitcast_fusion.1 = bf16[4,2,64,1024]{3,2,1,0:T(8,128)(2,1)} fusion(bf16[2,4,2,64,1024]{4,3,2,1,0:T(8,128)(2,1)} %collective-permute-done.13.refs_3_), kind=kLoop, calls=%fused_computation.10 | loop fusion | bytes 2097152 | tf_op jit(solution)/shard_map/squeeze | solution.py:503
  116.5 2.3 %slice_bitcast_fusion = bf16[4,2,64,1024]{3,2,1,0:T(8,128)(2,1)} fusion(bf16[2,4,2,64,1024]{4,3,2,1,0:T(8,128)(2,1)} %collective-permute-done.14.refs_4_), kind=kLoop, calls=%fused_computation.9 | loop fusion | bytes 2097152 | tf_op jit(solution)/shard_map/squeeze | solution.py:504
  118.8 1.8 %fusion.4 = bf16[512,1024]{1,0:T(8,128)(2,1)S(1)} fusion(bf16[512,1024]{1,0:T(8,128)(2,1)} %collective-permute-done.10, bf16[1,512,1024]{2,1,0:T(8,128)(2,1)S(1)} %copy-done.10), kind=kLoop, calls=%fused_computation.8 | loop fusion | flops 2097152 | bytes 3145728 | tf_op jit(solution)/shard_map/convert_element_type | solution.py:511
  120.6 3.2 %collective-permute-start.21 = (bf16[512,1024]{1,0:T(8,128)(2,1)S(1)}, bf16[512,1024]{1,0:T(8,128)(2,1)S(1)}, u32[]{:S(2)}, u32[]{:S(2)}) collective-permute-start(bf16[512,1024]{1,0:T(8,128)(2,1)S(1)} %fusion.4), channel_id=1, source_target_pairs={{0,2},{1,7},{2,4},{3,1},{4,6},{5,3},{6,0},{7,5},{8,10},{9,15},{10,... | collective-permute-start | bytes 3145736 | tf_op jit(solution)/shard_map/ppermute | solution.py:38
  123.8 0.5 collective-permute-start.19
  124.3 2.2 %collective-permute-start.20 = (bf16[4,2,64,1024]{3,2,1,0:T(8,128)(2,1)}, bf16[4,2,64,1024]{3,2,1,0:T(8,128)(2,1)S(1)}, u32[]{:S(2)}, u32[]{:S(2)}) collective-permute-start(bf16[4,2,64,1024]{3,2,1,0:T(8,128)(2,1)} %slice_bitcast_fusion), channel_id=1, source_target_pairs={{0,96},{1,25},{2,98},{3,27},{4,100},{5,29},{6,102},{7,31},{8,104},... | collective-permute-start | bytes 3145736 | tf_op jit(solution)/shard_map/ppermute | solution.py:38
  127.0 8.8 %fold.6 = (bf16[512,8192]{1,0:T(8,128)(2,1)}, bf16[4,2,64,1024]{3,2,1,0:T(8,128)(2,1)}, f32[512,1024]{1,0:T(8,128)S(1)}) custom-call(s32[5]{0:T(128)S(1)} %stack.108.at.refs_0_, bf16[512,8192]{1,0:T(8,128)(2,1)} %refs_1_.9, bf16[512,1024]{1,0:T(8,128)(2,1)S(1)} %copy-done, ...), custom_call_target="tpu_custom_call", output_to_operand_aliasing={{0}: (6, {}), {1}: (7, {})} | custom-call | bytes 1048576 | tf_op jit(solution)/shard_map/fold/pallas_call | solution.py:393
  135.8 1.4 copy-done.8
  137.2 8.6 %fold.7 = (bf16[512,8192]{1,0:T(8,128)(2,1)}, bf16[4,2,64,1024]{3,2,1,0:T(8,128)(2,1)}, f32[512,1024]{1,0:T(8,128)S(1)}) custom-call(s32[5]{0:T(128)S(1)} %stack.108.at.refs_0_, bf16[512,8192]{1,0:T(8,128)(2,1)} %refs_1_.9, bf16[512,1024]{1,0:T(8,128)(2,1)S(1)} %copy-done, ...), custom_call_target="tpu_custom_call", output_to_operand_aliasing={{0}: (6, {}), {1}: (7, {})} | custom-call | bytes 1048576 | tf_op jit(solution)/shard_map/fold/pallas_call | solution.py:393
  145.7 0.8 collective-permute-done.22
  147.6 0.6 collective-permute-start.27
  148.2 1.0 collective-permute-start.28
  149.3 5.3 %fold.8 = (bf16[512,8192]{1,0:T(8,128)(2,1)}, bf16[4,2,64,1024]{3,2,1,0:T(8,128)(2,1)}, f32[512,1024]{1,0:T(8,128)S(1)}) custom-call(s32[5]{0:T(128)S(1)} %stack.108.at.refs_0_, bf16[512,8192]{1,0:T(8,128)(2,1)} %refs_1_.9, bf16[512,1024]{1,0:T(8,128)(2,1)S(1)} %copy-done, ...), custom_call_target="tpu_custom_call", output_to_operand_aliasing={{0}: (7, {}), {1}: (8, {})} | custom-call | bytes 1048576 | tf_op jit(solution)/shard_map/fold/pallas_call | solution.py:393
  154.7 1.3 copy-done.7
  156.0 9.4 %fold.9 = (bf16[512,8192]{1,0:T(8,128)(2,1)}, bf16[4,2,64,1024]{3,2,1,0:T(8,128)(2,1)}, bf16[512,1024]{1,0:T(8,128)(2,1)}) custom-call(s32[5]{0:T(128)S(1)} %stack.108.at.refs_0_, bf16[512,8192]{1,0:T(8,128)(2,1)} %refs_1_.9, bf16[512,1024]{1,0:T(8,128)(2,1)S(1)} %copy-done, ...), custom_call_target="tpu_custom_call", output_to_operand_aliasing={{0}: (10, {}), {1}: (11, {})} | custom-call | bytes 1048576 | tf_op jit(solution)/shard_map/fold/pallas_call | solution.py:393
  165.4 1.9 %fusion.1 = f32[1,512,1024]{2,1,0:T(8,128)} fusion(bf16[512,1024]{1,0:T(8,128)(2,1)S(1)} %collective-permute-done.27, bf16[320,1024]{1,0:T(8,128)(2,1)S(1)} %collective-permute-done.28, bf16[192,1024]{1,0:T(8,128)(2,1)S(1)} %collective-permute-done.22, bf16[3,512,1024]{2,1,0:T(8,128)(2,1)S(1)} %copy-done.12), kind=kLoop, calls=%fused_computation.2 | loop fusion | flops 4194304 | bytes 5242880 | tf_op jit(solution)/shard_map/broadcast_in_dim | solution.py:540
  (74 shorter events, 4.6 us)
Async XLA Ops:
  0.7 5.8 %copy-start = (bf16[512,1024]{1,0:T(8,128)(2,1)S(1)}, bf16[512,1024]{1,0:T(8,128)(2,1)}, u32[]{:S(2)}) copy-start(bf16[512,1024]{1,0:T(8,128)(2,1)} %refs_2_.9) | copy-start | bytes 3145732
  0.7 5.9 %copy-start.13 = (bf16[1,512,1024]{2,1,0:T(8,128)(2,1)S(1)}, bf16[1,512,1024]{2,1,0:T(8,128)(2,1)}, u32[]{:S(2)}) copy-start(bf16[1,512,1024]{2,1,0:T(8,128)(2,1)} %param.5) | copy-start | bytes 3145732
  5.1 10.1 %collective-permute-start.3 = (bf16[512,4096]{1,0:T(8,128)(2,1)}, bf16[512,4096]{1,0:T(8,128)(2,1)}, u32[]{:S(2)}, u32[]{:S(2)}) collective-permute-start(bf16[512,4096]{1,0:T(8,128)(2,1)} %half.1), channel_id=1, source_target_pairs={{0,1},{1,0},{2,3},{3,2},{4,5},{5,4},{6,7},{7,6},{8,9},{9,8},{10,11... | collective-permute-start | bytes 12582920 | tf_op jit(solution)/shard_map/ppermute | solution.py:38
  6.6 8.2 %collective-permute-start.4 = (bf16[512,1024]{1,0:T(8,128)(2,1)S(1)}, bf16[512,1024]{1,0:T(8,128)(2,1)S(1)}, u32[]{:S(2)}, u32[]{:S(2)}) collective-permute-start(bf16[512,1024]{1,0:T(8,128)(2,1)S(1)} %copy-done), channel_id=1, source_target_pairs={{0,1},{1,0},{2,3},{3,2},{4,5},{5,4},{6,7},{7,6},{8,9},{9,8},{10,11... | collective-permute-start | bytes 3145736 | tf_op jit(solution)/shard_map/ppermute | solution.py:38
  7.5 14.3 %collective-permute-start = (bf16[2,64,1024]{2,1,0:T(8,128)(2,1)}, bf16[2,64,1024]{2,1,0:T(8,128)(2,1)S(1)}, u32[]{:S(2)}, u32[]{:S(2)}) collective-permute-start(bf16[2,64,1024]{2,1,0:T(8,128)(2,1)} %get-tuple-element.110), channel_id=1, source_target_pairs={{0,64},{1,65},{2,66},{3,67},{4,68},{5,69},{6,70},{7,71},{8,72},{9,... | collective-permute-start | bytes 786440 | tf_op jit(solution)/shard_map/ppermute | solution.py:38
  10.4 12.8 %collective-permute-start.1 = (bf16[2,64,1024]{2,1,0:T(8,128)(2,1)}, bf16[2,64,1024]{2,1,0:T(8,128)(2,1)}, u32[]{:S(2)}, u32[]{:S(2)}) collective-permute-start(bf16[2,64,1024]{2,1,0:T(8,128)(2,1)} %get-tuple-element.109), channel_id=1, source_target_pairs={{0,32},{1,33},{2,34},{3,35},{4,36},{5,37},{6,38},{7,39},{8,40},{9,... | collective-permute-start | bytes 786440 | tf_op jit(solution)/shard_map/ppermute | solution.py:38
  10.7 12.5 %collective-permute-start.2 = (bf16[2,64,1024]{2,1,0:T(8,128)(2,1)S(1)}, bf16[2,64,1024]{2,1,0:T(8,128)(2,1)}, u32[]{:S(2)}, u32[]{:S(2)}) collective-permute-start(bf16[2,64,1024]{2,1,0:T(8,128)(2,1)S(1)} %get-tuple-element.108), channel_id=1, source_target_pairs={{0,96},{1,97},{2,98},{3,99},{4,100},{5,101},{6,102},{7,103},{8,104... | collective-permute-start | bytes 786440 | tf_op jit(solution)/shard_map/ppermute | solution.py:38
  13.1 18.4 %copy-start.14 = (f32[1,1,64,1024]{3,2,1,0:T(8,128)S(1)}, f32[1,1,64,1024]{3,2,1,0:T(8,128)}, u32[]{:S(2)}) copy-start(f32[1,1,64,1024]{3,2,1,0:T(8,128)} %param.7) | copy-start | bytes 786436
  13.1 18.4 %copy-start.15 = (f32[1,1,64,1024]{3,2,1,0:T(8,128)S(1)}, f32[1,1,64,1024]{3,2,1,0:T(8,128)}, u32[]{:S(2)}) copy-start(f32[1,1,64,1024]{3,2,1,0:T(8,128)} %param.6) | copy-start | bytes 786436
  14.7 6.1 %copy-start.2 = (bf16[512,1024]{1,0:T(8,128)(2,1)}, bf16[512,1024]{1,0:T(8,128)(2,1)S(1)}, u32[]{:S(2)}) copy-start(bf16[512,1024]{1,0:T(8,128)(2,1)S(1)} %collective-permute-done.4.cot_theirs) | copy-start | bytes 3145732
  20.9 1.0 copy-start.11
  24.5 7.0 %collective-permute-start.5 = (bf16[64,1024]{1,0:T(8,128)(2,1)S(1)}, bf16[64,1024]{1,0:T(8,128)(2,1)S(1)}, u32[]{:S(2)}, u32[]{:S(2)}) collective-permute-start(bf16[64,1024]{1,0:T(8,128)(2,1)S(1)} %fusion.9), channel_id=1, source_target_pairs={{0,16},{1,17},{2,18},{3,19},{4,20},{5,21},{6,22},{7,23},{8,24},{9,... | collective-permute-start | bytes 393224 | tf_op jit(solution)/shard_map/ppermute | solution.py:38
  28.3 26.9 %collective-permute-start.15 = (bf16[512,1024]{1,0:T(8,128)(2,1)}, bf16[512,1024]{1,0:T(8,128)(2,1)}, u32[]{:S(2)}, u32[]{:S(2)}) collective-permute-start(bf16[512,1024]{1,0:T(8,128)(2,1)} %copy-done.11), channel_id=1, source_target_pairs={{0,2},{1,7},{2,4},{3,1},{4,6},{5,3},{6,0},{7,5},{8,10},{9,15},{10,... | collective-permute-start | bytes 3145736 | tf_op jit(solution)/shard_map/ppermute | solution.py:38
  32.5 3.9 %collective-permute-start.6 = (bf16[64,1024]{1,0:T(8,128)(2,1)S(1)}, bf16[64,1024]{1,0:T(8,128)(2,1)S(1)}, u32[]{:S(2)}, u32[]{:S(2)}) collective-permute-start(bf16[64,1024]{1,0:T(8,128)(2,1)S(1)} %get-tuple-element.106), channel_id=1, source_target_pairs={{0,1},{1,0},{2,3},{3,2},{4,5},{5,4},{6,7},{7,6},{8,9},{9,8},{10,11... | collective-permute-start | bytes 393224 | tf_op jit(solution)/shard_map/ppermute | solution.py:38
  33.6 32.3 %collective-permute-start.10 = (bf16[512,1024]{1,0:T(8,128)(2,1)}, bf16[512,1024]{1,0:T(8,128)(2,1)}, u32[]{:S(2)}, u32[]{:S(2)}) collective-permute-start(bf16[512,1024]{1,0:T(8,128)(2,1)} %bitcast.15), channel_id=1, source_target_pairs={{0,2},{1,7},{2,4},{3,1},{4,6},{5,3},{6,0},{7,5},{8,10},{9,15},{10,... | collective-permute-start | bytes 3145736 | tf_op jit(solution)/shard_map/ppermute | solution.py:38
  36.4 11.5 %collective-permute-start.7 = (bf16[2,64,1024]{2,1,0:T(8,128)(2,1)S(1)}, bf16[2,64,1024]{2,1,0:T(8,128)(2,1)S(1)}, u32[]{:S(2)}, u32[]{:S(2)}) collective-permute-start(bf16[2,64,1024]{2,1,0:T(8,128)(2,1)S(1)} %maximum_select_fusion), channel_id=1, source_target_pairs={{0,0},{1,5},{2,2},{3,7},{4,4},{5,1},{6,6},{7,3},{8,8},{9,13},{10,1... | collective-permute-start | bytes 786440 | tf_op jit(solution)/shard_map/ppermute | solution.py:38
  39.5 12.1 %collective-permute-start.8 = (bf16[2,64,1024]{2,1,0:T(8,128)(2,1)S(1)}, bf16[2,64,1024]{2,1,0:T(8,128)(2,1)S(1)}, u32[]{:S(2)}, u32[]{:S(2)}) collective-permute-start(bf16[2,64,1024]{2,1,0:T(8,128)(2,1)S(1)} %maximum_select_fusion), channel_id=1, source_target_pairs={{0,6},{1,3},{2,0},{3,5},{4,2},{5,7},{6,4},{7,1},{8,14},{9,11},{10,... | collective-permute-start | bytes 786440 | tf_op jit(solution)/shard_map/ppermute | solution.py:38
  51.6 3.6 %copy-start.3 = (bf16[512,1024]{1,0:T(8,128)(2,1)S(1)}, bf16[512,1024]{1,0:T(8,128)(2,1)}, u32[]{:S(2)}) copy-start(bf16[512,1024]{1,0:T(8,128)(2,1)} %copy-done.2) | copy-start | bytes 3145732
  51.7 14.3 %collective-permute-start.9 = (bf16[2,2,64,1024]{3,2,1,0:T(8,128)(2,1)S(1)}, bf16[2,2,64,1024]{3,2,1,0:T(8,128)(2,1)S(1)}, u32[]{:S(2)}, u32[]{:S(2)}) collective-permute-start(bf16[2,2,64,1024]{3,2,1,0:T(8,128)(2,1)S(1)} %pad_maximum_fusion), channel_id=1, source_target_pairs={{0,24},{1,97},{2,26},{3,99},{4,28},{5,101},{6,30},{7,103},{8,0},{9... | collective-permute-start | bytes 1572872 | tf_op jit(solution)/shard_map/ppermute | solution.py:38
  54.3 21.8 %collective-permute-start.11 = (bf16[2,2,64,1024]{3,2,1,0:T(8,128)(2,1)S(1)}, bf16[2,2,64,1024]{3,2,1,0:T(8,128)(2,1)S(1)}, u32[]{:S(2)}, u32[]{:S(2)}) collective-permute-start(bf16[2,2,64,1024]{3,2,1,0:T(8,128)(2,1)S(1)} %pad_maximum_fusion), channel_id=1, source_target_pairs={{0,16},{1,65},{2,18},{3,67},{4,20},{5,69},{6,22},{7,71},{8,24},{9,... | collective-permute-start | bytes 1572872 | tf_op jit(solution)/shard_map/ppermute | solution.py:38
  54.8 21.4 %collective-permute-start.12 = (bf16[2,2,64,1024]{3,2,1,0:T(8,128)(2,1)S(1)}, bf16[2,2,64,1024]{3,2,1,0:T(8,128)(2,1)S(1)}, u32[]{:S(2)}, u32[]{:S(2)}) collective-permute-start(bf16[2,2,64,1024]{3,2,1,0:T(8,128)(2,1)S(1)} %pad_maximum_fusion), channel_id=1, source_target_pairs={{0,8},{1,33},{2,10},{3,35},{4,12},{5,37},{6,14},{7,39},{8,16},{9,4... | collective-permute-start | bytes 1572872 | tf_op jit(solution)/shard_map/ppermute | solution.py:38
  61.3 15.0 %copy-start.9 = (bf16[1,512,1024]{2,1,0:T(8,128)(2,1)}, bf16[1,512,1024]{2,1,0:T(8,128)(2,1)S(1)}, u32[]{:S(2)}) copy-start(bf16[1,512,1024]{2,1,0:T(8,128)(2,1)S(1)} %get-tuple-element.76) | copy-start | bytes 3145732
  65.9 22.8 %collective-permute-start.16 = (bf16[512,1024]{1,0:T(8,128)(2,1)}, bf16[512,1024]{1,0:T(8,128)(2,1)}, u32[]{:S(2)}, u32[]{:S(2)}) collective-permute-start(bf16[512,1024]{1,0:T(8,128)(2,1)} %get-tuple-element.68), channel_id=1, source_target_pairs={{0,2},{1,7},{2,4},{3,1},{4,6},{5,3},{6,0},{7,5},{8,10},{9,15},{10,... | collective-permute-start | bytes 3145736 | tf_op jit(solution)/shard_map/ppermute | solution.py:38
  76.2 25.7 %copy-start.1 = (bf16[2,4,2,64,1024]{4,3,2,1,0:T(8,128)(2,1)}, bf16[2,4,2,64,1024]{4,3,2,1,0:T(8,128)(2,1)S(1)}, u32[]{:S(2)}) copy-start(bf16[2,4,2,64,1024]{4,3,2,1,0:T(8,128)(2,1)S(1)} %bitcast_dynamic-update-slice_fusion.3.refs_3_) | copy-start | bytes 6291460
  76.3 25.7 %collective-permute-start.18 = (bf16[2,4,2,64,1024]{4,3,2,1,0:T(8,128)(2,1)S(1)}, bf16[2,4,2,64,1024]{4,3,2,1,0:T(8,128)(2,1)}, u32[]{:S(2)}, u32[]{:S(2)}) collective-permute-start(bf16[2,4,2,64,1024]{4,3,2,1,0:T(8,128)(2,1)S(1)} %bitcast_dynamic-update-slice_fusion.3.refs_3_), channel_id=1, source_target_pairs={{0,1},{1,0},{2,3},{3,2},{4,5},{5,4},{6,7},{7,6},{8,9},{9,8},{10,11... | collective-permute-start | bytes 6291464 | tf_op jit(solution)/shard_map/ppermute | solution.py:38
  76.4 37.3 %collective-permute-start.13 = (bf16[2,4,2,64,1024]{4,3,2,1,0:T(8,128)(2,1)S(1)}, bf16[2,4,2,64,1024]{4,3,2,1,0:T(8,128)(2,1)}, u32[]{:S(2)}, u32[]{:S(2)}) collective-permute-start(bf16[2,4,2,64,1024]{4,3,2,1,0:T(8,128)(2,1)S(1)} %bitcast_dynamic-update-slice_fusion.3.refs_3_), channel_id=1, source_target_pairs={{0,32},{1,9},{2,34},{3,11},{4,36},{5,13},{6,38},{7,15},{8,40},{9,1... | collective-permute-start | bytes 6291464 | tf_op jit(solution)/shard_map/ppermute | solution.py:38
  76.9 36.7 %collective-permute-start.14 = (bf16[2,4,2,64,1024]{4,3,2,1,0:T(8,128)(2,1)S(1)}, bf16[2,4,2,64,1024]{4,3,2,1,0:T(8,128)(2,1)}, u32[]{:S(2)}, u32[]{:S(2)}) collective-permute-start(bf16[2,4,2,64,1024]{4,3,2,1,0:T(8,128)(2,1)S(1)} %bitcast_dynamic-update-slice_fusion.3.refs_3_), channel_id=1, source_target_pairs={{0,96},{1,25},{2,98},{3,27},{4,100},{5,29},{6,102},{7,31},{8,104},... | collective-permute-start | bytes 6291464 | tf_op jit(solution)/shard_map/ppermute | solution.py:38
  88.7 1.2 copy-start.4
  99.1 14.5 %collective-permute-start.17 = (bf16[512,1024]{1,0:T(8,128)(2,1)S(1)}, bf16[512,1024]{1,0:T(8,128)(2,1)S(1)}, u32[]{:S(2)}, u32[]{:S(2)}) collective-permute-start(bf16[512,1024]{1,0:T(8,128)(2,1)S(1)} %get-tuple-element.69), channel_id=1, source_target_pairs={{0,2},{1,7},{2,4},{3,1},{4,6},{5,3},{6,0},{7,5},{8,10},{9,15},{10,... | collective-permute-start | bytes 3145736 | tf_op jit(solution)/shard_map/ppermute | solution.py:38
  107.1 11.7 %copy-start.5 = (f32[512,1024]{1,0:T(8,128)}, f32[512,1024]{1,0:T(8,128)S(1)}, u32[]{:S(2)}) copy-start(f32[512,1024]{1,0:T(8,128)S(1)} %get-tuple-element.80.refs_5_) | copy-start | bytes 6291460
  113.7 5.1 %copy-start.10 = (bf16[1,512,1024]{2,1,0:T(8,128)(2,1)S(1)}, bf16[1,512,1024]{2,1,0:T(8,128)(2,1)}, u32[]{:S(2)}) copy-start(bf16[1,512,1024]{2,1,0:T(8,128)(2,1)} %copy-done.9) | copy-start | bytes 3145732
  113.7 13.2 %collective-permute-start.23 = (bf16[2,4,2,64,1024]{4,3,2,1,0:T(8,128)(2,1)}, bf16[2,4,2,64,1024]{4,3,2,1,0:T(8,128)(2,1)S(1)}, u32[]{:S(2)}, u32[]{:S(2)}) collective-permute-start(bf16[2,4,2,64,1024]{4,3,2,1,0:T(8,128)(2,1)} %collective-permute-done.13.refs_3_), channel_id=1, source_target_pairs={{0,1},{1,0},{2,3},{3,2},{4,5},{5,4},{6,7},{7,6},{8,9},{9,8},{10,11... | collective-permute-start | bytes 6291464 | tf_op jit(solution)/shard_map/ppermute | solution.py:38
  113.8 23.4 %collective-permute-start.24 = (bf16[2,4,2,64,1024]{4,3,2,1,0:T(8,128)(2,1)}, bf16[2,4,2,64,1024]{4,3,2,1,0:T(8,128)(2,1)}, u32[]{:S(2)}, u32[]{:S(2)}) collective-permute-start(bf16[2,4,2,64,1024]{4,3,2,1,0:T(8,128)(2,1)} %collective-permute-done.14.refs_4_), channel_id=1, source_target_pairs={{0,1},{1,0},{2,3},{3,2},{4,5},{5,4},{6,7},{7,6},{8,9},{9,8},{10,11... | collective-permute-start | bytes 6291464 | tf_op jit(solution)/shard_map/ppermute | solution.py:38
  118.8 7.7 %copy-start.12 = (bf16[3,512,1024]{2,1,0:T(8,128)(2,1)S(1)}, bf16[3,512,1024]{2,1,0:T(8,128)(2,1)}, u32[]{:S(2)}) copy-start(bf16[3,512,1024]{2,1,0:T(8,128)(2,1)} %get-tuple-element.78) | copy-start | bytes 9437188
  120.6 26.0 %collective-permute-start.21 = (bf16[512,1024]{1,0:T(8,128)(2,1)S(1)}, bf16[512,1024]{1,0:T(8,128)(2,1)S(1)}, u32[]{:S(2)}, u32[]{:S(2)}) collective-permute-start(bf16[512,1024]{1,0:T(8,128)(2,1)S(1)} %fusion.4), channel_id=1, source_target_pairs={{0,2},{1,7},{2,4},{3,1},{4,6},{5,3},{6,0},{7,5},{8,10},{9,15},{10,... | collective-permute-start | bytes 3145736 | tf_op jit(solution)/shard_map/ppermute | solution.py:38
  123.8 22.8 %collective-permute-start.19 = (bf16[4,2,64,1024]{3,2,1,0:T(8,128)(2,1)}, bf16[4,2,64,1024]{3,2,1,0:T(8,128)(2,1)S(1)}, u32[]{:S(2)}, u32[]{:S(2)}) collective-permute-start(bf16[4,2,64,1024]{3,2,1,0:T(8,128)(2,1)} %slice_bitcast_fusion.1), channel_id=1, source_target_pairs={{0,32},{1,9},{2,34},{3,11},{4,36},{5,13},{6,38},{7,15},{8,40},{9,1... | collective-permute-start | bytes 3145736 | tf_op jit(solution)/shard_map/ppermute | solution.py:38
  124.3 22.3 %collective-permute-start.20 = (bf16[4,2,64,1024]{3,2,1,0:T(8,128)(2,1)}, bf16[4,2,64,1024]{3,2,1,0:T(8,128)(2,1)S(1)}, u32[]{:S(2)}, u32[]{:S(2)}) collective-permute-start(bf16[4,2,64,1024]{3,2,1,0:T(8,128)(2,1)} %slice_bitcast_fusion), channel_id=1, source_target_pairs={{0,96},{1,25},{2,98},{3,27},{4,100},{5,29},{6,102},{7,31},{8,104},... | collective-permute-start | bytes 3145736 | tf_op jit(solution)/shard_map/ppermute | solution.py:38
  126.9 19.7 %collective-permute-start.22 = (bf16[192,1024]{1,0:T(8,128)(2,1)S(1)}, bf16[192,1024]{1,0:T(8,128)(2,1)S(1)}, u32[]{:S(2)}, u32[]{:S(2)}) collective-permute-start(bf16[192,1024]{1,0:T(8,128)(2,1)S(1)} %slice.28), channel_id=1, source_target_pairs={{0,8},{1,9},{2,10},{3,11},{4,12},{5,13},{6,14},{7,15},{8,0},{9,1},... | collective-permute-start | bytes 1179656 | tf_op jit(solution)/shard_map/ppermute | solution.py:38
  135.8 1.4 copy-start.8
  145.7 2.5 %copy-start.6 = (f32[512,1024]{1,0:T(8,128)}, f32[512,1024]{1,0:T(8,128)S(1)}, u32[]{:S(2)}) copy-start(f32[512,1024]{1,0:T(8,128)S(1)} %get-tuple-element.91.refs_6_) | copy-start | bytes 6291460
  146.6 9.4 %collective-permute-start.25 = (bf16[4,2,64,1024]{3,2,1,0:T(8,128)(2,1)S(1)}, bf16[4,2,64,1024]{3,2,1,0:T(8,128)(2,1)S(1)}, u32[]{:S(2)}, u32[]{:S(2)}) collective-permute-start(bf16[4,2,64,1024]{3,2,1,0:T(8,128)(2,1)S(1)} %collective-permute-done.19.refs_4_), channel_id=1, source_target_pairs={{0,1},{1,0},{2,3},{3,2},{4,5},{5,4},{6,7},{7,6},{8,9},{9,8},{10,11... | collective-permute-start | bytes 3145736 | tf_op jit(solution)/shard_map/ppermute | solution.py:38
  146.7 9.3 %collective-permute-start.26 = (bf16[4,2,64,1024]{3,2,1,0:T(8,128)(2,1)S(1)}, bf16[4,2,64,1024]{3,2,1,0:T(8,128)(2,1)S(1)}, u32[]{:S(2)}, u32[]{:S(2)}) collective-permute-start(bf16[4,2,64,1024]{3,2,1,0:T(8,128)(2,1)S(1)} %collective-permute-done.20.refs_5_), channel_id=1, source_target_pairs={{0,1},{1,0},{2,3},{3,2},{4,5},{5,4},{6,7},{7,6},{8,9},{9,8},{10,11... | collective-permute-start | bytes 3145736 | tf_op jit(solution)/shard_map/ppermute | solution.py:38
  147.6 17.9 %collective-permute-start.27 = (bf16[512,1024]{1,0:T(8,128)(2,1)S(1)}, bf16[512,1024]{1,0:T(8,128)(2,1)S(1)}, u32[]{:S(2)}, u32[]{:S(2)}) collective-permute-start(bf16[512,1024]{1,0:T(8,128)(2,1)S(1)} %fusion.2), channel_id=1, source_target_pairs={{0,2},{1,7},{2,4},{3,1},{4,6},{5,3},{6,0},{7,5},{8,10},{9,15},{10,... | collective-permute-start | bytes 3145736 | tf_op jit(solution)/shard_map/ppermute | solution.py:38
  148.2 17.2 %collective-permute-start.28 = (bf16[320,1024]{1,0:T(8,128)(2,1)S(1)}, bf16[320,1024]{1,0:T(8,128)(2,1)S(1)}, u32[]{:S(2)}, u32[]{:S(2)}) collective-permute-start(bf16[320,1024]{1,0:T(8,128)(2,1)S(1)} %slice.29), channel_id=1, source_target_pairs={{0,8},{1,9},{2,10},{3,11},{4,12},{5,13},{6,14},{7,15},{8,0},{9,1},... | collective-permute-start | bytes 1966088 | tf_op jit(solution)/shard_map/ppermute | solution.py:38
  154.7 1.3 copy-start.7

commit v4 on v2

--- a/solution.py
+++ b/solution.py
@@ -1,3 +1,4 @@
+import functools
 import itertools
 
 import jax
@@ -16,7 +17,7 @@
 D = 8192
 COLS = 1024
 SCALE = D ** (-0.5)
-VMEM = 48 * 1024 * 1024
+VMEM = 24 * 1024 * 1024
 ANY = pl.BlockSpec(memory_space=pl.ANY)
 BF = jnp.bfloat16
 F32 = jnp.float32
@@ -95,31 +96,35 @@
     )(at, tokens)
 
 
-def grad_kernel(blocks, mine, theirs, cot, cot_theirs, out, *rest):
+def grad_kernel(adds, blocks, mine, theirs, cot, cot_theirs, *refs):
+    arrived, (out, *rest) = refs[:adds], refs[adds:]
     dims = (((0,), (0,)), ((), ()))
     total = lax.dot_general(mine[...], cot[...], dims, preferred_element_type=F32)
     total += lax.dot_general(
         theirs[...], cot_theirs[...], dims, preferred_element_type=F32
     )
-    total = (total * SCALE).astype(out.dtype)
+    total = total * SCALE
 
     @pl.when(pl.program_id(0) == 0)
     def _():
-        out[...] = total
+        first = total
+        for part in arrived:
+            first = first + part[...].astype(F32)
+        out[...] = first.astype(BF)
 
     for more in rest:
 
         @pl.when(pl.program_id(0) > 0)
         def _(more=more):
-            more[0] = total
-
-
-def grad_blocks(blocks, core, tokens, tokens_theirs, cot, cot_theirs):
+            more[0] = total.astype(BF)
+
+
+def grad_blocks(blocks, core, tokens, tokens_theirs, cot, cot_theirs, arrived):
     count = len(blocks)
     table = jnp.stack([2 * g + core for g in blocks] + blocks).astype(jnp.int32)
     whole = pl.BlockSpec((TOK, COLS), lambda m, b: (0, 0))
     return pl.pallas_call(
-        grad_kernel,
+        functools.partial(grad_kernel, len(arrived)),
         out_shape=[
             jax.ShapeDtypeStruct((512, COLS), BF),
             jax.ShapeDtypeStruct((count - 1, 512, COLS), BF),
@@ -132,7 +137,8 @@
                 pl.BlockSpec((TOK, 512), lambda m, b: (0, b[count + m])),
                 whole,
                 whole,
-            ],
+            ]
+            + [whole] * len(arrived),
             out_specs=[
                 whole,
                 pl.BlockSpec((1, 512, COLS), lambda m, b: (jnp.maximum(m - 1, 0), 0, 0)),
@@ -140,31 +146,28 @@
         ),
         compiler_params=params(),
         cost_estimate=pl.CostEstimate(
-            flops=0,
-            bytes_accessed=1 << 20,
+            flops=count * 4 * TOK * 512 * COLS,
+            bytes_accessed=(count * 2 + 2) << 20,
             transcendentals=0,
         ),
         name="grad",
-    )(table, tokens, tokens_theirs, cot, cot_theirs)
+    )(table, tokens, tokens_theirs, cot, cot_theirs, *arrived)
 
 
 OFFSETS = (0, -1, 2, 1)
 
 
-def fold_kernel(groups, chunks, first, last, *refs):
+def fold_kernel(groups, mine, theirs, first, last, *refs):
     refs = list(refs)
     at, tokens, cot = refs[:3]
     refs = refs[3:]
-    mine = {key: refs.pop(0) for key in chunks}
-    theirs = {key: refs.pop(0) for key in chunks}
+    mine = {key: refs.pop(0) for key in mine}
+    theirs = {key: refs.pop(0) for key in theirs}
     if not first:
         acc_in, _, _ = refs.pop(0), refs.pop(0), refs.pop(0)
     grad_out, weights_out, key_out = refs.pop(0), refs.pop(0), refs.pop(0)
-    w, tok, grad, cot_v, acc, w_sem, tok_sem, out_sem, own_sem, cot_sem, acc_sem = (
-        refs[:11]
-    )
-    if last:
-        key_v = refs[11]
+    w, tok, grad, cot_v, w_sem, tok_sem, out_sem, own_sem, cot_sem = refs[:9]
+    acc = refs[9] if last else key_out
     x, z, y, c = at[0], at[1], at[2], at[4]
 
     def part(held, s, dy):
@@ -211,7 +214,6 @@
                     ).start()
 
         here = 0 if group[0] == "x" else 1
-
         @pl.when(c == here)
         def _():
             start(mine)
@@ -262,8 +264,7 @@
     if first:
         acc[...] = jnp.zeros_like(acc)
     else:
-        acc_copy = pltpu.make_async_copy(acc_in, acc, acc_sem)
-        acc_copy.start()
+        acc[...] = acc_in[...]
     cot_copy.wait()
 
     @pl.loop(0, count)
@@ -299,12 +300,6 @@
                 stores(k)
 
         whole(tok, tok_sem, slot).wait()
-        if not first:
-
-            @pl.when(i == 0)
-            def _():
-                acc_copy.wait()
-
         acc[...] += jnp.dot(tok[slot], rows, preferred_element_type=F32)
         for k in range(count):
             if holds_own(groups[k]):
@@ -314,14 +309,9 @@
                     weights_store(k).wait()
 
     if last:
-        key_v[...] = (acc[...] * SCALE).astype(BF)
-        key_copy = pltpu.make_async_copy(key_v, key_out, acc_sem)
-    else:
-        key_copy = pltpu.make_async_copy(acc, key_out, acc_sem)
-    key_copy.start()
+        key_out[...] = (acc[...] * SCALE).astype(BF)
     for i in range(max(count - 3, 0), count):
         whole(grad, out_sem, i % 3).wait()
-    key_copy.wait()
 
 
 def fold(at, tokens, cot, groups, mine, theirs, carry, last):
@@ -343,24 +333,26 @@
         pltpu.VMEM((3, TOK, 512), BF),
         pltpu.VMEM((3, TOK, 512), BF),
         pltpu.VMEM((TOK, COLS), BF),
-        pltpu.VMEM((TOK, COLS), F32),
         dma((3,)),
         dma((3,)),
         dma((3,)),
         dma((3,)),
         dma(()),
-        dma(()),
     ]
     if last:
-        scratch += [pltpu.VMEM((TOK, COLS), BF)]
+        scratch += [pltpu.VMEM((TOK, COLS), F32)]
+    in_vmem = pl.BlockSpec(memory_space=pltpu.VMEM)
+    in_specs = [pl.BlockSpec(memory_space=pltpu.SMEM)] + [ANY] * (len(operands) - 1)
+    if not first:
+        in_specs[-3] = in_vmem
     def kernel(*refs):
-        fold_kernel(groups, list(mine), first, last, *refs)
+        fold_kernel(groups, list(mine), list(theirs), first, last, *refs)
 
     return pl.pallas_call(
         kernel,
         out_shape=shapes,
-        in_specs=[pl.BlockSpec(memory_space=pltpu.SMEM)] + [ANY] * (len(operands) - 1),
-        out_specs=[ANY] * len(shapes),
+        in_specs=in_specs,
+        out_specs=[ANY, ANY, in_vmem],
         scratch_shapes=scratch,
         input_output_aliases=aliases,
         compiler_params=params(),
@@ -382,12 +374,14 @@
     tokens_theirs = swap_core(other_half(at, tokens))
     cot_theirs = swap_core(key_cot)
 
-    def grads(which, tokens_theirs):
+    def grads(which, tokens_theirs, *arrived):
         blocks = [
             (zl if half else 1 - zl) * 4 + ((y - way * (s + 1) + 8) & 3)
             for half, s in which
         ]
-        return grad_blocks(blocks, c, tokens, tokens_theirs, key_cot, cot_theirs)
+        return grad_blocks(
+            blocks, c, tokens, tokens_theirs, key_cot, cot_theirs, arrived
+        )
 
     def add(*parts):
         total = parts[0].astype(F32)
@@ -402,7 +396,7 @@
         got.append(permute(piece, lambda px, pz, py, pc: (px + d, pz, py, pc)))
     first, first_b = grads([(0, 0), (1, 0)], tokens_theirs)
     *got, first, first_b = lax.optimization_barrier((*got, first, first_b[0]))
-    arrived, arrived_b = ring_y(first), ring_y(first_b)
+    arrived = ring_y(first)
     part = add(lax.dynamic_index_in_dim(by_x, x, 0, False), *got)
     crossing = lax.dynamic_index_in_dim(part, 1 - zh, 0, False).astype(BF)
     crossing = permute(crossing, lambda px, pz, py, pc: (px, pz + 2, py, pc))
@@ -434,22 +428,20 @@
             )
         return whole
 
-    owned, late = lax.optimization_barrier((owned, tokens_theirs))
-    second, second_b = grads([(0, 1), (1, 1)], late)
     other, arrived = lax.optimization_barrier((swap_core(owned), arrived))
     both = jnp.where(c == 0, jnp.stack([owned, other]), jnp.stack([other, owned]))
     near = permute(both, lambda px, pz, py, pc: (px, pz, py - 1 + 2 * pc, pc))
     far = permute(both, lambda px, pz, py, pc: (px, pz, py + 2 * pc, pc))
     c0 = jnp.stack([far, near])
-    c0, second, second_b, late = lax.optimization_barrier(
-        (c0, second, second_b[0], late)
-    )
-    third, rest = grads([(0, 2), (0, 3), (1, 2), (1, 3)], late)
+    c0, first_b, late = lax.optimization_barrier((c0, first_b, tokens_theirs))
+    arrived_b = ring_y(first_b)
+    second, second_b = grads([(0, 1), (1, 1)], late, arrived)
     parts = [short_way(c0, d) for d in (1, 2, 3)]
-    arrived = ring_y(add(second, arrived).astype(BF))
-    parts[0], arrived_b = lax.optimization_barrier((parts[0], arrived_b))
+    arrived = ring_y(second)
+    second_b = second_b[0]
     c1 = in_order([c0] + parts, jnp.where(c == 0, z, x))
-    c1, third, rest, arrived = lax.optimization_barrier((c1, third, rest, arrived))
+    c1, late = lax.optimization_barrier((c1, late))
+    third, rest = grads([(0, 2), (0, 3), (1, 2), (1, 3)], late, arrived)
 
     mine, theirs = {0: c1}, {0: swap_core(c1)}
     mine[1], mine[3] = long_way(c1, 1), long_way(c1, -1)
@@ -461,7 +453,7 @@
         )
 
     carry = fold_of([("x", 0, 0), ("x", 0, 1)], [0], None, False)
-    arrived = ring_y(add(third, arrived).astype(BF))
+    arrived = ring_y(third)
     mine[1], mine[3], arrived, arrived_b, *carry = lax.optimization_barrier(
         (mine[1], mine[3], arrived, arrived_b, *carry)
     )
@@ -471,23 +463,21 @@
     crossed = add(rest[0], arrived).astype(BF)
     crossed = [
         permute(half, lambda px, pz, py, pc: (px, pz ^ 1, py, pc))
-        for half in (crossed[:256], crossed[256:])
+        for half in (crossed[:192], crossed[192:])
     ]
     arrived_b = ring_y(add(second_b, arrived_b).astype(BF))
-    carry = fold_of(
-        [("x", s, dy) for s in (1, 3) for dy in range(2)]
-        + [("z", (1, 3), dy, p) for dy in range(2) for p in range(2)],
-        [1, 3], carry, False,
-    )
+    groups = [("x", s, dy) for s in (1, 3) for dy in range(2)]
+    groups += [("z", (1, 3), dy, p) for dy in range(2) for p in range(2)]
+    carry = fold_of(groups, [1, 3], carry, False)
     mine[2, 0], mine[2, 1], arrived_b, crossed[0], *carry = lax.optimization_barrier(
         (mine[2, 0], mine[2, 1], arrived_b, crossed[0], *carry)
     )
     theirs[2, 0], theirs[2, 1] = swap_core(mine[2, 0]), swap_core(mine[2, 1])
     arrived_b = ring_y(add(rest[1], arrived_b).astype(BF))
+    groups = [("x", 2, dy) for dy in range(2)]
+    groups += [("z", (0, 2), dy, p) for dy in range(2) for p in range(2)]
     grad_tokens, shard_weights, keys_out = fold_of(
-        [("x", 2, dy) for dy in range(2)]
-        + [("z", (0, 2), dy, p) for dy in range(2) for p in range(2)],
-        [0, (2, 0), (2, 1)], carry, True,
+        groups, [0, (2, 0), (2, 1)], carry, True
     )
     arrived_b, *crossed, keys_out = lax.optimization_barrier(
         (arrived_b, *crossed, keys_out)

time: 156 us -> 165 us (1.058)
  local copies, waits for them, and re-layouts: 6.38 us -> 22.2 us
  waiting for transfers between devices: 39.1 us -> 33.3 us
  starting transfers between devices: 38.4 us -> 44 us
  other arithmetic: 13.1 us -> 8.75 us
  Pallas kernels: 57.7 us -> 54.6 us
    unnamed x30 -> x36, local copies, waits for them, and re-layouts: 1.58 us -> 18 us
    ppermute x29, waiting for transfers between devices: 39.1 us -> 33.3 us  [permute(): return lax.ppermute(value, AXES, pairs)]
    ppermute x29, starting transfers between devices: 38.4 us -> 44 us  [permute(): return lax.ppermute(value, AXES, pairs)]
    convert_element_type x2 -> x0, other arithmetic: 4.24 us -> none  [the longest x1 2.6 us: per_device(): arrived = ring_y(add(second, arrived).astype(BF))]
    dynamic_update_slice x4, local copies, waits for them, and re-layouts: 3.29 us -> 0.2 us  [in_order(): lax.dynamic_update_slice_in_dim(whole, part[:, None], here + d & 3, 1)]
    pallas_call x6, Pallas kernels: 53.3 us -> 51.3 us  [the longest x3 31.7 us: fold(): pl.pallas_call(kernel, out_shape=shapes, in_specs=in_specs, out_specs=[AN...]
  transfers between devices with their start and end apart: 29 -> 29, of which waited for: 13 -> 12; matrix products, arithmetic and copies ran while one was open for 10% -> 5% of each run, Pallas kernels for 34% -> 31%
where the time goes in v4:
time: 165 us; the launch traced here: 164 us
  Pallas kernels  54.6 us (33%)
  starting transfers between devices  44 us (27%)
  waiting for transfers between devices  33.3 us (20%)
  local copies, waits for them, and re-layouts  22.2 us (13%)
  other arithmetic  8.75 us (5%)
    ppermute x29, starting transfers between devices, permute(): return lax.ppermute(value, AXES, pairs)  44 us
    ppermute x29, waiting for transfers between devices, permute(): return lax.ppermute(value, AXES, pairs)  33.3 us
    pallas_call x3, Pallas kernels, fold(): pl.pallas_call(kernel, out_shape=shapes, in_specs=in_specs, out_specs=[AN...  31.7 us
    pallas_call x3, Pallas kernels, grad_blocks(): pl.pallas_call(functools.partial(grad_kernel, len(arrived)), out_shape=[j...  19.6 us
    unnamed x36, local copies, waits for them, and re-layouts  18 us
    pallas_call x1, Pallas kernels, other_half(): pl.pallas_call(half_kernel, out_shape=jax.ShapeDtypeStruct((TOK, D // 2),...  3.36 us
  transfers between devices with their start and end apart: 29, of which 12 were waited for; matrix products, arithmetic and copies ran while one was open for 5% of the time, Pallas kernels for 31%

profile of v4, /device:TPU:1, one launch (start us, length us, event | category | flops | bytes accessed | tf_op | source)
XLA Modules:
  0.0 163.8 jit_solution(763552330091917328)
XLA Ops:
  0.7 3.4 %copy-done = bf16[512,8192]{1,0:T(8,128)(2,1)S(1)} copy-done((bf16[512,8192]{1,0:T(8,128)(2,1)S(1)}, bf16[512,8192]{1,0:T(8,128)(2,1)}, u32[]{:S(2)}) %copy-start) | copy-done | bytes 8388632
  4.1 3.4 %half.1 = bf16[512,4096]{1,0:T(8,128)(2,1)} custom-call(s32[5]{0:T(128)S(1)} %stack.108.at.refs_0_, bf16[512,8192]{1,0:T(8,128)(2,1)S(1)} %copy-done), custom_call_target="tpu_custom_call" | custom-call | bytes 8388608 | tf_op jit(solution)/shard_map/half/pallas_call | solution.py:81
  7.5 1.5 collective-permute-start.3
  9.1 0.9 dynamic-slice_bitcast_fusion
  9.9 2.8 %collective-permute-start = (bf16[2,64,1024]{2,1,0:T(8,128)(2,1)}, bf16[2,64,1024]{2,1,0:T(8,128)(2,1)S(1)}, u32[]{:S(2)}, u32[]{:S(2)}) collective-permute-start(bf16[2,64,1024]{2,1,0:T(8,128)(2,1)} %get-tuple-element.100), channel_id=1, source_target_pairs={{0,64},{1,65},{2,66},{3,67},{4,68},{5,69},{6,70},{7,71},{8,72},{9,... | collective-permute-start | bytes 786440 | tf_op jit(solution)/shard_map/ppermute | solution.py:38
  13.1 2.4 %collective-permute-start.2 = (bf16[2,64,1024]{2,1,0:T(8,128)(2,1)S(1)}, bf16[2,64,1024]{2,1,0:T(8,128)(2,1)S(1)}, u32[]{:S(2)}, u32[]{:S(2)}) collective-permute-start(bf16[2,64,1024]{2,1,0:T(8,128)(2,1)S(1)} %get-tuple-element.98), channel_id=1, source_target_pairs={{0,96},{1,97},{2,98},{3,99},{4,100},{5,101},{6,102},{7,103},{8,104... | collective-permute-start | bytes 786440 | tf_op jit(solution)/shard_map/ppermute | solution.py:38
  15.5 1.6 collective-permute-done.4.cot_theirs
  17.6 3.4 %copy-done.1 = bf16[512,8192]{1,0:T(8,128)(2,1)S(1)} copy-done((bf16[512,8192]{1,0:T(8,128)(2,1)S(1)}, bf16[512,8192]{1,0:T(8,128)(2,1)}, u32[]{:S(2)}) %copy-start.1) | copy-done | bytes 8388632
  21.0 5.6 %grad.3 = (bf16[512,1024]{1,0:T(8,128)(2,1)}, bf16[1,512,1024]{2,1,0:T(8,128)(2,1)S(1)}) custom-call(s32[4]{0:T(128)S(1)} %pad_add_fusion.blocks, bf16[512,8192]{1,0:T(8,128)(2,1)S(1)} %copy-done.1, bf16[512,4096]{1,0:T(8,128)(2,1)} %collective-permute-done.3.theirs, bf16[512,1024]{1,0:T(8,128)(2,1)S(1)} %copy-done.5, ...), custom_call_target="tpu_custom_call" | custom-call | flops 2147483648 | bytes 6291456 | tf_op jit(solution)/shard_map/grad/pallas_call | solution.py:126
  26.6 1.0 copy-done.10
  28.4 2.8 %collective-permute-start.7 = (bf16[512,1024]{1,0:T(8,128)(2,1)}, bf16[512,1024]{1,0:T(8,128)(2,1)S(1)}, u32[]{:S(2)}, u32[]{:S(2)}) collective-permute-start(bf16[512,1024]{1,0:T(8,128)(2,1)} %get-tuple-element.56), channel_id=1, source_target_pairs={{0,2},{1,7},{2,4},{3,1},{4,6},{5,3},{6,0},{7,5},{8,10},{9,15},{10,... | collective-permute-start | bytes 3145736 | tf_op jit(solution)/shard_map/ppermute | solution.py:38
  31.2 1.3 fusion.6
  33.4 3.7 %collective-permute-start.5 = (bf16[64,1024]{1,0:T(8,128)(2,1)S(1)}, bf16[64,1024]{1,0:T(8,128)(2,1)}, u32[]{:S(2)}, u32[]{:S(2)}) collective-permute-start(bf16[64,1024]{1,0:T(8,128)(2,1)S(1)} %fusion.9), channel_id=1, source_target_pairs={{0,16},{1,17},{2,18},{3,19},{4,20},{5,21},{6,22},{7,23},{8,24},{9,... | collective-permute-start | bytes 393224 | tf_op jit(solution)/shard_map/ppermute | solution.py:38
  37.1 3.3 %collective-permute-done.5 = bf16[64,1024]{1,0:T(8,128)(2,1)} collective-permute-done((bf16[64,1024]{1,0:T(8,128)(2,1)S(1)}, bf16[64,1024]{1,0:T(8,128)(2,1)}, u32[]{:S(2)}, u32[]{:S(2)}) %collective-permute-start.5) | collective-permute-done | bytes 131104 | tf_op jit(solution)/shard_map/ppermute | solution.py:38
  40.3 2.0 %fusion.10 = (bf16[64,1024]{1,0:T(8,128)(2,1)S(1)}, f32[64,1024]{1,0:T(8,128)}, f32[1,1,64,1024]{3,2,1,0:T(8,128)}) fusion(f32[1,1,64,1024]{3,2,1,0:T(8,128)S(1)} %copy-done.13, bf16[64,1024]{1,0:T(8,128)(2,1)} %collective-permute-done.5, f32[2,64,1024]{2,1,0:T(8,128)} %copy-done.11, s32[]{:T(128)S(6)} %select_n.48, f32[1,1,64,1024]{3,2,1,0:T(8,128)} %param.6), kind=kLoop, calls=%fused_computation.32 | loop fusion | flops 655360 | bytes 1572868 | tf_op jit(solution)/shard_map/convert_element_type | solution.py:409
  42.5 1.2 collective-permute-done.6
  44.3 1.0 maximum_select_fusion
  45.4 3.5 %collective-permute-start.8 = (bf16[2,64,1024]{2,1,0:T(8,128)(2,1)S(1)}, bf16[2,64,1024]{2,1,0:T(8,128)(2,1)}, u32[]{:S(2)}, u32[]{:S(2)}) collective-permute-start(bf16[2,64,1024]{2,1,0:T(8,128)(2,1)S(1)} %maximum_select_fusion), channel_id=1, source_target_pairs={{0,0},{1,5},{2,2},{3,7},{4,4},{5,1},{6,6},{7,3},{8,8},{9,13},{10,1... | collective-permute-start | bytes 786440 | tf_op jit(solution)/shard_map/ppermute | solution.py:38
  48.8 1.1 collective-permute-start.9
  49.9 4.3 %collective-permute-done.8 = bf16[2,64,1024]{2,1,0:T(8,128)(2,1)} collective-permute-done((bf16[2,64,1024]{2,1,0:T(8,128)(2,1)S(1)}, bf16[2,64,1024]{2,1,0:T(8,128)(2,1)}, u32[]{:S(2)}, u32[]{:S(2)}) %collective-permute-start.8) | collective-permute-done | bytes 262176 | tf_op jit(solution)/shard_map/ppermute | solution.py:38
  54.2 2.7 %collective-permute-done.9 = bf16[2,64,1024]{2,1,0:T(8,128)(2,1)} collective-permute-done((bf16[2,64,1024]{2,1,0:T(8,128)(2,1)S(1)}, bf16[2,64,1024]{2,1,0:T(8,128)(2,1)}, u32[]{:S(2)}, u32[]{:S(2)}) %collective-permute-start.9) | collective-permute-done | bytes 262176 | tf_op jit(solution)/shard_map/ppermute | solution.py:38
  56.9 1.1 pad_maximum_fusion
  58.0 2.6 %collective-permute-start.10 = (bf16[2,2,64,1024]{3,2,1,0:T(8,128)(2,1)S(1)}, bf16[2,2,64,1024]{3,2,1,0:T(8,128)(2,1)S(1)}, u32[]{:S(2)}, u32[]{:S(2)}) collective-permute-start(bf16[2,2,64,1024]{3,2,1,0:T(8,128)(2,1)S(1)} %pad_maximum_fusion), channel_id=1, source_target_pairs={{0,24},{1,97},{2,26},{3,99},{4,28},{5,101},{6,30},{7,103},{8,0},{9... | collective-permute-start | bytes 1572872 | tf_op jit(solution)/shard_map/ppermute | solution.py:38
  61.7 3.4 %copy-done.2 = bf16[512,8192]{1,0:T(8,128)(2,1)S(1)} copy-done((bf16[512,8192]{1,0:T(8,128)(2,1)S(1)}, bf16[512,8192]{1,0:T(8,128)(2,1)}, u32[]{:S(2)}) %copy-start.2) | copy-done | bytes 8388632
  65.1 5.7 %grad.4 = (bf16[512,1024]{1,0:T(8,128)(2,1)}, bf16[1,512,1024]{2,1,0:T(8,128)(2,1)S(1)}) custom-call(s32[4]{0:T(128)S(1)} %pad_add_fusion.1.blocks, bf16[512,8192]{1,0:T(8,128)(2,1)S(1)} %copy-done.2, bf16[512,4096]{1,0:T(8,128)(2,1)} %collective-permute-done.3.theirs, bf16[512,1024]{1,0:T(8,128)(2,1)S(1)} %copy-done.5, ...), custom_call_target="tpu_custom_call" | custom-call | flops 2147483648 | bytes 6291456 | tf_op jit(solution)/shard_map/grad/pallas_call | solution.py:126
  70.8 1.6 collective-permute-start.15
  72.9 3.2 %collective-permute-done.12 = bf16[2,2,64,1024]{3,2,1,0:T(8,128)(2,1)S(1)} collective-permute-done((bf16[2,2,64,1024]{3,2,1,0:T(8,128)(2,1)S(1)}, bf16[2,2,64,1024]{3,2,1,0:T(8,128)(2,1)S(1)}, u32[]{:S(2)}, u32[]{:S(2)}) %collective-permute-start.12) | collective-permute-done | bytes 524320 | tf_op jit(solution)/shard_map/ppermute | solution.py:38
  76.1 1.8 %collective-permute-start.18 = (bf16[2,4,2,64,1024]{4,3,2,1,0:T(8,128)(2,1)S(1)}, bf16[2,4,2,64,1024]{4,3,2,1,0:T(8,128)(2,1)}, u32[]{:S(2)}, u32[]{:S(2)}) collective-permute-start(bf16[2,4,2,64,1024]{4,3,2,1,0:T(8,128)(2,1)S(1)} %bitcast_dynamic-update-slice_fusion.3.refs_3_), channel_id=1, source_target_pairs={{0,1},{1,0},{2,3},{3,2},{4,5},{5,4},{6,7},{7,6},{8,9},{9,8},{10,11... | collective-permute-start | bytes 6291464 | tf_op jit(solution)/shard_map/ppermute | solution.py:38
  78.0 2.7 %collective-permute-start.14 = (bf16[2,4,2,64,1024]{4,3,2,1,0:T(8,128)(2,1)S(1)}, bf16[2,4,2,64,1024]{4,3,2,1,0:T(8,128)(2,1)}, u32[]{:S(2)}, u32[]{:S(2)}) collective-permute-start(bf16[2,4,2,64,1024]{4,3,2,1,0:T(8,128)(2,1)S(1)} %bitcast_dynamic-update-slice_fusion.3.refs_3_), channel_id=1, source_target_pairs={{0,96},{1,25},{2,98},{3,27},{4,100},{5,29},{6,102},{7,31},{8,104},... | collective-permute-start | bytes 6291464 | tf_op jit(solution)/shard_map/ppermute | solution.py:38
  80.7 3.1 %collective-permute-start.17 = (bf16[512,1024]{1,0:T(8,128)(2,1)}, bf16[512,1024]{1,0:T(8,128)(2,1)S(1)}, u32[]{:S(2)}, u32[]{:S(2)}) collective-permute-start(bf16[512,1024]{1,0:T(8,128)(2,1)} %bitcast.93), channel_id=1, source_target_pairs={{0,2},{1,7},{2,4},{3,1},{4,6},{5,3},{6,0},{7,5},{8,10},{9,15},{10,... | collective-permute-start | bytes 3145736 | tf_op jit(solution)/shard_map/ppermute | solution.py:38
  83.8 1.3 collective-permute-done.15.refs_0_
  85.0 3.4 %copy-done.3 = bf16[512,8192]{1,0:T(8,128)(2,1)S(1)} copy-done((bf16[512,8192]{1,0:T(8,128)(2,1)S(1)}, bf16[512,8192]{1,0:T(8,128)(2,1)}, u32[]{:S(2)}) %copy-start.3) | copy-done | bytes 8388632
  88.4 1.2 copy-done.7
  89.7 8.4 %grad.5 = (bf16[512,1024]{1,0:T(8,128)(2,1)S(1)}, bf16[3,512,1024]{2,1,0:T(8,128)(2,1)S(1)}) custom-call(s32[8]{0:T(128)S(1)} %stack.124.blocks, bf16[512,8192]{1,0:T(8,128)(2,1)S(1)} %copy-done.3, bf16[512,4096]{1,0:T(8,128)(2,1)} %collective-permute-done.3.theirs, bf16[512,1024]{1,0:T(8,128)(2,1)S(1)} %copy-done.5, bf16[512,1024]{1,0:T(8,128)(2,1)S(1)} %copy-done.7, ...), custom_call_target="tpu_custom_call" | custom-call | flops 4294967296 | bytes 10485760 | tf_op jit(solution)/shard_map/grad/pallas_call | solution.py:126
  98.0 2.9 %collective-permute-start.16 = (bf16[512,1024]{1,0:T(8,128)(2,1)S(1)}, bf16[512,1024]{1,0:T(8,128)(2,1)S(1)}, u32[]{:S(2)}, u32[]{:S(2)}) collective-permute-start(bf16[512,1024]{1,0:T(8,128)(2,1)S(1)} %get-tuple-element.65), channel_id=1, source_target_pairs={{0,2},{1,7},{2,4},{3,1},{4,6},{5,3},{6,0},{7,5},{8,10},{9,15},{10,... | collective-permute-start | bytes 3145736 | tf_op jit(solution)/shard_map/ppermute | solution.py:38
  101.0 4.9 %fold.3 = (bf16[512,8192]{1,0:T(8,128)(2,1)}, bf16[4,2,64,1024]{3,2,1,0:T(8,128)(2,1)}, f32[512,1024]{1,0:T(8,128)S(1)}) custom-call(s32[5]{0:T(128)S(1)} %stack.108.at.refs_0_, bf16[512,8192]{1,0:T(8,128)(2,1)S(1)} %copy-done.4, bf16[512,1024]{1,0:T(8,128)(2,1)S(1)} %copy-done.5, ...), custom_call_target="tpu_custom_call" | custom-call | bytes 1048576 | tf_op jit(solution)/shard_map/fold/pallas_call | solution.py:351
  105.9 6.8 %collective-permute-done.16 = bf16[512,1024]{1,0:T(8,128)(2,1)S(1)} collective-permute-done((bf16[512,1024]{1,0:T(8,128)(2,1)S(1)}, bf16[512,1024]{1,0:T(8,128)(2,1)S(1)}, u32[]{:S(2)}, u32[]{:S(2)}) %collective-permute-start.16) | collective-permute-done | bytes 1048608 | tf_op jit(solution)/shard_map/ppermute | solution.py:38
  112.7 4.9 %collective-permute-start.23 = (bf16[2,4,2,64,1024]{4,3,2,1,0:T(8,128)(2,1)}, bf16[2,4,2,64,1024]{4,3,2,1,0:T(8,128)(2,1)S(1)}, u32[]{:S(2)}, u32[]{:S(2)}) collective-permute-start(bf16[2,4,2,64,1024]{4,3,2,1,0:T(8,128)(2,1)} %collective-permute-done.13.refs_3_), channel_id=1, source_target_pairs={{0,1},{1,0},{2,3},{3,2},{4,5},{5,4},{6,7},{7,6},{8,9},{9,8},{10,11... | collective-permute-start | bytes 6291464 | tf_op jit(solution)/shard_map/ppermute | solution.py:38
  117.7 1.3 slice_bitcast_fusion.1
  119.0 1.3 slice_bitcast_fusion
  121.3 2.0 %collective-permute-start.19 = (bf16[4,2,64,1024]{3,2,1,0:T(8,128)(2,1)S(1)}, bf16[4,2,64,1024]{3,2,1,0:T(8,128)(2,1)S(1)}, u32[]{:S(2)}, u32[]{:S(2)}) collective-permute-start(bf16[4,2,64,1024]{3,2,1,0:T(8,128)(2,1)S(1)} %slice_bitcast_fusion.1), channel_id=1, source_target_pairs={{0,32},{1,9},{2,34},{3,11},{4,36},{5,13},{6,38},{7,15},{8,40},{9,1... | collective-permute-start | bytes 3145736 | tf_op jit(solution)/shard_map/ppermute | solution.py:38
  124.5 0.8 collective-permute-start.22
  125.3 14.5 %fold.4 = (bf16[512,8192]{1,0:T(8,128)(2,1)}, bf16[4,2,64,1024]{3,2,1,0:T(8,128)(2,1)}, f32[512,1024]{1,0:T(8,128)S(1)}) custom-call(s32[5]{0:T(128)S(1)} %stack.108.at.refs_0_, bf16[512,8192]{1,0:T(8,128)(2,1)S(1)} %copy-done.4, bf16[512,1024]{1,0:T(8,128)(2,1)S(1)} %copy-done.5, ...), custom_call_target="tpu_custom_call", output_to_operand_aliasing={{0}: (8, {}), {1}: (9, {})} | custom-call | bytes 1048576 | tf_op jit(solution)/shard_map/fold/pallas_call | solution.py:351
  139.8 5.6 %collective-permute-done.22 = bf16[192,1024]{1,0:T(8,128)(2,1)S(1)} collective-permute-done((bf16[192,1024]{1,0:T(8,128)(2,1)S(1)}, bf16[192,1024]{1,0:T(8,128)(2,1)S(1)}, u32[]{:S(2)}, u32[]{:S(2)}) %collective-permute-start.22) | collective-permute-done | bytes 393248 | tf_op jit(solution)/shard_map/ppermute | solution.py:38
  146.7 1.4 collective-permute-done.25.refs_7_
  148.1 1.5 collective-permute-done.26.refs_8_
  149.6 12.2 %fold.5 = (bf16[512,8192]{1,0:T(8,128)(2,1)}, bf16[4,2,64,1024]{3,2,1,0:T(8,128)(2,1)}, bf16[512,1024]{1,0:T(8,128)(2,1)}) custom-call(s32[5]{0:T(128)S(1)} %stack.108.at.refs_0_, bf16[512,8192]{1,0:T(8,128)(2,1)S(1)} %copy-done.4, bf16[512,1024]{1,0:T(8,128)(2,1)S(1)} %copy-done.5, ...), custom_call_target="tpu_custom_call", output_to_operand_aliasing={{0}: (10, {}), {1}: (11, {})} | custom-call | bytes 1048576 | tf_op jit(solution)/shard_map/fold/pallas_call | solution.py:351
  161.9 1.9 %fusion.1 = f32[1,512,1024]{2,1,0:T(8,128)} fusion(bf16[512,1024]{1,0:T(8,128)(2,1)S(1)} %collective-permute-done.27, bf16[320,1024]{1,0:T(8,128)(2,1)S(1)} %collective-permute-done.28, bf16[192,1024]{1,0:T(8,128)(2,1)S(1)} %collective-permute-done.22, bf16[3,512,1024]{2,1,0:T(8,128)(2,1)S(1)} %get-tuple-element.74), kind=kLoop, calls=%fused_computation.2 | loop fusion | flops 4194304 | bytes 5242880 | tf_op jit(solution)/shard_map/broadcast_in_dim | solution.py:494
  (76 shorter events, 8.8 us)
Async XLA Ops:
  0.7 3.4 %copy-start = (bf16[512,8192]{1,0:T(8,128)(2,1)S(1)}, bf16[512,8192]{1,0:T(8,128)(2,1)}, u32[]{:S(2)}) copy-start(bf16[512,8192]{1,0:T(8,128)(2,1)} %refs_1_.5) | copy-start | bytes 25165828
  4.1 4.9 %copy-start.5 = (bf16[512,1024]{1,0:T(8,128)(2,1)S(1)}, bf16[512,1024]{1,0:T(8,128)(2,1)}, u32[]{:S(2)}) copy-start(bf16[512,1024]{1,0:T(8,128)(2,1)} %refs_2_.5) | copy-start | bytes 3145732
  4.1 5.0 %copy-start.12 = (bf16[1,512,1024]{2,1,0:T(8,128)(2,1)S(1)}, bf16[1,512,1024]{2,1,0:T(8,128)(2,1)}, u32[]{:S(2)}) copy-start(bf16[1,512,1024]{2,1,0:T(8,128)(2,1)} %param.5) | copy-start | bytes 3145732
  7.5 10.1 %collective-permute-start.3 = (bf16[512,4096]{1,0:T(8,128)(2,1)}, bf16[512,4096]{1,0:T(8,128)(2,1)}, u32[]{:S(2)}, u32[]{:S(2)}) collective-permute-start(bf16[512,4096]{1,0:T(8,128)(2,1)} %half.1), channel_id=1, source_target_pairs={{0,1},{1,0},{2,3},{3,2},{4,5},{5,4},{6,7},{7,6},{8,9},{9,8},{10,11... | collective-permute-start | bytes 12582920 | tf_op jit(solution)/shard_map/ppermute | solution.py:38
  9.0 8.2 %collective-permute-start.4 = (bf16[512,1024]{1,0:T(8,128)(2,1)S(1)}, bf16[512,1024]{1,0:T(8,128)(2,1)S(1)}, u32[]{:S(2)}, u32[]{:S(2)}) collective-permute-start(bf16[512,1024]{1,0:T(8,128)(2,1)S(1)} %copy-done.5), channel_id=1, source_target_pairs={{0,1},{1,0},{2,3},{3,2},{4,5},{5,4},{6,7},{7,6},{8,9},{9,8},{10,11... | collective-permute-start | bytes 3145736 | tf_op jit(solution)/shard_map/ppermute | solution.py:38
  9.9 17.6 %collective-permute-start = (bf16[2,64,1024]{2,1,0:T(8,128)(2,1)}, bf16[2,64,1024]{2,1,0:T(8,128)(2,1)S(1)}, u32[]{:S(2)}, u32[]{:S(2)}) collective-permute-start(bf16[2,64,1024]{2,1,0:T(8,128)(2,1)} %get-tuple-element.100), channel_id=1, source_target_pairs={{0,64},{1,65},{2,66},{3,67},{4,68},{5,69},{6,70},{7,71},{8,72},{9,... | collective-permute-start | bytes 786440 | tf_op jit(solution)/shard_map/ppermute | solution.py:38
  12.8 14.8 %collective-permute-start.1 = (bf16[2,64,1024]{2,1,0:T(8,128)(2,1)}, bf16[2,64,1024]{2,1,0:T(8,128)(2,1)S(1)}, u32[]{:S(2)}, u32[]{:S(2)}) collective-permute-start(bf16[2,64,1024]{2,1,0:T(8,128)(2,1)} %get-tuple-element.99), channel_id=1, source_target_pairs={{0,32},{1,33},{2,34},{3,35},{4,36},{5,37},{6,38},{7,39},{8,40},{9,... | collective-permute-start | bytes 786440 | tf_op jit(solution)/shard_map/ppermute | solution.py:38
  13.1 14.5 %collective-permute-start.2 = (bf16[2,64,1024]{2,1,0:T(8,128)(2,1)S(1)}, bf16[2,64,1024]{2,1,0:T(8,128)(2,1)S(1)}, u32[]{:S(2)}, u32[]{:S(2)}) collective-permute-start(bf16[2,64,1024]{2,1,0:T(8,128)(2,1)S(1)} %get-tuple-element.98), channel_id=1, source_target_pairs={{0,96},{1,97},{2,98},{3,99},{4,100},{5,101},{6,102},{7,103},{8,104... | collective-permute-start | bytes 786440 | tf_op jit(solution)/shard_map/ppermute | solution.py:38
  17.1 44.6 %copy-start.6 = (bf16[512,1024]{1,0:T(8,128)(2,1)}, bf16[512,1024]{1,0:T(8,128)(2,1)S(1)}, u32[]{:S(2)}) copy-start(bf16[512,1024]{1,0:T(8,128)(2,1)S(1)} %collective-permute-done.4.cot_theirs) | copy-start | bytes 3145732
  17.6 3.4 %copy-start.1 = (bf16[512,8192]{1,0:T(8,128)(2,1)S(1)}, bf16[512,8192]{1,0:T(8,128)(2,1)}, u32[]{:S(2)}) copy-start(bf16[512,8192]{1,0:T(8,128)(2,1)} %refs_1_.5) | copy-start | bytes 25165828
  21.0 19.3 %copy-start.13 = (f32[1,1,64,1024]{3,2,1,0:T(8,128)S(1)}, f32[1,1,64,1024]{3,2,1,0:T(8,128)}, u32[]{:S(2)}) copy-start(f32[1,1,64,1024]{3,2,1,0:T(8,128)} %param.7) | copy-start | bytes 786436
  26.6 1.0 copy-start.10
  27.5 0.7 copy-start.14
  27.6 0.8 copy-start.15
  27.6 0.8 copy-start.16
  28.4 15.3 %collective-permute-start.7 = (bf16[512,1024]{1,0:T(8,128)(2,1)}, bf16[512,1024]{1,0:T(8,128)(2,1)S(1)}, u32[]{:S(2)}, u32[]{:S(2)}) collective-permute-start(bf16[512,1024]{1,0:T(8,128)(2,1)} %get-tuple-element.56), channel_id=1, source_target_pairs={{0,2},{1,7},{2,4},{3,1},{4,6},{5,3},{6,0},{7,5},{8,10},{9,15},{10,... | collective-permute-start | bytes 3145736 | tf_op jit(solution)/shard_map/ppermute | solution.py:38
  32.6 0.8 copy-start.11
  33.4 6.9 %collective-permute-start.5 = (bf16[64,1024]{1,0:T(8,128)(2,1)S(1)}, bf16[64,1024]{1,0:T(8,128)(2,1)}, u32[]{:S(2)}, u32[]{:S(2)}) collective-permute-start(bf16[64,1024]{1,0:T(8,128)(2,1)S(1)} %fusion.9), channel_id=1, source_target_pairs={{0,16},{1,17},{2,18},{3,19},{4,20},{5,21},{6,22},{7,23},{8,24},{9,... | collective-permute-start | bytes 393224 | tf_op jit(solution)/shard_map/ppermute | solution.py:38
  42.3 1.3 collective-permute-start.6
  43.7 0.7 copy-start.17
  45.4 8.8 %collective-permute-start.8 = (bf16[2,64,1024]{2,1,0:T(8,128)(2,1)S(1)}, bf16[2,64,1024]{2,1,0:T(8,128)(2,1)}, u32[]{:S(2)}, u32[]{:S(2)}) collective-permute-start(bf16[2,64,1024]{2,1,0:T(8,128)(2,1)S(1)} %maximum_select_fusion), channel_id=1, source_target_pairs={{0,0},{1,5},{2,2},{3,7},{4,4},{5,1},{6,6},{7,3},{8,8},{9,13},{10,1... | collective-permute-start | bytes 786440 | tf_op jit(solution)/shard_map/ppermute | solution.py:38
  48.8 8.1 %collective-permute-start.9 = (bf16[2,64,1024]{2,1,0:T(8,128)(2,1)S(1)}, bf16[2,64,1024]{2,1,0:T(8,128)(2,1)}, u32[]{:S(2)}, u32[]{:S(2)}) collective-permute-start(bf16[2,64,1024]{2,1,0:T(8,128)(2,1)S(1)} %maximum_select_fusion), channel_id=1, source_target_pairs={{0,6},{1,3},{2,0},{3,5},{4,2},{5,7},{6,4},{7,1},{8,14},{9,11},{10,... | collective-permute-start | bytes 786440 | tf_op jit(solution)/shard_map/ppermute | solution.py:38
  58.0 14.8 %collective-permute-start.10 = (bf16[2,2,64,1024]{3,2,1,0:T(8,128)(2,1)S(1)}, bf16[2,2,64,1024]{3,2,1,0:T(8,128)(2,1)S(1)}, u32[]{:S(2)}, u32[]{:S(2)}) collective-permute-start(bf16[2,2,64,1024]{3,2,1,0:T(8,128)(2,1)S(1)} %pad_maximum_fusion), channel_id=1, source_target_pairs={{0,24},{1,97},{2,26},{3,99},{4,28},{5,101},{6,30},{7,103},{8,0},{9... | collective-permute-start | bytes 1572872 | tf_op jit(solution)/shard_map/ppermute | solution.py:38
  60.6 12.2 %collective-permute-start.11 = (bf16[2,2,64,1024]{3,2,1,0:T(8,128)(2,1)S(1)}, bf16[2,2,64,1024]{3,2,1,0:T(8,128)(2,1)S(1)}, u32[]{:S(2)}, u32[]{:S(2)}) collective-permute-start(bf16[2,2,64,1024]{3,2,1,0:T(8,128)(2,1)S(1)} %pad_maximum_fusion), channel_id=1, source_target_pairs={{0,16},{1,65},{2,18},{3,67},{4,20},{5,69},{6,22},{7,71},{8,24},{9,... | collective-permute-start | bytes 1572872 | tf_op jit(solution)/shard_map/ppermute | solution.py:38
  61.1 14.9 %collective-permute-start.12 = (bf16[2,2,64,1024]{3,2,1,0:T(8,128)(2,1)S(1)}, bf16[2,2,64,1024]{3,2,1,0:T(8,128)(2,1)S(1)}, u32[]{:S(2)}, u32[]{:S(2)}) collective-permute-start(bf16[2,2,64,1024]{3,2,1,0:T(8,128)(2,1)S(1)} %pad_maximum_fusion), channel_id=1, source_target_pairs={{0,8},{1,33},{2,10},{3,35},{4,12},{5,37},{6,14},{7,39},{8,16},{9,4... | collective-permute-start | bytes 1572872 | tf_op jit(solution)/shard_map/ppermute | solution.py:38
  61.7 3.4 %copy-start.2 = (bf16[512,8192]{1,0:T(8,128)(2,1)S(1)}, bf16[512,8192]{1,0:T(8,128)(2,1)}, u32[]{:S(2)}) copy-start(bf16[512,8192]{1,0:T(8,128)(2,1)} %refs_1_.5) | copy-start | bytes 25165828
  70.8 2.0 %copy-start.8 = (bf16[1,512,1024]{2,1,0:T(8,128)(2,1)}, bf16[1,512,1024]{2,1,0:T(8,128)(2,1)S(1)}, u32[]{:S(2)}) copy-start(bf16[1,512,1024]{2,1,0:T(8,128)(2,1)S(1)} %get-tuple-element.72) | copy-start | bytes 3145732
  70.8 14.3 %collective-permute-start.15 = (bf16[512,1024]{1,0:T(8,128)(2,1)}, bf16[512,1024]{1,0:T(8,128)(2,1)}, u32[]{:S(2)}, u32[]{:S(2)}) collective-permute-start(bf16[512,1024]{1,0:T(8,128)(2,1)} %get-tuple-element.64), channel_id=1, source_target_pairs={{0,2},{1,7},{2,4},{3,1},{4,6},{5,3},{6,0},{7,5},{8,10},{9,15},{10,... | collective-permute-start | bytes 3145736 | tf_op jit(solution)/shard_map/ppermute | solution.py:38
  76.1 24.8 %collective-permute-start.18 = (bf16[2,4,2,64,1024]{4,3,2,1,0:T(8,128)(2,1)S(1)}, bf16[2,4,2,64,1024]{4,3,2,1,0:T(8,128)(2,1)}, u32[]{:S(2)}, u32[]{:S(2)}) collective-permute-start(bf16[2,4,2,64,1024]{4,3,2,1,0:T(8,128)(2,1)S(1)} %bitcast_dynamic-update-slice_fusion.3.refs_3_), channel_id=1, source_target_pairs={{0,1},{1,0},{2,3},{3,2},{4,5},{5,4},{6,7},{7,6},{8,9},{9,8},{10,11... | collective-permute-start | bytes 6291464 | tf_op jit(solution)/shard_map/ppermute | solution.py:38
  78.0 34.7 %collective-permute-start.13 = (bf16[2,4,2,64,1024]{4,3,2,1,0:T(8,128)(2,1)S(1)}, bf16[2,4,2,64,1024]{4,3,2,1,0:T(8,128)(2,1)}, u32[]{:S(2)}, u32[]{:S(2)}) collective-permute-start(bf16[2,4,2,64,1024]{4,3,2,1,0:T(8,128)(2,1)S(1)} %bitcast_dynamic-update-slice_fusion.3.refs_3_), channel_id=1, source_target_pairs={{0,32},{1,9},{2,34},{3,11},{4,36},{5,13},{6,38},{7,15},{8,40},{9,1... | collective-permute-start | bytes 6291464 | tf_op jit(solution)/shard_map/ppermute | solution.py:38
  78.0 34.7 %collective-permute-start.14 = (bf16[2,4,2,64,1024]{4,3,2,1,0:T(8,128)(2,1)S(1)}, bf16[2,4,2,64,1024]{4,3,2,1,0:T(8,128)(2,1)}, u32[]{:S(2)}, u32[]{:S(2)}) collective-permute-start(bf16[2,4,2,64,1024]{4,3,2,1,0:T(8,128)(2,1)S(1)} %bitcast_dynamic-update-slice_fusion.3.refs_3_), channel_id=1, source_target_pairs={{0,96},{1,25},{2,98},{3,27},{4,100},{5,29},{6,102},{7,31},{8,104},... | collective-permute-start | bytes 6291464 | tf_op jit(solution)/shard_map/ppermute | solution.py:38
  80.7 25.2 %collective-permute-start.17 = (bf16[512,1024]{1,0:T(8,128)(2,1)}, bf16[512,1024]{1,0:T(8,128)(2,1)S(1)}, u32[]{:S(2)}, u32[]{:S(2)}) collective-permute-start(bf16[512,1024]{1,0:T(8,128)(2,1)} %bitcast.93), channel_id=1, source_target_pairs={{0,2},{1,7},{2,4},{3,1},{4,6},{5,3},{6,0},{7,5},{8,10},{9,15},{10,... | collective-permute-start | bytes 3145736 | tf_op jit(solution)/shard_map/ppermute | solution.py:38
  85.0 3.4 %copy-start.3 = (bf16[512,8192]{1,0:T(8,128)(2,1)S(1)}, bf16[512,8192]{1,0:T(8,128)(2,1)}, u32[]{:S(2)}) copy-start(bf16[512,8192]{1,0:T(8,128)(2,1)} %refs_1_.5) | copy-start | bytes 25165828
  88.4 1.2 copy-start.7
  89.7 11.3 %copy-start.4 = (bf16[512,8192]{1,0:T(8,128)(2,1)S(1)}, bf16[512,8192]{1,0:T(8,128)(2,1)}, u32[]{:S(2)}) copy-start(bf16[512,8192]{1,0:T(8,128)(2,1)} %refs_1_.5) | copy-start | bytes 25165828
  98.0 14.6 %collective-permute-start.16 = (bf16[512,1024]{1,0:T(8,128)(2,1)S(1)}, bf16[512,1024]{1,0:T(8,128)(2,1)S(1)}, u32[]{:S(2)}, u32[]{:S(2)}) collective-permute-start(bf16[512,1024]{1,0:T(8,128)(2,1)S(1)} %get-tuple-element.65), channel_id=1, source_target_pairs={{0,2},{1,7},{2,4},{3,1},{4,6},{5,3},{6,0},{7,5},{8,10},{9,15},{10,... | collective-permute-start | bytes 3145736 | tf_op jit(solution)/shard_map/ppermute | solution.py:38
  112.7 7.6 %copy-start.9 = (bf16[1,512,1024]{2,1,0:T(8,128)(2,1)S(1)}, bf16[1,512,1024]{2,1,0:T(8,128)(2,1)}, u32[]{:S(2)}) copy-start(bf16[1,512,1024]{2,1,0:T(8,128)(2,1)} %copy-done.8) | copy-start | bytes 3145732
  112.7 11.8 %collective-permute-start.23 = (bf16[2,4,2,64,1024]{4,3,2,1,0:T(8,128)(2,1)}, bf16[2,4,2,64,1024]{4,3,2,1,0:T(8,128)(2,1)S(1)}, u32[]{:S(2)}, u32[]{:S(2)}) collective-permute-start(bf16[2,4,2,64,1024]{4,3,2,1,0:T(8,128)(2,1)} %collective-permute-done.13.refs_3_), channel_id=1, source_target_pairs={{0,1},{1,0},{2,3},{3,2},{4,5},{5,4},{6,7},{7,6},{8,9},{9,8},{10,11... | collective-permute-start | bytes 6291464 | tf_op jit(solution)/shard_map/ppermute | solution.py:38
  117.6 7.7 %collective-permute-start.24 = (bf16[2,4,2,64,1024]{4,3,2,1,0:T(8,128)(2,1)}, bf16[2,4,2,64,1024]{4,3,2,1,0:T(8,128)(2,1)S(1)}, u32[]{:S(2)}, u32[]{:S(2)}) collective-permute-start(bf16[2,4,2,64,1024]{4,3,2,1,0:T(8,128)(2,1)} %collective-permute-done.14.refs_4_), channel_id=1, source_target_pairs={{0,1},{1,0},{2,3},{3,2},{4,5},{5,4},{6,7},{7,6},{8,9},{9,8},{10,11... | collective-permute-start | bytes 6291464 | tf_op jit(solution)/shard_map/ppermute | solution.py:38
  120.7 24.6 %collective-permute-start.21 = (bf16[512,1024]{1,0:T(8,128)(2,1)S(1)}, bf16[512,1024]{1,0:T(8,128)(2,1)S(1)}, u32[]{:S(2)}, u32[]{:S(2)}) collective-permute-start(bf16[512,1024]{1,0:T(8,128)(2,1)S(1)} %fusion.4), channel_id=1, source_target_pairs={{0,2},{1,7},{2,4},{3,1},{4,6},{5,3},{6,0},{7,5},{8,10},{9,15},{10,... | collective-permute-start | bytes 3145736 | tf_op jit(solution)/shard_map/ppermute | solution.py:38
  121.3 24.0 %collective-permute-start.19 = (bf16[4,2,64,1024]{3,2,1,0:T(8,128)(2,1)S(1)}, bf16[4,2,64,1024]{3,2,1,0:T(8,128)(2,1)S(1)}, u32[]{:S(2)}, u32[]{:S(2)}) collective-permute-start(bf16[4,2,64,1024]{3,2,1,0:T(8,128)(2,1)S(1)} %slice_bitcast_fusion.1), channel_id=1, source_target_pairs={{0,32},{1,9},{2,34},{3,11},{4,36},{5,13},{6,38},{7,15},{8,40},{9,1... | collective-permute-start | bytes 3145736 | tf_op jit(solution)/shard_map/ppermute | solution.py:38
  123.3 22.1 %collective-permute-start.20 = (bf16[4,2,64,1024]{3,2,1,0:T(8,128)(2,1)S(1)}, bf16[4,2,64,1024]{3,2,1,0:T(8,128)(2,1)S(1)}, u32[]{:S(2)}, u32[]{:S(2)}) collective-permute-start(bf16[4,2,64,1024]{3,2,1,0:T(8,128)(2,1)S(1)} %slice_bitcast_fusion), channel_id=1, source_target_pairs={{0,96},{1,25},{2,98},{3,27},{4,100},{5,29},{6,102},{7,31},{8,104},... | collective-permute-start | bytes 3145736 | tf_op jit(solution)/shard_map/ppermute | solution.py:38
  124.5 20.9 %collective-permute-start.22 = (bf16[192,1024]{1,0:T(8,128)(2,1)S(1)}, bf16[192,1024]{1,0:T(8,128)(2,1)S(1)}, u32[]{:S(2)}, u32[]{:S(2)}) collective-permute-start(bf16[192,1024]{1,0:T(8,128)(2,1)S(1)} %slice.28), channel_id=1, source_target_pairs={{0,8},{1,9},{2,10},{3,11},{4,12},{5,13},{6,14},{7,15},{8,0},{9,1},... | collective-permute-start | bytes 1179656 | tf_op jit(solution)/shard_map/ppermute | solution.py:38
  145.4 2.7 %collective-permute-start.25 = (bf16[4,2,64,1024]{3,2,1,0:T(8,128)(2,1)S(1)}, bf16[4,2,64,1024]{3,2,1,0:T(8,128)(2,1)S(1)}, u32[]{:S(2)}, u32[]{:S(2)}) collective-permute-start(bf16[4,2,64,1024]{3,2,1,0:T(8,128)(2,1)S(1)} %collective-permute-done.19.refs_4_), channel_id=1, source_target_pairs={{0,1},{1,0},{2,3},{3,2},{4,5},{5,4},{6,7},{7,6},{8,9},{9,8},{10,11... | collective-permute-start | bytes 3145736 | tf_op jit(solution)/shard_map/ppermute | solution.py:38
  145.5 4.1 %collective-permute-start.26 = (bf16[4,2,64,1024]{3,2,1,0:T(8,128)(2,1)S(1)}, bf16[4,2,64,1024]{3,2,1,0:T(8,128)(2,1)S(1)}, u32[]{:S(2)}, u32[]{:S(2)}) collective-permute-start(bf16[4,2,64,1024]{3,2,1,0:T(8,128)(2,1)S(1)} %collective-permute-done.20.refs_5_), channel_id=1, source_target_pairs={{0,1},{1,0},{2,3},{3,2},{4,5},{5,4},{6,7},{7,6},{8,9},{9,8},{10,11... | collective-permute-start | bytes 3145736 | tf_op jit(solution)/shard_map/ppermute | solution.py:38
  146.4 15.5 %collective-permute-start.27 = (bf16[512,1024]{1,0:T(8,128)(2,1)S(1)}, bf16[512,1024]{1,0:T(8,128)(2,1)S(1)}, u32[]{:S(2)}, u32[]{:S(2)}) collective-permute-start(bf16[512,1024]{1,0:T(8,128)(2,1)S(1)} %fusion.2), channel_id=1, source_target_pairs={{0,2},{1,7},{2,4},{3,1},{4,6},{5,3},{6,0},{7,5},{8,10},{9,15},{10,... | collective-permute-start | bytes 3145736 | tf_op jit(solution)/shard_map/ppermute | solution.py:38
  146.6 15.3 %collective-permute-start.28 = (bf16[320,1024]{1,0:T(8,128)(2,1)S(1)}, bf16[320,1024]{1,0:T(8,128)(2,1)S(1)}, u32[]{:S(2)}, u32[]{:S(2)}) collective-permute-start(bf16[320,1024]{1,0:T(8,128)(2,1)S(1)} %slice.29), channel_id=1, source_target_pairs={{0,8},{1,9},{2,10},{3,11},{4,12},{5,13},{6,14},{7,15},{8,0},{9,1},... | collective-permute-start | bytes 1966088 | tf_op jit(solution)/shard_map/ppermute | solution.py:38

commit v5 on v4

--- a/solution.py
+++ b/solution.py
@@ -17,7 +17,8 @@
 D = 8192
 COLS = 1024
 SCALE = D ** (-0.5)
-VMEM = 24 * 1024 * 1024
+VMEM = 48 * 1024 * 1024
+FOLD_VMEM = 40 * 1024 * 1024
 ANY = pl.BlockSpec(memory_space=pl.ANY)
 BF = jnp.bfloat16
 F32 = jnp.float32
@@ -46,8 +47,8 @@
     return permute(value, lambda x, z, y, c: (x, z, y + 1 - 2 * c, c))
 
 
-def params(**more):
-    return pltpu.CompilerParams(vmem_limit_bytes=VMEM, **more)
+def params(limit=VMEM):
+    return pltpu.CompilerParams(vmem_limit_bytes=limit)
 
 
 def half_kernel(at, tokens, out, held, in_sem, out_sem):
@@ -355,7 +356,7 @@
         out_specs=[ANY, ANY, in_vmem],
         scratch_shapes=scratch,
         input_output_aliases=aliases,
-        compiler_params=params(),
+        compiler_params=params(FOLD_VMEM),
         cost_estimate=pl.CostEstimate(
             flops=0, bytes_accessed=1 << 20,
             transcendentals=0,

time: 165 us -> 157 us (0.952)
  local copies, waits for them, and re-layouts: 22.2 us -> 10.5 us
  waiting for transfers between devices: 33.3 us -> 40.2 us
  starting transfers between devices: 44 us -> 39.6 us
    unnamed x36 -> x26, local copies, waits for them, and re-layouts: 18 us -> 4.44 us
    ppermute x29, waiting for transfers between devices: 33.3 us -> 40.2 us  [permute(): return lax.ppermute(value, AXES, pairs)]
    ppermute x29, starting transfers between devices: 44 us -> 39.6 us  [permute(): return lax.ppermute(value, AXES, pairs)]
  transfers between devices with their start and end apart: 29 -> 29, of which waited for: 12 -> 14; matrix products, arithmetic and copies ran while one was open for 5% -> 7% of each run, Pallas kernels for 31% -> 33%
where the time goes in v5:
time: 157 us; the launch traced here: 155 us
  Pallas kernels  55.4 us (35%)
  waiting for transfers between devices  40.2 us (26%)
  starting transfers between devices  39.6 us (25%)
  local copies, waits for them, and re-layouts  10.5 us (7%)
  other arithmetic  8.75 us (6%)
    ppermute x29, waiting for transfers between devices, permute(): return lax.ppermute(value, AXES, pairs)  40.2 us
    ppermute x29, starting transfers between devices, permute(): return lax.ppermute(value, AXES, pairs)  39.6 us
    pallas_call x3, Pallas kernels, fold(): pl.pallas_call(kernel, out_shape=shapes, in_specs=in_specs, out_specs=[AN...  30.4 us
    pallas_call x3, Pallas kernels, grad_blocks(): pl.pallas_call(functools.partial(grad_kernel, len(arrived)), out_shape=[j...  20.7 us
    unnamed x26, local copies, waits for them, and re-layouts  4.44 us
    pallas_call x1, Pallas kernels, other_half(): pl.pallas_call(half_kernel, out_shape=jax.ShapeDtypeStruct((TOK, D // 2),...  4.33 us
  transfers between devices with their start and end apart: 29, of which 14 were waited for; matrix products, arithmetic and copies ran while one was open for 7% of the time, Pallas kernels for 33%

profile of v5, /device:TPU:1, one launch (start us, length us, event | category | flops | bytes accessed | tf_op | source)
XLA Modules:
  0.0 155.4 jit_solution(9473590890225867506)
XLA Ops:
  0.7 4.3 %half.1 = bf16[512,4096]{1,0:T(8,128)(2,1)} custom-call(s32[5]{0:T(128)S(1)} %stack.108.at.refs_0_, bf16[512,8192]{1,0:T(8,128)(2,1)} %refs_1_.5), custom_call_target="tpu_custom_call" | custom-call | bytes 8388608 | tf_op jit(solution)/shard_map/half/pallas_call | solution.py:82
  5.1 1.5 collective-permute-start.3
  6.7 0.9 dynamic-slice_bitcast_fusion
  7.5 2.8 %collective-permute-start = (bf16[2,64,1024]{2,1,0:T(8,128)(2,1)}, bf16[2,64,1024]{2,1,0:T(8,128)(2,1)S(1)}, u32[]{:S(2)}, u32[]{:S(2)}) collective-permute-start(bf16[2,64,1024]{2,1,0:T(8,128)(2,1)} %get-tuple-element.100), channel_id=1, source_target_pairs={{0,64},{1,65},{2,66},{3,67},{4,68},{5,69},{6,70},{7,71},{8,72},{9,... | collective-permute-start | bytes 786440 | tf_op jit(solution)/shard_map/ppermute | solution.py:39
  10.7 2.4 %collective-permute-start.2 = (bf16[2,64,1024]{2,1,0:T(8,128)(2,1)S(1)}, bf16[2,64,1024]{2,1,0:T(8,128)(2,1)S(1)}, u32[]{:S(2)}, u32[]{:S(2)}) collective-permute-start(bf16[2,64,1024]{2,1,0:T(8,128)(2,1)S(1)} %get-tuple-element.98), channel_id=1, source_target_pairs={{0,96},{1,97},{2,98},{3,99},{4,100},{5,101},{6,102},{7,103},{8,104... | collective-permute-start | bytes 786440 | tf_op jit(solution)/shard_map/ppermute | solution.py:39
  13.1 1.6 %collective-permute-done.4.cot_theirs = bf16[512,1024]{1,0:T(8,128)(2,1)S(1)} collective-permute-done((bf16[512,1024]{1,0:T(8,128)(2,1)S(1)}, bf16[512,1024]{1,0:T(8,128)(2,1)S(1)}, u32[]{:S(2)}, u32[]{:S(2)}) %collective-permute-start.4) | collective-permute-done | bytes 1048608 | tf_op jit(solution)/shard_map/ppermute | solution.py:39
  15.2 5.7 %grad.3 = (bf16[512,1024]{1,0:T(8,128)(2,1)}, bf16[1,512,1024]{2,1,0:T(8,128)(2,1)S(1)}) custom-call(s32[4]{0:T(128)S(1)} %pad_add_fusion.blocks, bf16[512,8192]{1,0:T(8,128)(2,1)} %refs_1_.5, bf16[512,4096]{1,0:T(8,128)(2,1)} %collective-permute-done.3.theirs, bf16[512,1024]{1,0:T(8,128)(2,1)S(1)} %copy-done, ...), custom_call_target="tpu_custom_call" | custom-call | flops 2147483648 | bytes 6291456 | tf_op jit(solution)/shard_map/grad/pallas_call | solution.py:127
  20.9 1.0 copy-done.5
  21.9 1.2 collective-permute-done.1
  23.1 0.7 copy-done.10
  23.9 2.8 %collective-permute-start.7 = (bf16[512,1024]{1,0:T(8,128)(2,1)}, bf16[512,1024]{1,0:T(8,128)(2,1)S(1)}, u32[]{:S(2)}, u32[]{:S(2)}) collective-permute-start(bf16[512,1024]{1,0:T(8,128)(2,1)} %get-tuple-element.56), channel_id=1, source_target_pairs={{0,2},{1,7},{2,4},{3,1},{4,6},{5,3},{6,0},{7,5},{8,10},{9,15},{10,... | collective-permute-start | bytes 3145736 | tf_op jit(solution)/shard_map/ppermute | solution.py:39
  26.7 1.3 fusion.6
  28.1 0.8 copy-done.7
  28.9 3.7 %collective-permute-start.5 = (bf16[64,1024]{1,0:T(8,128)(2,1)S(1)}, bf16[64,1024]{1,0:T(8,128)(2,1)S(1)}, u32[]{:S(2)}, u32[]{:S(2)}) collective-permute-start(bf16[64,1024]{1,0:T(8,128)(2,1)S(1)} %fusion.9), channel_id=1, source_target_pairs={{0,16},{1,17},{2,18},{3,19},{4,20},{5,21},{6,22},{7,23},{8,24},{9,... | collective-permute-start | bytes 393224 | tf_op jit(solution)/shard_map/ppermute | solution.py:39
  32.5 3.3 %collective-permute-done.5 = bf16[64,1024]{1,0:T(8,128)(2,1)S(1)} collective-permute-done((bf16[64,1024]{1,0:T(8,128)(2,1)S(1)}, bf16[64,1024]{1,0:T(8,128)(2,1)S(1)}, u32[]{:S(2)}, u32[]{:S(2)}) %collective-permute-start.5) | collective-permute-done | bytes 131104 | tf_op jit(solution)/shard_map/ppermute | solution.py:39
  35.9 2.0 %fusion.10 = (bf16[64,1024]{1,0:T(8,128)(2,1)S(1)}, f32[64,1024]{1,0:T(8,128)}, f32[1,1,64,1024]{3,2,1,0:T(8,128)}) fusion(f32[1,1,64,1024]{3,2,1,0:T(8,128)} %param.7, bf16[64,1024]{1,0:T(8,128)(2,1)S(1)} %collective-permute-done.5, f32[2,64,1024]{2,1,0:T(8,128)} %copy-done.7, s32[]{:T(128)S(6)} %select_n.48, f32[1,1,64,1024]{3,2,1,0:T(8,128)} %param.6), kind=kLoop, calls=%fused_computation.32 | loop fusion | flops 655360 | bytes 1572868 | tf_op jit(solution)/shard_map/convert_element_type | solution.py:410
  38.2 1.0 collective-permute-done.6
  39.9 1.0 maximum_select_fusion
  40.9 3.5 %collective-permute-start.8 = (bf16[2,64,1024]{2,1,0:T(8,128)(2,1)S(1)}, bf16[2,64,1024]{2,1,0:T(8,128)(2,1)}, u32[]{:S(2)}, u32[]{:S(2)}) collective-permute-start(bf16[2,64,1024]{2,1,0:T(8,128)(2,1)S(1)} %maximum_select_fusion), channel_id=1, source_target_pairs={{0,0},{1,5},{2,2},{3,7},{4,4},{5,1},{6,6},{7,3},{8,8},{9,13},{10,1... | collective-permute-start | bytes 786440 | tf_op jit(solution)/shard_map/ppermute | solution.py:39
  44.3 1.0 collective-permute-start.9
  45.4 4.4 %collective-permute-done.8 = bf16[2,64,1024]{2,1,0:T(8,128)(2,1)} collective-permute-done((bf16[2,64,1024]{2,1,0:T(8,128)(2,1)S(1)}, bf16[2,64,1024]{2,1,0:T(8,128)(2,1)}, u32[]{:S(2)}, u32[]{:S(2)}) %collective-permute-start.8) | collective-permute-done | bytes 262176 | tf_op jit(solution)/shard_map/ppermute | solution.py:39
  49.7 2.7 %collective-permute-done.9 = bf16[2,64,1024]{2,1,0:T(8,128)(2,1)} collective-permute-done((bf16[2,64,1024]{2,1,0:T(8,128)(2,1)S(1)}, bf16[2,64,1024]{2,1,0:T(8,128)(2,1)}, u32[]{:S(2)}, u32[]{:S(2)}) %collective-permute-start.9) | collective-permute-done | bytes 262176 | tf_op jit(solution)/shard_map/ppermute | solution.py:39
  52.4 1.1 pad_maximum_fusion
  53.5 2.4 %collective-permute-start.10 = (bf16[2,2,64,1024]{3,2,1,0:T(8,128)(2,1)S(1)}, bf16[2,2,64,1024]{3,2,1,0:T(8,128)(2,1)S(1)}, u32[]{:S(2)}, u32[]{:S(2)}) collective-permute-start(bf16[2,2,64,1024]{3,2,1,0:T(8,128)(2,1)S(1)} %pad_maximum_fusion), channel_id=1, source_target_pairs={{0,24},{1,97},{2,26},{3,99},{4,28},{5,101},{6,30},{7,103},{8,0},{9... | collective-permute-start | bytes 1572872 | tf_op jit(solution)/shard_map/ppermute | solution.py:39
  56.0 0.7 collective-permute-start.11
  56.7 5.8 %grad.4 = (bf16[512,1024]{1,0:T(8,128)(2,1)}, bf16[1,512,1024]{2,1,0:T(8,128)(2,1)S(1)}) custom-call(s32[4]{0:T(128)S(1)} %pad_add_fusion.1.blocks, bf16[512,8192]{1,0:T(8,128)(2,1)} %refs_1_.5, bf16[512,4096]{1,0:T(8,128)(2,1)} %collective-permute-done.3.theirs, bf16[512,1024]{1,0:T(8,128)(2,1)S(1)} %copy-done, ...), custom_call_target="tpu_custom_call" | custom-call | flops 2147483648 | bytes 6291456 | tf_op jit(solution)/shard_map/grad/pallas_call | solution.py:127
  62.5 1.8 %collective-permute-start.15 = (bf16[512,1024]{1,0:T(8,128)(2,1)}, bf16[512,1024]{1,0:T(8,128)(2,1)}, u32[]{:S(2)}, u32[]{:S(2)}) collective-permute-start(bf16[512,1024]{1,0:T(8,128)(2,1)} %get-tuple-element.64), channel_id=1, source_target_pairs={{0,2},{1,7},{2,4},{3,1},{4,6},{5,3},{6,0},{7,5},{8,10},{9,15},{10,... | collective-permute-start | bytes 3145736 | tf_op jit(solution)/shard_map/ppermute | solution.py:39
  64.6 3.1 %collective-permute-done.10 = bf16[2,2,64,1024]{3,2,1,0:T(8,128)(2,1)S(1)} collective-permute-done((bf16[2,2,64,1024]{3,2,1,0:T(8,128)(2,1)S(1)}, bf16[2,2,64,1024]{3,2,1,0:T(8,128)(2,1)S(1)}, u32[]{:S(2)}, u32[]{:S(2)}) %collective-permute-start.10) | collective-permute-done | bytes 524320 | tf_op jit(solution)/shard_map/ppermute | solution.py:39
  67.8 3.8 %collective-permute-done.12 = bf16[2,2,64,1024]{3,2,1,0:T(8,128)(2,1)S(1)} collective-permute-done((bf16[2,2,64,1024]{3,2,1,0:T(8,128)(2,1)S(1)}, bf16[2,2,64,1024]{3,2,1,0:T(8,128)(2,1)S(1)}, u32[]{:S(2)}, u32[]{:S(2)}) %collective-permute-start.12) | collective-permute-done | bytes 524320 | tf_op jit(solution)/shard_map/ppermute | solution.py:39
  71.6 2.1 %collective-permute-start.18 = (bf16[2,4,2,64,1024]{4,3,2,1,0:T(8,128)(2,1)S(1)}, bf16[2,4,2,64,1024]{4,3,2,1,0:T(8,128)(2,1)}, u32[]{:S(2)}, u32[]{:S(2)}) collective-permute-start(bf16[2,4,2,64,1024]{4,3,2,1,0:T(8,128)(2,1)S(1)} %bitcast_dynamic-update-slice_fusion.3.refs_3_), channel_id=1, source_target_pairs={{0,1},{1,0},{2,3},{3,2},{4,5},{5,4},{6,7},{7,6},{8,9},{9,8},{10,11... | collective-permute-start | bytes 6291464 | tf_op jit(solution)/shard_map/ppermute | solution.py:39
  73.7 2.7 %collective-permute-start.14 = (bf16[2,4,2,64,1024]{4,3,2,1,0:T(8,128)(2,1)S(1)}, bf16[2,4,2,64,1024]{4,3,2,1,0:T(8,128)(2,1)}, u32[]{:S(2)}, u32[]{:S(2)}) collective-permute-start(bf16[2,4,2,64,1024]{4,3,2,1,0:T(8,128)(2,1)S(1)} %bitcast_dynamic-update-slice_fusion.3.refs_3_), channel_id=1, source_target_pairs={{0,96},{1,25},{2,98},{3,27},{4,100},{5,29},{6,102},{7,31},{8,104},... | collective-permute-start | bytes 6291464 | tf_op jit(solution)/shard_map/ppermute | solution.py:39
  76.4 2.9 %collective-permute-start.17 = (bf16[512,1024]{1,0:T(8,128)(2,1)}, bf16[512,1024]{1,0:T(8,128)(2,1)S(1)}, u32[]{:S(2)}, u32[]{:S(2)}) collective-permute-start(bf16[512,1024]{1,0:T(8,128)(2,1)} %bitcast.93), channel_id=1, source_target_pairs={{0,2},{1,7},{2,4},{3,1},{4,6},{5,3},{6,0},{7,5},{8,10},{9,15},{10,... | collective-permute-start | bytes 3145736 | tf_op jit(solution)/shard_map/ppermute | solution.py:39
  79.4 1.2 copy-done.2
  80.6 9.3 %grad.5 = (bf16[512,1024]{1,0:T(8,128)(2,1)S(1)}, bf16[3,512,1024]{2,1,0:T(8,128)(2,1)}) custom-call(s32[8]{0:T(128)S(1)} %stack.124.blocks, bf16[512,8192]{1,0:T(8,128)(2,1)} %refs_1_.5, bf16[512,4096]{1,0:T(8,128)(2,1)} %collective-permute-done.3.theirs, bf16[512,1024]{1,0:T(8,128)(2,1)S(1)} %copy-done, bf16[512,1024]{1,0:T(8,128)(2,1)S(1)} %copy-done.2, ...), custom_call_target="tpu_custom_call" | custom-call | flops 4294967296 | bytes 10485760 | tf_op jit(solution)/shard_map/grad/pallas_call | solution.py:127
  89.9 5.1 %fold.3 = (bf16[512,8192]{1,0:T(8,128)(2,1)}, bf16[4,2,64,1024]{3,2,1,0:T(8,128)(2,1)}, f32[512,1024]{1,0:T(8,128)S(1)}) custom-call(s32[5]{0:T(128)S(1)} %stack.108.at.refs_0_, bf16[512,8192]{1,0:T(8,128)(2,1)} %refs_1_.5, bf16[512,1024]{1,0:T(8,128)(2,1)S(1)} %copy-done, bf16[2,4,2,64,1024]{4,3,2,1,0:T(8,128)(2,1)S(1)} %bitcast_dynamic-update-slice_fusion.3.refs_3_, ...), custom_call_target="tpu_custom_call" | custom-call | bytes 1048576 | tf_op jit(solution)/shard_map/fold/pallas_call | solution.py:352
  95.0 8.7 %collective-permute-done.16 = bf16[512,1024]{1,0:T(8,128)(2,1)S(1)} collective-permute-done((bf16[512,1024]{1,0:T(8,128)(2,1)S(1)}, bf16[512,1024]{1,0:T(8,128)(2,1)S(1)}, u32[]{:S(2)}, u32[]{:S(2)}) %collective-permute-start.16) | collective-permute-done | bytes 1048608 | tf_op jit(solution)/shard_map/ppermute | solution.py:39
  103.8 3.6 %collective-permute-start.23 = (bf16[2,4,2,64,1024]{4,3,2,1,0:T(8,128)(2,1)}, bf16[2,4,2,64,1024]{4,3,2,1,0:T(8,128)(2,1)S(1)}, u32[]{:S(2)}, u32[]{:S(2)}) collective-permute-start(bf16[2,4,2,64,1024]{4,3,2,1,0:T(8,128)(2,1)} %collective-permute-done.13.refs_3_), channel_id=1, source_target_pairs={{0,1},{1,0},{2,3},{3,2},{4,5},{5,4},{6,7},{7,6},{8,9},{9,8},{10,11... | collective-permute-start | bytes 6291464 | tf_op jit(solution)/shard_map/ppermute | solution.py:39
  107.5 2.3 %slice_bitcast_fusion.1 = bf16[4,2,64,1024]{3,2,1,0:T(8,128)(2,1)} fusion(bf16[2,4,2,64,1024]{4,3,2,1,0:T(8,128)(2,1)} %collective-permute-done.13.refs_3_), kind=kLoop, calls=%fused_computation.10 | loop fusion | bytes 2097152 | tf_op jit(solution)/shard_map/squeeze | solution.py:461
  109.8 2.3 %slice_bitcast_fusion = bf16[4,2,64,1024]{3,2,1,0:T(8,128)(2,1)} fusion(bf16[2,4,2,64,1024]{4,3,2,1,0:T(8,128)(2,1)} %collective-permute-done.14.refs_4_), kind=kLoop, calls=%fused_computation.9 | loop fusion | bytes 2097152 | tf_op jit(solution)/shard_map/squeeze | solution.py:462
  113.0 1.9 %collective-permute-start.19 = (bf16[4,2,64,1024]{3,2,1,0:T(8,128)(2,1)}, bf16[4,2,64,1024]{3,2,1,0:T(8,128)(2,1)S(1)}, u32[]{:S(2)}, u32[]{:S(2)}) collective-permute-start(bf16[4,2,64,1024]{3,2,1,0:T(8,128)(2,1)} %slice_bitcast_fusion.1), channel_id=1, source_target_pairs={{0,32},{1,9},{2,34},{3,11},{4,36},{5,13},{6,38},{7,15},{8,40},{9,1... | collective-permute-start | bytes 3145736 | tf_op jit(solution)/shard_map/ppermute | solution.py:39
  114.9 0.7 collective-permute-start.20
  116.1 0.8 collective-permute-start.22
  116.9 13.6 %fold.4 = (bf16[512,8192]{1,0:T(8,128)(2,1)}, bf16[4,2,64,1024]{3,2,1,0:T(8,128)(2,1)}, f32[512,1024]{1,0:T(8,128)S(1)}) custom-call(s32[5]{0:T(128)S(1)} %stack.108.at.refs_0_, bf16[512,8192]{1,0:T(8,128)(2,1)} %refs_1_.5, bf16[512,1024]{1,0:T(8,128)(2,1)S(1)} %copy-done, ...), custom_call_target="tpu_custom_call", output_to_operand_aliasing={{0}: (8, {}), {1}: (9, {})} | custom-call | bytes 1048576 | tf_op jit(solution)/shard_map/fold/pallas_call | solution.py:352
  130.6 6.7 %collective-permute-done.22 = bf16[192,1024]{1,0:T(8,128)(2,1)S(1)} collective-permute-done((bf16[192,1024]{1,0:T(8,128)(2,1)S(1)}, bf16[192,1024]{1,0:T(8,128)(2,1)S(1)}, u32[]{:S(2)}, u32[]{:S(2)}) %collective-permute-start.22) | collective-permute-done | bytes 393248 | tf_op jit(solution)/shard_map/ppermute | solution.py:39
  138.5 1.4 collective-permute-done.25.refs_7_
  140.0 1.5 collective-permute-done.26.refs_8_
  141.5 11.7 %fold.5 = (bf16[512,8192]{1,0:T(8,128)(2,1)}, bf16[4,2,64,1024]{3,2,1,0:T(8,128)(2,1)}, bf16[512,1024]{1,0:T(8,128)(2,1)}) custom-call(s32[5]{0:T(128)S(1)} %stack.108.at.refs_0_, bf16[512,8192]{1,0:T(8,128)(2,1)} %refs_1_.5, bf16[512,1024]{1,0:T(8,128)(2,1)S(1)} %copy-done, ...), custom_call_target="tpu_custom_call", output_to_operand_aliasing={{0}: (10, {}), {1}: (11, {})} | custom-call | bytes 1048576 | tf_op jit(solution)/shard_map/fold/pallas_call | solution.py:352
  153.5 1.9 %fusion.1 = f32[1,512,1024]{2,1,0:T(8,128)} fusion(bf16[512,1024]{1,0:T(8,128)(2,1)S(1)} %collective-permute-done.27, bf16[320,1024]{1,0:T(8,128)(2,1)S(1)} %collective-permute-done.28, bf16[192,1024]{1,0:T(8,128)(2,1)S(1)} %collective-permute-done.22, bf16[3,512,1024]{2,1,0:T(8,128)(2,1)S(1)} %copy-done.6), kind=kLoop, calls=%fused_computation.2 | loop fusion | flops 4194304 | bytes 5242880 | tf_op jit(solution)/shard_map/broadcast_in_dim | solution.py:495
  (66 shorter events, 6.0 us)
Async XLA Ops:
  0.7 5.8 %copy-start = (bf16[512,1024]{1,0:T(8,128)(2,1)S(1)}, bf16[512,1024]{1,0:T(8,128)(2,1)}, u32[]{:S(2)}) copy-start(bf16[512,1024]{1,0:T(8,128)(2,1)} %refs_2_.5) | copy-start | bytes 3145732
  0.7 5.9 %copy-start.8 = (bf16[1,512,1024]{2,1,0:T(8,128)(2,1)S(1)}, bf16[1,512,1024]{2,1,0:T(8,128)(2,1)}, u32[]{:S(2)}) copy-start(bf16[1,512,1024]{2,1,0:T(8,128)(2,1)} %param.5) | copy-start | bytes 3145732
  5.1 10.1 %collective-permute-start.3 = (bf16[512,4096]{1,0:T(8,128)(2,1)}, bf16[512,4096]{1,0:T(8,128)(2,1)}, u32[]{:S(2)}, u32[]{:S(2)}) collective-permute-start(bf16[512,4096]{1,0:T(8,128)(2,1)} %half.1), channel_id=1, source_target_pairs={{0,1},{1,0},{2,3},{3,2},{4,5},{5,4},{6,7},{7,6},{8,9},{9,8},{10,11... | collective-permute-start | bytes 12582920 | tf_op jit(solution)/shard_map/ppermute | solution.py:39
  6.6 8.2 %collective-permute-start.4 = (bf16[512,1024]{1,0:T(8,128)(2,1)S(1)}, bf16[512,1024]{1,0:T(8,128)(2,1)S(1)}, u32[]{:S(2)}, u32[]{:S(2)}) collective-permute-start(bf16[512,1024]{1,0:T(8,128)(2,1)S(1)} %copy-done), channel_id=1, source_target_pairs={{0,1},{1,0},{2,3},{3,2},{4,5},{5,4},{6,7},{7,6},{8,9},{9,8},{10,11... | collective-permute-start | bytes 3145736 | tf_op jit(solution)/shard_map/ppermute | solution.py:39
  7.5 14.3 %collective-permute-start = (bf16[2,64,1024]{2,1,0:T(8,128)(2,1)}, bf16[2,64,1024]{2,1,0:T(8,128)(2,1)S(1)}, u32[]{:S(2)}, u32[]{:S(2)}) collective-permute-start(bf16[2,64,1024]{2,1,0:T(8,128)(2,1)} %get-tuple-element.100), channel_id=1, source_target_pairs={{0,64},{1,65},{2,66},{3,67},{4,68},{5,69},{6,70},{7,71},{8,72},{9,... | collective-permute-start | bytes 786440 | tf_op jit(solution)/shard_map/ppermute | solution.py:39
  10.4 12.7 %collective-permute-start.1 = (bf16[2,64,1024]{2,1,0:T(8,128)(2,1)}, bf16[2,64,1024]{2,1,0:T(8,128)(2,1)S(1)}, u32[]{:S(2)}, u32[]{:S(2)}) collective-permute-start(bf16[2,64,1024]{2,1,0:T(8,128)(2,1)} %get-tuple-element.99), channel_id=1, source_target_pairs={{0,32},{1,33},{2,34},{3,35},{4,36},{5,37},{6,38},{7,39},{8,40},{9,... | collective-permute-start | bytes 786440 | tf_op jit(solution)/shard_map/ppermute | solution.py:39
  10.7 12.4 %collective-permute-start.2 = (bf16[2,64,1024]{2,1,0:T(8,128)(2,1)S(1)}, bf16[2,64,1024]{2,1,0:T(8,128)(2,1)S(1)}, u32[]{:S(2)}, u32[]{:S(2)}) collective-permute-start(bf16[2,64,1024]{2,1,0:T(8,128)(2,1)S(1)} %get-tuple-element.98), channel_id=1, source_target_pairs={{0,96},{1,97},{2,98},{3,99},{4,100},{5,101},{6,102},{7,103},{8,104... | collective-permute-start | bytes 786440 | tf_op jit(solution)/shard_map/ppermute | solution.py:39
  14.7 42.0 %copy-start.1 = (bf16[512,1024]{1,0:T(8,128)(2,1)}, bf16[512,1024]{1,0:T(8,128)(2,1)S(1)}, u32[]{:S(2)}) copy-start(bf16[512,1024]{1,0:T(8,128)(2,1)S(1)} %collective-permute-done.4.cot_theirs) | copy-start | bytes 3145732
  20.9 1.0 copy-start.5
  21.9 1.2 copy-start.9
  23.1 0.7 copy-start.10
  23.1 0.8 copy-start.11
  23.9 15.3 %collective-permute-start.7 = (bf16[512,1024]{1,0:T(8,128)(2,1)}, bf16[512,1024]{1,0:T(8,128)(2,1)S(1)}, u32[]{:S(2)}, u32[]{:S(2)}) collective-permute-start(bf16[512,1024]{1,0:T(8,128)(2,1)} %get-tuple-element.56), channel_id=1, source_target_pairs={{0,2},{1,7},{2,4},{3,1},{4,6},{5,3},{6,0},{7,5},{8,10},{9,15},{10,... | collective-permute-start | bytes 3145736 | tf_op jit(solution)/shard_map/ppermute | solution.py:39
  28.0 0.8 copy-start.7
  28.9 7.0 %collective-permute-start.5 = (bf16[64,1024]{1,0:T(8,128)(2,1)S(1)}, bf16[64,1024]{1,0:T(8,128)(2,1)S(1)}, u32[]{:S(2)}, u32[]{:S(2)}) collective-permute-start(bf16[64,1024]{1,0:T(8,128)(2,1)S(1)} %fusion.9), channel_id=1, source_target_pairs={{0,16},{1,17},{2,18},{3,19},{4,20},{5,21},{6,22},{7,23},{8,24},{9,... | collective-permute-start | bytes 393224 | tf_op jit(solution)/shard_map/ppermute | solution.py:39
  37.9 1.3 collective-permute-start.6
  39.2 0.7 copy-start.12
  40.9 8.8 %collective-permute-start.8 = (bf16[2,64,1024]{2,1,0:T(8,128)(2,1)S(1)}, bf16[2,64,1024]{2,1,0:T(8,128)(2,1)}, u32[]{:S(2)}, u32[]{:S(2)}) collective-permute-start(bf16[2,64,1024]{2,1,0:T(8,128)(2,1)S(1)} %maximum_select_fusion), channel_id=1, source_target_pairs={{0,0},{1,5},{2,2},{3,7},{4,4},{5,1},{6,6},{7,3},{8,8},{9,13},{10,1... | collective-permute-start | bytes 786440 | tf_op jit(solution)/shard_map/ppermute | solution.py:39
  44.3 8.1 %collective-permute-start.9 = (bf16[2,64,1024]{2,1,0:T(8,128)(2,1)S(1)}, bf16[2,64,1024]{2,1,0:T(8,128)(2,1)}, u32[]{:S(2)}, u32[]{:S(2)}) collective-permute-start(bf16[2,64,1024]{2,1,0:T(8,128)(2,1)S(1)} %maximum_select_fusion), channel_id=1, source_target_pairs={{0,6},{1,3},{2,0},{3,5},{4,2},{5,7},{6,4},{7,1},{8,14},{9,11},{10,... | collective-permute-start | bytes 786440 | tf_op jit(solution)/shard_map/ppermute | solution.py:39
  53.5 14.2 %collective-permute-start.10 = (bf16[2,2,64,1024]{3,2,1,0:T(8,128)(2,1)S(1)}, bf16[2,2,64,1024]{3,2,1,0:T(8,128)(2,1)S(1)}, u32[]{:S(2)}, u32[]{:S(2)}) collective-permute-start(bf16[2,2,64,1024]{3,2,1,0:T(8,128)(2,1)S(1)} %pad_maximum_fusion), channel_id=1, source_target_pairs={{0,24},{1,97},{2,26},{3,99},{4,28},{5,101},{6,30},{7,103},{8,0},{9... | collective-permute-start | bytes 1572872 | tf_op jit(solution)/shard_map/ppermute | solution.py:39
  56.0 11.7 %collective-permute-start.11 = (bf16[2,2,64,1024]{3,2,1,0:T(8,128)(2,1)S(1)}, bf16[2,2,64,1024]{3,2,1,0:T(8,128)(2,1)S(1)}, u32[]{:S(2)}, u32[]{:S(2)}) collective-permute-start(bf16[2,2,64,1024]{3,2,1,0:T(8,128)(2,1)S(1)} %pad_maximum_fusion), channel_id=1, source_target_pairs={{0,16},{1,65},{2,18},{3,67},{4,20},{5,69},{6,22},{7,71},{8,24},{9,... | collective-permute-start | bytes 1572872 | tf_op jit(solution)/shard_map/ppermute | solution.py:39
  56.7 14.9 %collective-permute-start.12 = (bf16[2,2,64,1024]{3,2,1,0:T(8,128)(2,1)S(1)}, bf16[2,2,64,1024]{3,2,1,0:T(8,128)(2,1)S(1)}, u32[]{:S(2)}, u32[]{:S(2)}) collective-permute-start(bf16[2,2,64,1024]{3,2,1,0:T(8,128)(2,1)S(1)} %pad_maximum_fusion), channel_id=1, source_target_pairs={{0,8},{1,33},{2,10},{3,35},{4,12},{5,37},{6,14},{7,39},{8,16},{9,4... | collective-permute-start | bytes 1572872 | tf_op jit(solution)/shard_map/ppermute | solution.py:39
  62.5 5.2 %copy-start.3 = (bf16[1,512,1024]{2,1,0:T(8,128)(2,1)}, bf16[1,512,1024]{2,1,0:T(8,128)(2,1)S(1)}, u32[]{:S(2)}) copy-start(bf16[1,512,1024]{2,1,0:T(8,128)(2,1)S(1)} %get-tuple-element.72) | copy-start | bytes 3145732
  62.5 16.9 %collective-permute-start.15 = (bf16[512,1024]{1,0:T(8,128)(2,1)}, bf16[512,1024]{1,0:T(8,128)(2,1)}, u32[]{:S(2)}, u32[]{:S(2)}) collective-permute-start(bf16[512,1024]{1,0:T(8,128)(2,1)} %get-tuple-element.64), channel_id=1, source_target_pairs={{0,2},{1,7},{2,4},{3,1},{4,6},{5,3},{6,0},{7,5},{8,10},{9,15},{10,... | collective-permute-start | bytes 3145736 | tf_op jit(solution)/shard_map/ppermute | solution.py:39
  71.6 18.3 %collective-permute-start.18 = (bf16[2,4,2,64,1024]{4,3,2,1,0:T(8,128)(2,1)S(1)}, bf16[2,4,2,64,1024]{4,3,2,1,0:T(8,128)(2,1)}, u32[]{:S(2)}, u32[]{:S(2)}) collective-permute-start(bf16[2,4,2,64,1024]{4,3,2,1,0:T(8,128)(2,1)S(1)} %bitcast_dynamic-update-slice_fusion.3.refs_3_), channel_id=1, source_target_pairs={{0,1},{1,0},{2,3},{3,2},{4,5},{5,4},{6,7},{7,6},{8,9},{9,8},{10,11... | collective-permute-start | bytes 6291464 | tf_op jit(solution)/shard_map/ppermute | solution.py:39
  73.7 30.1 %collective-permute-start.13 = (bf16[2,4,2,64,1024]{4,3,2,1,0:T(8,128)(2,1)S(1)}, bf16[2,4,2,64,1024]{4,3,2,1,0:T(8,128)(2,1)}, u32[]{:S(2)}, u32[]{:S(2)}) collective-permute-start(bf16[2,4,2,64,1024]{4,3,2,1,0:T(8,128)(2,1)S(1)} %bitcast_dynamic-update-slice_fusion.3.refs_3_), channel_id=1, source_target_pairs={{0,32},{1,9},{2,34},{3,11},{4,36},{5,13},{6,38},{7,15},{8,40},{9,1... | collective-permute-start | bytes 6291464 | tf_op jit(solution)/shard_map/ppermute | solution.py:39
  73.7 30.1 %collective-permute-start.14 = (bf16[2,4,2,64,1024]{4,3,2,1,0:T(8,128)(2,1)S(1)}, bf16[2,4,2,64,1024]{4,3,2,1,0:T(8,128)(2,1)}, u32[]{:S(2)}, u32[]{:S(2)}) collective-permute-start(bf16[2,4,2,64,1024]{4,3,2,1,0:T(8,128)(2,1)S(1)} %bitcast_dynamic-update-slice_fusion.3.refs_3_), channel_id=1, source_target_pairs={{0,96},{1,25},{2,98},{3,27},{4,100},{5,29},{6,102},{7,31},{8,104},... | collective-permute-start | bytes 6291464 | tf_op jit(solution)/shard_map/ppermute | solution.py:39
  76.4 18.6 %collective-permute-start.17 = (bf16[512,1024]{1,0:T(8,128)(2,1)}, bf16[512,1024]{1,0:T(8,128)(2,1)S(1)}, u32[]{:S(2)}, u32[]{:S(2)}) collective-permute-start(bf16[512,1024]{1,0:T(8,128)(2,1)} %bitcast.93), channel_id=1, source_target_pairs={{0,2},{1,7},{2,4},{3,1},{4,6},{5,3},{6,0},{7,5},{8,10},{9,15},{10,... | collective-permute-start | bytes 3145736 | tf_op jit(solution)/shard_map/ppermute | solution.py:39
  79.4 1.2 copy-start.2
  89.8 13.9 %collective-permute-start.16 = (bf16[512,1024]{1,0:T(8,128)(2,1)S(1)}, bf16[512,1024]{1,0:T(8,128)(2,1)S(1)}, u32[]{:S(2)}, u32[]{:S(2)}) collective-permute-start(bf16[512,1024]{1,0:T(8,128)(2,1)S(1)} %get-tuple-element.65), channel_id=1, source_target_pairs={{0,2},{1,7},{2,4},{3,1},{4,6},{5,3},{6,0},{7,5},{8,10},{9,15},{10,... | collective-permute-start | bytes 3145736 | tf_op jit(solution)/shard_map/ppermute | solution.py:39
  103.8 8.2 %copy-start.4 = (bf16[1,512,1024]{2,1,0:T(8,128)(2,1)S(1)}, bf16[1,512,1024]{2,1,0:T(8,128)(2,1)}, u32[]{:S(2)}) copy-start(bf16[1,512,1024]{2,1,0:T(8,128)(2,1)} %copy-done.3) | copy-start | bytes 3145732
  103.8 12.3 %collective-permute-start.23 = (bf16[2,4,2,64,1024]{4,3,2,1,0:T(8,128)(2,1)}, bf16[2,4,2,64,1024]{4,3,2,1,0:T(8,128)(2,1)S(1)}, u32[]{:S(2)}, u32[]{:S(2)}) collective-permute-start(bf16[2,4,2,64,1024]{4,3,2,1,0:T(8,128)(2,1)} %collective-permute-done.13.refs_3_), channel_id=1, source_target_pairs={{0,1},{1,0},{2,3},{3,2},{4,5},{5,4},{6,7},{7,6},{8,9},{9,8},{10,11... | collective-permute-start | bytes 6291464 | tf_op jit(solution)/shard_map/ppermute | solution.py:39
  107.4 9.5 %collective-permute-start.24 = (bf16[2,4,2,64,1024]{4,3,2,1,0:T(8,128)(2,1)}, bf16[2,4,2,64,1024]{4,3,2,1,0:T(8,128)(2,1)S(1)}, u32[]{:S(2)}, u32[]{:S(2)}) collective-permute-start(bf16[2,4,2,64,1024]{4,3,2,1,0:T(8,128)(2,1)} %collective-permute-done.14.refs_4_), channel_id=1, source_target_pairs={{0,1},{1,0},{2,3},{3,2},{4,5},{5,4},{6,7},{7,6},{8,9},{9,8},{10,11... | collective-permute-start | bytes 6291464 | tf_op jit(solution)/shard_map/ppermute | solution.py:39
  112.0 3.7 %copy-start.6 = (bf16[3,512,1024]{2,1,0:T(8,128)(2,1)S(1)}, bf16[3,512,1024]{2,1,0:T(8,128)(2,1)}, u32[]{:S(2)}) copy-start(bf16[3,512,1024]{2,1,0:T(8,128)(2,1)} %get-tuple-element.74) | copy-start | bytes 9437188
  112.4 24.8 %collective-permute-start.21 = (bf16[512,1024]{1,0:T(8,128)(2,1)S(1)}, bf16[512,1024]{1,0:T(8,128)(2,1)S(1)}, u32[]{:S(2)}, u32[]{:S(2)}) collective-permute-start(bf16[512,1024]{1,0:T(8,128)(2,1)S(1)} %fusion.4), channel_id=1, source_target_pairs={{0,2},{1,7},{2,4},{3,1},{4,6},{5,3},{6,0},{7,5},{8,10},{9,15},{10,... | collective-permute-start | bytes 3145736 | tf_op jit(solution)/shard_map/ppermute | solution.py:39
  113.0 24.2 %collective-permute-start.19 = (bf16[4,2,64,1024]{3,2,1,0:T(8,128)(2,1)}, bf16[4,2,64,1024]{3,2,1,0:T(8,128)(2,1)S(1)}, u32[]{:S(2)}, u32[]{:S(2)}) collective-permute-start(bf16[4,2,64,1024]{3,2,1,0:T(8,128)(2,1)} %slice_bitcast_fusion.1), channel_id=1, source_target_pairs={{0,32},{1,9},{2,34},{3,11},{4,36},{5,13},{6,38},{7,15},{8,40},{9,1... | collective-permute-start | bytes 3145736 | tf_op jit(solution)/shard_map/ppermute | solution.py:39
  114.9 22.3 %collective-permute-start.20 = (bf16[4,2,64,1024]{3,2,1,0:T(8,128)(2,1)}, bf16[4,2,64,1024]{3,2,1,0:T(8,128)(2,1)S(1)}, u32[]{:S(2)}, u32[]{:S(2)}) collective-permute-start(bf16[4,2,64,1024]{3,2,1,0:T(8,128)(2,1)} %slice_bitcast_fusion), channel_id=1, source_target_pairs={{0,96},{1,25},{2,98},{3,27},{4,100},{5,29},{6,102},{7,31},{8,104},... | collective-permute-start | bytes 3145736 | tf_op jit(solution)/shard_map/ppermute | solution.py:39
  116.1 21.1 %collective-permute-start.22 = (bf16[192,1024]{1,0:T(8,128)(2,1)S(1)}, bf16[192,1024]{1,0:T(8,128)(2,1)S(1)}, u32[]{:S(2)}, u32[]{:S(2)}) collective-permute-start(bf16[192,1024]{1,0:T(8,128)(2,1)S(1)} %slice.28), channel_id=1, source_target_pairs={{0,8},{1,9},{2,10},{3,11},{4,12},{5,13},{6,14},{7,15},{8,0},{9,1},... | collective-permute-start | bytes 1179656 | tf_op jit(solution)/shard_map/ppermute | solution.py:39
  137.2 2.7 %collective-permute-start.25 = (bf16[4,2,64,1024]{3,2,1,0:T(8,128)(2,1)S(1)}, bf16[4,2,64,1024]{3,2,1,0:T(8,128)(2,1)S(1)}, u32[]{:S(2)}, u32[]{:S(2)}) collective-permute-start(bf16[4,2,64,1024]{3,2,1,0:T(8,128)(2,1)S(1)} %collective-permute-done.19.refs_4_), channel_id=1, source_target_pairs={{0,1},{1,0},{2,3},{3,2},{4,5},{5,4},{6,7},{7,6},{8,9},{9,8},{10,11... | collective-permute-start | bytes 3145736 | tf_op jit(solution)/shard_map/ppermute | solution.py:39
  137.3 4.1 %collective-permute-start.26 = (bf16[4,2,64,1024]{3,2,1,0:T(8,128)(2,1)S(1)}, bf16[4,2,64,1024]{3,2,1,0:T(8,128)(2,1)S(1)}, u32[]{:S(2)}, u32[]{:S(2)}) collective-permute-start(bf16[4,2,64,1024]{3,2,1,0:T(8,128)(2,1)S(1)} %collective-permute-done.20.refs_5_), channel_id=1, source_target_pairs={{0,1},{1,0},{2,3},{3,2},{4,5},{5,4},{6,7},{7,6},{8,9},{9,8},{10,11... | collective-permute-start | bytes 3145736 | tf_op jit(solution)/shard_map/ppermute | solution.py:39
  138.2 15.2 %collective-permute-start.27 = (bf16[512,1024]{1,0:T(8,128)(2,1)S(1)}, bf16[512,1024]{1,0:T(8,128)(2,1)S(1)}, u32[]{:S(2)}, u32[]{:S(2)}) collective-permute-start(bf16[512,1024]{1,0:T(8,128)(2,1)S(1)} %fusion.2), channel_id=1, source_target_pairs={{0,2},{1,7},{2,4},{3,1},{4,6},{5,3},{6,0},{7,5},{8,10},{9,15},{10,... | collective-permute-start | bytes 3145736 | tf_op jit(solution)/shard_map/ppermute | solution.py:39
  138.4 15.0 %collective-permute-start.28 = (bf16[320,1024]{1,0:T(8,128)(2,1)S(1)}, bf16[320,1024]{1,0:T(8,128)(2,1)S(1)}, u32[]{:S(2)}, u32[]{:S(2)}) collective-permute-start(bf16[320,1024]{1,0:T(8,128)(2,1)S(1)} %slice.29), channel_id=1, source_target_pairs={{0,8},{1,9},{2,10},{3,11},{4,12},{5,13},{6,14},{7,15},{8,0},{9,1},... | collective-permute-start | bytes 1966088 | tf_op jit(solution)/shard_map/ppermute | solution.py:39

commit v6 on v5

--- a/solution.py
+++ b/solution.py
@@ -436,13 +436,14 @@
     c0 = jnp.stack([far, near])
     c0, first_b, late = lax.optimization_barrier((c0, first_b, tokens_theirs))
     arrived_b = ring_y(first_b)
-    second, second_b = grads([(0, 1), (1, 1)], late, arrived)
+    (second,) = grads([(0, 1)], late, arrived)
     parts = [short_way(c0, d) for d in (1, 2, 3)]
     arrived = ring_y(second)
-    second_b = second_b[0]
     c1 = in_order([c0] + parts, jnp.where(c == 0, z, x))
     c1, late = lax.optimization_barrier((c1, late))
-    third, rest = grads([(0, 2), (0, 3), (1, 2), (1, 3)], late, arrived)
+    (third,) = grads([(0, 2)], late, arrived)
+    third, late = lax.optimization_barrier((third, late))
+    second_b, rest = grads([(1, 1), (0, 3), (1, 2), (1, 3)], late)
 
     mine, theirs = {0: c1}, {0: swap_core(c1)}
     mine[1], mine[3] = long_way(c1, 1), long_way(c1, -1)
@@ -455,8 +456,8 @@
 
     carry = fold_of([("x", 0, 0), ("x", 0, 1)], [0], None, False)
     arrived = ring_y(third)
-    mine[1], mine[3], arrived, arrived_b, *carry = lax.optimization_barrier(
-        (mine[1], mine[3], arrived, arrived_b, *carry)
+    mine[1], mine[3], arrived, arrived_b, rest, *carry = lax.optimization_barrier(
+        (mine[1], mine[3], arrived, arrived_b, rest, *carry)
     )
     mine[2, 0] = long_way(mine[1][0], 1)
     mine[2, 1] = long_way(mine[3][1], -1)

time: 157 us -> 154 us (0.981)
  waiting for transfers between devices: 40.2 us -> 31.9 us
  local copies, waits for them, and re-layouts: 10.5 us -> 13.1 us
  Pallas kernels: 55.4 us -> 57.6 us
    ppermute x29, waiting for transfers between devices: 40.2 us -> 31.9 us  [permute(): return lax.ppermute(value, AXES, pairs)]
    pallas_call x3 -> x4, Pallas kernels: 20.7 us -> 22.9 us  [grad_blocks(): pl.pallas_call(functools.partial(grad_kernel, len(arrived)), out_shape=[j...]
    dynamic_update_slice x4, local copies, waits for them, and re-layouts: 0.18 us -> 2.25 us  [in_order(): lax.dynamic_update_slice_in_dim(whole, part[:, None], here + d & 3, 1)]
    unnamed x26 -> x22, local copies, waits for them, and re-layouts: 4.44 us -> 5.01 us
  transfers between devices with their start and end apart: 29 -> 29, of which waited for: 14 -> 14; matrix products, arithmetic and copies ran while one was open for 7% -> 10% of each run, Pallas kernels for 33% -> 35%
where the time goes in v6:
time: 154 us; the launch traced here: 153 us
  Pallas kernels  57.6 us (37%)
  starting transfers between devices  39.2 us (25%)
  waiting for transfers between devices  31.9 us (21%)
  local copies, waits for them, and re-layouts  13.1 us (9%)
  other arithmetic  10.2 us (7%)
    ppermute x29, starting transfers between devices, permute(): return lax.ppermute(value, AXES, pairs)  39.2 us
    ppermute x29, waiting for transfers between devices, permute(): return lax.ppermute(value, AXES, pairs)  31.9 us
    pallas_call x3, Pallas kernels, fold(): pl.pallas_call(kernel, out_shape=shapes, in_specs=in_specs, out_specs=[AN...  30.4 us
    pallas_call x4, Pallas kernels, grad_blocks(): pl.pallas_call(functools.partial(grad_kernel, len(arrived)), out_shape=[j...  22.9 us
    unnamed x22, local copies, waits for them, and re-layouts  5.01 us
    pallas_call x1, Pallas kernels, other_half(): pl.pallas_call(half_kernel, out_shape=jax.ShapeDtypeStruct((TOK, D // 2),...  4.33 us
  transfers between devices with their start and end apart: 29, of which 14 were waited for; matrix products, arithmetic and copies ran while one was open for 10% of the time, Pallas kernels for 35%

profile of v6, /device:TPU:1, one launch (start us, length us, event | category | flops | bytes accessed | tf_op | source)
XLA Modules:
  0.0 153.0 jit_solution(6578152917281164621)
XLA Ops:
  0.7 4.3 %half.1 = bf16[512,4096]{1,0:T(8,128)(2,1)} custom-call(s32[5]{0:T(128)S(1)} %stack.111.at.refs_0_, bf16[512,8192]{1,0:T(8,128)(2,1)} %refs_1_.5), custom_call_target="tpu_custom_call" | custom-call | bytes 8388608 | tf_op jit(solution)/shard_map/half/pallas_call | solution.py:82
  5.1 1.5 collective-permute-start.3
  7.5 2.8 %collective-permute-start = (bf16[2,64,1024]{2,1,0:T(8,128)(2,1)}, bf16[2,64,1024]{2,1,0:T(8,128)(2,1)S(1)}, u32[]{:S(2)}, u32[]{:S(2)}) collective-permute-start(bf16[2,64,1024]{2,1,0:T(8,128)(2,1)} %get-tuple-element.102), channel_id=1, source_target_pairs={{0,64},{1,65},{2,66},{3,67},{4,68},{5,69},{6,70},{7,71},{8,72},{9,... | collective-permute-start | bytes 786440 | tf_op jit(solution)/shard_map/ppermute | solution.py:39
  10.7 2.4 %collective-permute-start.2 = (bf16[2,64,1024]{2,1,0:T(8,128)(2,1)S(1)}, bf16[2,64,1024]{2,1,0:T(8,128)(2,1)S(1)}, u32[]{:S(2)}, u32[]{:S(2)}) collective-permute-start(bf16[2,64,1024]{2,1,0:T(8,128)(2,1)S(1)} %get-tuple-element.100), channel_id=1, source_target_pairs={{0,96},{1,97},{2,98},{3,99},{4,100},{5,101},{6,102},{7,103},{8,104... | collective-permute-start | bytes 786440 | tf_op jit(solution)/shard_map/ppermute | solution.py:39
  13.1 1.6 %collective-permute-done.4.cot_theirs = bf16[512,1024]{1,0:T(8,128)(2,1)S(1)} collective-permute-done((bf16[512,1024]{1,0:T(8,128)(2,1)S(1)}, bf16[512,1024]{1,0:T(8,128)(2,1)S(1)}, u32[]{:S(2)}, u32[]{:S(2)}) %collective-permute-start.4) | collective-permute-done | bytes 1048608 | tf_op jit(solution)/shard_map/ppermute | solution.py:39
  15.2 5.7 %grad.4 = (bf16[512,1024]{1,0:T(8,128)(2,1)}, bf16[1,512,1024]{2,1,0:T(8,128)(2,1)S(1)}) custom-call(s32[4]{0:T(128)S(1)} %pad_add_fusion.blocks, bf16[512,8192]{1,0:T(8,128)(2,1)} %refs_1_.5, bf16[512,4096]{1,0:T(8,128)(2,1)} %collective-permute-done.3.theirs, bf16[512,1024]{1,0:T(8,128)(2,1)S(1)} %copy-done, ...), custom_call_target="tpu_custom_call" | custom-call | flops 2147483648 | bytes 6291456 | tf_op jit(solution)/shard_map/grad/pallas_call | solution.py:127
  20.9 1.0 copy-done.4
  21.9 1.2 collective-permute-done.1
  23.9 2.8 %collective-permute-start.7 = (bf16[512,1024]{1,0:T(8,128)(2,1)}, bf16[512,1024]{1,0:T(8,128)(2,1)S(1)}, u32[]{:S(2)}, u32[]{:S(2)}) collective-permute-start(bf16[512,1024]{1,0:T(8,128)(2,1)} %get-tuple-element.57), channel_id=1, source_target_pairs={{0,2},{1,7},{2,4},{3,1},{4,6},{5,3},{6,0},{7,5},{8,10},{9,15},{10,... | collective-permute-start | bytes 3145736 | tf_op jit(solution)/shard_map/ppermute | solution.py:39
  26.7 1.3 fusion.5
  28.9 3.7 %collective-permute-start.5 = (bf16[64,1024]{1,0:T(8,128)(2,1)S(1)}, bf16[64,1024]{1,0:T(8,128)(2,1)S(1)}, u32[]{:S(2)}, u32[]{:S(2)}) collective-permute-start(bf16[64,1024]{1,0:T(8,128)(2,1)S(1)} %fusion.8), channel_id=1, source_target_pairs={{0,16},{1,17},{2,18},{3,19},{4,20},{5,21},{6,22},{7,23},{8,24},{9,... | collective-permute-start | bytes 393224 | tf_op jit(solution)/shard_map/ppermute | solution.py:39
  32.5 3.3 %collective-permute-done.5 = bf16[64,1024]{1,0:T(8,128)(2,1)S(1)} collective-permute-done((bf16[64,1024]{1,0:T(8,128)(2,1)S(1)}, bf16[64,1024]{1,0:T(8,128)(2,1)S(1)}, u32[]{:S(2)}, u32[]{:S(2)}) %collective-permute-start.5) | collective-permute-done | bytes 131104 | tf_op jit(solution)/shard_map/ppermute | solution.py:39
  35.9 2.0 %fusion.9 = (bf16[64,1024]{1,0:T(8,128)(2,1)S(1)}, f32[64,1024]{1,0:T(8,128)}, f32[1,1,64,1024]{3,2,1,0:T(8,128)}) fusion(f32[1,1,64,1024]{3,2,1,0:T(8,128)} %param.7, bf16[64,1024]{1,0:T(8,128)(2,1)S(1)} %collective-permute-done.5, f32[2,64,1024]{2,1,0:T(8,128)} %copy-done.6, s32[]{:T(128)S(6)} %select_n.48, f32[1,1,64,1024]{3,2,1,0:T(8,128)} %param.6), kind=kLoop, calls=%fused_computation.32 | loop fusion | flops 655360 | bytes 1572868 | tf_op jit(solution)/shard_map/convert_element_type | solution.py:410
  38.2 1.0 collective-permute-done.6
  39.2 3.7 %collective-permute-start.8 = (bf16[2,64,1024]{2,1,0:T(8,128)(2,1)S(1)}, bf16[2,64,1024]{2,1,0:T(8,128)(2,1)S(1)}, u32[]{:S(2)}, u32[]{:S(2)}) collective-permute-start(bf16[2,64,1024]{2,1,0:T(8,128)(2,1)S(1)} %maximum_select_fusion), channel_id=1, source_target_pairs={{0,0},{1,5},{2,2},{3,7},{4,4},{5,1},{6,6},{7,3},{8,8},{9,13},{10,1... | collective-permute-start | bytes 786440 | tf_op jit(solution)/shard_map/ppermute | solution.py:39
  43.0 1.4 collective-permute-start.9
  44.4 3.6 %collective-permute-done.8 = bf16[2,64,1024]{2,1,0:T(8,128)(2,1)S(1)} collective-permute-done((bf16[2,64,1024]{2,1,0:T(8,128)(2,1)S(1)}, bf16[2,64,1024]{2,1,0:T(8,128)(2,1)S(1)}, u32[]{:S(2)}, u32[]{:S(2)}) %collective-permute-start.8) | collective-permute-done | bytes 262176 | tf_op jit(solution)/shard_map/ppermute | solution.py:39
  48.0 2.7 %collective-permute-done.9 = bf16[2,64,1024]{2,1,0:T(8,128)(2,1)S(1)} collective-permute-done((bf16[2,64,1024]{2,1,0:T(8,128)(2,1)S(1)}, bf16[2,64,1024]{2,1,0:T(8,128)(2,1)S(1)}, u32[]{:S(2)}, u32[]{:S(2)}) %collective-permute-start.9) | collective-permute-done | bytes 262176 | tf_op jit(solution)/shard_map/ppermute | solution.py:39
  51.5 2.3 %collective-permute-start.10 = (bf16[2,2,64,1024]{3,2,1,0:T(8,128)(2,1)}, bf16[2,2,64,1024]{3,2,1,0:T(8,128)(2,1)}, u32[]{:S(2)}, u32[]{:S(2)}) collective-permute-start(bf16[2,2,64,1024]{3,2,1,0:T(8,128)(2,1)} %pad_maximum_fusion), channel_id=1, source_target_pairs={{0,24},{1,97},{2,26},{3,99},{4,28},{5,101},{6,30},{7,103},{8,0},{9... | collective-permute-start | bytes 1572872 | tf_op jit(solution)/shard_map/ppermute | solution.py:39
  54.6 4.0 %grad.5 = bf16[512,1024]{1,0:T(8,128)(2,1)} custom-call(s32[2]{0:T(128)S(1)} %pad_add_fusion.2.blocks, bf16[512,8192]{1,0:T(8,128)(2,1)} %refs_1_.5, bf16[512,4096]{1,0:T(8,128)(2,1)} %collective-permute-done.3.theirs, bf16[512,1024]{1,0:T(8,128)(2,1)S(1)} %copy-done, bf16[512,1024]{1,0:T(8,128)(2,1)S(1)} %collective-permute-done.4.cot_theirs, ...), custom_call_target="tpu_custom_call" | custom-call | flops 1073741824 | bytes 4194304 | tf_op jit(solution)/shard_map/grad/pallas_call | solution.py:127
  58.7 1.8 %collective-permute-start.15 = (bf16[512,1024]{1,0:T(8,128)(2,1)}, bf16[512,1024]{1,0:T(8,128)(2,1)}, u32[]{:S(2)}, u32[]{:S(2)}) collective-permute-start(bf16[512,1024]{1,0:T(8,128)(2,1)} %grad.5), channel_id=1, source_target_pairs={{0,2},{1,7},{2,4},{3,1},{4,6},{5,3},{6,0},{7,5},{8,10},{9,15},{10,... | collective-permute-start | bytes 3145736 | tf_op jit(solution)/shard_map/ppermute | solution.py:39
  60.7 1.1 bitcast_dynamic-update-slice_fusion.2
  61.8 4.2 %collective-permute-done.10 = bf16[2,2,64,1024]{3,2,1,0:T(8,128)(2,1)} collective-permute-done((bf16[2,2,64,1024]{3,2,1,0:T(8,128)(2,1)}, bf16[2,2,64,1024]{3,2,1,0:T(8,128)(2,1)}, u32[]{:S(2)}, u32[]{:S(2)}) %collective-permute-start.10) | collective-permute-done | bytes 524320 | tf_op jit(solution)/shard_map/ppermute | solution.py:39
  65.9 1.1 bitcast_dynamic-update-slice_fusion.1
  67.1 2.6 %collective-permute-done.12 = bf16[2,2,64,1024]{3,2,1,0:T(8,128)(2,1)S(1)} collective-permute-done((bf16[2,2,64,1024]{3,2,1,0:T(8,128)(2,1)}, bf16[2,2,64,1024]{3,2,1,0:T(8,128)(2,1)S(1)}, u32[]{:S(2)}, u32[]{:S(2)}) %collective-permute-start.12) | collective-permute-done | bytes 524320 | tf_op jit(solution)/shard_map/ppermute | solution.py:39
  69.8 1.7 %collective-permute-start.18 = (bf16[2,4,2,64,1024]{4,3,2,1,0:T(8,128)(2,1)S(1)}, bf16[2,4,2,64,1024]{4,3,2,1,0:T(8,128)(2,1)}, u32[]{:S(2)}, u32[]{:S(2)}) collective-permute-start(bf16[2,4,2,64,1024]{4,3,2,1,0:T(8,128)(2,1)S(1)} %bitcast_dynamic-update-slice_fusion.3.refs_3_), channel_id=1, source_target_pairs={{0,1},{1,0},{2,3},{3,2},{4,5},{5,4},{6,7},{7,6},{8,9},{9,8},{10,11... | collective-permute-start | bytes 6291464 | tf_op jit(solution)/shard_map/ppermute | solution.py:39
  71.5 2.6 %collective-permute-start.14 = (bf16[2,4,2,64,1024]{4,3,2,1,0:T(8,128)(2,1)S(1)}, bf16[2,4,2,64,1024]{4,3,2,1,0:T(8,128)(2,1)}, u32[]{:S(2)}, u32[]{:S(2)}) collective-permute-start(bf16[2,4,2,64,1024]{4,3,2,1,0:T(8,128)(2,1)S(1)} %bitcast_dynamic-update-slice_fusion.3.refs_3_), channel_id=1, source_target_pairs={{0,96},{1,25},{2,98},{3,27},{4,100},{5,29},{6,102},{7,31},{8,104},... | collective-permute-start | bytes 6291464 | tf_op jit(solution)/shard_map/ppermute | solution.py:39
  74.2 3.4 %collective-permute-start.17 = (bf16[512,1024]{1,0:T(8,128)(2,1)}, bf16[512,1024]{1,0:T(8,128)(2,1)}, u32[]{:S(2)}, u32[]{:S(2)}) collective-permute-start(bf16[512,1024]{1,0:T(8,128)(2,1)} %bitcast.90), channel_id=1, source_target_pairs={{0,2},{1,7},{2,4},{3,1},{4,6},{5,3},{6,0},{7,5},{8,10},{9,15},{10,... | collective-permute-start | bytes 3145736 | tf_op jit(solution)/shard_map/ppermute | solution.py:39
  77.6 1.2 copy-done.2
  78.8 4.3 %grad.6 = bf16[512,1024]{1,0:T(8,128)(2,1)} custom-call(s32[2]{0:T(128)S(1)} %pad_add_fusion.1.blocks, bf16[512,8192]{1,0:T(8,128)(2,1)} %refs_1_.5, bf16[512,4096]{1,0:T(8,128)(2,1)} %collective-permute-done.3.theirs, bf16[512,1024]{1,0:T(8,128)(2,1)S(1)} %copy-done, bf16[512,1024]{1,0:T(8,128)(2,1)S(1)} %copy-done.2, ...), custom_call_target="tpu_custom_call" | custom-call | flops 1073741824 | bytes 4194304 | tf_op jit(solution)/shard_map/grad/pallas_call | solution.py:127
  83.3 1.2 copy-done.3
  84.5 8.8 %grad.7 = (bf16[512,1024]{1,0:T(8,128)(2,1)S(1)}, bf16[3,512,1024]{2,1,0:T(8,128)(2,1)}) custom-call(s32[8]{0:T(128)S(1)} %stack.133.blocks, bf16[512,8192]{1,0:T(8,128)(2,1)} %refs_1_.5, bf16[512,4096]{1,0:T(8,128)(2,1)} %collective-permute-done.3.theirs, bf16[512,1024]{1,0:T(8,128)(2,1)S(1)} %copy-done, bf16[512,1024]{1,0:T(8,128)(2,1)S(1)} %copy-done.3), custom_call_target="tpu_custom_call" | custom-call | flops 4294967296 | bytes 10485760 | tf_op jit(solution)/shard_map/grad/pallas_call | solution.py:127
  93.3 5.1 %fold.3 = (bf16[512,8192]{1,0:T(8,128)(2,1)}, bf16[4,2,64,1024]{3,2,1,0:T(8,128)(2,1)}, f32[512,1024]{1,0:T(8,128)S(1)}) custom-call(s32[5]{0:T(128)S(1)} %stack.111.at.refs_0_, bf16[512,8192]{1,0:T(8,128)(2,1)} %refs_1_.5, bf16[512,1024]{1,0:T(8,128)(2,1)S(1)} %copy-done, bf16[2,4,2,64,1024]{4,3,2,1,0:T(8,128)(2,1)S(1)} %bitcast_dynamic-update-slice_fusion.3.refs_3_, ...), custom_call_target="tpu_custom_call" | custom-call | bytes 1048576 | tf_op jit(solution)/shard_map/fold/pallas_call | solution.py:352
  98.4 2.5 %collective-permute-done.16 = bf16[512,1024]{1,0:T(8,128)(2,1)} collective-permute-done((bf16[512,1024]{1,0:T(8,128)(2,1)}, bf16[512,1024]{1,0:T(8,128)(2,1)}, u32[]{:S(2)}, u32[]{:S(2)}) %collective-permute-start.16) | collective-permute-done | bytes 1048608 | tf_op jit(solution)/shard_map/ppermute | solution.py:39
  100.9 2.0 %collective-permute-start.23 = (bf16[2,4,2,64,1024]{4,3,2,1,0:T(8,128)(2,1)}, bf16[2,4,2,64,1024]{4,3,2,1,0:T(8,128)(2,1)S(1)}, u32[]{:S(2)}, u32[]{:S(2)}) collective-permute-start(bf16[2,4,2,64,1024]{4,3,2,1,0:T(8,128)(2,1)} %collective-permute-done.13.refs_3_), channel_id=1, source_target_pairs={{0,1},{1,0},{2,3},{3,2},{4,5},{5,4},{6,7},{7,6},{8,9},{9,8},{10,11... | collective-permute-start | bytes 6291464 | tf_op jit(solution)/shard_map/ppermute | solution.py:39
  102.9 2.3 %slice_bitcast_fusion.1 = bf16[4,2,64,1024]{3,2,1,0:T(8,128)(2,1)} fusion(bf16[2,4,2,64,1024]{4,3,2,1,0:T(8,128)(2,1)} %collective-permute-done.13.refs_3_), kind=kLoop, calls=%fused_computation.9 | loop fusion | bytes 2097152 | tf_op jit(solution)/shard_map/squeeze | solution.py:462
  105.2 2.3 %slice_bitcast_fusion = bf16[4,2,64,1024]{3,2,1,0:T(8,128)(2,1)} fusion(bf16[2,4,2,64,1024]{4,3,2,1,0:T(8,128)(2,1)} %collective-permute-done.14.refs_4_), kind=kLoop, calls=%fused_computation.8 | loop fusion | bytes 2097152 | tf_op jit(solution)/shard_map/squeeze | solution.py:463
  107.4 1.8 %add_convert_fusion = bf16[512,1024]{1,0:T(8,128)(2,1)S(1)} fusion(bf16[512,1024]{1,0:T(8,128)(2,1)} %collective-permute-done.17, bf16[512,1024]{1,0:T(8,128)(2,1)S(1)} %get-tuple-element.74), kind=kLoop, calls=%fused_computation.7 | loop fusion | flops 2097152 | bytes 3145728 | tf_op jit(solution)/shard_map/convert_element_type | solution.py:470
  109.2 1.8 %collective-permute-start.21 = (bf16[512,1024]{1,0:T(8,128)(2,1)S(1)}, bf16[512,1024]{1,0:T(8,128)(2,1)S(1)}, u32[]{:S(2)}, u32[]{:S(2)}) collective-permute-start(bf16[512,1024]{1,0:T(8,128)(2,1)S(1)} %add_convert_fusion), channel_id=1, source_target_pairs={{0,2},{1,7},{2,4},{3,1},{4,6},{5,3},{6,0},{7,5},{8,10},{9,15},{10,... | collective-permute-start | bytes 3145736 | tf_op jit(solution)/shard_map/ppermute | solution.py:39
  111.0 2.7 %collective-permute-start.20 = (bf16[4,2,64,1024]{3,2,1,0:T(8,128)(2,1)}, bf16[4,2,64,1024]{3,2,1,0:T(8,128)(2,1)S(1)}, u32[]{:S(2)}, u32[]{:S(2)}) collective-permute-start(bf16[4,2,64,1024]{3,2,1,0:T(8,128)(2,1)} %slice_bitcast_fusion), channel_id=1, source_target_pairs={{0,96},{1,25},{2,98},{3,27},{4,100},{5,29},{6,102},{7,31},{8,104},... | collective-permute-start | bytes 3145736 | tf_op jit(solution)/shard_map/ppermute | solution.py:39
  113.7 1.6 %fusion.3 = bf16[512,1024]{1,0:T(8,128)(2,1)S(1)} fusion(bf16[512,1024]{1,0:T(8,128)(2,1)} %collective-permute-done.16, bf16[3,512,1024]{2,1,0:T(8,128)(2,1)S(1)} %copy-done.5), kind=kLoop, calls=%fused_computation.6 | loop fusion | flops 2097152 | bytes 3145728 | tf_op jit(solution)/shard_map/convert_element_type | solution.py:465
  115.5 13.6 %fold.4 = (bf16[512,8192]{1,0:T(8,128)(2,1)}, bf16[4,2,64,1024]{3,2,1,0:T(8,128)(2,1)}, f32[512,1024]{1,0:T(8,128)S(1)}) custom-call(s32[5]{0:T(128)S(1)} %stack.111.at.refs_0_, bf16[512,8192]{1,0:T(8,128)(2,1)} %refs_1_.5, bf16[512,1024]{1,0:T(8,128)(2,1)S(1)} %copy-done, ...), custom_call_target="tpu_custom_call", output_to_operand_aliasing={{0}: (8, {}), {1}: (9, {})} | custom-call | bytes 1048576 | tf_op jit(solution)/shard_map/fold/pallas_call | solution.py:352
  129.1 4.2 %collective-permute-done.22 = bf16[192,1024]{1,0:T(8,128)(2,1)S(1)} collective-permute-done((bf16[192,1024]{1,0:T(8,128)(2,1)S(1)}, bf16[192,1024]{1,0:T(8,128)(2,1)S(1)}, u32[]{:S(2)}, u32[]{:S(2)}) %collective-permute-start.22) | collective-permute-done | bytes 393248 | tf_op jit(solution)/shard_map/ppermute | solution.py:39
  134.8 1.3 collective-permute-done.25.refs_7_
  136.1 1.5 collective-permute-done.26.refs_8_
  137.6 11.7 %fold.5 = (bf16[512,8192]{1,0:T(8,128)(2,1)}, bf16[4,2,64,1024]{3,2,1,0:T(8,128)(2,1)}, bf16[512,1024]{1,0:T(8,128)(2,1)}) custom-call(s32[5]{0:T(128)S(1)} %stack.111.at.refs_0_, bf16[512,8192]{1,0:T(8,128)(2,1)} %refs_1_.5, bf16[512,1024]{1,0:T(8,128)(2,1)S(1)} %copy-done, ...), custom_call_target="tpu_custom_call", output_to_operand_aliasing={{0}: (10, {}), {1}: (11, {})} | custom-call | bytes 1048576 | tf_op jit(solution)/shard_map/fold/pallas_call | solution.py:352
  149.2 1.8 %collective-permute-done.28 = bf16[320,1024]{1,0:T(8,128)(2,1)S(1)} collective-permute-done((bf16[320,1024]{1,0:T(8,128)(2,1)S(1)}, bf16[320,1024]{1,0:T(8,128)(2,1)S(1)}, u32[]{:S(2)}, u32[]{:S(2)}) %collective-permute-start.28) | collective-permute-done | bytes 655392 | tf_op jit(solution)/shard_map/ppermute | solution.py:39
  151.0 1.9 %fusion.1 = f32[1,512,1024]{2,1,0:T(8,128)} fusion(bf16[512,1024]{1,0:T(8,128)(2,1)S(1)} %collective-permute-done.27, bf16[320,1024]{1,0:T(8,128)(2,1)S(1)} %collective-permute-done.28, bf16[192,1024]{1,0:T(8,128)(2,1)S(1)} %collective-permute-done.22, bf16[3,512,1024]{2,1,0:T(8,128)(2,1)S(1)} %copy-done.5), kind=kLoop, calls=%fused_computation.2 | loop fusion | flops 4194304 | bytes 5242880 | tf_op jit(solution)/shard_map/broadcast_in_dim | solution.py:496
  (64 shorter events, 7.7 us)
Async XLA Ops:
  0.7 5.8 %copy-start = (bf16[512,1024]{1,0:T(8,128)(2,1)S(1)}, bf16[512,1024]{1,0:T(8,128)(2,1)}, u32[]{:S(2)}) copy-start(bf16[512,1024]{1,0:T(8,128)(2,1)} %refs_2_.5) | copy-start | bytes 3145732
  0.7 5.9 %copy-start.7 = (bf16[1,512,1024]{2,1,0:T(8,128)(2,1)S(1)}, bf16[1,512,1024]{2,1,0:T(8,128)(2,1)}, u32[]{:S(2)}) copy-start(bf16[1,512,1024]{2,1,0:T(8,128)(2,1)} %param.5) | copy-start | bytes 3145732
  5.1 10.1 %collective-permute-start.3 = (bf16[512,4096]{1,0:T(8,128)(2,1)}, bf16[512,4096]{1,0:T(8,128)(2,1)}, u32[]{:S(2)}, u32[]{:S(2)}) collective-permute-start(bf16[512,4096]{1,0:T(8,128)(2,1)} %half.1), channel_id=1, source_target_pairs={{0,1},{1,0},{2,3},{3,2},{4,5},{5,4},{6,7},{7,6},{8,9},{9,8},{10,11... | collective-permute-start | bytes 12582920 | tf_op jit(solution)/shard_map/ppermute | solution.py:39
  6.6 8.2 %collective-permute-start.4 = (bf16[512,1024]{1,0:T(8,128)(2,1)S(1)}, bf16[512,1024]{1,0:T(8,128)(2,1)S(1)}, u32[]{:S(2)}, u32[]{:S(2)}) collective-permute-start(bf16[512,1024]{1,0:T(8,128)(2,1)S(1)} %copy-done), channel_id=1, source_target_pairs={{0,1},{1,0},{2,3},{3,2},{4,5},{5,4},{6,7},{7,6},{8,9},{9,8},{10,11... | collective-permute-start | bytes 3145736 | tf_op jit(solution)/shard_map/ppermute | solution.py:39
  7.5 14.3 %collective-permute-start = (bf16[2,64,1024]{2,1,0:T(8,128)(2,1)}, bf16[2,64,1024]{2,1,0:T(8,128)(2,1)S(1)}, u32[]{:S(2)}, u32[]{:S(2)}) collective-permute-start(bf16[2,64,1024]{2,1,0:T(8,128)(2,1)} %get-tuple-element.102), channel_id=1, source_target_pairs={{0,64},{1,65},{2,66},{3,67},{4,68},{5,69},{6,70},{7,71},{8,72},{9,... | collective-permute-start | bytes 786440 | tf_op jit(solution)/shard_map/ppermute | solution.py:39
  10.4 12.7 %collective-permute-start.1 = (bf16[2,64,1024]{2,1,0:T(8,128)(2,1)}, bf16[2,64,1024]{2,1,0:T(8,128)(2,1)S(1)}, u32[]{:S(2)}, u32[]{:S(2)}) collective-permute-start(bf16[2,64,1024]{2,1,0:T(8,128)(2,1)} %get-tuple-element.101), channel_id=1, source_target_pairs={{0,32},{1,33},{2,34},{3,35},{4,36},{5,37},{6,38},{7,39},{8,40},{9,... | collective-permute-start | bytes 786440 | tf_op jit(solution)/shard_map/ppermute | solution.py:39
  10.7 12.4 %collective-permute-start.2 = (bf16[2,64,1024]{2,1,0:T(8,128)(2,1)S(1)}, bf16[2,64,1024]{2,1,0:T(8,128)(2,1)S(1)}, u32[]{:S(2)}, u32[]{:S(2)}) collective-permute-start(bf16[2,64,1024]{2,1,0:T(8,128)(2,1)S(1)} %get-tuple-element.100), channel_id=1, source_target_pairs={{0,96},{1,97},{2,98},{3,99},{4,100},{5,101},{6,102},{7,103},{8,104... | collective-permute-start | bytes 786440 | tf_op jit(solution)/shard_map/ppermute | solution.py:39
  14.7 39.9 %copy-start.1 = (bf16[512,1024]{1,0:T(8,128)(2,1)}, bf16[512,1024]{1,0:T(8,128)(2,1)S(1)}, u32[]{:S(2)}) copy-start(bf16[512,1024]{1,0:T(8,128)(2,1)S(1)} %collective-permute-done.4.cot_theirs) | copy-start | bytes 3145732
  20.9 1.0 copy-start.4
  21.9 1.2 copy-start.8
  23.1 0.7 copy-start.9
  23.1 0.8 copy-start.10
  23.9 15.3 %collective-permute-start.7 = (bf16[512,1024]{1,0:T(8,128)(2,1)}, bf16[512,1024]{1,0:T(8,128)(2,1)S(1)}, u32[]{:S(2)}, u32[]{:S(2)}) collective-permute-start(bf16[512,1024]{1,0:T(8,128)(2,1)} %get-tuple-element.57), channel_id=1, source_target_pairs={{0,2},{1,7},{2,4},{3,1},{4,6},{5,3},{6,0},{7,5},{8,10},{9,15},{10,... | collective-permute-start | bytes 3145736 | tf_op jit(solution)/shard_map/ppermute | solution.py:39
  28.0 0.8 copy-start.6
  28.9 7.0 %collective-permute-start.5 = (bf16[64,1024]{1,0:T(8,128)(2,1)S(1)}, bf16[64,1024]{1,0:T(8,128)(2,1)S(1)}, u32[]{:S(2)}, u32[]{:S(2)}) collective-permute-start(bf16[64,1024]{1,0:T(8,128)(2,1)S(1)} %fusion.8), channel_id=1, source_target_pairs={{0,16},{1,17},{2,18},{3,19},{4,20},{5,21},{6,22},{7,23},{8,24},{9,... | collective-permute-start | bytes 393224 | tf_op jit(solution)/shard_map/ppermute | solution.py:39
  37.9 1.3 collective-permute-start.6
  39.2 8.7 %collective-permute-start.8 = (bf16[2,64,1024]{2,1,0:T(8,128)(2,1)S(1)}, bf16[2,64,1024]{2,1,0:T(8,128)(2,1)S(1)}, u32[]{:S(2)}, u32[]{:S(2)}) collective-permute-start(bf16[2,64,1024]{2,1,0:T(8,128)(2,1)S(1)} %maximum_select_fusion), channel_id=1, source_target_pairs={{0,0},{1,5},{2,2},{3,7},{4,4},{5,1},{6,6},{7,3},{8,8},{9,13},{10,1... | collective-permute-start | bytes 786440 | tf_op jit(solution)/shard_map/ppermute | solution.py:39
  43.0 7.7 %collective-permute-start.9 = (bf16[2,64,1024]{2,1,0:T(8,128)(2,1)S(1)}, bf16[2,64,1024]{2,1,0:T(8,128)(2,1)S(1)}, u32[]{:S(2)}, u32[]{:S(2)}) collective-permute-start(bf16[2,64,1024]{2,1,0:T(8,128)(2,1)S(1)} %maximum_select_fusion), channel_id=1, source_target_pairs={{0,6},{1,3},{2,0},{3,5},{4,2},{5,7},{6,4},{7,1},{8,14},{9,11},{10,... | collective-permute-start | bytes 786440 | tf_op jit(solution)/shard_map/ppermute | solution.py:39
  51.5 14.4 %collective-permute-start.10 = (bf16[2,2,64,1024]{3,2,1,0:T(8,128)(2,1)}, bf16[2,2,64,1024]{3,2,1,0:T(8,128)(2,1)}, u32[]{:S(2)}, u32[]{:S(2)}) collective-permute-start(bf16[2,2,64,1024]{3,2,1,0:T(8,128)(2,1)} %pad_maximum_fusion), channel_id=1, source_target_pairs={{0,24},{1,97},{2,26},{3,99},{4,28},{5,101},{6,30},{7,103},{8,0},{9... | collective-permute-start | bytes 1572872 | tf_op jit(solution)/shard_map/ppermute | solution.py:39
  53.9 13.1 %collective-permute-start.11 = (bf16[2,2,64,1024]{3,2,1,0:T(8,128)(2,1)}, bf16[2,2,64,1024]{3,2,1,0:T(8,128)(2,1)S(1)}, u32[]{:S(2)}, u32[]{:S(2)}) collective-permute-start(bf16[2,2,64,1024]{3,2,1,0:T(8,128)(2,1)} %pad_maximum_fusion), channel_id=1, source_target_pairs={{0,16},{1,65},{2,18},{3,67},{4,20},{5,69},{6,22},{7,71},{8,24},{9,... | collective-permute-start | bytes 1572872 | tf_op jit(solution)/shard_map/ppermute | solution.py:39
  54.6 15.1 %collective-permute-start.12 = (bf16[2,2,64,1024]{3,2,1,0:T(8,128)(2,1)}, bf16[2,2,64,1024]{3,2,1,0:T(8,128)(2,1)S(1)}, u32[]{:S(2)}, u32[]{:S(2)}) collective-permute-start(bf16[2,2,64,1024]{3,2,1,0:T(8,128)(2,1)} %pad_maximum_fusion), channel_id=1, source_target_pairs={{0,8},{1,33},{2,10},{3,35},{4,12},{5,37},{6,14},{7,39},{8,16},{9,4... | collective-permute-start | bytes 1572872 | tf_op jit(solution)/shard_map/ppermute | solution.py:39
  58.7 18.9 %collective-permute-start.15 = (bf16[512,1024]{1,0:T(8,128)(2,1)}, bf16[512,1024]{1,0:T(8,128)(2,1)}, u32[]{:S(2)}, u32[]{:S(2)}) collective-permute-start(bf16[512,1024]{1,0:T(8,128)(2,1)} %grad.5), channel_id=1, source_target_pairs={{0,2},{1,7},{2,4},{3,1},{4,6},{5,3},{6,0},{7,5},{8,10},{9,15},{10,... | collective-permute-start | bytes 3145736 | tf_op jit(solution)/shard_map/ppermute | solution.py:39
  69.8 23.5 %collective-permute-start.18 = (bf16[2,4,2,64,1024]{4,3,2,1,0:T(8,128)(2,1)S(1)}, bf16[2,4,2,64,1024]{4,3,2,1,0:T(8,128)(2,1)}, u32[]{:S(2)}, u32[]{:S(2)}) collective-permute-start(bf16[2,4,2,64,1024]{4,3,2,1,0:T(8,128)(2,1)S(1)} %bitcast_dynamic-update-slice_fusion.3.refs_3_), channel_id=1, source_target_pairs={{0,1},{1,0},{2,3},{3,2},{4,5},{5,4},{6,7},{7,6},{8,9},{9,8},{10,11... | collective-permute-start | bytes 6291464 | tf_op jit(solution)/shard_map/ppermute | solution.py:39
  71.4 29.4 %collective-permute-start.13 = (bf16[2,4,2,64,1024]{4,3,2,1,0:T(8,128)(2,1)S(1)}, bf16[2,4,2,64,1024]{4,3,2,1,0:T(8,128)(2,1)}, u32[]{:S(2)}, u32[]{:S(2)}) collective-permute-start(bf16[2,4,2,64,1024]{4,3,2,1,0:T(8,128)(2,1)S(1)} %bitcast_dynamic-update-slice_fusion.3.refs_3_), channel_id=1, source_target_pairs={{0,32},{1,9},{2,34},{3,11},{4,36},{5,13},{6,38},{7,15},{8,40},{9,1... | collective-permute-start | bytes 6291464 | tf_op jit(solution)/shard_map/ppermute | solution.py:39
  71.5 29.4 %collective-permute-start.14 = (bf16[2,4,2,64,1024]{4,3,2,1,0:T(8,128)(2,1)S(1)}, bf16[2,4,2,64,1024]{4,3,2,1,0:T(8,128)(2,1)}, u32[]{:S(2)}, u32[]{:S(2)}) collective-permute-start(bf16[2,4,2,64,1024]{4,3,2,1,0:T(8,128)(2,1)S(1)} %bitcast_dynamic-update-slice_fusion.3.refs_3_), channel_id=1, source_target_pairs={{0,96},{1,25},{2,98},{3,27},{4,100},{5,29},{6,102},{7,31},{8,104},... | collective-permute-start | bytes 6291464 | tf_op jit(solution)/shard_map/ppermute | solution.py:39
  74.2 24.2 %collective-permute-start.17 = (bf16[512,1024]{1,0:T(8,128)(2,1)}, bf16[512,1024]{1,0:T(8,128)(2,1)}, u32[]{:S(2)}, u32[]{:S(2)}) collective-permute-start(bf16[512,1024]{1,0:T(8,128)(2,1)} %bitcast.90), channel_id=1, source_target_pairs={{0,2},{1,7},{2,4},{3,1},{4,6},{5,3},{6,0},{7,5},{8,10},{9,15},{10,... | collective-permute-start | bytes 3145736 | tf_op jit(solution)/shard_map/ppermute | solution.py:39
  77.6 1.2 copy-start.2
  83.1 17.7 %collective-permute-start.16 = (bf16[512,1024]{1,0:T(8,128)(2,1)}, bf16[512,1024]{1,0:T(8,128)(2,1)}, u32[]{:S(2)}, u32[]{:S(2)}) collective-permute-start(bf16[512,1024]{1,0:T(8,128)(2,1)} %grad.6), channel_id=1, source_target_pairs={{0,2},{1,7},{2,4},{3,1},{4,6},{5,3},{6,0},{7,5},{8,10},{9,15},{10,... | collective-permute-start | bytes 3145736 | tf_op jit(solution)/shard_map/ppermute | solution.py:39
  83.3 1.2 copy-start.3
  100.9 14.5 %collective-permute-start.23 = (bf16[2,4,2,64,1024]{4,3,2,1,0:T(8,128)(2,1)}, bf16[2,4,2,64,1024]{4,3,2,1,0:T(8,128)(2,1)S(1)}, u32[]{:S(2)}, u32[]{:S(2)}) collective-permute-start(bf16[2,4,2,64,1024]{4,3,2,1,0:T(8,128)(2,1)} %collective-permute-done.13.refs_3_), channel_id=1, source_target_pairs={{0,1},{1,0},{2,3},{3,2},{4,5},{5,4},{6,7},{7,6},{8,9},{9,8},{10,11... | collective-permute-start | bytes 6291464 | tf_op jit(solution)/shard_map/ppermute | solution.py:39
  102.8 12.7 %collective-permute-start.24 = (bf16[2,4,2,64,1024]{4,3,2,1,0:T(8,128)(2,1)}, bf16[2,4,2,64,1024]{4,3,2,1,0:T(8,128)(2,1)S(1)}, u32[]{:S(2)}, u32[]{:S(2)}) collective-permute-start(bf16[2,4,2,64,1024]{4,3,2,1,0:T(8,128)(2,1)} %collective-permute-done.14.refs_4_), channel_id=1, source_target_pairs={{0,1},{1,0},{2,3},{3,2},{4,5},{5,4},{6,7},{7,6},{8,9},{9,8},{10,11... | collective-permute-start | bytes 6291464 | tf_op jit(solution)/shard_map/ppermute | solution.py:39
  107.4 6.3 %copy-start.5 = (bf16[3,512,1024]{2,1,0:T(8,128)(2,1)S(1)}, bf16[3,512,1024]{2,1,0:T(8,128)(2,1)}, u32[]{:S(2)}) copy-start(bf16[3,512,1024]{2,1,0:T(8,128)(2,1)} %get-tuple-element.76) | copy-start | bytes 9437188
  109.2 24.1 %collective-permute-start.21 = (bf16[512,1024]{1,0:T(8,128)(2,1)S(1)}, bf16[512,1024]{1,0:T(8,128)(2,1)S(1)}, u32[]{:S(2)}, u32[]{:S(2)}) collective-permute-start(bf16[512,1024]{1,0:T(8,128)(2,1)S(1)} %add_convert_fusion), channel_id=1, source_target_pairs={{0,2},{1,7},{2,4},{3,1},{4,6},{5,3},{6,0},{7,5},{8,10},{9,15},{10,... | collective-permute-start | bytes 3145736 | tf_op jit(solution)/shard_map/ppermute | solution.py:39
  111.0 22.3 %collective-permute-start.19 = (bf16[4,2,64,1024]{3,2,1,0:T(8,128)(2,1)}, bf16[4,2,64,1024]{3,2,1,0:T(8,128)(2,1)S(1)}, u32[]{:S(2)}, u32[]{:S(2)}) collective-permute-start(bf16[4,2,64,1024]{3,2,1,0:T(8,128)(2,1)} %slice_bitcast_fusion.1), channel_id=1, source_target_pairs={{0,32},{1,9},{2,34},{3,11},{4,36},{5,13},{6,38},{7,15},{8,40},{9,1... | collective-permute-start | bytes 3145736 | tf_op jit(solution)/shard_map/ppermute | solution.py:39
  111.0 22.3 %collective-permute-start.20 = (bf16[4,2,64,1024]{3,2,1,0:T(8,128)(2,1)}, bf16[4,2,64,1024]{3,2,1,0:T(8,128)(2,1)S(1)}, u32[]{:S(2)}, u32[]{:S(2)}) collective-permute-start(bf16[4,2,64,1024]{3,2,1,0:T(8,128)(2,1)} %slice_bitcast_fusion), channel_id=1, source_target_pairs={{0,96},{1,25},{2,98},{3,27},{4,100},{5,29},{6,102},{7,31},{8,104},... | collective-permute-start | bytes 3145736 | tf_op jit(solution)/shard_map/ppermute | solution.py:39
  115.4 17.9 %collective-permute-start.22 = (bf16[192,1024]{1,0:T(8,128)(2,1)S(1)}, bf16[192,1024]{1,0:T(8,128)(2,1)S(1)}, u32[]{:S(2)}, u32[]{:S(2)}) collective-permute-start(bf16[192,1024]{1,0:T(8,128)(2,1)S(1)} %slice.28), channel_id=1, source_target_pairs={{0,8},{1,9},{2,10},{3,11},{4,12},{5,13},{6,14},{7,15},{8,0},{9,1},... | collective-permute-start | bytes 1179656 | tf_op jit(solution)/shard_map/ppermute | solution.py:39
  133.3 2.7 %collective-permute-start.25 = (bf16[4,2,64,1024]{3,2,1,0:T(8,128)(2,1)S(1)}, bf16[4,2,64,1024]{3,2,1,0:T(8,128)(2,1)S(1)}, u32[]{:S(2)}, u32[]{:S(2)}) collective-permute-start(bf16[4,2,64,1024]{3,2,1,0:T(8,128)(2,1)S(1)} %collective-permute-done.19.refs_4_), channel_id=1, source_target_pairs={{0,1},{1,0},{2,3},{3,2},{4,5},{5,4},{6,7},{7,6},{8,9},{9,8},{10,11... | collective-permute-start | bytes 3145736 | tf_op jit(solution)/shard_map/ppermute | solution.py:39
  133.4 4.1 %collective-permute-start.26 = (bf16[4,2,64,1024]{3,2,1,0:T(8,128)(2,1)S(1)}, bf16[4,2,64,1024]{3,2,1,0:T(8,128)(2,1)S(1)}, u32[]{:S(2)}, u32[]{:S(2)}) collective-permute-start(bf16[4,2,64,1024]{3,2,1,0:T(8,128)(2,1)S(1)} %collective-permute-done.20.refs_5_), channel_id=1, source_target_pairs={{0,1},{1,0},{2,3},{3,2},{4,5},{5,4},{6,7},{7,6},{8,9},{9,8},{10,11... | collective-permute-start | bytes 3145736 | tf_op jit(solution)/shard_map/ppermute | solution.py:39
  134.4 16.7 %collective-permute-start.27 = (bf16[512,1024]{1,0:T(8,128)(2,1)S(1)}, bf16[512,1024]{1,0:T(8,128)(2,1)S(1)}, u32[]{:S(2)}, u32[]{:S(2)}) collective-permute-start(bf16[512,1024]{1,0:T(8,128)(2,1)S(1)} %fusion.2), channel_id=1, source_target_pairs={{0,2},{1,7},{2,4},{3,1},{4,6},{5,3},{6,0},{7,5},{8,10},{9,15},{10,... | collective-permute-start | bytes 3145736 | tf_op jit(solution)/shard_map/ppermute | solution.py:39
  134.6 16.4 %collective-permute-start.28 = (bf16[320,1024]{1,0:T(8,128)(2,1)S(1)}, bf16[320,1024]{1,0:T(8,128)(2,1)S(1)}, u32[]{:S(2)}, u32[]{:S(2)}) collective-permute-start(bf16[320,1024]{1,0:T(8,128)(2,1)S(1)} %slice.29), channel_id=1, source_target_pairs={{0,8},{1,9},{2,10},{3,11},{4,12},{5,13},{6,14},{7,15},{8,0},{9,1},... | collective-permute-start | bytes 1966088 | tf_op jit(solution)/shard_map/ppermute | solution.py:39

commit v7 on v6

--- a/solution.py
+++ b/solution.py
@@ -17,8 +17,8 @@
 D = 8192
 COLS = 1024
 SCALE = D ** (-0.5)
-VMEM = 48 * 1024 * 1024
-FOLD_VMEM = 40 * 1024 * 1024
+VMEM = 44 * 1024 * 1024
+FOLD_VMEM = 28 * 1024 * 1024
 ANY = pl.BlockSpec(memory_space=pl.ANY)
 BF = jnp.bfloat16
 F32 = jnp.float32
@@ -456,8 +456,9 @@
 
     carry = fold_of([("x", 0, 0), ("x", 0, 1)], [0], None, False)
     arrived = ring_y(third)
-    mine[1], mine[3], arrived, arrived_b, rest, *carry = lax.optimization_barrier(
-        (mine[1], mine[3], arrived, arrived_b, rest, *carry)
+    summed_b = add(second_b, arrived_b).astype(BF)
+    mine[1], mine[3], arrived, summed_b, rest, *carry = lax.optimization_barrier(
+        (mine[1], mine[3], arrived, summed_b, rest, *carry)
     )
     mine[2, 0] = long_way(mine[1][0], 1)
     mine[2, 1] = long_way(mine[3][1], -1)
@@ -467,7 +468,7 @@
         permute(half, lambda px, pz, py, pc: (px, pz ^ 1, py, pc))
         for half in (crossed[:192], crossed[192:])
     ]
-    arrived_b = ring_y(add(second_b, arrived_b).astype(BF))
+    arrived_b = ring_y(summed_b)
     groups = [("x", s, dy) for s in (1, 3) for dy in range(2)]
     groups += [("z", (1, 3), dy, p) for dy in range(2) for p in range(2)]
     carry = fold_of(groups, [1, 3], carry, False)

time: 154 us -> 152 us (0.987)
  waiting for transfers between devices: 31.9 us -> 27.6 us
    ppermute x29, waiting for transfers between devices: 31.9 us -> 27.6 us  [permute(): return lax.ppermute(value, AXES, pairs)]
    unnamed x22, local copies, waits for them, and re-layouts: 5.01 us -> 7.98 us
  transfers between devices with their start and end apart: 29 -> 29, of which waited for: 14 -> 12; matrix products, arithmetic and copies ran while one was open for 10% -> 9% of each run, Pallas kernels for 35% -> 36%
where the time goes in v7:
time: 152 us; the launch traced here: 151 us
  Pallas kernels  58.4 us (38%)
  starting transfers between devices  39.2 us (26%)
  waiting for transfers between devices  27.6 us (18%)
  local copies, waits for them, and re-layouts  14.2 us (9%)
  other arithmetic  11 us (7%)
    ppermute x29, starting transfers between devices, permute(): return lax.ppermute(value, AXES, pairs)  39.2 us
    pallas_call x3, Pallas kernels, fold(): pl.pallas_call(kernel, out_shape=shapes, in_specs=in_specs, out_specs=[AN...  31.8 us
    ppermute x29, waiting for transfers between devices, permute(): return lax.ppermute(value, AXES, pairs)  27.6 us
    pallas_call x4, Pallas kernels, grad_blocks(): pl.pallas_call(functools.partial(grad_kernel, len(arrived)), out_shape=[j...  22.2 us
    unnamed x22, local copies, waits for them, and re-layouts  7.98 us
    pallas_call x1, Pallas kernels, other_half(): pl.pallas_call(half_kernel, out_shape=jax.ShapeDtypeStruct((TOK, D // 2),...  4.33 us
  transfers between devices with their start and end apart: 29, of which 12 were waited for; matrix products, arithmetic and copies ran while one was open for 9% of the time, Pallas kernels for 36%

profile of v7, /device:TPU:1, one launch (start us, length us, event | category | flops | bytes accessed | tf_op | source)
XLA Modules:
  0.0 151.4 jit_solution(957665350103165533)
XLA Ops:
  0.7 4.3 %half.1 = bf16[512,4096]{1,0:T(8,128)(2,1)} custom-call(s32[5]{0:T(128)S(1)} %stack.111.at.refs_0_, bf16[512,8192]{1,0:T(8,128)(2,1)} %refs_1_.5), custom_call_target="tpu_custom_call" | custom-call | bytes 8388608 | tf_op jit(solution)/shard_map/half/pallas_call | solution.py:82
  5.1 1.5 collective-permute-start.3
  6.7 0.9 dynamic-slice_bitcast_fusion
  7.5 2.8 %collective-permute-start = (bf16[2,64,1024]{2,1,0:T(8,128)(2,1)}, bf16[2,64,1024]{2,1,0:T(8,128)(2,1)S(1)}, u32[]{:S(2)}, u32[]{:S(2)}) collective-permute-start(bf16[2,64,1024]{2,1,0:T(8,128)(2,1)} %get-tuple-element.102), channel_id=1, source_target_pairs={{0,64},{1,65},{2,66},{3,67},{4,68},{5,69},{6,70},{7,71},{8,72},{9,... | collective-permute-start | bytes 786440 | tf_op jit(solution)/shard_map/ppermute | solution.py:39
  10.7 2.4 %collective-permute-start.2 = (bf16[2,64,1024]{2,1,0:T(8,128)(2,1)S(1)}, bf16[2,64,1024]{2,1,0:T(8,128)(2,1)}, u32[]{:S(2)}, u32[]{:S(2)}) collective-permute-start(bf16[2,64,1024]{2,1,0:T(8,128)(2,1)S(1)} %get-tuple-element.100), channel_id=1, source_target_pairs={{0,96},{1,97},{2,98},{3,99},{4,100},{5,101},{6,102},{7,103},{8,104... | collective-permute-start | bytes 786440 | tf_op jit(solution)/shard_map/ppermute | solution.py:39
  13.1 1.6 %collective-permute-done.4.cot_theirs = bf16[512,1024]{1,0:T(8,128)(2,1)S(1)} collective-permute-done((bf16[512,1024]{1,0:T(8,128)(2,1)S(1)}, bf16[512,1024]{1,0:T(8,128)(2,1)S(1)}, u32[]{:S(2)}, u32[]{:S(2)}) %collective-permute-start.4) | collective-permute-done | bytes 1048608 | tf_op jit(solution)/shard_map/ppermute | solution.py:39
  15.2 6.1 %grad.4 = (bf16[512,1024]{1,0:T(8,128)(2,1)}, bf16[1,512,1024]{2,1,0:T(8,128)(2,1)}) custom-call(s32[4]{0:T(128)S(1)} %pad_add_fusion.blocks, bf16[512,8192]{1,0:T(8,128)(2,1)} %refs_1_.5, bf16[512,4096]{1,0:T(8,128)(2,1)} %collective-permute-done.3.theirs, bf16[512,1024]{1,0:T(8,128)(2,1)S(1)} %copy-done.1, ...), custom_call_target="tpu_custom_call" | custom-call | flops 2147483648 | bytes 6291456 | tf_op jit(solution)/shard_map/grad/pallas_call | solution.py:127
  21.3 1.8 %collective-permute-done.1 = bf16[2,64,1024]{2,1,0:T(8,128)(2,1)S(1)} collective-permute-done((bf16[2,64,1024]{2,1,0:T(8,128)(2,1)}, bf16[2,64,1024]{2,1,0:T(8,128)(2,1)S(1)}, u32[]{:S(2)}, u32[]{:S(2)}) %collective-permute-start.1) | collective-permute-done | bytes 262176 | tf_op jit(solution)/shard_map/ppermute | solution.py:39
  23.8 2.8 %collective-permute-start.7 = (bf16[512,1024]{1,0:T(8,128)(2,1)}, bf16[512,1024]{1,0:T(8,128)(2,1)S(1)}, u32[]{:S(2)}, u32[]{:S(2)}) collective-permute-start(bf16[512,1024]{1,0:T(8,128)(2,1)} %get-tuple-element.57), channel_id=1, source_target_pairs={{0,2},{1,7},{2,4},{3,1},{4,6},{5,3},{6,0},{7,5},{8,10},{9,15},{10,... | collective-permute-start | bytes 3145736 | tf_op jit(solution)/shard_map/ppermute | solution.py:39
  26.6 1.3 fusion.5
  28.8 3.7 %collective-permute-start.5 = (bf16[64,1024]{1,0:T(8,128)(2,1)S(1)}, bf16[64,1024]{1,0:T(8,128)(2,1)}, u32[]{:S(2)}, u32[]{:S(2)}) collective-permute-start(bf16[64,1024]{1,0:T(8,128)(2,1)S(1)} %fusion.8), channel_id=1, source_target_pairs={{0,16},{1,17},{2,18},{3,19},{4,20},{5,21},{6,22},{7,23},{8,24},{9,... | collective-permute-start | bytes 393224 | tf_op jit(solution)/shard_map/ppermute | solution.py:39
  32.5 3.4 %collective-permute-done.5 = bf16[64,1024]{1,0:T(8,128)(2,1)} collective-permute-done((bf16[64,1024]{1,0:T(8,128)(2,1)S(1)}, bf16[64,1024]{1,0:T(8,128)(2,1)}, u32[]{:S(2)}, u32[]{:S(2)}) %collective-permute-start.5) | collective-permute-done | bytes 131104 | tf_op jit(solution)/shard_map/ppermute | solution.py:39
  35.8 2.0 %fusion.9 = (bf16[64,1024]{1,0:T(8,128)(2,1)S(1)}, f32[64,1024]{1,0:T(8,128)}, f32[1,1,64,1024]{3,2,1,0:T(8,128)}) fusion(f32[1,1,64,1024]{3,2,1,0:T(8,128)S(1)} %copy-done.7, bf16[64,1024]{1,0:T(8,128)(2,1)} %collective-permute-done.5, f32[2,64,1024]{2,1,0:T(8,128)} %copy-done.5, s32[]{:T(128)S(6)} %select_n.48, f32[1,1,64,1024]{3,2,1,0:T(8,128)} %param.6), kind=kLoop, calls=%fused_computation.32 | loop fusion | flops 655360 | bytes 1572868 | tf_op jit(solution)/shard_map/convert_element_type | solution.py:410
  38.1 1.1 collective-permute-done.6
  39.8 1.0 maximum_select_fusion
  40.9 3.5 %collective-permute-start.8 = (bf16[2,64,1024]{2,1,0:T(8,128)(2,1)S(1)}, bf16[2,64,1024]{2,1,0:T(8,128)(2,1)S(1)}, u32[]{:S(2)}, u32[]{:S(2)}) collective-permute-start(bf16[2,64,1024]{2,1,0:T(8,128)(2,1)S(1)} %maximum_select_fusion), channel_id=1, source_target_pairs={{0,0},{1,5},{2,2},{3,7},{4,4},{5,1},{6,6},{7,3},{8,8},{9,13},{10,1... | collective-permute-start | bytes 786440 | tf_op jit(solution)/shard_map/ppermute | solution.py:39
  44.3 1.0 collective-permute-start.9
  45.3 4.3 %collective-permute-done.8 = bf16[2,64,1024]{2,1,0:T(8,128)(2,1)S(1)} collective-permute-done((bf16[2,64,1024]{2,1,0:T(8,128)(2,1)S(1)}, bf16[2,64,1024]{2,1,0:T(8,128)(2,1)S(1)}, u32[]{:S(2)}, u32[]{:S(2)}) %collective-permute-start.8) | collective-permute-done | bytes 262176 | tf_op jit(solution)/shard_map/ppermute | solution.py:39
  49.6 2.7 %collective-permute-done.9 = bf16[2,64,1024]{2,1,0:T(8,128)(2,1)S(1)} collective-permute-done((bf16[2,64,1024]{2,1,0:T(8,128)(2,1)S(1)}, bf16[2,64,1024]{2,1,0:T(8,128)(2,1)S(1)}, u32[]{:S(2)}, u32[]{:S(2)}) %collective-permute-start.9) | collective-permute-done | bytes 262176 | tf_op jit(solution)/shard_map/ppermute | solution.py:39
  53.1 1.9 %collective-permute-start.10 = (bf16[2,2,64,1024]{3,2,1,0:T(8,128)(2,1)}, bf16[2,2,64,1024]{3,2,1,0:T(8,128)(2,1)}, u32[]{:S(2)}, u32[]{:S(2)}) collective-permute-start(bf16[2,2,64,1024]{3,2,1,0:T(8,128)(2,1)} %pad_maximum_fusion), channel_id=1, source_target_pairs={{0,24},{1,97},{2,26},{3,99},{4,28},{5,101},{6,30},{7,103},{8,0},{9... | collective-permute-start | bytes 1572872 | tf_op jit(solution)/shard_map/ppermute | solution.py:39
  55.1 1.4 collective-permute-start.11
  56.5 4.0 %grad.5 = bf16[512,1024]{1,0:T(8,128)(2,1)} custom-call(s32[2]{0:T(128)S(1)} %pad_add_fusion.2.blocks, bf16[512,8192]{1,0:T(8,128)(2,1)} %refs_1_.5, bf16[512,4096]{1,0:T(8,128)(2,1)} %collective-permute-done.3.theirs, bf16[512,1024]{1,0:T(8,128)(2,1)S(1)} %copy-done.1, bf16[512,1024]{1,0:T(8,128)(2,1)S(1)} %collective-permute-done.4.cot_theirs, ...), custom_call_target="tpu_custom_call" | custom-call | flops 1073741824 | bytes 4194304 | tf_op jit(solution)/shard_map/grad/pallas_call | solution.py:127
  60.5 0.9 collective-permute-start.15
  61.7 1.1 bitcast_dynamic-update-slice_fusion.2
  62.8 4.4 %collective-permute-done.10 = bf16[2,2,64,1024]{3,2,1,0:T(8,128)(2,1)} collective-permute-done((bf16[2,2,64,1024]{3,2,1,0:T(8,128)(2,1)}, bf16[2,2,64,1024]{3,2,1,0:T(8,128)(2,1)}, u32[]{:S(2)}, u32[]{:S(2)}) %collective-permute-start.10) | collective-permute-done | bytes 524320 | tf_op jit(solution)/shard_map/ppermute | solution.py:39
  67.1 1.1 bitcast_dynamic-update-slice_fusion.1
  68.3 2.6 %collective-permute-done.12 = bf16[2,2,64,1024]{3,2,1,0:T(8,128)(2,1)S(1)} collective-permute-done((bf16[2,2,64,1024]{3,2,1,0:T(8,128)(2,1)}, bf16[2,2,64,1024]{3,2,1,0:T(8,128)(2,1)S(1)}, u32[]{:S(2)}, u32[]{:S(2)}) %collective-permute-start.12) | collective-permute-done | bytes 524320 | tf_op jit(solution)/shard_map/ppermute | solution.py:39
  70.9 1.4 collective-permute-start.18
  72.6 2.4 %collective-permute-start.14 = (bf16[2,4,2,64,1024]{4,3,2,1,0:T(8,128)(2,1)S(1)}, bf16[2,4,2,64,1024]{4,3,2,1,0:T(8,128)(2,1)}, u32[]{:S(2)}, u32[]{:S(2)}) collective-permute-start(bf16[2,4,2,64,1024]{4,3,2,1,0:T(8,128)(2,1)S(1)} %bitcast_dynamic-update-slice_fusion.3.refs_3_), channel_id=1, source_target_pairs={{0,96},{1,25},{2,98},{3,27},{4,100},{5,29},{6,102},{7,31},{8,104},... | collective-permute-start | bytes 6291464 | tf_op jit(solution)/shard_map/ppermute | solution.py:39
  75.0 3.4 %collective-permute-start.17 = (bf16[512,1024]{1,0:T(8,128)(2,1)}, bf16[512,1024]{1,0:T(8,128)(2,1)}, u32[]{:S(2)}, u32[]{:S(2)}) collective-permute-start(bf16[512,1024]{1,0:T(8,128)(2,1)} %bitcast.15), channel_id=1, source_target_pairs={{0,2},{1,7},{2,4},{3,1},{4,6},{5,3},{6,0},{7,5},{8,10},{9,15},{10,... | collective-permute-start | bytes 3145736 | tf_op jit(solution)/shard_map/ppermute | solution.py:39
  78.4 1.2 copy-done.3
  79.7 4.4 %grad.6 = bf16[512,1024]{1,0:T(8,128)(2,1)} custom-call(s32[2]{0:T(128)S(1)} %pad_add_fusion.1.blocks, bf16[512,8192]{1,0:T(8,128)(2,1)} %refs_1_.5, bf16[512,4096]{1,0:T(8,128)(2,1)} %collective-permute-done.3.theirs, bf16[512,1024]{1,0:T(8,128)(2,1)S(1)} %copy-done.1, bf16[512,1024]{1,0:T(8,128)(2,1)S(1)} %copy-done.3, ...), custom_call_target="tpu_custom_call" | custom-call | flops 1073741824 | bytes 4194304 | tf_op jit(solution)/shard_map/grad/pallas_call | solution.py:127
  84.1 1.2 copy-done.4
  85.3 7.8 %grad.7 = (bf16[512,1024]{1,0:T(8,128)(2,1)S(1)}, bf16[3,512,1024]{2,1,0:T(8,128)(2,1)S(1)}) custom-call(s32[8]{0:T(128)S(1)} %stack.133.blocks, bf16[512,8192]{1,0:T(8,128)(2,1)} %refs_1_.5, bf16[512,4096]{1,0:T(8,128)(2,1)} %collective-permute-done.3.theirs, bf16[512,1024]{1,0:T(8,128)(2,1)S(1)} %copy-done.1, bf16[512,1024]{1,0:T(8,128)(2,1)S(1)} %copy-done.4), custom_call_target="tpu_custom_call" | custom-call | flops 4294967296 | bytes 10485760 | tf_op jit(solution)/shard_map/grad/pallas_call | solution.py:127
  93.1 1.6 %add_convert_fusion = bf16[512,1024]{1,0:T(8,128)(2,1)S(1)} fusion(bf16[512,1024]{1,0:T(8,128)(2,1)} %collective-permute-done.17, bf16[512,1024]{1,0:T(8,128)(2,1)S(1)} %get-tuple-element.67), kind=kLoop, calls=%fused_computation.7 | loop fusion | flops 2097152 | bytes 3145728 | tf_op jit(solution)/shard_map/convert_element_type | solution.py:459
  94.8 3.4 %copy-done = bf16[512,8192]{1,0:T(8,128)(2,1)S(1)} copy-done((bf16[512,8192]{1,0:T(8,128)(2,1)S(1)}, bf16[512,8192]{1,0:T(8,128)(2,1)}, u32[]{:S(2)}) %copy-start) | copy-done | bytes 8388632
  98.2 5.1 %fold.3 = (bf16[512,8192]{1,0:T(8,128)(2,1)}, bf16[4,2,64,1024]{3,2,1,0:T(8,128)(2,1)}, f32[512,1024]{1,0:T(8,128)S(1)}) custom-call(s32[5]{0:T(128)S(1)} %stack.111.at.refs_0_, bf16[512,8192]{1,0:T(8,128)(2,1)S(1)} %copy-done, bf16[512,1024]{1,0:T(8,128)(2,1)S(1)} %copy-done.1, bf16[2,4,2,64,1024]{4,3,2,1,0:T(8,128)(2,1)S(1)} %bitcast_dynamic-update-slice_fusion.3.refs_3_, ...), custom_call_target="tpu_custom_call" | custom-call | bytes 1048576 | tf_op jit(solution)/shard_map/fold/pallas_call | solution.py:352
  103.9 1.3 slice_bitcast_fusion.1
  105.7 1.3 slice_bitcast_fusion
  107.0 2.3 %collective-permute-start.20 = (bf16[4,2,64,1024]{3,2,1,0:T(8,128)(2,1)S(1)}, bf16[4,2,64,1024]{3,2,1,0:T(8,128)(2,1)S(1)}, u32[]{:S(2)}, u32[]{:S(2)}) collective-permute-start(bf16[4,2,64,1024]{3,2,1,0:T(8,128)(2,1)S(1)} %slice_bitcast_fusion), channel_id=1, source_target_pairs={{0,96},{1,25},{2,98},{3,27},{4,100},{5,29},{6,102},{7,31},{8,104},... | collective-permute-start | bytes 3145736 | tf_op jit(solution)/shard_map/ppermute | solution.py:39
  109.3 1.5 %collective-permute-start.21 = (bf16[512,1024]{1,0:T(8,128)(2,1)S(1)}, bf16[512,1024]{1,0:T(8,128)(2,1)S(1)}, u32[]{:S(2)}, u32[]{:S(2)}) collective-permute-start(bf16[512,1024]{1,0:T(8,128)(2,1)S(1)} %add_convert_fusion), channel_id=1, source_target_pairs={{0,2},{1,7},{2,4},{3,1},{4,6},{5,3},{6,0},{7,5},{8,10},{9,15},{10,... | collective-permute-start | bytes 3145736 | tf_op jit(solution)/shard_map/ppermute | solution.py:39
  110.9 1.6 %fusion.3 = bf16[512,1024]{1,0:T(8,128)(2,1)S(1)} fusion(bf16[512,1024]{1,0:T(8,128)(2,1)} %collective-permute-done.16, bf16[3,512,1024]{2,1,0:T(8,128)(2,1)S(1)} %get-tuple-element.76), kind=kLoop, calls=%fused_computation.6 | loop fusion | flops 2097152 | bytes 3145728 | tf_op jit(solution)/shard_map/convert_element_type | solution.py:466
  113.2 14.5 %fold.4 = (bf16[512,8192]{1,0:T(8,128)(2,1)}, bf16[4,2,64,1024]{3,2,1,0:T(8,128)(2,1)}, f32[512,1024]{1,0:T(8,128)S(1)}) custom-call(s32[5]{0:T(128)S(1)} %stack.111.at.refs_0_, bf16[512,8192]{1,0:T(8,128)(2,1)S(1)} %copy-done, bf16[512,1024]{1,0:T(8,128)(2,1)S(1)} %copy-done.1, ...), custom_call_target="tpu_custom_call", output_to_operand_aliasing={{0}: (8, {}), {1}: (9, {})} | custom-call | bytes 1048576 | tf_op jit(solution)/shard_map/fold/pallas_call | solution.py:352
  127.7 1.4 collective-permute-done.22
  130.2 3.0 %collective-permute-start.27 = (bf16[512,1024]{1,0:T(8,128)(2,1)S(1)}, bf16[512,1024]{1,0:T(8,128)(2,1)S(1)}, u32[]{:S(2)}, u32[]{:S(2)}) collective-permute-start(bf16[512,1024]{1,0:T(8,128)(2,1)S(1)} %fusion.2), channel_id=1, source_target_pairs={{0,2},{1,7},{2,4},{3,1},{4,6},{5,3},{6,0},{7,5},{8,10},{9,15},{10,... | collective-permute-start | bytes 3145736 | tf_op jit(solution)/shard_map/ppermute | solution.py:39
  133.4 12.2 %fold.5 = (bf16[512,8192]{1,0:T(8,128)(2,1)}, bf16[4,2,64,1024]{3,2,1,0:T(8,128)(2,1)}, bf16[512,1024]{1,0:T(8,128)(2,1)}) custom-call(s32[5]{0:T(128)S(1)} %stack.111.at.refs_0_, bf16[512,8192]{1,0:T(8,128)(2,1)S(1)} %copy-done, bf16[512,1024]{1,0:T(8,128)(2,1)S(1)} %copy-done.1, ...), custom_call_target="tpu_custom_call", output_to_operand_aliasing={{0}: (10, {}), {1}: (11, {})} | custom-call | bytes 1048576 | tf_op jit(solution)/shard_map/fold/pallas_call | solution.py:352
  145.6 3.8 %collective-permute-done.28 = bf16[320,1024]{1,0:T(8,128)(2,1)S(1)} collective-permute-done((bf16[320,1024]{1,0:T(8,128)(2,1)S(1)}, bf16[320,1024]{1,0:T(8,128)(2,1)S(1)}, u32[]{:S(2)}, u32[]{:S(2)}) %collective-permute-start.28) | collective-permute-done | bytes 655392 | tf_op jit(solution)/shard_map/ppermute | solution.py:39
  149.4 1.9 %fusion.1 = f32[1,512,1024]{2,1,0:T(8,128)} fusion(bf16[512,1024]{1,0:T(8,128)(2,1)S(1)} %collective-permute-done.27, bf16[320,1024]{1,0:T(8,128)(2,1)S(1)} %collective-permute-done.28, bf16[192,1024]{1,0:T(8,128)(2,1)S(1)} %collective-permute-done.22, bf16[3,512,1024]{2,1,0:T(8,128)(2,1)S(1)} %get-tuple-element.76), kind=kLoop, calls=%fused_computation.2 | loop fusion | flops 4194304 | bytes 5242880 | tf_op jit(solution)/shard_map/broadcast_in_dim | solution.py:497
  (64 shorter events, 8.2 us)
Async XLA Ops:
  0.7 5.8 %copy-start.1 = (bf16[512,1024]{1,0:T(8,128)(2,1)S(1)}, bf16[512,1024]{1,0:T(8,128)(2,1)}, u32[]{:S(2)}) copy-start(bf16[512,1024]{1,0:T(8,128)(2,1)} %refs_2_.5) | copy-start | bytes 3145732
  0.7 5.9 %copy-start.6 = (bf16[1,512,1024]{2,1,0:T(8,128)(2,1)S(1)}, bf16[1,512,1024]{2,1,0:T(8,128)(2,1)}, u32[]{:S(2)}) copy-start(bf16[1,512,1024]{2,1,0:T(8,128)(2,1)} %param.5) | copy-start | bytes 3145732
  5.1 10.1 %collective-permute-start.3 = (bf16[512,4096]{1,0:T(8,128)(2,1)}, bf16[512,4096]{1,0:T(8,128)(2,1)}, u32[]{:S(2)}, u32[]{:S(2)}) collective-permute-start(bf16[512,4096]{1,0:T(8,128)(2,1)} %half.1), channel_id=1, source_target_pairs={{0,1},{1,0},{2,3},{3,2},{4,5},{5,4},{6,7},{7,6},{8,9},{9,8},{10,11... | collective-permute-start | bytes 12582920 | tf_op jit(solution)/shard_map/ppermute | solution.py:39
  6.6 8.2 %collective-permute-start.4 = (bf16[512,1024]{1,0:T(8,128)(2,1)S(1)}, bf16[512,1024]{1,0:T(8,128)(2,1)S(1)}, u32[]{:S(2)}, u32[]{:S(2)}) collective-permute-start(bf16[512,1024]{1,0:T(8,128)(2,1)S(1)} %copy-done.1), channel_id=1, source_target_pairs={{0,1},{1,0},{2,3},{3,2},{4,5},{5,4},{6,7},{7,6},{8,9},{9,8},{10,11... | collective-permute-start | bytes 3145736 | tf_op jit(solution)/shard_map/ppermute | solution.py:39
  7.5 13.7 %collective-permute-start = (bf16[2,64,1024]{2,1,0:T(8,128)(2,1)}, bf16[2,64,1024]{2,1,0:T(8,128)(2,1)S(1)}, u32[]{:S(2)}, u32[]{:S(2)}) collective-permute-start(bf16[2,64,1024]{2,1,0:T(8,128)(2,1)} %get-tuple-element.102), channel_id=1, source_target_pairs={{0,64},{1,65},{2,66},{3,67},{4,68},{5,69},{6,70},{7,71},{8,72},{9,... | collective-permute-start | bytes 786440 | tf_op jit(solution)/shard_map/ppermute | solution.py:39
  10.4 12.7 %collective-permute-start.1 = (bf16[2,64,1024]{2,1,0:T(8,128)(2,1)}, bf16[2,64,1024]{2,1,0:T(8,128)(2,1)S(1)}, u32[]{:S(2)}, u32[]{:S(2)}) collective-permute-start(bf16[2,64,1024]{2,1,0:T(8,128)(2,1)} %get-tuple-element.101), channel_id=1, source_target_pairs={{0,32},{1,33},{2,34},{3,35},{4,36},{5,37},{6,38},{7,39},{8,40},{9,... | collective-permute-start | bytes 786440 | tf_op jit(solution)/shard_map/ppermute | solution.py:39
  10.7 12.4 %collective-permute-start.2 = (bf16[2,64,1024]{2,1,0:T(8,128)(2,1)S(1)}, bf16[2,64,1024]{2,1,0:T(8,128)(2,1)}, u32[]{:S(2)}, u32[]{:S(2)}) collective-permute-start(bf16[2,64,1024]{2,1,0:T(8,128)(2,1)S(1)} %get-tuple-element.100), channel_id=1, source_target_pairs={{0,96},{1,97},{2,98},{3,99},{4,100},{5,101},{6,102},{7,103},{8,104... | collective-permute-start | bytes 786440 | tf_op jit(solution)/shard_map/ppermute | solution.py:39
  13.1 22.7 %copy-start.7 = (f32[1,1,64,1024]{3,2,1,0:T(8,128)S(1)}, f32[1,1,64,1024]{3,2,1,0:T(8,128)}, u32[]{:S(2)}) copy-start(f32[1,1,64,1024]{3,2,1,0:T(8,128)} %param.7) | copy-start | bytes 786436
  14.7 41.7 %copy-start.2 = (bf16[512,1024]{1,0:T(8,128)(2,1)}, bf16[512,1024]{1,0:T(8,128)(2,1)S(1)}, u32[]{:S(2)}) copy-start(bf16[512,1024]{1,0:T(8,128)(2,1)S(1)} %collective-permute-done.4.cot_theirs) | copy-start | bytes 3145732
  21.3 1.8 %copy-start.8 = (bf16[2,64,1024]{2,1,0:T(8,128)(2,1)}, bf16[2,64,1024]{2,1,0:T(8,128)(2,1)S(1)}, u32[]{:S(2)}) copy-start(bf16[2,64,1024]{2,1,0:T(8,128)(2,1)S(1)} %collective-permute-done) | copy-start | bytes 786436
  23.1 0.7 copy-start.9
  23.8 15.4 %collective-permute-start.7 = (bf16[512,1024]{1,0:T(8,128)(2,1)}, bf16[512,1024]{1,0:T(8,128)(2,1)S(1)}, u32[]{:S(2)}, u32[]{:S(2)}) collective-permute-start(bf16[512,1024]{1,0:T(8,128)(2,1)} %get-tuple-element.57), channel_id=1, source_target_pairs={{0,2},{1,7},{2,4},{3,1},{4,6},{5,3},{6,0},{7,5},{8,10},{9,15},{10,... | collective-permute-start | bytes 3145736 | tf_op jit(solution)/shard_map/ppermute | solution.py:39
  28.0 0.8 copy-start.5
  28.8 7.1 %collective-permute-start.5 = (bf16[64,1024]{1,0:T(8,128)(2,1)S(1)}, bf16[64,1024]{1,0:T(8,128)(2,1)}, u32[]{:S(2)}, u32[]{:S(2)}) collective-permute-start(bf16[64,1024]{1,0:T(8,128)(2,1)S(1)} %fusion.8), channel_id=1, source_target_pairs={{0,16},{1,17},{2,18},{3,19},{4,20},{5,21},{6,22},{7,23},{8,24},{9,... | collective-permute-start | bytes 393224 | tf_op jit(solution)/shard_map/ppermute | solution.py:39
  37.8 1.3 collective-permute-start.6
  39.2 0.7 copy-start.10
  40.9 8.7 %collective-permute-start.8 = (bf16[2,64,1024]{2,1,0:T(8,128)(2,1)S(1)}, bf16[2,64,1024]{2,1,0:T(8,128)(2,1)S(1)}, u32[]{:S(2)}, u32[]{:S(2)}) collective-permute-start(bf16[2,64,1024]{2,1,0:T(8,128)(2,1)S(1)} %maximum_select_fusion), channel_id=1, source_target_pairs={{0,0},{1,5},{2,2},{3,7},{4,4},{5,1},{6,6},{7,3},{8,8},{9,13},{10,1... | collective-permute-start | bytes 786440 | tf_op jit(solution)/shard_map/ppermute | solution.py:39
  44.3 8.0 %collective-permute-start.9 = (bf16[2,64,1024]{2,1,0:T(8,128)(2,1)S(1)}, bf16[2,64,1024]{2,1,0:T(8,128)(2,1)S(1)}, u32[]{:S(2)}, u32[]{:S(2)}) collective-permute-start(bf16[2,64,1024]{2,1,0:T(8,128)(2,1)S(1)} %maximum_select_fusion), channel_id=1, source_target_pairs={{0,6},{1,3},{2,0},{3,5},{4,2},{5,7},{6,4},{7,1},{8,14},{9,11},{10,... | collective-permute-start | bytes 786440 | tf_op jit(solution)/shard_map/ppermute | solution.py:39
  53.1 14.0 %collective-permute-start.10 = (bf16[2,2,64,1024]{3,2,1,0:T(8,128)(2,1)}, bf16[2,2,64,1024]{3,2,1,0:T(8,128)(2,1)}, u32[]{:S(2)}, u32[]{:S(2)}) collective-permute-start(bf16[2,2,64,1024]{3,2,1,0:T(8,128)(2,1)} %pad_maximum_fusion), channel_id=1, source_target_pairs={{0,24},{1,97},{2,26},{3,99},{4,28},{5,101},{6,30},{7,103},{8,0},{9... | collective-permute-start | bytes 1572872 | tf_op jit(solution)/shard_map/ppermute | solution.py:39
  55.1 13.1 %collective-permute-start.11 = (bf16[2,2,64,1024]{3,2,1,0:T(8,128)(2,1)}, bf16[2,2,64,1024]{3,2,1,0:T(8,128)(2,1)S(1)}, u32[]{:S(2)}, u32[]{:S(2)}) collective-permute-start(bf16[2,2,64,1024]{3,2,1,0:T(8,128)(2,1)} %pad_maximum_fusion), channel_id=1, source_target_pairs={{0,16},{1,65},{2,18},{3,67},{4,20},{5,69},{6,22},{7,71},{8,24},{9,... | collective-permute-start | bytes 1572872 | tf_op jit(solution)/shard_map/ppermute | solution.py:39
  56.5 14.4 %collective-permute-start.12 = (bf16[2,2,64,1024]{3,2,1,0:T(8,128)(2,1)}, bf16[2,2,64,1024]{3,2,1,0:T(8,128)(2,1)S(1)}, u32[]{:S(2)}, u32[]{:S(2)}) collective-permute-start(bf16[2,2,64,1024]{3,2,1,0:T(8,128)(2,1)} %pad_maximum_fusion), channel_id=1, source_target_pairs={{0,8},{1,33},{2,10},{3,35},{4,12},{5,37},{6,14},{7,39},{8,16},{9,4... | collective-permute-start | bytes 1572872 | tf_op jit(solution)/shard_map/ppermute | solution.py:39
  60.5 18.0 %collective-permute-start.15 = (bf16[512,1024]{1,0:T(8,128)(2,1)}, bf16[512,1024]{1,0:T(8,128)(2,1)}, u32[]{:S(2)}, u32[]{:S(2)}) collective-permute-start(bf16[512,1024]{1,0:T(8,128)(2,1)} %grad.5), channel_id=1, source_target_pairs={{0,2},{1,7},{2,4},{3,1},{4,6},{5,3},{6,0},{7,5},{8,10},{9,15},{10,... | collective-permute-start | bytes 3145736 | tf_op jit(solution)/shard_map/ppermute | solution.py:39
  70.9 23.9 %collective-permute-start.18 = (bf16[2,4,2,64,1024]{4,3,2,1,0:T(8,128)(2,1)S(1)}, bf16[2,4,2,64,1024]{4,3,2,1,0:T(8,128)(2,1)}, u32[]{:S(2)}, u32[]{:S(2)}) collective-permute-start(bf16[2,4,2,64,1024]{4,3,2,1,0:T(8,128)(2,1)S(1)} %bitcast_dynamic-update-slice_fusion.3.refs_3_), channel_id=1, source_target_pairs={{0,1},{1,0},{2,3},{3,2},{4,5},{5,4},{6,7},{7,6},{8,9},{9,8},{10,11... | collective-permute-start | bytes 6291464 | tf_op jit(solution)/shard_map/ppermute | solution.py:39
  72.3 31.0 %collective-permute-start.13 = (bf16[2,4,2,64,1024]{4,3,2,1,0:T(8,128)(2,1)S(1)}, bf16[2,4,2,64,1024]{4,3,2,1,0:T(8,128)(2,1)}, u32[]{:S(2)}, u32[]{:S(2)}) collective-permute-start(bf16[2,4,2,64,1024]{4,3,2,1,0:T(8,128)(2,1)S(1)} %bitcast_dynamic-update-slice_fusion.3.refs_3_), channel_id=1, source_target_pairs={{0,32},{1,9},{2,34},{3,11},{4,36},{5,13},{6,38},{7,15},{8,40},{9,1... | collective-permute-start | bytes 6291464 | tf_op jit(solution)/shard_map/ppermute | solution.py:39
  72.6 30.8 %collective-permute-start.14 = (bf16[2,4,2,64,1024]{4,3,2,1,0:T(8,128)(2,1)S(1)}, bf16[2,4,2,64,1024]{4,3,2,1,0:T(8,128)(2,1)}, u32[]{:S(2)}, u32[]{:S(2)}) collective-permute-start(bf16[2,4,2,64,1024]{4,3,2,1,0:T(8,128)(2,1)S(1)} %bitcast_dynamic-update-slice_fusion.3.refs_3_), channel_id=1, source_target_pairs={{0,96},{1,25},{2,98},{3,27},{4,100},{5,29},{6,102},{7,31},{8,104},... | collective-permute-start | bytes 6291464 | tf_op jit(solution)/shard_map/ppermute | solution.py:39
  75.0 18.1 %collective-permute-start.17 = (bf16[512,1024]{1,0:T(8,128)(2,1)}, bf16[512,1024]{1,0:T(8,128)(2,1)}, u32[]{:S(2)}, u32[]{:S(2)}) collective-permute-start(bf16[512,1024]{1,0:T(8,128)(2,1)} %bitcast.15), channel_id=1, source_target_pairs={{0,2},{1,7},{2,4},{3,1},{4,6},{5,3},{6,0},{7,5},{8,10},{9,15},{10,... | collective-permute-start | bytes 3145736 | tf_op jit(solution)/shard_map/ppermute | solution.py:39
  78.4 1.2 copy-start.3
  84.0 19.3 %collective-permute-start.16 = (bf16[512,1024]{1,0:T(8,128)(2,1)}, bf16[512,1024]{1,0:T(8,128)(2,1)}, u32[]{:S(2)}, u32[]{:S(2)}) collective-permute-start(bf16[512,1024]{1,0:T(8,128)(2,1)} %grad.6), channel_id=1, source_target_pairs={{0,2},{1,7},{2,4},{3,1},{4,6},{5,3},{6,0},{7,5},{8,10},{9,15},{10,... | collective-permute-start | bytes 3145736 | tf_op jit(solution)/shard_map/ppermute | solution.py:39
  84.1 1.2 copy-start.4
  94.8 3.4 %copy-start = (bf16[512,8192]{1,0:T(8,128)(2,1)S(1)}, bf16[512,8192]{1,0:T(8,128)(2,1)}, u32[]{:S(2)}) copy-start(bf16[512,8192]{1,0:T(8,128)(2,1)} %refs_1_.5) | copy-start | bytes 25165828
  103.3 9.2 %collective-permute-start.23 = (bf16[2,4,2,64,1024]{4,3,2,1,0:T(8,128)(2,1)}, bf16[2,4,2,64,1024]{4,3,2,1,0:T(8,128)(2,1)S(1)}, u32[]{:S(2)}, u32[]{:S(2)}) collective-permute-start(bf16[2,4,2,64,1024]{4,3,2,1,0:T(8,128)(2,1)} %collective-permute-done.13.refs_3_), channel_id=1, source_target_pairs={{0,1},{1,0},{2,3},{3,2},{4,5},{5,4},{6,7},{7,6},{8,9},{9,8},{10,11... | collective-permute-start | bytes 6291464 | tf_op jit(solution)/shard_map/ppermute | solution.py:39
  103.6 9.6 %collective-permute-start.24 = (bf16[2,4,2,64,1024]{4,3,2,1,0:T(8,128)(2,1)}, bf16[2,4,2,64,1024]{4,3,2,1,0:T(8,128)(2,1)S(1)}, u32[]{:S(2)}, u32[]{:S(2)}) collective-permute-start(bf16[2,4,2,64,1024]{4,3,2,1,0:T(8,128)(2,1)} %collective-permute-done.14.refs_4_), channel_id=1, source_target_pairs={{0,1},{1,0},{2,3},{3,2},{4,5},{5,4},{6,7},{7,6},{8,9},{9,8},{10,11... | collective-permute-start | bytes 6291464 | tf_op jit(solution)/shard_map/ppermute | solution.py:39
  105.2 23.9 %collective-permute-start.19 = (bf16[4,2,64,1024]{3,2,1,0:T(8,128)(2,1)S(1)}, bf16[4,2,64,1024]{3,2,1,0:T(8,128)(2,1)S(1)}, u32[]{:S(2)}, u32[]{:S(2)}) collective-permute-start(bf16[4,2,64,1024]{3,2,1,0:T(8,128)(2,1)S(1)} %slice_bitcast_fusion.1), channel_id=1, source_target_pairs={{0,32},{1,9},{2,34},{3,11},{4,36},{5,13},{6,38},{7,15},{8,40},{9,1... | collective-permute-start | bytes 3145736 | tf_op jit(solution)/shard_map/ppermute | solution.py:39
  107.0 22.2 %collective-permute-start.20 = (bf16[4,2,64,1024]{3,2,1,0:T(8,128)(2,1)S(1)}, bf16[4,2,64,1024]{3,2,1,0:T(8,128)(2,1)S(1)}, u32[]{:S(2)}, u32[]{:S(2)}) collective-permute-start(bf16[4,2,64,1024]{3,2,1,0:T(8,128)(2,1)S(1)} %slice_bitcast_fusion), channel_id=1, source_target_pairs={{0,96},{1,25},{2,98},{3,27},{4,100},{5,29},{6,102},{7,31},{8,104},... | collective-permute-start | bytes 3145736 | tf_op jit(solution)/shard_map/ppermute | solution.py:39
  109.3 19.8 %collective-permute-start.21 = (bf16[512,1024]{1,0:T(8,128)(2,1)S(1)}, bf16[512,1024]{1,0:T(8,128)(2,1)S(1)}, u32[]{:S(2)}, u32[]{:S(2)}) collective-permute-start(bf16[512,1024]{1,0:T(8,128)(2,1)S(1)} %add_convert_fusion), channel_id=1, source_target_pairs={{0,2},{1,7},{2,4},{3,1},{4,6},{5,3},{6,0},{7,5},{8,10},{9,15},{10,... | collective-permute-start | bytes 3145736 | tf_op jit(solution)/shard_map/ppermute | solution.py:39
  112.6 16.6 %collective-permute-start.22 = (bf16[192,1024]{1,0:T(8,128)(2,1)S(1)}, bf16[192,1024]{1,0:T(8,128)(2,1)S(1)}, u32[]{:S(2)}, u32[]{:S(2)}) collective-permute-start(bf16[192,1024]{1,0:T(8,128)(2,1)S(1)} %slice.28), channel_id=1, source_target_pairs={{0,8},{1,9},{2,10},{3,11},{4,12},{5,13},{6,14},{7,15},{8,0},{9,1},... | collective-permute-start | bytes 1179656 | tf_op jit(solution)/shard_map/ppermute | solution.py:39
  129.1 4.2 %collective-permute-start.25 = (bf16[4,2,64,1024]{3,2,1,0:T(8,128)(2,1)S(1)}, bf16[4,2,64,1024]{3,2,1,0:T(8,128)(2,1)S(1)}, u32[]{:S(2)}, u32[]{:S(2)}) collective-permute-start(bf16[4,2,64,1024]{3,2,1,0:T(8,128)(2,1)S(1)} %collective-permute-done.19.refs_4_), channel_id=1, source_target_pairs={{0,1},{1,0},{2,3},{3,2},{4,5},{5,4},{6,7},{7,6},{8,9},{9,8},{10,11... | collective-permute-start | bytes 3145736 | tf_op jit(solution)/shard_map/ppermute | solution.py:39
  129.2 4.1 %collective-permute-start.26 = (bf16[4,2,64,1024]{3,2,1,0:T(8,128)(2,1)S(1)}, bf16[4,2,64,1024]{3,2,1,0:T(8,128)(2,1)S(1)}, u32[]{:S(2)}, u32[]{:S(2)}) collective-permute-start(bf16[4,2,64,1024]{3,2,1,0:T(8,128)(2,1)S(1)} %collective-permute-done.20.refs_5_), channel_id=1, source_target_pairs={{0,1},{1,0},{2,3},{3,2},{4,5},{5,4},{6,7},{7,6},{8,9},{9,8},{10,11... | collective-permute-start | bytes 3145736 | tf_op jit(solution)/shard_map/ppermute | solution.py:39
  130.2 19.3 %collective-permute-start.27 = (bf16[512,1024]{1,0:T(8,128)(2,1)S(1)}, bf16[512,1024]{1,0:T(8,128)(2,1)S(1)}, u32[]{:S(2)}, u32[]{:S(2)}) collective-permute-start(bf16[512,1024]{1,0:T(8,128)(2,1)S(1)} %fusion.2), channel_id=1, source_target_pairs={{0,2},{1,7},{2,4},{3,1},{4,6},{5,3},{6,0},{7,5},{8,10},{9,15},{10,... | collective-permute-start | bytes 3145736 | tf_op jit(solution)/shard_map/ppermute | solution.py:39
  133.2 16.2 %collective-permute-start.28 = (bf16[320,1024]{1,0:T(8,128)(2,1)S(1)}, bf16[320,1024]{1,0:T(8,128)(2,1)S(1)}, u32[]{:S(2)}, u32[]{:S(2)}) collective-permute-start(bf16[320,1024]{1,0:T(8,128)(2,1)S(1)} %slice.29), channel_id=1, source_target_pairs={{0,8},{1,9},{2,10},{3,11},{4,12},{5,13},{6,14},{7,15},{8,0},{9,1},... | collective-permute-start | bytes 1966088 | tf_op jit(solution)/shard_map/ppermute | solution.py:39
